TPU v7x, 32 devices: a whole 2x2x4 slice. The times are simulated.
32 devices in a mesh: gx: 4 (over y, x), gy: 2 (over core), gz: 4 (over z).
Axes of the slice: x: 2, y: 2, z: 4, core: 2. Of those that a mesh axis runs over, the one named last changes fastest.
Arguments:
- volume: bfloat16 [48, 64, 16384], P(None, 'gz', ('gx', 'gy')), may hold values from -6 to 6
- tissue: int32 [32, 8, 4], replicated, may hold values 0 or 1
- w_down1: bfloat16 [8, 64, 48], replicated, may hold values from -0.4375 to 0.4375
- b_down1: float32 [64], replicated, may hold values from -1.5 to 1.5
- w_conv1a: bfloat16 [27, 64, 64], replicated, may hold values from -0.21875 to 0.21875
- b_conv1a: float32 [64], replicated, may hold values from -1.5 to 1.5
- w_conv1b: bfloat16 [27, 64, 64], replicated, may hold values from -0.21875 to 0.21875
- b_conv1b: float32 [64], replicated, may hold values from -1.5 to 1.5
- w_down2: bfloat16 [8, 96, 64], replicated, may hold values from -0.375 to 0.375
- b_down2: float32 [96], replicated, may hold values from -1.5 to 1.5
- w_conv2a: bfloat16 [27, 96, 96], replicated, may hold values from -0.15625 to 0.15625
- b_conv2a: float32 [96], replicated, may hold values from -1.5 to 1.5
- w_conv2b: bfloat16 [27, 96, 96], replicated, may hold values from -0.15625 to 0.15625
- b_conv2b: float32 [96], replicated, may hold values from -1.5 to 1.5
Outputs:
- level_one: bfloat16 [64, 32, 4096], P(None, 'gz', ('gx', 'gy'))
- level_two: bfloat16 [96, 16, 1024], P(None, 'gz', ('gx', 'gy'))
All inputs are finite; a program needn't handle non-finite values.
Results may differ from a plain program's by a relative error of at most 0.012.
Values may be sent and summed in bfloat16 or wider, within the bound.
No kernel may reach another device: no remote copies, remote signals or barrier semaphores. Data moves between devices by JAX's collectives and lax.ppermute only.
A program may use at most 128 MiB of HBM per device.

v0:
```python
import functools

import jax
import jax.numpy as jnp
from jax import lax
from jax.experimental import pallas as pl
from jax.experimental.pallas import tpu as pltpu
from jax.sharding import PartitionSpec as P

CX = 64
CY = 32
X1 = CX // 2
Y1 = CY // 2
X2 = X1 // 2
Y2 = Y1 // 2
Z1 = 8
Z2 = 4
C0 = 48
C1 = 64
C2 = 96
CP = 128
HALO = 6
XB = 10
PITCH1 = 48
PITCH2 = 32
BF = jnp.bfloat16
F32 = jnp.float32
NN = (((1,), (0,)), ((), ()))
NT = (((1,), (1,)), ((), ()))
VMEM_BYTES = 40 * 1024 * 1024


def mm(a, b, dims=NN):
    return lax.dot_general(a, b, dims, preferred_element_type=F32)


def iota(shape, dim):
    return lax.broadcasted_iota(jnp.int32, shape, dim)


def one_hot(flag):
    return jnp.where(flag, 1.0, 0.0).astype(BF)


class Window:
    def __init__(self, n_gy):
        self.one_sided = n_gy == 2
        sides = 1 if self.one_sided else 2
        self.sides = sides
        self.rows = Y1 + HALO * sides
        self.rows_a = self.rows - sides
        self.rows_b = self.rows - 2 * sides
        self.rows_2 = self.rows_b // 2
        self.blocks = 6 if self.one_sided else 8

    def index(self):
        return lax.axis_index("gy") if self.one_sided else 1

    def start_a(self):
        return self.index()

    def start_b(self):
        return 2 * self.index()

    def own(self):
        return HALO * self.index()

    def own_b(self):
        return 4 * self.index()

    def own_2(self):
        return 2 * self.index()

    def shift(self):
        return 2 * self.index()


def mask_rows(tab, y_start, rows, pitch, x_start, x_cells, y_cells, y_shift, window):
    shape = (rows, pitch, 128)
    y_block = lax.div(iota(shape, 0) + (y_start + y_shift), y_cells)
    x_block = lax.div(iota(shape, 1) + (x_start + x_cells), x_cells)
    x_block = jnp.minimum(x_block, XB - 1)
    hit = one_hot(y_block * XB + x_block == iota(shape, 2)).reshape(rows * pitch, 128)
    return mm(hit, tab)


def split_cells(v, dest, first):
    kz = v.shape[0]
    shape = (4 * CX, 4 * CX)
    r = iota(shape, 0)
    a, b, y, x = r // 128, (r // 64) % 2, (r // 32) % 2, r % 32
    select = one_hot((2 * y + b) * CX + 2 * x + a == iota(shape, 1))
    cells = mm(select, v, NT).astype(BF)
    for ab in range(4):
        dest[pl.ds(first, 64), ab * kz : (ab + 1) * kz] = cells[64 * ab : 64 * ab + 64]


def down1_own_kernel(v_ref, w_ref, b_ref, out_ref, wd_ref, cells_ref):
    step = pl.program_id(0)
    steps = pl.num_programs(0)
    z0 = v_ref.shape[1]
    kz = C0 * z0
    lanes = Z1 * C1

    @pl.when(step == 0)
    def _():
        r = iota((kz, 2 * C0), 0)
        l = iota((kz, 2 * C0), 1)
        spread = one_hot((r // z0 == l % C0) & (r % 2 == l // C0))
        keep = (iota((kz, lanes), 0) % z0) // 2 == iota((kz, lanes), 1) // C1
        for ab in range(4):
            pair = w_ref[2 * ab : 2 * ab + 2].reshape(2 * C0, C1)
            wide = jnp.concatenate([pair] * Z1, axis=1)
            wd_ref[ab * kz : (ab + 1) * kz, :] = jnp.where(keep, mm(spread, wide), 0.0).astype(BF)

    for part in range(2):
        v = v_ref[:, :, part * 256 : part * 256 + 256].reshape(kz, 256)
        split_cells(v, cells_ref, pl.multiple_of(step * 128 + part * 64, 64))

    @pl.when(step == steps - 1)
    def _():
        acc = mm(cells_ref[...], wd_ref[...])
        out_ref[...] = jnp.maximum(acc + b_ref[...], 0.0).astype(BF)


def down1_window_kernel(window, v_ref, own_ref, wd_ref, b_ref, tab_ref, out_ref, lo_ref, hi_ref, cells_ref):
    z0 = v_ref.shape[1]
    kz = C0 * z0
    parts = v_ref.shape[2] // 256
    for part in range(parts):
        split_cells(v_ref[:, :, part * 256 : part * 256 + 256].reshape(kz, 256), cells_ref, part * 64)
    acc = mm(cells_ref[...], wd_ref[...])
    halo = jnp.maximum(acc + b_ref[...], 0.0).astype(BF)
    tab = tab_ref[:, 128:256]

    def put(value, start, rows):
        mask = mask_rows(tab, start, rows, X1, 0, 4, 4, window.shift(), window).astype(BF)
        for q in range(4):
            piece = (value[:, q * 128 : q * 128 + 128] * mask).reshape(rows, X1, 128)
            out_ref[pl.ds(start, rows), :, q * 128 : q * 128 + 128] = piece
            if q == 0:
                lo_ref[pl.ds(start, rows)] = piece
            if q == 3:
                hi_ref[pl.ds(start, rows)] = piece

    put(own_ref[...], window.own(), Y1)
    if window.one_sided:
        put(halo, Y1 * (1 - window.index()), HALO)
    else:
        put(halo[: HALO * X1], 0, HALO)
        put(halo[HALO * X1 :], HALO + Y1, HALO)


def banded_kernel(group, chan, pad, w_refs, t_refs):
    for w_ref, t_ref in zip(w_refs, t_refs):
        t_ref[...] = jnp.zeros_like(t_ref)
        for j in range(3):
            for i in range(3):
                for zo in range(group):
                    for k in range(3):
                        lane = i * (group + 2) * pad + (zo + k) * pad
                        t_ref[j, zo * pad : zo * pad + chan, lane : lane + chan] = w_ref[9 * i + 3 * j + k]


def banded(w_first, w_second, group, chan, pad):
    shape = jax.ShapeDtypeStruct((3, group * pad, 3 * (group + 2) * pad), BF)

    def kernel(w1, w2, t1, t2):
        banded_kernel(group, chan, pad, (w1, w2), (t1, t2))

    return pl.pallas_call(
        kernel,
        out_shape=(shape, shape),
        compiler_params=pltpu.CompilerParams(vmem_limit_bytes=VMEM_BYTES),
    )(w_first, w_second)


def conv_group(copies, t_ref, y_first, rows, pitch, lane, group_in, group_out, group_full):
    total = None
    for j in range(3):
        parts = [c[pl.ds(y_first + j, rows), 0:pitch, lane : lane + group_in] for c in copies]
        left = jnp.concatenate([p.reshape(rows * pitch, group_in) for p in parts], axis=1)
        if group_in == group_full:
            right = t_ref[j, 0:group_out, :]
        else:
            right = jnp.concatenate([t_ref[j, 0:group_out, i * group_full : i * group_full + group_in] for i in range(3)], axis=1)
        term = mm(left, right, NT)
        total = term if total is None else total + term
    return total


def fill_copies(copies, pieces, xl_ref, xr_ref, rows, pitch):
    lane = 0
    for ref, first, width in pieces:
        inner = ref[:, :, first : first + width]
        left = xl_ref[:, :, lane : lane + width]
        right = xr_ref[:, :, lane : lane + width]
        cells = inner.shape[1]
        for s in range(3):
            spare = jnp.zeros((rows, pitch - cells - 4 + s, width), BF)
            line = [inner, right, spare] if s == 2 else [left[:, s:], inner, right, spare]
            copies[s][1 : rows + 1, :, lane : lane + width] = jnp.concatenate(line, axis=1)
        lane += width
    for s in range(3):
        edge = jnp.zeros((1, pitch, lane), BF)
        copies[s][0:1] = edge
        copies[s][rows + 1 : rows + 2] = edge


def shift_copies(base, copies, rows, cells):
    for s, copy in enumerate(copies, 1):
        copy[...] = base[:, s : s + cells, :]


def level_one_kernel(
    window, win_ref, zl_ref, zr_ref, xl_ref, xr_ref, ta_ref, tb_ref, ba_ref, bb_ref, wd_ref, bd_ref, tab_ref, tab2_ref,
    one_ref, lo_ref, hi_ref, a0, a1, a2, i0, i1, i2, feat_ref, d_ref,
):
    rows = window.rows
    pieces = [(zl_ref, 0, 128)] + [(win_ref, 128 * q, 128) for q in range(4)] + [(zr_ref, 0, 128)]
    fill_copies((a0, a1, a2), pieces, xl_ref, xr_ref, rows, PITCH1)

    ya, na = window.start_a(), window.rows_a
    mask = mask_rows(tab_ref[...], ya, na, PITCH1, -1, 4, 4, window.shift(), window)
    i0[0:1] = jnp.zeros((1,) + i0.shape[1:], BF)
    i0[rows + 1 : rows + 2] = jnp.zeros((1,) + i0.shape[1:], BF)
    for g, (lane, width, out) in enumerate(((0, 384, 256), (256, 384, 256), (512, 256, 128))):
        acc = conv_group((a0, a1, a2), ta_ref, ya, na, PITCH1, lane, width, out, 384)
        for q in range(out // 128):
            chunk = 2 * g + q
            which = 0 if chunk == 0 else (2 if chunk == 4 else 1)
            value = jnp.maximum(acc[:, q * 128 : q * 128 + 128] + ba_ref[...], 0.0) * mask[:, which * 128 : which * 128 + 128]
            i0[pl.ds(ya + 1, na), :, chunk * 128 : chunk * 128 + 128] = value.astype(BF).reshape(na, PITCH1, 128)

    shift_copies(i0, (i1, i2), rows, X1)
    yb, nb = window.start_b(), window.rows_b
    mask = mask_rows(tab_ref[:, 128:256], yb, nb, X1, 0, 4, 4, window.shift(), window)
    for g in range(2):
        acc = conv_group((i0, i1, i2), tb_ref, yb, nb, X1, 256 * g, 384, 256, 384)
        for q in range(2):
            value = jnp.maximum(acc[:, q * 128 : q * 128 + 128] + bb_ref[...], 0.0) * mask
            feat_ref[:, (2 * g + q) * 128 : (2 * g + q + 1) * 128] = value.astype(BF)

    lanes = Z1 * C1
    r = iota((lanes, lanes), 0)
    order = one_hot((r % Z1) * C1 + r // Z1 == iota((lanes, lanes), 1))
    own = feat_ref[pl.ds(pl.multiple_of(window.own_b() * X1, 128), Y1 * X1), :]
    one_ref[...] = mm(order, own, NT).astype(BF)

    done = 0
    while done < nb:
        n = min(8, nb - done)
        size = n * X1
        quarter = size // 4
        r = iota((size, size), 0)
        ab = r // quarter
        y = (r % quarter) // X2
        select = one_hot((2 * y + ab % 2) * X1 + 2 * (r % X2) + ab // 2 == iota((size, size), 1))
        cells = mm(select, feat_ref[done * X1 : done * X1 + size, :]).astype(BF)
        for q in range(4):
            d_ref[q, done // 2 * X2 : done // 2 * X2 + quarter, :] = cells[q * quarter : (q + 1) * quarter]
        done += n
    n2 = window.rows_2
    mask = mask_rows(tab2_ref[:, 128:256], 0, n2, X2, 0, 2, 2, window.shift(), window)
    for z in range(Z2):
        left = jnp.concatenate([d_ref[q, :, z * 128 : z * 128 + 128] for q in range(4)], axis=1)
        value = (jnp.maximum(mm(left, wd_ref[...]) + bd_ref[...], 0.0) * mask).astype(BF).reshape(n2, X2, CP)
        (lo_ref, hi_ref)[z // 2][:, :, z % 2 * CP : (z % 2 + 1) * CP] = value


def level_two_kernel(
    window, zl_ref, lo_ref, hi_ref, zr_ref, xl_ref, xr_ref, ta_ref, tb_ref, ba_ref, bb_ref, tab_ref,
    out_ref, a0, a1, a2, i0, i1, i2,
):
    rows = window.rows_2
    pieces = [(ref, 128 * q, 128) for ref in (zl_ref, lo_ref, hi_ref, zr_ref) for q in range(2)]
    fill_copies((a0, a1, a2), pieces, xl_ref, xr_ref, rows, PITCH2)
    mask = mask_rows(tab_ref[...], 0, rows, PITCH2, -1, 2, 2, window.shift(), window)
    i0[0:1] = jnp.zeros((1,) + i0.shape[1:], BF)
    i0[rows + 1 : rows + 2] = jnp.zeros((1,) + i0.shape[1:], BF)
    for g in range(3):
        acc = conv_group((a0, a1, a2), ta_ref, 0, rows, PITCH2, 256 * g, 512, 256, 512)
        for q in range(2):
            chunk = 2 * g + q
            which = 0 if chunk == 0 else (2 if chunk == 5 else 1)
            value = jnp.maximum(acc[:, q * 128 : q * 128 + 128] + ba_ref[...], 0.0) * mask[:, which * 128 : which * 128 + 128]
            i0[1 : rows + 1, :, chunk * 128 : chunk * 128 + 128] = value.astype(BF).reshape(rows, PITCH2, 128)
    shift_copies(i0, (i1, i2), rows, X2)
    first = window.own_2()
    mask = mask_rows(tab_ref[:, 128:256], first, Y2, X2, 0, 2, 2, window.shift(), window)
    feat = []
    for g in range(2):
        acc = conv_group((i0, i1, i2), tb_ref, first, Y2, X2, 256 * g, 512, 256, 512)
        for q in range(2):
            feat.append((jnp.maximum(acc[:, q * 128 : q * 128 + 128] + bb_ref[...], 0.0) * mask).astype(BF))
    shape = (C2 * Z2, Z2 * CP)
    r = iota(shape, 0)
    order = one_hot((r % Z2) * CP + r // Z2 == iota(shape, 1))
    out_ref[...] = mm(order, jnp.concatenate(feat, axis=1), NT).astype(BF)


def shift_along(low_edge, high_edge, axis):
    count = lax.axis_size(axis)
    below = lax.ppermute(high_edge, axis, [(i, i + 1) for i in range(count - 1)])
    above = lax.ppermute(low_edge, axis, [(i + 1, i) for i in range(count - 1)])
    return below, above


def params():
    return pltpu.CompilerParams(vmem_limit_bytes=VMEM_BYTES)


def local(
    window, volume, tissue, w_down1, b_down1, w_conv1a, b_conv1a, w_conv1b, b_conv1b,
    w_down2, b_down2, w_conv2a, b_conv2a, w_conv2b, b_conv2b,
):
    index_x = lax.axis_index("gx")
    index_y = lax.axis_index("gy")
    index_z = lax.axis_index("gz")
    depth = volume.shape[1]
    kz = C0 * depth
    send_lanes = 2 * HALO * CX
    last = volume.shape[2] - send_lanes

    if window.one_sided:
        edge = lax.dynamic_slice_in_dim(volume, (1 - index_y) * last, send_lanes, 2)
        halo = lax.ppermute(edge, "gy", [(0, 1), (1, 0)])
    else:
        halo = jnp.concatenate(shift_along(volume[:, :, :send_lanes], volume[:, :, last:], "gy"), axis=2)

    def pad_lanes(value):
        return jnp.pad(value, [(0, 0)] * (value.ndim - 1) + [(0, CP - value.shape[-1])])

    flags = jnp.pad(tissue, ((1, 1), (2, 2), (1, 1)))
    y_first = 2 * index_y if window.one_sided else 4 * index_y
    y_first = y_first + (2 if window.one_sided else 0)
    flags = lax.dynamic_slice(flags, (8 * index_x, y_first, index_z), (XB, window.blocks, 3))
    flags = flags.transpose(1, 0, 2).reshape(window.blocks * XB, 3).astype(BF)
    flags = jnp.pad(flags, ((0, 128 - window.blocks * XB), (0, 0)))
    tab2 = jnp.repeat(flags, 128, axis=1)
    tab1 = jnp.repeat(flags[:, jnp.array([0, 1, 1, 1, 1, 2])], 64, axis=1)

    lanes1 = Z1 * C1
    bias1 = jnp.tile(b_down1, Z1)[None]
    own, wd1 = pl.pallas_call(
        down1_own_kernel,
        grid=(volume.shape[2] // 512,),
        in_specs=[
            pl.BlockSpec((C0, depth, 512), lambda i: (0, 0, i)),
            pl.BlockSpec((8, C0, C1), lambda i: (0, 0, 0)),
            pl.BlockSpec((1, lanes1), lambda i: (0, 0)),
        ],
        out_specs=[
            pl.BlockSpec((Y1 * X1, lanes1), lambda i: (0, 0)),
            pl.BlockSpec((4 * kz, lanes1), lambda i: (0, 0)),
        ],
        out_shape=[
            jax.ShapeDtypeStruct((Y1 * X1, lanes1), BF),
            jax.ShapeDtypeStruct((4 * kz, lanes1), BF),
        ],
        scratch_shapes=[pltpu.VMEM((Y1 * X1, 4 * kz), BF)],
        compiler_params=params(),
    )(volume, jnp.swapaxes(w_down1, 1, 2), bias1)

    rows = window.rows
    win, z_lo, z_hi = pl.pallas_call(
        functools.partial(down1_window_kernel, window),
        out_shape=[
            jax.ShapeDtypeStruct((rows, X1, lanes1), BF),
            jax.ShapeDtypeStruct((rows, X1, 2 * C1), BF),
            jax.ShapeDtypeStruct((rows, X1, 2 * C1), BF),
        ],
        scratch_shapes=[pltpu.VMEM((window.sides * HALO * X1, 4 * kz), BF)],
        compiler_params=params(),
    )(halo, own, wd1, bias1, tab1)

    t1a, t1b = banded(w_conv1a, w_conv1b, 4, C1, C1)
    t2a, t2b = banded(w_conv2a, w_conv2b, 2, C2, CP)

    z_below, z_above = shift_along(z_lo, z_hi, "gz")
    low = jnp.concatenate([z_below[:, :2], win[:, :2], z_above[:, :2]], axis=2)
    high = jnp.concatenate([z_below[:, X1 - 2 :], win[:, X1 - 2 :], z_above[:, X1 - 2 :]], axis=2)
    x_below, x_above = shift_along(low, high, "gx")

    n2 = window.rows_2
    one, d_lo, d_hi = pl.pallas_call(
        functools.partial(level_one_kernel, window),
        out_shape=[
            jax.ShapeDtypeStruct((C1 * Z1, Y1 * X1), BF),
            jax.ShapeDtypeStruct((n2, X2, 2 * CP), BF),
            jax.ShapeDtypeStruct((n2, X2, 2 * CP), BF),
        ],
        scratch_shapes=[pltpu.VMEM((rows + 2, PITCH1, (Z1 + 4) * C1), BF)] * 3
        + [pltpu.VMEM((rows + 2, PITCH1, (Z1 + 2) * C1), BF)]
        + [pltpu.VMEM((rows + 2, X1, (Z1 + 2) * C1), BF)] * 2
        + [pltpu.VMEM((window.rows_b * X1, lanes1), BF), pltpu.VMEM((4, n2 * X2, lanes1), BF)],
        compiler_params=params(),
    )(
        win, z_below, z_above, x_below, x_above, t1a, t1b, jnp.tile(b_conv1a, 2)[None], jnp.tile(b_conv1b, 2)[None],
        pad_lanes(jnp.swapaxes(w_down2, 1, 2).reshape(8 * C1, C2)), pad_lanes(b_down2[None]), tab1, tab2,
    )

    z_below, z_above = shift_along(d_lo, d_hi, "gz")
    line = [z_below, d_lo, d_hi, z_above]
    low = jnp.concatenate([p[:, :2] for p in line], axis=2)
    high = jnp.concatenate([p[:, X2 - 2 :] for p in line], axis=2)
    x_below, x_above = shift_along(low, high, "gx")
    two = pl.pallas_call(
        functools.partial(level_two_kernel, window),
        out_shape=jax.ShapeDtypeStruct((C2 * Z2, Y2 * X2), BF),
        scratch_shapes=[pltpu.VMEM((n2 + 2, PITCH2, (Z2 + 4) * CP), BF)] * 3
        + [pltpu.VMEM((n2 + 2, PITCH2, (Z2 + 2) * CP), BF)]
        + [pltpu.VMEM((n2 + 2, X2, (Z2 + 2) * CP), BF)] * 2,
        compiler_params=params(),
    )(
        z_below, d_lo, d_hi, z_above, x_below, x_above, t2a, t2b, pad_lanes(b_conv2a[None]), pad_lanes(b_conv2b[None]), tab2
    )
    return one.reshape(C1, Z1, Y1 * X1), two.reshape(C2, Z2, Y2 * X2)


def solution(mesh):
    block = P(None, "gz", ("gx", "gy"))
    return jax.shard_map(
        functools.partial(local, Window(mesh.shape["gy"])),
        mesh=mesh,
        in_specs=(block,) + (P(),) * 13,
        out_specs=(block, block),
        check_vma=False,
    )
```

profile of v0, /device:TPU:12, one launch (start us, length us, event | category | flops | bytes accessed | tf_op | source)
XLA Modules:
  0.0 70.0 jit_solution(5194557719972529496)
XLA Ops:
  0.7 2.5 %constant_dynamic-slice_fusion = bf16[48,16,768]{2,1,0:T(8,128)(2,1)} fusion(bf16[48,16,2048]{2,1,0:T(8,128)(2,1)} %v_ref.1, s32[]{:T(128)S(6)} %select_n.15), kind=kLoop, calls=%fused_computation.9 | loop fusion | bytes 2359300 | tf_op jit(solution)/shard_map/dynamic_slice | solution.py:326
  3.2 0.1 fusion.1
  3.3 0.1 convert_element_type.19
  3.4 0.6 gather_fusion
  4.0 0.1 copy.21.tab_ref
  4.1 0.1 broadcast_in_dim_tile.9.b_ref
  4.2 1.9 %copy-done = bf16[48,16,2048]{2,1,0:T(8,128)(2,1)S(1)} copy-done((bf16[48,16,2048]{2,1,0:T(8,128)(2,1)S(1)}, bf16[48,16,2048]{2,1,0:T(8,128)(2,1)}, u32[]{:S(2)}) %copy-start) | copy-done | bytes 3145752
  6.1 4.5 %shard_map.158 = (bf16[512,512]{1,0:T(8,128)(2,1)S(1)}, bf16[3072,512]{1,0:T(8,128)(2,1)S(1)}) custom-call(bf16[48,16,2048]{2,1,0:T(8,128)(2,1)S(1)} %copy-done, bf16[8,48,64]{2,1,0:T(8,128)(2,1)S(1)} %bitcast.16, f32[1,512]{1,0:T(1,128)S(1)} %broadcast_in_dim_tile.9.b_ref), custom_call_target="tpu_custom_call" | custom-call | tf_op jit(solution)/shard_map/pallas_call | solution.py:345
  10.7 1.3 %shard_map.159 = (bf16[22,32,512]{2,1,0:T(8,128)(2,1)S(1)}, bf16[22,32,128]{2,1,0:T(8,128)(2,1)S(1)}, bf16[22,32,128]{2,1,0:T(8,128)(2,1)S(1)}) custom-call(bf16[48,16,768]{2,1,0:T(8,128)(2,1)S(1)} %collective-permute-done.v_ref, bf16[512,512]{1,0:T(8,128)(2,1)S(1)} %get-tuple-element.14.own_ref, bf16[3072,512]{1,0:T(8,128)(2,1)S(1)} %get-tuple-element.15.wd_ref, ...), custom_call_target="tpu_custom_call" | custom-call | tf_op jit(solution)/shard_map/pallas_call | solution.py:366
  11.9 3.5 %collective-permute-start.1 = (bf16[22,32,128]{2,1,0:T(8,128)(2,1)S(1)}, bf16[22,32,128]{2,1,0:T(8,128)(2,1)S(1)}, u32[]{:S(2)}, u32[]{:S(2)}) collective-permute-start(bf16[22,32,128]{2,1,0:T(8,128)(2,1)S(1)} %get-tuple-element.17), channel_id=1, source_target_pairs={{0,1},{1,2},{2,3},{4,5},{5,6},{6,7},{8,9},{9,10},{10,11},{12,13},{... | collective-permute-start | bytes 540680 | tf_op jit(solution)/shard_map/ppermute | solution.py:304
  15.4 2.4 %collective-permute-start.2 = (bf16[22,32,128]{2,1,0:T(8,128)(2,1)S(1)}, bf16[22,32,128]{2,1,0:T(8,128)(2,1)S(1)}, u32[]{:S(2)}, u32[]{:S(2)}) collective-permute-start(bf16[22,32,128]{2,1,0:T(8,128)(2,1)S(1)} %get-tuple-element.18), channel_id=1, source_target_pairs={{1,0},{2,1},{3,2},{5,4},{6,5},{7,6},{9,8},{10,9},{11,10},{13,12},{... | collective-permute-start | bytes 540680 | tf_op jit(solution)/shard_map/ppermute | solution.py:305
  17.8 0.1 fusion.2
  17.9 2.9 %collective-permute-done.1.zl_ref = bf16[22,32,128]{2,1,0:T(8,128)(2,1)S(1)} collective-permute-done((bf16[22,32,128]{2,1,0:T(8,128)(2,1)S(1)}, bf16[22,32,128]{2,1,0:T(8,128)(2,1)S(1)}, u32[]{:S(2)}, u32[]{:S(2)}) %collective-permute-start.1) | collective-permute-done | bytes 180256 | tf_op jit(solution)/shard_map/ppermute | solution.py:304
  20.8 3.2 %collective-permute-done.2.zr_ref = bf16[22,32,128]{2,1,0:T(8,128)(2,1)S(1)} collective-permute-done((bf16[22,32,128]{2,1,0:T(8,128)(2,1)S(1)}, bf16[22,32,128]{2,1,0:T(8,128)(2,1)S(1)}, u32[]{:S(2)}, u32[]{:S(2)}) %collective-permute-start.2) | collective-permute-done | bytes 180256 | tf_op jit(solution)/shard_map/ppermute | solution.py:305
  24.0 0.1 pad_maximum_fusion.1
  24.1 3.3 %collective-permute-start.4 = (bf16[22,2,768]{2,1,0:T(2,128)(2,1)S(1)}, bf16[22,2,768]{2,1,0:T(2,128)(2,1)S(1)}, u32[]{:S(2)}, u32[]{:S(2)}) collective-permute-start(bf16[22,2,768]{2,1,0:T(2,128)(2,1)S(1)} %pad_maximum_fusion.1), channel_id=1, source_target_pairs={{8,0},{16,8},{24,16},{9,1},{17,9},{25,17},{10,2},{18,10},{26,18},{... | collective-permute-start | bytes 202760 | tf_op jit(solution)/shard_map/ppermute | solution.py:305
  27.5 2.7 %collective-permute-start.3 = (bf16[22,2,768]{2,1,0:T(2,128)(2,1)S(1)}, bf16[22,2,768]{2,1,0:T(2,128)(2,1)S(1)}, u32[]{:S(2)}, u32[]{:S(2)}) collective-permute-start(bf16[22,2,768]{2,1,0:T(2,128)(2,1)S(1)} %pad_maximum_fusion), channel_id=1, source_target_pairs={{0,8},{8,16},{16,24},{1,9},{9,17},{17,25},{2,10},{10,18},{18,26},{... | collective-permute-start | bytes 202760 | tf_op jit(solution)/shard_map/ppermute | solution.py:304
  30.3 0.1 copy.23.tab2_ref.tab_ref
  30.4 0.1 broadcast_in_dim_tile.10.ba_ref
  30.5 0.1 broadcast_in_dim_tile.11.bb_ref
  30.6 1.2 %shard_map.160 = (bf16[3,256,1152]{2,1,0:T(8,128)(2,1)S(1)}, bf16[3,256,1152]{2,1,0:T(8,128)(2,1)S(1)}) custom-call(bf16[27,64,64]{2,1,0:T(8,128)(2,1)S(1)} %copy-done.3, bf16[27,64,64]{2,1,0:T(8,128)(2,1)S(1)} %copy-done.4), custom_call_target="tpu_custom_call" | custom-call | tf_op jit(solution)/shard_map/pallas_call | solution.py:171
  31.9 2.7 %collective-permute-done.3.xl_ref = bf16[22,2,768]{2,1,0:T(2,128)(2,1)S(1)} collective-permute-done((bf16[22,2,768]{2,1,0:T(2,128)(2,1)S(1)}, bf16[22,2,768]{2,1,0:T(2,128)(2,1)S(1)}, u32[]{:S(2)}, u32[]{:S(2)}) %collective-permute-start.3) | collective-permute-done | bytes 67616 | tf_op jit(solution)/shard_map/ppermute | solution.py:304
  34.6 10.8 %shard_map.161 = (bf16[512,512]{1,0:T(8,128)(2,1)}, bf16[10,16,256]{2,1,0:T(8,128)(2,1)S(1)}, bf16[10,16,256]{2,1,0:T(8,128)(2,1)S(1)}) custom-call(bf16[22,32,512]{2,1,0:T(8,128)(2,1)S(1)} %get-tuple-element.16.win_ref, bf16[22,32,128]{2,1,0:T(8,128)(2,1)S(1)} %collective-permute-done.1.zl_ref, bf16[22,32,128]{2,1,0:T(8,128)(2,1)S(1)} %collective-permute-done.2.zr_ref, ...), custom_call_target="tpu_custom_call" | custom-call | tf_op jit(solution)/shard_map/pallas_call | solution.py:386
  45.4 3.5 %collective-permute-start.5 = (bf16[10,16,256]{2,1,0:T(8,128)(2,1)S(1)}, bf16[10,16,256]{2,1,0:T(8,128)(2,1)S(1)}, u32[]{:S(2)}, u32[]{:S(2)}) collective-permute-start(bf16[10,16,256]{2,1,0:T(8,128)(2,1)S(1)} %get-tuple-element.22.hi_ref), channel_id=1, source_target_pairs={{0,1},{1,2},{2,3},{4,5},{5,6},{6,7},{8,9},{9,10},{10,11},{12,13},{... | collective-permute-start | bytes 245768 | tf_op jit(solution)/shard_map/ppermute | solution.py:304
  49.0 2.3 %collective-permute-start.6 = (bf16[10,16,256]{2,1,0:T(8,128)(2,1)S(1)}, bf16[10,16,256]{2,1,0:T(8,128)(2,1)S(1)}, u32[]{:S(2)}, u32[]{:S(2)}) collective-permute-start(bf16[10,16,256]{2,1,0:T(8,128)(2,1)S(1)} %get-tuple-element.23.lo_ref), channel_id=1, source_target_pairs={{1,0},{2,1},{3,2},{5,4},{6,5},{7,6},{9,8},{10,9},{11,10},{13,12},{... | collective-permute-start | bytes 245768 | tf_op jit(solution)/shard_map/ppermute | solution.py:305
  51.3 0.4 collective-permute-done.5.zl_ref
  51.8 3.5 %collective-permute-done.6.zr_ref = bf16[10,16,256]{2,1,0:T(8,128)(2,1)S(1)} collective-permute-done((bf16[10,16,256]{2,1,0:T(8,128)(2,1)S(1)}, bf16[10,16,256]{2,1,0:T(8,128)(2,1)S(1)}, u32[]{:S(2)}, u32[]{:S(2)}) %collective-permute-start.6) | collective-permute-done | bytes 81952 | tf_op jit(solution)/shard_map/ppermute | solution.py:305
  55.4 1.9 %collective-permute-start.8 = (bf16[10,2,1024]{2,1,0:T(2,128)(2,1)S(1)}, bf16[10,2,1024]{2,1,0:T(2,128)(2,1)S(1)}, u32[]{:S(2)}, u32[]{:S(2)}) collective-permute-start(bf16[10,2,1024]{2,1,0:T(2,128)(2,1)S(1)} %pad_maximum_fusion.3), channel_id=1, source_target_pairs={{8,0},{16,8},{24,16},{9,1},{17,9},{25,17},{10,2},{18,10},{26,18},{... | collective-permute-start | bytes 122888 | tf_op jit(solution)/shard_map/ppermute | solution.py:305
  57.3 4.1 %collective-permute-start.7 = (bf16[10,2,1024]{2,1,0:T(2,128)(2,1)S(1)}, bf16[10,2,1024]{2,1,0:T(2,128)(2,1)S(1)}, u32[]{:S(2)}, u32[]{:S(2)}) collective-permute-start(bf16[10,2,1024]{2,1,0:T(2,128)(2,1)S(1)} %pad_maximum_fusion.2), channel_id=1, source_target_pairs={{0,8},{8,16},{16,24},{1,9},{9,17},{17,25},{2,10},{10,18},{18,26},{... | collective-permute-start | bytes 122888 | tf_op jit(solution)/shard_map/ppermute | solution.py:304
  61.6 0.6 shard_map.162
  62.2 1.9 %collective-permute-done.7.xl_ref = bf16[10,2,1024]{2,1,0:T(2,128)(2,1)S(1)} collective-permute-done((bf16[10,2,1024]{2,1,0:T(2,128)(2,1)S(1)}, bf16[10,2,1024]{2,1,0:T(2,128)(2,1)S(1)}, u32[]{:S(2)}, u32[]{:S(2)}) %collective-permute-start.7) | collective-permute-done | bytes 40992 | tf_op jit(solution)/shard_map/ppermute | solution.py:304
  64.1 5.8 %shard_map.163 = bf16[384,128]{1,0:T(8,128)(2,1)} custom-call(bf16[10,16,256]{2,1,0:T(8,128)(2,1)S(1)} %collective-permute-done.5.zl_ref, bf16[10,16,256]{2,1,0:T(8,128)(2,1)S(1)} %get-tuple-element.23.lo_ref, bf16[10,16,256]{2,1,0:T(8,128)(2,1)S(1)} %get-tuple-element.22.hi_ref, bf16[10,16,256]{2,1,0:T(8,128)(2,1)S(1)} %collective-permute-done.6.zr_ref, ...), custom_call_target="tpu_custom_call" | custom-call | tf_op jit(solution)/shard_map/pallas_call | solution.py:408
  (54 shorter events, 0.5 us)
Async XLA Ops:
  0.6 2.7 %copy-start.9 = (s32[6]{0:T(128)S(1)}, s32[6]{0:T(128)}, u32[]{:S(2)}) copy-start(s32[6]{0:T(128)} %constant.59) | copy-start | bytes 76
  0.6 2.5 %copy-start.7 = (s32[32,8,4]{0,2,1:T(4,128)S(1)}, s32[32,8,4]{0,2,1:T(4,128)}, u32[]{:S(2)}) copy-start(s32[32,8,4]{0,2,1:T(4,128)} %param.16) | copy-start | bytes 12292
  0.7 3.5 %copy-start.8 = (f32[64]{0:T(128)S(1)}, f32[64]{0:T(128)}, u32[]{:S(2)}) copy-start(f32[64]{0:T(128)} %param.18) | copy-start | bytes 772
  0.7 3.6 %copy-start.5 = (bf16[8,64,48]{1,2,0:T(8,128)(2,1)S(1)}, bf16[8,64,48]{1,2,0:T(8,128)(2,1)}, u32[]{:S(2)}) copy-start(bf16[8,64,48]{1,2,0:T(8,128)(2,1)} %param.17) | copy-start | bytes 147460
  3.2 7.4 %collective-permute-start = (bf16[48,16,768]{2,1,0:T(8,128)(2,1)}, bf16[48,16,768]{2,1,0:T(8,128)(2,1)S(1)}, u32[]{:S(2)}, u32[]{:S(2)}) collective-permute-start(bf16[48,16,768]{2,1,0:T(8,128)(2,1)} %constant_dynamic-slice_fusion), channel_id=1, source_target_pairs={{0,4},{4,0},{1,5},{5,1},{2,6},{6,2},{3,7},{7,3},{8,12},{12,8},{9,1... | collective-permute-start | bytes 3538952 | tf_op jit(solution)/shard_map/ppermute | solution.py:327
  4.2 1.9 %copy-start = (bf16[48,16,2048]{2,1,0:T(8,128)(2,1)S(1)}, bf16[48,16,2048]{2,1,0:T(8,128)(2,1)}, u32[]{:S(2)}) copy-start(bf16[48,16,2048]{2,1,0:T(8,128)(2,1)} %v_ref.1) | copy-start | bytes 9437188
  10.6 19.8 %copy-start.6 = (bf16[8,96,64]{1,2,0:T(8,128)(2,1)S(1)}, bf16[8,96,64]{1,2,0:T(8,128)(2,1)}, u32[]{:S(2)}) copy-start(bf16[8,96,64]{1,2,0:T(8,128)(2,1)} %param.23) | copy-start | bytes 294916
  10.6 19.8 %copy-start.10 = (f32[64]{0:T(128)S(1)}, f32[64]{0:T(128)}, u32[]{:S(2)}) copy-start(f32[64]{0:T(128)} %param.20) | copy-start | bytes 772
  10.6 19.9 %copy-start.11 = (f32[64]{0:T(128)S(1)}, f32[64]{0:T(128)}, u32[]{:S(2)}) copy-start(f32[64]{0:T(128)} %param.22) | copy-start | bytes 772
  10.6 20.0 %copy-start.3 = (bf16[27,64,64]{2,1,0:T(8,128)(2,1)S(1)}, bf16[27,64,64]{2,1,0:T(8,128)(2,1)}, u32[]{:S(2)}) copy-start(bf16[27,64,64]{2,1,0:T(8,128)(2,1)} %w1.2) | copy-start | bytes 663556
  10.6 20.0 %copy-start.4 = (bf16[27,64,64]{2,1,0:T(8,128)(2,1)S(1)}, bf16[27,64,64]{2,1,0:T(8,128)(2,1)}, u32[]{:S(2)}) copy-start(bf16[27,64,64]{2,1,0:T(8,128)(2,1)} %w2.2) | copy-start | bytes 663556
  10.6 21.2 %copy-start.12 = (f32[96]{0:T(128)S(1)}, f32[96]{0:T(128)}, u32[]{:S(2)}) copy-start(f32[96]{0:T(128)} %param.24) | copy-start | bytes 1156
  11.9 8.8 %collective-permute-start.1 = (bf16[22,32,128]{2,1,0:T(8,128)(2,1)S(1)}, bf16[22,32,128]{2,1,0:T(8,128)(2,1)S(1)}, u32[]{:S(2)}, u32[]{:S(2)}) collective-permute-start(bf16[22,32,128]{2,1,0:T(8,128)(2,1)S(1)} %get-tuple-element.17), channel_id=1, source_target_pairs={{0,1},{1,2},{2,3},{4,5},{5,6},{6,7},{8,9},{9,10},{10,11},{12,13},{... | collective-permute-start | bytes 540680 | tf_op jit(solution)/shard_map/ppermute | solution.py:304
  15.4 8.6 %collective-permute-start.2 = (bf16[22,32,128]{2,1,0:T(8,128)(2,1)S(1)}, bf16[22,32,128]{2,1,0:T(8,128)(2,1)S(1)}, u32[]{:S(2)}, u32[]{:S(2)}) collective-permute-start(bf16[22,32,128]{2,1,0:T(8,128)(2,1)S(1)} %get-tuple-element.18), channel_id=1, source_target_pairs={{1,0},{2,1},{3,2},{5,4},{6,5},{7,6},{9,8},{10,9},{11,10},{13,12},{... | collective-permute-start | bytes 540680 | tf_op jit(solution)/shard_map/ppermute | solution.py:305
  24.1 7.7 %collective-permute-start.4 = (bf16[22,2,768]{2,1,0:T(2,128)(2,1)S(1)}, bf16[22,2,768]{2,1,0:T(2,128)(2,1)S(1)}, u32[]{:S(2)}, u32[]{:S(2)}) collective-permute-start(bf16[22,2,768]{2,1,0:T(2,128)(2,1)S(1)} %pad_maximum_fusion.1), channel_id=1, source_target_pairs={{8,0},{16,8},{24,16},{9,1},{17,9},{25,17},{10,2},{18,10},{26,18},{... | collective-permute-start | bytes 202760 | tf_op jit(solution)/shard_map/ppermute | solution.py:305
  27.5 7.1 %collective-permute-start.3 = (bf16[22,2,768]{2,1,0:T(2,128)(2,1)S(1)}, bf16[22,2,768]{2,1,0:T(2,128)(2,1)S(1)}, u32[]{:S(2)}, u32[]{:S(2)}) collective-permute-start(bf16[22,2,768]{2,1,0:T(2,128)(2,1)S(1)} %pad_maximum_fusion), channel_id=1, source_target_pairs={{0,8},{8,16},{16,24},{1,9},{9,17},{17,25},{2,10},{10,18},{18,26},{... | collective-permute-start | bytes 202760 | tf_op jit(solution)/shard_map/ppermute | solution.py:304
  34.6 26.9 %copy-start.13 = (f32[96]{0:T(128)S(1)}, f32[96]{0:T(128)}, u32[]{:S(2)}) copy-start(f32[96]{0:T(128)} %param.26) | copy-start | bytes 1156
  34.6 26.9 %copy-start.14 = (f32[96]{0:T(128)S(1)}, f32[96]{0:T(128)}, u32[]{:S(2)}) copy-start(f32[96]{0:T(128)} %param.28) | copy-start | bytes 1156
  34.6 26.9 %copy-start.1 = (bf16[27,96,96]{2,1,0:T(8,128)(2,1)S(1)}, bf16[27,96,96]{2,1,0:T(8,128)(2,1)}, u32[]{:S(2)}) copy-start(bf16[27,96,96]{2,1,0:T(8,128)(2,1)} %w1.3) | copy-start | bytes 1492996
  34.6 26.9 %copy-start.2 = (bf16[27,96,96]{2,1,0:T(8,128)(2,1)S(1)}, bf16[27,96,96]{2,1,0:T(8,128)(2,1)}, u32[]{:S(2)}) copy-start(bf16[27,96,96]{2,1,0:T(8,128)(2,1)} %w2.3) | copy-start | bytes 1492996
  45.4 6.3 %collective-permute-start.5 = (bf16[10,16,256]{2,1,0:T(8,128)(2,1)S(1)}, bf16[10,16,256]{2,1,0:T(8,128)(2,1)S(1)}, u32[]{:S(2)}, u32[]{:S(2)}) collective-permute-start(bf16[10,16,256]{2,1,0:T(8,128)(2,1)S(1)} %get-tuple-element.22.hi_ref), channel_id=1, source_target_pairs={{0,1},{1,2},{2,3},{4,5},{5,6},{6,7},{8,9},{9,10},{10,11},{12,13},{... | collective-permute-start | bytes 245768 | tf_op jit(solution)/shard_map/ppermute | solution.py:304
  49.0 6.3 %collective-permute-start.6 = (bf16[10,16,256]{2,1,0:T(8,128)(2,1)S(1)}, bf16[10,16,256]{2,1,0:T(8,128)(2,1)S(1)}, u32[]{:S(2)}, u32[]{:S(2)}) collective-permute-start(bf16[10,16,256]{2,1,0:T(8,128)(2,1)S(1)} %get-tuple-element.23.lo_ref), channel_id=1, source_target_pairs={{1,0},{2,1},{3,2},{5,4},{6,5},{7,6},{9,8},{10,9},{11,10},{13,12},{... | collective-permute-start | bytes 245768 | tf_op jit(solution)/shard_map/ppermute | solution.py:305
  55.4 6.8 %collective-permute-start.8 = (bf16[10,2,1024]{2,1,0:T(2,128)(2,1)S(1)}, bf16[10,2,1024]{2,1,0:T(2,128)(2,1)S(1)}, u32[]{:S(2)}, u32[]{:S(2)}) collective-permute-start(bf16[10,2,1024]{2,1,0:T(2,128)(2,1)S(1)} %pad_maximum_fusion.3), channel_id=1, source_target_pairs={{8,0},{16,8},{24,16},{9,1},{17,9},{25,17},{10,2},{18,10},{26,18},{... | collective-permute-start | bytes 122888 | tf_op jit(solution)/shard_map/ppermute | solution.py:305
  57.3 6.8 %collective-permute-start.7 = (bf16[10,2,1024]{2,1,0:T(2,128)(2,1)S(1)}, bf16[10,2,1024]{2,1,0:T(2,128)(2,1)S(1)}, u32[]{:S(2)}, u32[]{:S(2)}) collective-permute-start(bf16[10,2,1024]{2,1,0:T(2,128)(2,1)S(1)} %pad_maximum_fusion.2), channel_id=1, source_target_pairs={{0,8},{8,16},{16,24},{1,9},{9,17},{17,25},{2,10},{10,18},{18,26},{... | collective-permute-start | bytes 122888 | tf_op jit(solution)/shard_map/ppermute | solution.py:304
where the time goes:
time: 70.3 us; the launch traced here: 70 us
  Pallas kernels  24.2 us (34%)
  starting transfers between devices  23.8 us (34%)
  waiting for transfers between devices  14.7 us (21%)
  local copies, waits for them, and re-layouts  5.89 us (8%)
  between operations  1.05 us (1%)
    ppermute x4, starting transfers between devices, shift_along(): lax.ppermute(high_edge, axis, [(i, i + 1) for i in range(count - 1)])  13.8 us
    pallas_call x1, Pallas kernels, local(): pl.pallas_call(functools.partial(level_one_kernel, window), out_shape=[ja...  10.8 us
    ppermute x4, starting transfers between devices, shift_along(): above = lax.ppermute(low_edge, axis, [(i + 1, i) for i in range(count - 1)])  9.97 us
    ppermute x4, waiting for transfers between devices, shift_along(): lax.ppermute(high_edge, axis, [(i, i + 1) for i in range(count - 1)])  7.99 us
    ppermute x4, waiting for transfers between devices, shift_along(): above = lax.ppermute(low_edge, axis, [(i + 1, i) for i in range(count - 1)])  6.73 us
    pallas_call x1, Pallas kernels, local(): pl.pallas_call(functools.partial(level_two_kernel, window), out_shape=jax...  5.82 us
    pallas_call x1, Pallas kernels, local(): pl.pallas_call(down1_own_kernel, grid=(volume.shape[2] // 512,), in_specs...  4.46 us
    dynamic_slice x1, local copies, waits for them, and re-layouts, local(): edge = lax.dynamic_slice_in_dim(volume, (1 - index_y) * last, send_lanes, 2)  2.48 us
  transfers between devices with their start and end apart: 9, of which 6 were waited for; matrix products, arithmetic and copies ran while one was open for 2% of the time, Pallas kernels for 9%

commit v1 on v0

--- a/solution.py
+++ b/solution.py
@@ -95,32 +95,39 @@
         dest[pl.ds(first, 64), ab * kz : (ab + 1) * kz] = cells[64 * ab : 64 * ab + 64]
 
 
-def down1_own_kernel(v_ref, w_ref, b_ref, out_ref, wd_ref, cells_ref):
-    step = pl.program_id(0)
-    steps = pl.num_programs(0)
+def edge_kernel(last, v_ref, out_ref, sem):
+    start = pl.multiple_of((1 - lax.axis_index("gy")) * last, 128)
+    copy = pltpu.make_async_copy(v_ref.at[:, :, pl.ds(start, out_ref.shape[2])], out_ref, sem)
+    copy.start()
+    copy.wait()
+
+
+def down1_own_kernel(v_ref, w_ref, b_ref, out_ref, wd_ref, field_ref, cells_ref, sems):
     z0 = v_ref.shape[1]
     kz = C0 * z0
     lanes = Z1 * C1
-
-    @pl.when(step == 0)
-    def _():
-        r = iota((kz, 2 * C0), 0)
-        l = iota((kz, 2 * C0), 1)
-        spread = one_hot((r // z0 == l % C0) & (r % 2 == l // C0))
-        keep = (iota((kz, lanes), 0) % z0) // 2 == iota((kz, lanes), 1) // C1
-        for ab in range(4):
-            pair = w_ref[2 * ab : 2 * ab + 2].reshape(2 * C0, C1)
-            wide = jnp.concatenate([pair] * Z1, axis=1)
-            wd_ref[ab * kz : (ab + 1) * kz, :] = jnp.where(keep, mm(spread, wide), 0.0).astype(BF)
-
-    for part in range(2):
-        v = v_ref[:, :, part * 256 : part * 256 + 256].reshape(kz, 256)
-        split_cells(v, cells_ref, pl.multiple_of(step * 128 + part * 64, 64))
-
-    @pl.when(step == steps - 1)
-    def _():
-        acc = mm(cells_ref[...], wd_ref[...])
-        out_ref[...] = jnp.maximum(acc + b_ref[...], 0.0).astype(BF)
+    copies = []
+    for n in range(sems.shape[0]):
+        cut = (slice(None), slice(None), slice(n * 512, n * 512 + 512))
+        copies.append(pltpu.make_async_copy(v_ref.at[cut], field_ref.at[cut], sems.at[n]))
+        copies[-1].start()
+
+    r = iota((kz, 2 * C0), 0)
+    l = iota((kz, 2 * C0), 1)
+    spread = one_hot((r // z0 == l % C0) & (r % 2 == l // C0))
+    keep = (iota((kz, lanes), 0) % z0) // 2 == iota((kz, lanes), 1) // C1
+    for ab in range(4):
+        pair = w_ref[2 * ab : 2 * ab + 2].reshape(2 * C0, C1)
+        wide = jnp.concatenate([pair] * Z1, axis=1)
+        wd_ref[ab * kz : (ab + 1) * kz, :] = jnp.where(keep, mm(spread, wide), 0.0).astype(BF)
+
+    for n, copy in enumerate(copies):
+        copy.wait()
+        for part in range(2 * n, 2 * n + 2):
+            v = field_ref[:, :, part * 256 : part * 256 + 256].reshape(kz, 256)
+            split_cells(v, cells_ref, part * 64)
+    acc = mm(cells_ref[...], wd_ref[...])
+    out_ref[...] = jnp.maximum(acc + b_ref[...], 0.0).astype(BF)
 
 
 def down1_window_kernel(window, v_ref, own_ref, wd_ref, b_ref, tab_ref, out_ref, lo_ref, hi_ref, cells_ref):
@@ -299,10 +306,21 @@
     out_ref[...] = mm(order, jnp.concatenate(feat, axis=1), NT).astype(BF)
 
 
+def swap_pairs(count, first):
+    pairs = [(i, i) for i in range(first)]
+    for i in range(first, count, 2):
+        pairs += [(i, i + 1), (i + 1, i)] if i + 1 < count else [(i, i)]
+    return pairs
+
+
 def shift_along(low_edge, high_edge, axis):
     count = lax.axis_size(axis)
-    below = lax.ppermute(high_edge, axis, [(i, i + 1) for i in range(count - 1)])
-    above = lax.ppermute(low_edge, axis, [(i + 1, i) for i in range(count - 1)])
+    index = lax.axis_index(axis)
+    even = index % 2 == 0
+    one = lax.ppermute(jnp.where(even, high_edge, low_edge), axis, swap_pairs(count, 0))
+    two = lax.ppermute(jnp.where(even, low_edge, high_edge), axis, swap_pairs(count, 1))
+    below = jnp.where(index > 0, jnp.where(even, two, one), jnp.zeros_like(one))
+    above = jnp.where(index < count - 1, jnp.where(even, one, two), jnp.zeros_like(one))
     return below, above
 
 
@@ -323,7 +341,12 @@
     last = volume.shape[2] - send_lanes
 
     if window.one_sided:
-        edge = lax.dynamic_slice_in_dim(volume, (1 - index_y) * last, send_lanes, 2)
+        edge = pl.pallas_call(
+            functools.partial(edge_kernel, last),
+            in_specs=[pl.BlockSpec(memory_space=pltpu.HBM)],
+            out_shape=jax.ShapeDtypeStruct((C0, depth, send_lanes), BF),
+            scratch_shapes=[pltpu.SemaphoreType.DMA],
+        )(volume)
         halo = lax.ppermute(edge, "gy", [(0, 1), (1, 0)])
     else:
         halo = jnp.concatenate(shift_along(volume[:, :, :send_lanes], volume[:, :, last:], "gy"), axis=2)
@@ -344,21 +367,16 @@
     bias1 = jnp.tile(b_down1, Z1)[None]
     own, wd1 = pl.pallas_call(
         down1_own_kernel,
-        grid=(volume.shape[2] // 512,),
-        in_specs=[
-            pl.BlockSpec((C0, depth, 512), lambda i: (0, 0, i)),
-            pl.BlockSpec((8, C0, C1), lambda i: (0, 0, 0)),
-            pl.BlockSpec((1, lanes1), lambda i: (0, 0)),
-        ],
-        out_specs=[
-            pl.BlockSpec((Y1 * X1, lanes1), lambda i: (0, 0)),
-            pl.BlockSpec((4 * kz, lanes1), lambda i: (0, 0)),
-        ],
+        in_specs=[pl.BlockSpec(memory_space=pltpu.HBM)] + [pl.BlockSpec(memory_space=pltpu.VMEM)] * 2,
         out_shape=[
             jax.ShapeDtypeStruct((Y1 * X1, lanes1), BF),
             jax.ShapeDtypeStruct((4 * kz, lanes1), BF),
         ],
-        scratch_shapes=[pltpu.VMEM((Y1 * X1, 4 * kz), BF)],
+        scratch_shapes=[
+            pltpu.VMEM(volume.shape, BF),
+            pltpu.VMEM((Y1 * X1, 4 * kz), BF),
+            pltpu.SemaphoreType.DMA((volume.shape[2] // 512,)),
+        ],
         compiler_params=params(),
     )(volume, jnp.swapaxes(w_down1, 1, 2), bias1)
 

time: 70.3 us -> 61.2 us (0.87)
  the two profiles are of different devices: /device:TPU:12 before, /device:TPU:20 now
where the time goes in v1:
time: 61.2 us; the launch traced here: 61 us
  Pallas kernels  27.9 us (46%)
  waiting for transfers between devices  17 us (28%)
  starting transfers between devices  12.7 us (21%)
  local copies, waits for them, and re-layouts  1.53 us (2%)
  between operations  1.18 us (2%)
  other arithmetic  0.72 us (1%)
    pallas_call x1, Pallas kernels, local(): pl.pallas_call(functools.partial(level_one_kernel, window), out_shape=[ja...  10.8 us
    ppermute x4, waiting for transfers between devices, shift_along(): lax.ppermute(jnp.where(even, low_edge, high_edge), axis, swap_pairs(count...  10.8 us
    ppermute x4, starting transfers between devices, shift_along(): lax.ppermute(jnp.where(even, low_edge, high_edge), axis, swap_pairs(count...  9.26 us
    ppermute x4, waiting for transfers between devices, shift_along(): lax.ppermute(jnp.where(even, high_edge, low_edge), axis, swap_pairs(count...  6.16 us
    pallas_call x1, Pallas kernels, local(): pl.pallas_call(functools.partial(level_two_kernel, window), out_shape=jax...  5.82 us
    pallas_call x1, Pallas kernels, local(): pl.pallas_call(down1_own_kernel, in_specs=[pl.BlockSpec(memory_space=pltp...  4.44 us
    ppermute x4, starting transfers between devices, shift_along(): lax.ppermute(jnp.where(even, high_edge, low_edge), axis, swap_pairs(count...  3.33 us
    pallas_call x1, Pallas kernels, local(): pl.pallas_call(functools.partial(down1_window_kernel, window), out_shape=...  2.54 us
  transfers between devices with their start and end apart: 9, of which 7 were waited for; matrix products, arithmetic and copies ran while one was open for 2% of the time, Pallas kernels for 10%

profile of v1, /device:TPU:20, one launch (start us, length us, event | category | flops | bytes accessed | tf_op | source)
XLA Modules:
  0.0 61.0 jit_solution(11386708427493090178)
XLA Ops:
  0.7 2.5 %shard_map.158 = bf16[48,16,768]{2,1,0:T(8,128)(2,1)} custom-call(bf16[48,16,2048]{2,1,0:T(8,128)(2,1)} %v_ref.3), custom_call_target="tpu_custom_call" | custom-call | tf_op jit(solution)/shard_map/pallas_call | solution.py:344
  3.3 0.1 broadcast_in_dim_tile.9.b_ref
  3.4 0.1 fusion.1
  3.5 0.1 convert_element_type.19
  3.6 0.6 gather_fusion
  4.2 0.1 copy.21.tab_ref
  4.4 4.4 %shard_map.159 = (bf16[512,512]{1,0:T(8,128)(2,1)S(1)}, bf16[3072,512]{1,0:T(8,128)(2,1)S(1)}) custom-call(bf16[48,16,2048]{2,1,0:T(8,128)(2,1)S(1)} %copy-done, bf16[8,48,64]{2,1,0:T(8,128)(2,1)S(1)} %bitcast.16, f32[1,512]{1,0:T(1,128)S(1)} %broadcast_in_dim_tile.9.b_ref), custom_call_target="tpu_custom_call" | custom-call | tf_op jit(solution)/shard_map/pallas_call | solution.py:368
  8.9 2.5 %shard_map.160 = (bf16[22,32,512]{2,1,0:T(8,128)(2,1)S(1)}, bf16[22,32,128]{2,1,0:T(8,128)(2,1)S(1)}, bf16[22,32,128]{2,1,0:T(8,128)(2,1)S(1)}) custom-call(bf16[48,16,768]{2,1,0:T(8,128)(2,1)} %collective-permute-done.v_ref, bf16[512,512]{1,0:T(8,128)(2,1)S(1)} %get-tuple-element.14.own_ref, bf16[3072,512]{1,0:T(8,128)(2,1)S(1)} %get-tuple-element.15.wd_ref, ...), custom_call_target="tpu_custom_call" | custom-call | tf_op jit(solution)/shard_map/pallas_call | solution.py:384
  11.5 1.6 %collective-permute-start.2 = (bf16[22,32,128]{2,1,0:T(8,128)(2,1)S(1)}, bf16[22,32,128]{2,1,0:T(8,128)(2,1)S(1)}, u32[]{:S(2)}, u32[]{:S(2)}) collective-permute-start(bf16[22,32,128]{2,1,0:T(8,128)(2,1)S(1)} %get-tuple-element.33), channel_id=1, source_target_pairs={{0,1},{1,0},{2,3},{3,2},{4,5},{5,4},{6,7},{7,6},{8,9},{9,8},{10,11... | collective-permute-start | bytes 540680 | tf_op jit(solution)/shard_map/ppermute | solution.py:320
  13.1 1.9 %collective-permute-start.1 = (bf16[22,32,128]{2,1,0:T(8,128)(2,1)S(1)}, bf16[22,32,128]{2,1,0:T(8,128)(2,1)S(1)}, u32[]{:S(2)}, u32[]{:S(2)}) collective-permute-start(bf16[22,32,128]{2,1,0:T(8,128)(2,1)S(1)} %get-tuple-element.34), channel_id=1, source_target_pairs={{0,0},{1,2},{2,1},{3,3},{4,4},{5,6},{6,5},{7,7},{8,8},{9,10},{10,9... | collective-permute-start | bytes 540680 | tf_op jit(solution)/shard_map/ppermute | solution.py:321
  15.1 3.4 %collective-permute-done.2 = bf16[22,32,128]{2,1,0:T(8,128)(2,1)S(1)} collective-permute-done((bf16[22,32,128]{2,1,0:T(8,128)(2,1)S(1)}, bf16[22,32,128]{2,1,0:T(8,128)(2,1)S(1)}, u32[]{:S(2)}, u32[]{:S(2)}) %collective-permute-start.2) | collective-permute-done | bytes 180256 | tf_op jit(solution)/shard_map/ppermute | solution.py:320
  18.5 3.2 %collective-permute-done.1 = bf16[22,32,128]{2,1,0:T(8,128)(2,1)S(1)} collective-permute-done((bf16[22,32,128]{2,1,0:T(8,128)(2,1)S(1)}, bf16[22,32,128]{2,1,0:T(8,128)(2,1)S(1)}, u32[]{:S(2)}, u32[]{:S(2)}) %collective-permute-start.1) | collective-permute-done | bytes 180256 | tf_op jit(solution)/shard_map/ppermute | solution.py:321
  21.7 0.1 broadcast_select_fusion.5
  21.9 1.5 %collective-permute-start.4 = (bf16[22,2,768]{2,1,0:T(2,128)(2,1)S(1)}, bf16[22,2,768]{2,1,0:T(2,128)(2,1)S(1)}, u32[]{:S(2)}, u32[]{:S(2)}) collective-permute-start(bf16[22,2,768]{2,1,0:T(2,128)(2,1)S(1)} %get-tuple-element.45), channel_id=1, source_target_pairs={{0,8},{8,0},{16,24},{24,16},{1,9},{9,1},{17,25},{25,17},{2,10},{10... | collective-permute-start | bytes 202760 | tf_op jit(solution)/shard_map/ppermute | solution.py:320
  23.4 2.5 %collective-permute-start.3 = (bf16[22,2,768]{2,1,0:T(2,128)(2,1)S(1)}, bf16[22,2,768]{2,1,0:T(2,128)(2,1)S(1)}, u32[]{:S(2)}, u32[]{:S(2)}) collective-permute-start(bf16[22,2,768]{2,1,0:T(2,128)(2,1)S(1)} %get-tuple-element.46), channel_id=1, source_target_pairs={{0,0},{8,16},{16,8},{24,24},{1,1},{9,17},{17,9},{25,25},{2,2},{10,... | collective-permute-start | bytes 202760 | tf_op jit(solution)/shard_map/ppermute | solution.py:321
  26.0 0.1 broadcast_in_dim_tile.10.ba_ref
  26.1 0.1 broadcast_in_dim_tile.11.bb_ref
  26.3 0.1 copy.23.tab2_ref.tab_ref
  26.4 1.2 %shard_map.161 = (bf16[3,256,1152]{2,1,0:T(8,128)(2,1)S(1)}, bf16[3,256,1152]{2,1,0:T(8,128)(2,1)S(1)}) custom-call(bf16[27,64,64]{2,1,0:T(8,128)(2,1)S(1)} %copy-done.3, bf16[27,64,64]{2,1,0:T(8,128)(2,1)S(1)} %copy-done.4), custom_call_target="tpu_custom_call" | custom-call | tf_op jit(solution)/shard_map/pallas_call | solution.py:178
  27.6 2.9 %collective-permute-done.3 = bf16[22,2,768]{2,1,0:T(2,128)(2,1)S(1)} collective-permute-done((bf16[22,2,768]{2,1,0:T(2,128)(2,1)S(1)}, bf16[22,2,768]{2,1,0:T(2,128)(2,1)S(1)}, u32[]{:S(2)}, u32[]{:S(2)}) %collective-permute-start.3) | collective-permute-done | bytes 67616 | tf_op jit(solution)/shard_map/ppermute | solution.py:321
  30.5 0.1 broadcast_select_fusion.2
  30.7 10.8 %shard_map.162 = (bf16[512,512]{1,0:T(8,128)(2,1)}, bf16[10,16,256]{2,1,0:T(8,128)(2,1)S(1)}, bf16[10,16,256]{2,1,0:T(8,128)(2,1)S(1)}) custom-call(bf16[22,32,512]{2,1,0:T(8,128)(2,1)S(1)} %get-tuple-element.16.win_ref, bf16[22,32,128]{2,1,0:T(8,128)(2,1)S(1)} %get-tuple-element.32.zl_ref, bf16[22,32,128]{2,1,0:T(8,128)(2,1)S(1)} %get-tuple-element.31.zr_ref, ...), custom_call_target="tpu_custom_call" | custom-call | tf_op jit(solution)/shard_map/pallas_call | solution.py:404
  41.6 2.2 %collective-permute-start.5 = (bf16[10,16,256]{2,1,0:T(8,128)(2,1)S(1)}, bf16[10,16,256]{2,1,0:T(8,128)(2,1)S(1)}, u32[]{:S(2)}, u32[]{:S(2)}) collective-permute-start(bf16[10,16,256]{2,1,0:T(8,128)(2,1)S(1)} %get-tuple-element.42), channel_id=1, source_target_pairs={{0,0},{1,2},{2,1},{3,3},{4,4},{5,6},{6,5},{7,7},{8,8},{9,10},{10,9... | collective-permute-start | bytes 245768 | tf_op jit(solution)/shard_map/ppermute | solution.py:321
  43.9 2.2 %collective-permute-done.6 = bf16[10,16,256]{2,1,0:T(8,128)(2,1)S(1)} collective-permute-done((bf16[10,16,256]{2,1,0:T(8,128)(2,1)S(1)}, bf16[10,16,256]{2,1,0:T(8,128)(2,1)S(1)}, u32[]{:S(2)}, u32[]{:S(2)}) %collective-permute-start.6) | collective-permute-done | bytes 81952 | tf_op jit(solution)/shard_map/ppermute | solution.py:320
  46.1 1.9 %collective-permute-done.5 = bf16[10,16,256]{2,1,0:T(8,128)(2,1)S(1)} collective-permute-done((bf16[10,16,256]{2,1,0:T(8,128)(2,1)S(1)}, bf16[10,16,256]{2,1,0:T(8,128)(2,1)S(1)}, u32[]{:S(2)}, u32[]{:S(2)}) %collective-permute-start.5) | collective-permute-done | bytes 81952 | tf_op jit(solution)/shard_map/ppermute | solution.py:321
  48.0 0.1 broadcast_select_fusion.11
  48.3 2.6 %collective-permute-start.7 = (bf16[10,2,1024]{2,1,0:T(2,128)(2,1)S(1)}, bf16[10,2,1024]{2,1,0:T(2,128)(2,1)S(1)}, u32[]{:S(2)}, u32[]{:S(2)}) collective-permute-start(bf16[10,2,1024]{2,1,0:T(2,128)(2,1)S(1)} %broadcast_select_fusion.12), channel_id=1, source_target_pairs={{0,0},{8,16},{16,8},{24,24},{1,1},{9,17},{17,9},{25,25},{2,2},{10,... | collective-permute-start | bytes 122888 | tf_op jit(solution)/shard_map/ppermute | solution.py:321
  51.0 0.6 %shard_map.163 = (bf16[3,256,1536]{2,1,0:T(8,128)(2,1)S(1)}, bf16[3,256,1536]{2,1,0:T(8,128)(2,1)S(1)}) custom-call(bf16[27,96,96]{2,1,0:T(8,128)(2,1)S(1)} %copy-done.1, bf16[27,96,96]{2,1,0:T(8,128)(2,1)S(1)} %copy-done.2), custom_call_target="tpu_custom_call" | custom-call | tf_op jit(solution)/shard_map/pallas_call | solution.py:178
  51.6 0.6 collective-permute-done.8
  52.2 2.9 %collective-permute-done.7 = bf16[10,2,1024]{2,1,0:T(2,128)(2,1)S(1)} collective-permute-done((bf16[10,2,1024]{2,1,0:T(2,128)(2,1)S(1)}, bf16[10,2,1024]{2,1,0:T(2,128)(2,1)S(1)}, u32[]{:S(2)}, u32[]{:S(2)}) %collective-permute-start.7) | collective-permute-done | bytes 40992 | tf_op jit(solution)/shard_map/ppermute | solution.py:321
  55.1 0.1 broadcast_select_fusion.8
  55.2 5.8 %shard_map.164 = bf16[384,128]{1,0:T(8,128)(2,1)} custom-call(bf16[10,16,256]{2,1,0:T(8,128)(2,1)S(1)} %get-tuple-element.40.zl_ref, bf16[10,16,256]{2,1,0:T(8,128)(2,1)S(1)} %get-tuple-element.22.lo_ref, bf16[10,16,256]{2,1,0:T(8,128)(2,1)S(1)} %get-tuple-element.23.hi_ref, bf16[10,16,256]{2,1,0:T(8,128)(2,1)S(1)} %get-tuple-element.39.zr_ref, ...), custom_call_target="tpu_custom_call" | custom-call | tf_op jit(solution)/shard_map/pallas_call | solution.py:426
  (59 shorter events, 0.8 us)
Async XLA Ops:
  0.6 2.9 %copy-start.9 = (s32[6]{0:T(128)S(1)}, s32[6]{0:T(128)}, u32[]{:S(2)}) copy-start(s32[6]{0:T(128)} %constant.76) | copy-start | bytes 76
  0.6 3.7 %copy-start = (bf16[48,16,2048]{2,1,0:T(8,128)(2,1)S(1)}, bf16[48,16,2048]{2,1,0:T(8,128)(2,1)}, u32[]{:S(2)}) copy-start(bf16[48,16,2048]{2,1,0:T(8,128)(2,1)} %v_ref.3) | copy-start | bytes 9437188
  0.7 2.6 %copy-start.8 = (f32[64]{0:T(128)S(1)}, f32[64]{0:T(128)}, u32[]{:S(2)}) copy-start(f32[64]{0:T(128)} %param.18) | copy-start | bytes 772
  0.7 2.7 %copy-start.7 = (s32[32,8,4]{0,2,1:T(4,128)S(1)}, s32[32,8,4]{0,2,1:T(4,128)}, u32[]{:S(2)}) copy-start(s32[32,8,4]{0,2,1:T(4,128)} %param.16) | copy-start | bytes 12292
  0.7 3.7 %copy-start.5 = (bf16[8,64,48]{1,2,0:T(8,128)(2,1)S(1)}, bf16[8,64,48]{1,2,0:T(8,128)(2,1)}, u32[]{:S(2)}) copy-start(bf16[8,64,48]{1,2,0:T(8,128)(2,1)} %param.17) | copy-start | bytes 147460
  3.2 5.6 %collective-permute-start = (bf16[48,16,768]{2,1,0:T(8,128)(2,1)}, bf16[48,16,768]{2,1,0:T(8,128)(2,1)}, u32[]{:S(2)}, u32[]{:S(2)}) collective-permute-start(bf16[48,16,768]{2,1,0:T(8,128)(2,1)} %shard_map.158), channel_id=1, source_target_pairs={{0,4},{4,0},{1,5},{5,1},{2,6},{6,2},{3,7},{7,3},{8,12},{12,8},{9,1... | collective-permute-start | bytes 3538952 | tf_op jit(solution)/shard_map/ppermute | solution.py:350
  8.8 17.2 %copy-start.10 = (f32[64]{0:T(128)S(1)}, f32[64]{0:T(128)}, u32[]{:S(2)}) copy-start(f32[64]{0:T(128)} %param.20) | copy-start | bytes 772
  8.8 17.3 %copy-start.11 = (f32[64]{0:T(128)S(1)}, f32[64]{0:T(128)}, u32[]{:S(2)}) copy-start(f32[64]{0:T(128)} %param.22) | copy-start | bytes 772
  8.8 17.4 %copy-start.6 = (bf16[8,96,64]{1,2,0:T(8,128)(2,1)S(1)}, bf16[8,96,64]{1,2,0:T(8,128)(2,1)}, u32[]{:S(2)}) copy-start(bf16[8,96,64]{1,2,0:T(8,128)(2,1)} %param.23) | copy-start | bytes 294916
  11.4 15.0 %copy-start.3 = (bf16[27,64,64]{2,1,0:T(8,128)(2,1)S(1)}, bf16[27,64,64]{2,1,0:T(8,128)(2,1)}, u32[]{:S(2)}) copy-start(bf16[27,64,64]{2,1,0:T(8,128)(2,1)} %w1.2) | copy-start | bytes 663556
  11.4 15.0 %copy-start.4 = (bf16[27,64,64]{2,1,0:T(8,128)(2,1)S(1)}, bf16[27,64,64]{2,1,0:T(8,128)(2,1)}, u32[]{:S(2)}) copy-start(bf16[27,64,64]{2,1,0:T(8,128)(2,1)} %w2.2) | copy-start | bytes 663556
  11.4 16.2 %copy-start.12 = (f32[96]{0:T(128)S(1)}, f32[96]{0:T(128)}, u32[]{:S(2)}) copy-start(f32[96]{0:T(128)} %param.24) | copy-start | bytes 1156
  11.5 7.0 %collective-permute-start.2 = (bf16[22,32,128]{2,1,0:T(8,128)(2,1)S(1)}, bf16[22,32,128]{2,1,0:T(8,128)(2,1)S(1)}, u32[]{:S(2)}, u32[]{:S(2)}) collective-permute-start(bf16[22,32,128]{2,1,0:T(8,128)(2,1)S(1)} %get-tuple-element.33), channel_id=1, source_target_pairs={{0,1},{1,0},{2,3},{3,2},{4,5},{5,4},{6,7},{7,6},{8,9},{9,8},{10,11... | collective-permute-start | bytes 540680 | tf_op jit(solution)/shard_map/ppermute | solution.py:320
  13.1 8.5 %collective-permute-start.1 = (bf16[22,32,128]{2,1,0:T(8,128)(2,1)S(1)}, bf16[22,32,128]{2,1,0:T(8,128)(2,1)S(1)}, u32[]{:S(2)}, u32[]{:S(2)}) collective-permute-start(bf16[22,32,128]{2,1,0:T(8,128)(2,1)S(1)} %get-tuple-element.34), channel_id=1, source_target_pairs={{0,0},{1,2},{2,1},{3,3},{4,4},{5,6},{6,5},{7,7},{8,8},{9,10},{10,9... | collective-permute-start | bytes 540680 | tf_op jit(solution)/shard_map/ppermute | solution.py:321
  21.9 5.7 %collective-permute-start.4 = (bf16[22,2,768]{2,1,0:T(2,128)(2,1)S(1)}, bf16[22,2,768]{2,1,0:T(2,128)(2,1)S(1)}, u32[]{:S(2)}, u32[]{:S(2)}) collective-permute-start(bf16[22,2,768]{2,1,0:T(2,128)(2,1)S(1)} %get-tuple-element.45), channel_id=1, source_target_pairs={{0,8},{8,0},{16,24},{24,16},{1,9},{9,1},{17,25},{25,17},{2,10},{10... | collective-permute-start | bytes 202760 | tf_op jit(solution)/shard_map/ppermute | solution.py:320
  23.4 7.1 %collective-permute-start.3 = (bf16[22,2,768]{2,1,0:T(2,128)(2,1)S(1)}, bf16[22,2,768]{2,1,0:T(2,128)(2,1)S(1)}, u32[]{:S(2)}, u32[]{:S(2)}) collective-permute-start(bf16[22,2,768]{2,1,0:T(2,128)(2,1)S(1)} %get-tuple-element.46), channel_id=1, source_target_pairs={{0,0},{8,16},{16,8},{24,24},{1,1},{9,17},{17,9},{25,25},{2,2},{10,... | collective-permute-start | bytes 202760 | tf_op jit(solution)/shard_map/ppermute | solution.py:321
  30.6 20.2 %copy-start.13 = (f32[96]{0:T(128)S(1)}, f32[96]{0:T(128)}, u32[]{:S(2)}) copy-start(f32[96]{0:T(128)} %param.26) | copy-start | bytes 1156
  30.7 20.3 %copy-start.14 = (f32[96]{0:T(128)S(1)}, f32[96]{0:T(128)}, u32[]{:S(2)}) copy-start(f32[96]{0:T(128)} %param.28) | copy-start | bytes 1156
  30.7 20.3 %copy-start.1 = (bf16[27,96,96]{2,1,0:T(8,128)(2,1)S(1)}, bf16[27,96,96]{2,1,0:T(8,128)(2,1)}, u32[]{:S(2)}) copy-start(bf16[27,96,96]{2,1,0:T(8,128)(2,1)} %w1.3) | copy-start | bytes 1492996
  30.7 20.3 %copy-start.2 = (bf16[27,96,96]{2,1,0:T(8,128)(2,1)S(1)}, bf16[27,96,96]{2,1,0:T(8,128)(2,1)}, u32[]{:S(2)}) copy-start(bf16[27,96,96]{2,1,0:T(8,128)(2,1)} %w2.3) | copy-start | bytes 1492996
  41.5 4.5 %collective-permute-start.6 = (bf16[10,16,256]{2,1,0:T(8,128)(2,1)S(1)}, bf16[10,16,256]{2,1,0:T(8,128)(2,1)S(1)}, u32[]{:S(2)}, u32[]{:S(2)}) collective-permute-start(bf16[10,16,256]{2,1,0:T(8,128)(2,1)S(1)} %get-tuple-element.41), channel_id=1, source_target_pairs={{0,1},{1,0},{2,3},{3,2},{4,5},{5,4},{6,7},{7,6},{8,9},{9,8},{10,11... | collective-permute-start | bytes 245768 | tf_op jit(solution)/shard_map/ppermute | solution.py:320
  41.6 6.3 %collective-permute-start.5 = (bf16[10,16,256]{2,1,0:T(8,128)(2,1)S(1)}, bf16[10,16,256]{2,1,0:T(8,128)(2,1)S(1)}, u32[]{:S(2)}, u32[]{:S(2)}) collective-permute-start(bf16[10,16,256]{2,1,0:T(8,128)(2,1)S(1)} %get-tuple-element.42), channel_id=1, source_target_pairs={{0,0},{1,2},{2,1},{3,3},{4,4},{5,6},{6,5},{7,7},{8,8},{9,10},{10,9... | collective-permute-start | bytes 245768 | tf_op jit(solution)/shard_map/ppermute | solution.py:321
  48.1 4.1 %collective-permute-start.8 = (bf16[10,2,1024]{2,1,0:T(2,128)(2,1)S(1)}, bf16[10,2,1024]{2,1,0:T(2,128)(2,1)S(1)}, u32[]{:S(2)}, u32[]{:S(2)}) collective-permute-start(bf16[10,2,1024]{2,1,0:T(2,128)(2,1)S(1)} %get-tuple-element.26), channel_id=1, source_target_pairs={{0,8},{8,0},{16,24},{24,16},{1,9},{9,1},{17,25},{25,17},{2,10},{10... | collective-permute-start | bytes 122888 | tf_op jit(solution)/shard_map/ppermute | solution.py:320
  48.3 6.8 %collective-permute-start.7 = (bf16[10,2,1024]{2,1,0:T(2,128)(2,1)S(1)}, bf16[10,2,1024]{2,1,0:T(2,128)(2,1)S(1)}, u32[]{:S(2)}, u32[]{:S(2)}) collective-permute-start(bf16[10,2,1024]{2,1,0:T(2,128)(2,1)S(1)} %broadcast_select_fusion.12), channel_id=1, source_target_pairs={{0,0},{8,16},{16,8},{24,24},{1,1},{9,17},{17,9},{25,25},{2,2},{10,... | collective-permute-start | bytes 122888 | tf_op jit(solution)/shard_map/ppermute | solution.py:321

commit v2 on v1

v2 whole, which is shorter than its diff:
```python
import jax
import jax.numpy as jnp
from jax import lax
from jax.experimental import pallas as pl
from jax.experimental.pallas import tpu as pltpu
from jax.sharding import PartitionSpec as P

CX = 64
CY = 32
X1 = CX // 2
Y1 = CY // 2
X2 = X1 // 2
Y2 = Y1 // 2
Z1 = 8
Z2 = 4
C0 = 48
C1 = 64
C2 = 96
CP = 128
HALO = 2
XB = 10
YB = 6
ROWS1 = Y1 + 2 * HALO
ROWS2 = Y2 + 2 * HALO
EDGE = 16
PITCH2 = 32
BF = jnp.bfloat16
F32 = jnp.float32
NN = (((1,), (0,)), ((), ()))
NT = (((1,), (1,)), ((), ()))
VMEM_BYTES = 40 * 1024 * 1024


def mm(a, b, dims=NN):
    return lax.dot_general(a, b, dims, preferred_element_type=F32)


def iota(shape, dim):
    return lax.broadcasted_iota(jnp.int32, shape, dim)


def one_hot(flag):
    return jnp.where(flag, 1.0, 0.0).astype(BF)


def mask_rows(tab, y_start, rows, pitch, x_of, cell):
    shape = (rows, pitch, 128)
    y_block = lax.div(iota(shape, 0) + (y_start + cell), cell)
    x_block = jnp.minimum(lax.div(x_of(iota(shape, 1)) + cell, cell), XB - 1)
    hit = one_hot(y_block * XB + x_block == iota(shape, 2)).reshape(rows * pitch, 128)
    return mm(hit, tab)


def down1_kernel(v_ref, w_ref, b_ref, tab_ref, out_ref, wd_ref, field_ref, cells_ref, sems):
    z0 = v_ref.shape[1]
    kz = C0 * z0
    lanes = Z1 * C1
    copies = []
    for n in range(sems.shape[0]):
        cut = (slice(None), slice(None), slice(n * 256, n * 256 + 256))
        copies.append(pltpu.make_async_copy(v_ref.at[cut], field_ref.at[cut], sems.at[n]))
        copies[-1].start()

    r = iota((kz, 2 * C0), 0)
    l = iota((kz, 2 * C0), 1)
    spread = one_hot((r // z0 == l % C0) & (r % 2 == l // C0))
    keep = (iota((kz, lanes), 0) % z0) // 2 == iota((kz, lanes), 1) // C1
    for ab in range(4):
        pair = w_ref[2 * ab : 2 * ab + 2].reshape(2 * C0, C1)
        wide = jnp.concatenate([pair] * Z1, axis=1)
        wd_ref[ab * kz : (ab + 1) * kz, :] = jnp.where(keep, mm(spread, wide), 0.0).astype(BF)

    shape = (4 * CX, 4 * CX)
    r = iota(shape, 0)
    a, b, y, x = r // 128, (r // 64) % 2, (r // 32) % 2, r % 32
    select = one_hot((2 * y + b) * CX + 2 * x + a == iota(shape, 1))
    for n, copy in enumerate(copies):
        copy.wait()
        v = field_ref[:, :, n * 256 : n * 256 + 256].reshape(kz, 256)
        cells = mm(select, v, NT).astype(BF)
        for ab in range(4):
            cells_ref[n * 64 : n * 64 + 64, ab * kz : (ab + 1) * kz] = cells[64 * ab : 64 * ab + 64]
    mask = mask_rows(tab_ref[:, 128:256], 0, Y1, X1, lambda x: x, 4)
    acc = mm(cells_ref[...], wd_ref[...])
    for q in range(4):
        cut = slice(q * 128, q * 128 + 128)
        value = jnp.maximum(acc[:, cut] + b_ref[...], 0.0) * mask
        out_ref[:, :, cut] = value.astype(BF).reshape(Y1, X1, 128)


def banded(weights, group, pad):
    chan = weights.shape[1]

    def kernel(w_ref, t_ref):
        t_ref[...] = jnp.zeros_like(t_ref)
        for j in range(3):
            for i in range(3):
                for zo in range(group):
                    for k in range(3):
                        lane = i * (group + 2) * pad + (zo + k) * pad
                        t_ref[j, zo * pad : zo * pad + chan, lane : lane + chan] = w_ref[9 * i + 3 * j + k]

    return pl.pallas_call(
        kernel,
        out_shape=jax.ShapeDtypeStruct((3, group * pad, 3 * (group + 2) * pad), BF),
        compiler_params=params(),
        cost_estimate=cost(1e-6),
    )(weights)


def conv_group(taps, t_ref, y_first, rows, group_out, group_full):
    pitch = taps[0][0][0].shape[1]
    width = sum(piece[2] for piece in taps[0])
    total = None
    for j in range(3):
        parts = [ref[y_first + j : y_first + j + rows, :, lane : lane + n] for tap in taps for ref, lane, n in tap]
        left = jnp.concatenate([p.reshape(rows * pitch, p.shape[2]) for p in parts], axis=1)
        if width == group_full:
            right = t_ref[j, 0:group_out, :]
        else:
            right = jnp.concatenate([t_ref[j, 0:group_out, i * group_full : i * group_full + width] for i in range(3)], axis=1)
        term = mm(left, right, NT)
        total = term if total is None else total + term
    return total


def finish(acc, bias, mask, rows):
    value = jnp.maximum(acc + bias, 0.0) * mask
    return value.astype(BF).reshape(rows, value.shape[0] // rows, value.shape[1])


def fill_sides(left, right, lane, inner):
    cut = slice(lane, lane + inner.shape[2])
    none = jnp.zeros_like(inner[:, :1])
    left[:, :, cut] = jnp.concatenate([none, inner[:, :-1]], axis=1)
    right[:, :, cut] = jnp.concatenate([inner[:, 1:], none], axis=1)


def middle_kernel(win_ref, t_ref, b_ref, tab_ref, left_ref, right_ref, out_ref):
    for q in range(4):
        fill_sides(left_ref, right_ref, q * 128, win_ref[:, :, q * 128 : q * 128 + 128])
    rows = Y1 + 2
    mask = mask_rows(tab_ref[:, 128:256], -1, rows, X1, lambda x: x, 4)
    acc = conv_group([[(ref, 128, 384)] for ref in (left_ref, win_ref, right_ref)], t_ref, 0, rows, 256, 384)
    for q in range(2):
        cut = slice(q * 128, q * 128 + 128)
        out_ref[:, :, cut] = finish(acc[:, cut], b_ref[...], mask, rows)


def outer_kernel(win_ref, left_ref, right_ref, zl_ref, zr_ref, t_ref, b_ref, tab_ref, low_ref, high_ref, ll, lr, hl, hr):
    fill_sides(ll, lr, 0, zl_ref[...])
    fill_sides(hl, hr, 0, zr_ref[...])
    own = (left_ref, win_ref, right_ref)
    rows = Y1 + 2
    mask = mask_rows(tab_ref[...], -1, rows, X1, lambda x: x, 4)
    taps = [[(z, 0, 128), (ref, 0, 256)] for z, ref in zip((ll, zl_ref, lr), own)]
    acc = conv_group(taps, t_ref, 0, rows, 256, 384)
    for q in range(2):
        cut = slice(q * 128, q * 128 + 128)
        low_ref[:, :, cut] = finish(acc[:, cut], b_ref[...], mask[:, cut], rows)
    taps = [[(ref, 384, 128), (z, 0, 128)] for z, ref in zip((hl, zr_ref, hr), own)]
    acc = conv_group(taps, t_ref, 0, rows, 128, 384)
    high_ref[...] = finish(acc, b_ref[...], mask[:, 256:384], rows)


def fill_edges(copies, pieces):
    rows, pitch, lanes = copies[0].shape
    for lane in range(0, lanes, 128):
        line = [p[:, :, lane : lane + 128] for p in pieces]
        used = sum(p.shape[1] for p in line)
        for i, copy in enumerate(copies):
            moved = [line[0][:, i:]] + line[1:] if i < line[0].shape[1] else line[1:]
            spare = jnp.zeros((rows, pitch - used + i, 128), BF)
            copy[:, :, lane : lane + 128] = jnp.concatenate(moved + [spare], axis=1)


def level_one_kernel(
    xl_ref, low_ref, high_ref, xr_ref, g1_ref, g2_ref, g3_ref, ta_ref, tb_ref, ba_ref, bb_ref, wd_ref, bd_ref, tab_ref, tab2_ref,
    one_ref, down_ref, e0, e1, e2, i0, i1, i2, feat_ref, d_ref,
):
    fill_edges((e0, e1, e2), (xl_ref, low_ref, high_ref, xr_ref))
    rows = Y1 + 2
    mask = mask_rows(tab_ref[...], -1, rows, EDGE, lambda r: jnp.where(r < 4, r - 1, r + X1 - 5), 4)
    for g, (lane, width, out) in enumerate(((0, 384, 256), (256, 384, 256), (512, 256, 128))):
        acc = conv_group([[(e, lane, width)] for e in (e0, e1, e2)], ta_ref, 0, rows, out, 384)
        for q in range(out // 128):
            chunk = 2 * g + q
            which = 0 if chunk == 0 else (2 if chunk == 4 else 1)
            edge = finish(acc[:, q * 128 : q * 128 + 128], ba_ref[...], mask[:, which * 128 : which * 128 + 128], rows)
            inner = (g1_ref, g2_ref, g3_ref)[g][:, :, q * 128 : q * 128 + 128][:, 1:-1]
            cut = slice(chunk * 128, chunk * 128 + 128)
            i0[:, :, cut] = jnp.concatenate([edge[:, 0:2], inner], axis=1)
            i1[:, :, cut] = jnp.concatenate([edge[:, 1:2], inner, edge[:, 4:5]], axis=1)
            i2[:, :, cut] = jnp.concatenate([inner, edge[:, 4:6]], axis=1)

    mask = mask_rows(tab_ref[:, 128:256], 0, Y1, X1, lambda x: x, 4)
    for g in range(2):
        acc = conv_group([[(ref, 256 * g, 384)] for ref in (i0, i1, i2)], tb_ref, 0, Y1, 256, 384)
        for q in range(2):
            value = jnp.maximum(acc[:, q * 128 : q * 128 + 128] + bb_ref[...], 0.0) * mask
            feat_ref[:, (2 * g + q) * 128 : (2 * g + q + 1) * 128] = value.astype(BF)

    lanes = Z1 * C1
    size = 8 * X1
    quarter = size // 4
    r = iota((size, size), 0)
    ab = r // quarter
    y = (r % quarter) // X2
    select = one_hot((2 * y + ab % 2) * X1 + 2 * (r % X2) + ab // 2 == iota((size, size), 1))
    for n in range(Y1 // 8):
        cells = mm(select, feat_ref[n * size : n * size + size, :]).astype(BF)
        for q in range(4):
            d_ref[q, n * quarter : n * quarter + quarter, :] = cells[q * quarter : (q + 1) * quarter]
    mask = mask_rows(tab2_ref[:, 128:256], 0, Y2, X2, lambda x: x, 2)
    for z in range(Z2):
        left = jnp.concatenate([d_ref[q, :, z * 128 : z * 128 + 128] for q in range(4)], axis=1)
        down_ref[:, :, z * CP : z * CP + CP] = finish(mm(left, wd_ref[...]), bd_ref[...], mask, Y2)

    r = iota((lanes, lanes), 0)
    order = one_hot((r % Z1) * C1 + r // Z1 == iota((lanes, lanes), 1))
    one_ref[...] = mm(order, feat_ref[...], NT).astype(BF)


def level_two_kernel(
    win_ref, zl_ref, zr_ref, xl_ref, xr_ref, ta_ref, tb_ref, ba_ref, bb_ref, tab_ref, out_ref, a0, a1, a2, i0, i1, i2
):
    for chunk in range(8):
        ref, lane = (zl_ref, chunk) if chunk < 2 else ((win_ref, chunk - 2) if chunk < 6 else (zr_ref, chunk - 6))
        inner = ref[:, :, lane * 128 : lane * 128 + 128]
        cut = slice(chunk * 128, chunk * 128 + 128)
        left, right = xl_ref[:, :, cut], xr_ref[:, :, cut]
        for i, copy in enumerate((a0, a1, a2)):
            spare = jnp.zeros((ROWS2, PITCH2 - X2 - 4 + i, 128), BF)
            line = [inner, right, spare] if i == 2 else [left[:, i:], inner, right, spare]
            copy[:, :, cut] = jnp.concatenate(line, axis=1)
    rows = Y2 + 2
    mask = mask_rows(tab_ref[...], -1, rows, PITCH2, lambda x: x - 1, 2)
    for g in range(3):
        acc = conv_group([[(ref, 256 * g, 512)] for ref in (a0, a1, a2)], ta_ref, 0, rows, 256, 512)
        for q in range(2):
            chunk = 2 * g + q
            which = 0 if chunk == 0 else (2 if chunk == 5 else 1)
            value = finish(acc[:, q * 128 : q * 128 + 128], ba_ref[...], mask[:, which * 128 : which * 128 + 128], rows)
            cut = slice(chunk * 128, chunk * 128 + 128)
            for s, copy in enumerate((i0, i1, i2)):
                copy[:, :, cut] = value[:, s : s + X2]
    mask = mask_rows(tab_ref[:, 128:256], 0, Y2, X2, lambda x: x, 2)
    feat = []
    for g in range(2):
        acc = conv_group([[(ref, 256 * g, 512)] for ref in (i0, i1, i2)], tb_ref, 0, Y2, 256, 512)
        for q in range(2):
            feat.append((jnp.maximum(acc[:, q * 128 : q * 128 + 128] + bb_ref[...], 0.0) * mask).astype(BF))
    shape = (C2 * Z2, Z2 * CP)
    r = iota(shape, 0)
    order = one_hot((r % Z2) * CP + r // Z2 == iota(shape, 1))
    out_ref[...] = mm(order, jnp.concatenate(feat, axis=1), NT).astype(BF)


def swap_pairs(count, first):
    pairs = [(i, i) for i in range(first)]
    for i in range(first, count, 2):
        pairs += [(i, i + 1), (i + 1, i)] if i + 1 < count else [(i, i)]
    return pairs


def shift_along(low_edge, high_edge, axis):
    count = lax.axis_size(axis)
    index = lax.axis_index(axis)
    even = index % 2 == 0
    one = lax.ppermute(jnp.where(even, high_edge, low_edge), axis, swap_pairs(count, 0))
    two = one
    if count > 2:
        two = lax.ppermute(jnp.where(even, low_edge, high_edge), axis, swap_pairs(count, 1))
    below = jnp.where(index > 0, jnp.where(even, two, one), jnp.zeros_like(one))
    above = jnp.where(index < count - 1, jnp.where(even, one, two), jnp.zeros_like(one))
    return below, above


def params():
    return pltpu.CompilerParams(vmem_limit_bytes=VMEM_BYTES)


def cost(seconds):
    return pl.CostEstimate(flops=int(1e15 * seconds), bytes_accessed=0, transcendentals=0)


def shaped(*shape):
    return jax.ShapeDtypeStruct(shape, BF)


def pad_lanes(value):
    return jnp.pad(value, [(0, 0)] * (value.ndim - 1) + [(0, CP - value.shape[-1])])


def tissue_tables(tissue):
    flags = jnp.pad(tissue, 1)
    start = (8 * lax.axis_index("gx"), 4 * lax.axis_index("gy"), lax.axis_index("gz"))
    flags = lax.dynamic_slice(flags, start, (XB, YB, 3))
    flags = flags.transpose(1, 0, 2).reshape(YB * XB, 3).astype(F32)
    flags = jnp.pad(flags, ((0, 128 - YB * XB), (0, 0)))
    lane = iota((128, 384), 1)

    def spread(first, last):
        return jnp.where(lane < first, flags[:, 0:1], jnp.where(lane < last, flags[:, 1:2], flags[:, 2:3])).astype(BF)

    return spread(64, 320), spread(128, 256)


def local(
    volume, tissue, w_down1, b_down1, w_conv1a, b_conv1a, w_conv1b, b_conv1b,
    w_down2, b_down2, w_conv2a, b_conv2a, w_conv2b, b_conv2b,
):
    depth = volume.shape[1]
    kz = C0 * depth
    lanes1 = Z1 * C1
    tab1, tab2 = tissue_tables(tissue)
    own = pl.pallas_call(
        down1_kernel,
        in_specs=[pl.BlockSpec(memory_space=pltpu.HBM)] + [pl.BlockSpec(memory_space=pltpu.VMEM)] * 3,
        out_shape=shaped(Y1, X1, lanes1),
        scratch_shapes=[
            pltpu.VMEM((4 * kz, lanes1), BF),
            pltpu.VMEM(volume.shape, BF),
            pltpu.VMEM((Y1 * X1, 4 * kz), BF),
            pltpu.SemaphoreType.DMA((volume.shape[2] // 256,)),
        ],
        compiler_params=params(),
        cost_estimate=cost(4e-6),
    )(volume, jnp.swapaxes(w_down1, 1, 2), jnp.tile(b_down1, 2)[None], tab1)

    t1a = banded(w_conv1a, 4, C1)
    t1b = banded(w_conv1b, 4, C1)
    t2a = banded(w_conv2a, 2, CP)
    t2b = banded(w_conv2b, 2, CP)
    bias1a = jnp.tile(b_conv1a, 2)[None]

    y_below, y_above = shift_along(own[:HALO], own[Y1 - HALO :], "gy")
    win = jnp.concatenate([y_below, own, y_above], axis=0)
    z_below, z_above = shift_along(win[:, :, :128], win[:, :, lanes1 - 128 :], "gz")
    rows = Y1 + 2
    left, right, g2 = pl.pallas_call(
        middle_kernel,
        out_shape=[shaped(ROWS1, X1, lanes1), shaped(ROWS1, X1, lanes1), shaped(rows, X1, 256)],
        compiler_params=params(),
        cost_estimate=cost(3e-6),
    )(win, t1a, bias1a, tab1)

    low = jnp.concatenate([z_below[:, :2], win[:, :2], z_above[:, :2]], axis=2)
    high = jnp.concatenate([z_below[:, X1 - 2 :], win[:, X1 - 2 :], z_above[:, X1 - 2 :]], axis=2)
    x_below, x_above = shift_along(low, high, "gx")
    g1, g3 = pl.pallas_call(
        outer_kernel,
        out_shape=[shaped(rows, X1, 256), shaped(rows, X1, 128)],
        scratch_shapes=[pltpu.VMEM((ROWS1, X1, 128), BF)] * 4,
        compiler_params=params(),
        cost_estimate=cost(4e-6),
    )(win, left, right, z_below, z_above, t1a, bias1a, tab1)

    one, down = pl.pallas_call(
        level_one_kernel,
        out_shape=[shaped(lanes1, Y1 * X1), shaped(Y2, X2, Z2 * CP)],
        scratch_shapes=[pltpu.VMEM((ROWS1, EDGE, (Z1 + 4) * C1), BF)] * 3
        + [pltpu.VMEM((rows, X1, (Z1 + 2) * C1), BF)] * 3
        + [pltpu.VMEM((Y1 * X1, lanes1), BF), pltpu.VMEM((4, Y2 * X2, lanes1), BF)],
        compiler_params=params(),
        cost_estimate=cost(6e-6),
    )(
        x_below, low, high, x_above, g1, g2, g3, t1a, t1b, bias1a, jnp.tile(b_conv1b, 2)[None],
        pad_lanes(jnp.swapaxes(w_down2, 1, 2).reshape(8 * C1, C2)), pad_lanes(b_down2[None]), tab1, tab2,
    )

    y_below, y_above = shift_along(down[:HALO], down[Y2 - HALO :], "gy")
    win = jnp.concatenate([y_below, down, y_above], axis=0)
    z_below, z_above = shift_along(win[:, :, : 2 * CP], win[:, :, 2 * CP :], "gz")
    low = jnp.concatenate([z_below[:, :2], win[:, :2], z_above[:, :2]], axis=2)
    high = jnp.concatenate([z_below[:, X2 - 2 :], win[:, X2 - 2 :], z_above[:, X2 - 2 :]], axis=2)
    x_below, x_above = shift_along(low, high, "gx")
    two = pl.pallas_call(
        level_two_kernel,
        out_shape=shaped(C2 * Z2, Y2 * X2),
        scratch_shapes=[pltpu.VMEM((ROWS2, PITCH2, (Z2 + 4) * CP), BF)] * 3
        + [pltpu.VMEM((Y2 + 2, X2, (Z2 + 2) * CP), BF)] * 3,
        compiler_params=params(),
        cost_estimate=cost(5e-6),
    )(win, z_below, z_above, x_below, x_above, t2a, t2b, pad_lanes(b_conv2a[None]), pad_lanes(b_conv2b[None]), tab2)
    return one.reshape(C1, Z1, Y1 * X1), two.reshape(C2, Z2, Y2 * X2)


def solution(mesh):
    block = P(None, "gz", ("gx", "gy"))
    return jax.shard_map(
        local,
        mesh=mesh,
        in_specs=(block,) + (P(),) * 13,
        out_specs=(block, block),
        check_vma=False,
    )
```

time: 61.2 us -> 59.7 us (0.975)
  the two profiles are of different devices: /device:TPU:20 before, /device:TPU:10 now
where the time goes in v2:
time: 59.7 us; the launch traced here: 59.4 us
  Pallas kernels  23.8 us (40%)
  waiting for transfers between devices  14.6 us (24%)
  starting transfers between devices  13.8 us (23%)
  local copies, waits for them, and re-layouts  4.34 us (7%)
  other arithmetic  1.67 us (3%)
  between operations  1.1 us (2%)
    ppermute x4, starting transfers between devices, shift_along(): lax.ppermute(jnp.where(even, low_edge, high_edge), axis, swap_pairs(count...  12.7 us
    ppermute x4, waiting for transfers between devices, shift_along(): lax.ppermute(jnp.where(even, low_edge, high_edge), axis, swap_pairs(count...  9.53 us
    pallas_call x1, Pallas kernels, local(): pl.pallas_call(level_one_kernel, out_shape=[shaped(lanes1, Y1 * X1), shap...  6.31 us
    pallas_call x1, Pallas kernels, local(): pl.pallas_call(level_two_kernel, out_shape=shaped(C2 * Z2, Y2 * X2), scra...  6.13 us
    pallas_call x1, Pallas kernels, local(): pl.pallas_call(down1_kernel, in_specs=[pl.BlockSpec(memory_space=pltpu.HB...  5.82 us
    ppermute x6, waiting for transfers between devices, shift_along(): lax.ppermute(jnp.where(even, high_edge, low_edge), axis, swap_pairs(count...  5.07 us
    unnamed x24, local copies, waits for them, and re-layouts  3.08 us
    pallas_call x1, Pallas kernels, local(): pl.pallas_call(outer_kernel, out_shape=[shaped(rows, X1, 256), shaped(row...  2.15 us
  transfers between devices with their start and end apart: 10, of which 8 were waited for; matrix products, arithmetic and copies ran while one was open for 1% of the time, Pallas kernels for 9%

profile of v2, /device:TPU:10, one launch (start us, length us, event | category | flops | bytes accessed | tf_op | source)
XLA Modules:
  0.0 59.4 jit_solution(6159525300986780369)
XLA Ops:
  0.7 0.7 %tile.6 = f32[2,64]{1,0:T(2,128)S(1)} broadcast(f32[64]{0:T(128)} %param.17), dimensions={1} | broadcast | bytes 768 | tf_op jit(solution)/shard_map/tile | solution.py:329
  1.4 0.8 %fusion.1 = bf16[6,10,3]{1,2,0:T(4,128)(2,1)S(1)} fusion(s32[]{:T(128)S(6)} %select_n.229, s32[]{:T(128)S(6)} %select_n.230, s32[]{:T(128)S(6)} %select_n.231, s32[32,8,4]{0,2,1:T(4,128)} %param.15), kind=kLoop, calls=%fused_computation.36 | loop fusion | flops 180 | bytes 4468 | tf_op jit(solution)/shard_map/convert_element_type | solution.py:299
  2.3 0.1 select_convert_fusion
  2.5 1.9 %copy-done = bf16[48,16,2048]{2,1,0:T(8,128)(2,1)S(1)} copy-done((bf16[48,16,2048]{2,1,0:T(8,128)(2,1)S(1)}, bf16[48,16,2048]{2,1,0:T(8,128)(2,1)}, u32[]{:S(2)}) %copy-start) | copy-done | bytes 3145752
  4.4 0.9 %copy-done.5 = bf16[8,64,48]{1,2,0:T(8,128)(2,1)S(1)} copy-done((bf16[8,64,48]{1,2,0:T(8,128)(2,1)S(1)}, bf16[8,64,48]{1,2,0:T(8,128)(2,1)}, u32[]{:S(2)}) %copy-start.5) | copy-done | bytes 49176
  5.3 5.8 %shard_map.149 = bf16[16,32,512]{2,1,0:T(8,128)(2,1)S(1)} custom-call(bf16[48,16,2048]{2,1,0:T(8,128)(2,1)S(1)} %copy-done, bf16[8,48,64]{2,1,0:T(8,128)(2,1)S(1)} %bitcast.24, f32[1,128]{1,0:T(1,128)S(1)} %broadcast_in_dim_tile.9.b_ref, bf16[128,384]{1,0:T(8,128)(2,1)S(1)} %get-tuple-element.50.tab_ref), custom_call_target="tpu_custom_call" | custom-call | flops 4000000000 | tf_op jit(solution)/shard_map/pallas_call | solution.py:317
  11.5 0.6 %shard_map.150.t_ref.ta_ref = bf16[3,256,1152]{2,1,0:T(8,128)(2,1)S(1)} custom-call(bf16[27,64,64]{2,1,0:T(8,128)(2,1)S(1)} %copy-done.3), custom_call_target="tpu_custom_call" | custom-call | flops 1000000000 | tf_op jit(solution)/shard_map/pallas_call | solution.py:103
  12.2 0.6 %shard_map.153.tb_ref = bf16[3,256,1152]{2,1,0:T(8,128)(2,1)S(1)} custom-call(bf16[27,64,64]{2,1,0:T(8,128)(2,1)S(1)} %copy-done.4), custom_call_target="tpu_custom_call" | custom-call | flops 1000000000 | tf_op jit(solution)/shard_map/pallas_call | solution.py:103
  13.0 3.5 %collective-permute-start.1 = (bf16[20,32,128]{2,1,0:T(8,128)(2,1)S(1)}, bf16[20,32,128]{2,1,0:T(8,128)(2,1)S(1)}, u32[]{:S(2)}, u32[]{:S(2)}) collective-permute-start(bf16[20,32,128]{2,1,0:T(8,128)(2,1)S(1)} %get-tuple-element.21), channel_id=1, source_target_pairs={{0,0},{1,2},{2,1},{3,3},{4,4},{5,6},{6,5},{7,7},{8,8},{9,10},{10,9... | collective-permute-start | bytes 491528 | tf_op jit(solution)/shard_map/ppermute | solution.py:273
  16.6 1.5 %shard_map.151 = (bf16[20,32,512]{2,1,0:T(8,128)(2,1)S(1)}, bf16[20,32,512]{2,1,0:T(8,128)(2,1)S(1)}, bf16[18,32,256]{2,1,0:T(8,128)(2,1)S(1)}) custom-call(bf16[20,32,512]{2,1,0:T(8,128)(2,1)S(1)} %pad_maximum_fusion.win_ref, bf16[3,256,1152]{2,1,0:T(8,128)(2,1)S(1)} %shard_map.150.t_ref.ta_ref, f32[1,128]{1,0:T(1,128)S(1)} %broadcast_in_dim_tile.10.b_ref.ba_ref, ...), custom_call_target="tpu_custom_call" | custom-call | flops 3000000000 | tf_op jit(solution)/shard_map/pallas_call | solution.py:341
  18.2 3.2 %collective-permute-done.1 = bf16[20,32,128]{2,1,0:T(8,128)(2,1)S(1)} collective-permute-done((bf16[20,32,128]{2,1,0:T(8,128)(2,1)S(1)}, bf16[20,32,128]{2,1,0:T(8,128)(2,1)S(1)}, u32[]{:S(2)}, u32[]{:S(2)}) %collective-permute-start.1) | collective-permute-done | bytes 163872 | tf_op jit(solution)/shard_map/ppermute | solution.py:273
  21.4 1.4 %collective-permute-done.2 = bf16[20,32,128]{2,1,0:T(8,128)(2,1)S(1)} collective-permute-done((bf16[20,32,128]{2,1,0:T(8,128)(2,1)S(1)}, bf16[20,32,128]{2,1,0:T(8,128)(2,1)S(1)}, u32[]{:S(2)}, u32[]{:S(2)}) %collective-permute-start.2) | collective-permute-done | bytes 163872 | tf_op jit(solution)/shard_map/ppermute | solution.py:270
  22.9 0.1 broadcast_select_fusion.5
  23.1 3.6 %collective-permute-start.3 = (bf16[20,2,768]{2,1,0:T(2,128)(2,1)S(1)}, bf16[20,2,768]{2,1,0:T(2,128)(2,1)S(1)}, u32[]{:S(2)}, u32[]{:S(2)}) collective-permute-start(bf16[20,2,768]{2,1,0:T(2,128)(2,1)S(1)} %bitcast.26), channel_id=1, source_target_pairs={{0,0},{8,16},{16,8},{24,24},{1,1},{9,17},{17,9},{25,25},{2,2},{10,... | collective-permute-start | bytes 184328 | tf_op jit(solution)/shard_map/ppermute | solution.py:273
  26.7 2.2 %shard_map.152 = (bf16[18,32,256]{2,1,0:T(8,128)(2,1)S(1)}, bf16[18,32,128]{2,1,0:T(8,128)(2,1)S(1)}) custom-call(bf16[20,32,512]{2,1,0:T(8,128)(2,1)S(1)} %pad_maximum_fusion.win_ref, bf16[20,32,512]{2,1,0:T(8,128)(2,1)S(1)} %get-tuple-element.9.left_ref, bf16[20,32,512]{2,1,0:T(8,128)(2,1)S(1)} %get-tuple-element.10.right_ref, ...), custom_call_target="tpu_custom_call" | custom-call | flops 4000000000 | tf_op jit(solution)/shard_map/pallas_call | solution.py:351
  28.9 1.2 %collective-permute-done.3 = bf16[20,2,768]{2,1,0:T(2,128)(2,1)S(1)} collective-permute-done((bf16[20,2,768]{2,1,0:T(2,128)(2,1)S(1)}, bf16[20,2,768]{2,1,0:T(2,128)(2,1)S(1)}, u32[]{:S(2)}, u32[]{:S(2)}) %collective-permute-start.3) | collective-permute-done | bytes 61472 | tf_op jit(solution)/shard_map/ppermute | solution.py:273
  30.1 0.9 %collective-permute-done.4 = bf16[20,2,768]{2,1,0:T(2,128)(2,1)S(1)} collective-permute-done((bf16[20,2,768]{2,1,0:T(2,128)(2,1)S(1)}, bf16[20,2,768]{2,1,0:T(2,128)(2,1)S(1)}, u32[]{:S(2)}, u32[]{:S(2)}) %collective-permute-start.4) | collective-permute-done | bytes 61472 | tf_op jit(solution)/shard_map/ppermute | solution.py:270
  30.9 0.1 broadcast_select_fusion.2
  31.1 6.3 %shard_map.154 = (bf16[512,512]{1,0:T(8,128)(2,1)}, bf16[8,16,512]{2,1,0:T(8,128)(2,1)S(1)}) custom-call(bf16[20,2,768]{2,1,0:T(2,128)(2,1)S(1)} %get-tuple-element.36.xl_ref, bf16[20,2,768]{2,1,0:T(2,128)(2,1)S(1)} %get-tuple-element.18.low_ref, bf16[20,2,768]{2,1,0:T(2,128)(2,1)S(1)} %get-tuple-element.17.high_ref, ...), custom_call_target="tpu_custom_call" | custom-call | flops 6000000000 | tf_op jit(solution)/shard_map/pallas_call | solution.py:359
  37.5 0.3 shard_map.155.ta_ref
  37.8 0.2 copy-done.10
  38.1 0.6 %collective-permute-done.5 = bf16[2,16,512]{2,1,0:T(8,128)(2,1)S(1)} collective-permute-done((bf16[2,16,512]{2,1,0:T(8,128)(2,1)S(1)}, bf16[2,16,512]{2,1,0:T(8,128)(2,1)S(1)}, u32[]{:S(2)}, u32[]{:S(2)}) %collective-permute-start.5) | collective-permute-done | bytes 32800 | tf_op jit(solution)/shard_map/ppermute | solution.py:270
  38.8 0.4 collective-permute-start.7
  39.1 2.3 %collective-permute-start.6 = (bf16[12,16,256]{2,1,0:T(8,128)(2,1)S(1)}, bf16[12,16,256]{2,1,0:T(8,128)(2,1)S(1)}, u32[]{:S(2)}, u32[]{:S(2)}) collective-permute-start(bf16[12,16,256]{2,1,0:T(8,128)(2,1)S(1)} %get-tuple-element.30), channel_id=1, source_target_pairs={{0,0},{1,2},{2,1},{3,3},{4,4},{5,6},{6,5},{7,7},{8,8},{9,10},{10,9... | collective-permute-start | bytes 294920 | tf_op jit(solution)/shard_map/ppermute | solution.py:273
  41.5 2.2 %collective-permute-done.7 = bf16[12,16,256]{2,1,0:T(8,128)(2,1)S(1)} collective-permute-done((bf16[12,16,256]{2,1,0:T(8,128)(2,1)S(1)}, bf16[12,16,256]{2,1,0:T(8,128)(2,1)S(1)}, u32[]{:S(2)}, u32[]{:S(2)}) %collective-permute-start.7) | collective-permute-done | bytes 98336 | tf_op jit(solution)/shard_map/ppermute | solution.py:270
  43.7 1.9 %collective-permute-done.6 = bf16[12,16,256]{2,1,0:T(8,128)(2,1)S(1)} collective-permute-done((bf16[12,16,256]{2,1,0:T(8,128)(2,1)S(1)}, bf16[12,16,256]{2,1,0:T(8,128)(2,1)S(1)}, u32[]{:S(2)}, u32[]{:S(2)}) %collective-permute-start.6) | collective-permute-done | bytes 98336 | tf_op jit(solution)/shard_map/ppermute | solution.py:273
  45.7 0.1 broadcast_select_fusion.11
  45.8 0.5 collective-permute-start.9
  46.3 3.3 %collective-permute-start.8 = (bf16[12,2,1024]{2,1,0:T(2,128)(2,1)S(1)}, bf16[12,2,1024]{2,1,0:T(2,128)(2,1)S(1)}, u32[]{:S(2)}, u32[]{:S(2)}) collective-permute-start(bf16[12,2,1024]{2,1,0:T(2,128)(2,1)S(1)} %get-tuple-element.40), channel_id=1, source_target_pairs={{0,0},{8,16},{16,8},{24,24},{1,1},{9,17},{17,9},{25,25},{2,2},{10,... | collective-permute-start | bytes 147464 | tf_op jit(solution)/shard_map/ppermute | solution.py:273
  49.6 0.3 shard_map.156.tb_ref
  50.0 3.2 %collective-permute-done.8 = bf16[12,2,1024]{2,1,0:T(2,128)(2,1)S(1)} collective-permute-done((bf16[12,2,1024]{2,1,0:T(2,128)(2,1)S(1)}, bf16[12,2,1024]{2,1,0:T(2,128)(2,1)S(1)}, u32[]{:S(2)}, u32[]{:S(2)}) %collective-permute-start.8) | collective-permute-done | bytes 49184 | tf_op jit(solution)/shard_map/ppermute | solution.py:273
  53.2 6.1 %shard_map.157 = bf16[384,128]{1,0:T(8,128)(2,1)} custom-call(bf16[12,16,512]{2,1,0:T(8,128)(2,1)S(1)} %pad_maximum_fusion.1.win_ref, bf16[12,16,256]{2,1,0:T(8,128)(2,1)S(1)} %get-tuple-element.28.zl_ref, bf16[12,16,256]{2,1,0:T(8,128)(2,1)S(1)} %get-tuple-element.27.zr_ref, bf16[12,2,1024]{2,1,0:T(2,128)(2,1)S(1)} %get-tuple-element.38.xl_ref, ...), custom_call_target="tpu_custom_call" | custom-call | flops 5000000000 | tf_op jit(solution)/shard_map/pallas_call | solution.py:378
  (59 shorter events, 1.4 us)
Async XLA Ops:
  2.5 1.9 %copy-start = (bf16[48,16,2048]{2,1,0:T(8,128)(2,1)S(1)}, bf16[48,16,2048]{2,1,0:T(8,128)(2,1)}, u32[]{:S(2)}) copy-start(bf16[48,16,2048]{2,1,0:T(8,128)(2,1)} %v_ref.1) | copy-start | bytes 9437188
  4.4 0.9 %copy-start.5 = (bf16[8,64,48]{1,2,0:T(8,128)(2,1)S(1)}, bf16[8,64,48]{1,2,0:T(8,128)(2,1)}, u32[]{:S(2)}) copy-start(bf16[8,64,48]{1,2,0:T(8,128)(2,1)} %param.16) | copy-start | bytes 147460
  5.2 6.0 %copy-start.7 = (f32[64]{0:T(128)S(1)}, f32[64]{0:T(128)}, u32[]{:S(2)}) copy-start(f32[64]{0:T(128)} %param.19) | copy-start | bytes 772
  5.2 6.1 %copy-start.8 = (f32[64]{0:T(128)S(1)}, f32[64]{0:T(128)}, u32[]{:S(2)}) copy-start(f32[64]{0:T(128)} %param.21) | copy-start | bytes 772
  5.3 6.2 %copy-start.3 = (bf16[27,64,64]{2,1,0:T(8,128)(2,1)S(1)}, bf16[27,64,64]{2,1,0:T(8,128)(2,1)}, u32[]{:S(2)}) copy-start(bf16[27,64,64]{2,1,0:T(8,128)(2,1)} %w_ref.4) | copy-start | bytes 663556
  11.1 1.0 %copy-start.9 = (f32[96]{0:T(128)S(1)}, f32[96]{0:T(128)}, u32[]{:S(2)}) copy-start(f32[96]{0:T(128)} %param.23) | copy-start | bytes 1156
  11.1 1.0 %copy-start.6 = (bf16[8,96,64]{1,2,0:T(8,128)(2,1)S(1)}, bf16[8,96,64]{1,2,0:T(8,128)(2,1)}, u32[]{:S(2)}) copy-start(bf16[8,96,64]{1,2,0:T(8,128)(2,1)} %param.22) | copy-start | bytes 294916
  11.1 1.1 %copy-start.4 = (bf16[27,64,64]{2,1,0:T(8,128)(2,1)S(1)}, bf16[27,64,64]{2,1,0:T(8,128)(2,1)}, u32[]{:S(2)}) copy-start(bf16[27,64,64]{2,1,0:T(8,128)(2,1)} %w_ref.5) | copy-start | bytes 663556
  11.1 1.7 %collective-permute-start = (bf16[2,32,512]{2,1,0:T(8,128)(2,1)S(1)}, bf16[2,32,512]{2,1,0:T(8,128)(2,1)S(1)}, u32[]{:S(2)}, u32[]{:S(2)}) collective-permute-start(bf16[2,32,512]{2,1,0:T(8,128)(2,1)S(1)} %slice_select_fusion), channel_id=1, source_target_pairs={{0,4},{4,0},{1,5},{5,1},{2,6},{6,2},{3,7},{7,3},{8,12},{12,8},{9,1... | collective-permute-start | bytes 196616 | tf_op jit(solution)/shard_map/ppermute | solution.py:270
  13.0 8.4 %collective-permute-start.1 = (bf16[20,32,128]{2,1,0:T(8,128)(2,1)S(1)}, bf16[20,32,128]{2,1,0:T(8,128)(2,1)S(1)}, u32[]{:S(2)}, u32[]{:S(2)}) collective-permute-start(bf16[20,32,128]{2,1,0:T(8,128)(2,1)S(1)} %get-tuple-element.21), channel_id=1, source_target_pairs={{0,0},{1,2},{2,1},{3,3},{4,4},{5,6},{6,5},{7,7},{8,8},{9,10},{10,9... | collective-permute-start | bytes 491528 | tf_op jit(solution)/shard_map/ppermute | solution.py:273
  16.5 6.3 %collective-permute-start.2 = (bf16[20,32,128]{2,1,0:T(8,128)(2,1)S(1)}, bf16[20,32,128]{2,1,0:T(8,128)(2,1)S(1)}, u32[]{:S(2)}, u32[]{:S(2)}) collective-permute-start(bf16[20,32,128]{2,1,0:T(8,128)(2,1)S(1)} %get-tuple-element.22), channel_id=1, source_target_pairs={{0,1},{1,0},{2,3},{3,2},{4,5},{5,4},{6,7},{7,6},{8,9},{9,8},{10,11... | collective-permute-start | bytes 491528 | tf_op jit(solution)/shard_map/ppermute | solution.py:270
  23.1 7.0 %collective-permute-start.3 = (bf16[20,2,768]{2,1,0:T(2,128)(2,1)S(1)}, bf16[20,2,768]{2,1,0:T(2,128)(2,1)S(1)}, u32[]{:S(2)}, u32[]{:S(2)}) collective-permute-start(bf16[20,2,768]{2,1,0:T(2,128)(2,1)S(1)} %bitcast.26), channel_id=1, source_target_pairs={{0,0},{8,16},{16,8},{24,24},{1,1},{9,17},{17,9},{25,25},{2,2},{10,... | collective-permute-start | bytes 184328 | tf_op jit(solution)/shard_map/ppermute | solution.py:273
  26.7 4.3 %collective-permute-start.4 = (bf16[20,2,768]{2,1,0:T(2,128)(2,1)S(1)}, bf16[20,2,768]{2,1,0:T(2,128)(2,1)S(1)}, u32[]{:S(2)}, u32[]{:S(2)}) collective-permute-start(bf16[20,2,768]{2,1,0:T(2,128)(2,1)S(1)} %get-tuple-element.16), channel_id=1, source_target_pairs={{0,8},{8,0},{16,24},{24,16},{1,9},{9,1},{17,25},{25,17},{2,10},{10... | collective-permute-start | bytes 184328 | tf_op jit(solution)/shard_map/ppermute | solution.py:270
  31.1 6.4 %copy-start.1 = (bf16[27,96,96]{2,1,0:T(8,128)(2,1)S(1)}, bf16[27,96,96]{2,1,0:T(8,128)(2,1)}, u32[]{:S(2)}) copy-start(bf16[27,96,96]{2,1,0:T(8,128)(2,1)} %w_ref.6) | copy-start | bytes 1492996
  37.4 0.7 %copy-start.10 = (f32[96]{0:T(128)S(1)}, f32[96]{0:T(128)}, u32[]{:S(2)}) copy-start(f32[96]{0:T(128)} %param.25) | copy-start | bytes 1156
  37.4 0.7 %copy-start.11 = (f32[96]{0:T(128)S(1)}, f32[96]{0:T(128)}, u32[]{:S(2)}) copy-start(f32[96]{0:T(128)} %param.27) | copy-start | bytes 1156
  37.4 12.2 %copy-start.2 = (bf16[27,96,96]{2,1,0:T(8,128)(2,1)S(1)}, bf16[27,96,96]{2,1,0:T(8,128)(2,1)}, u32[]{:S(2)}) copy-start(bf16[27,96,96]{2,1,0:T(8,128)(2,1)} %w_ref.7) | copy-start | bytes 1492996
  37.4 1.3 %collective-permute-start.5 = (bf16[2,16,512]{2,1,0:T(8,128)(2,1)S(1)}, bf16[2,16,512]{2,1,0:T(8,128)(2,1)S(1)}, u32[]{:S(2)}, u32[]{:S(2)}) collective-permute-start(bf16[2,16,512]{2,1,0:T(8,128)(2,1)S(1)} %slice_select_fusion.1), channel_id=1, source_target_pairs={{0,4},{4,0},{1,5},{5,1},{2,6},{6,2},{3,7},{7,3},{8,12},{12,8},{9,1... | collective-permute-start | bytes 98312 | tf_op jit(solution)/shard_map/ppermute | solution.py:270
  38.8 4.9 %collective-permute-start.7 = (bf16[12,16,256]{2,1,0:T(8,128)(2,1)S(1)}, bf16[12,16,256]{2,1,0:T(8,128)(2,1)S(1)}, u32[]{:S(2)}, u32[]{:S(2)}) collective-permute-start(bf16[12,16,256]{2,1,0:T(8,128)(2,1)S(1)} %get-tuple-element.29), channel_id=1, source_target_pairs={{0,1},{1,0},{2,3},{3,2},{4,5},{5,4},{6,7},{7,6},{8,9},{9,8},{10,11... | collective-permute-start | bytes 294920 | tf_op jit(solution)/shard_map/ppermute | solution.py:270
  39.1 6.5 %collective-permute-start.6 = (bf16[12,16,256]{2,1,0:T(8,128)(2,1)S(1)}, bf16[12,16,256]{2,1,0:T(8,128)(2,1)S(1)}, u32[]{:S(2)}, u32[]{:S(2)}) collective-permute-start(bf16[12,16,256]{2,1,0:T(8,128)(2,1)S(1)} %get-tuple-element.30), channel_id=1, source_target_pairs={{0,0},{1,2},{2,1},{3,3},{4,4},{5,6},{6,5},{7,7},{8,8},{9,10},{10,9... | collective-permute-start | bytes 294920 | tf_op jit(solution)/shard_map/ppermute | solution.py:273
  45.8 4.2 %collective-permute-start.9 = (bf16[12,2,1024]{2,1,0:T(2,128)(2,1)S(1)}, bf16[12,2,1024]{2,1,0:T(2,128)(2,1)S(1)}, u32[]{:S(2)}, u32[]{:S(2)}) collective-permute-start(bf16[12,2,1024]{2,1,0:T(2,128)(2,1)S(1)} %get-tuple-element.39), channel_id=1, source_target_pairs={{0,8},{8,0},{16,24},{24,16},{1,9},{9,1},{17,25},{25,17},{2,10},{10... | collective-permute-start | bytes 147464 | tf_op jit(solution)/shard_map/ppermute | solution.py:270
  46.3 6.9 %collective-permute-start.8 = (bf16[12,2,1024]{2,1,0:T(2,128)(2,1)S(1)}, bf16[12,2,1024]{2,1,0:T(2,128)(2,1)S(1)}, u32[]{:S(2)}, u32[]{:S(2)}) collective-permute-start(bf16[12,2,1024]{2,1,0:T(2,128)(2,1)S(1)} %get-tuple-element.40), channel_id=1, source_target_pairs={{0,0},{8,16},{16,8},{24,24},{1,1},{9,17},{17,9},{25,25},{2,2},{10,... | collective-permute-start | bytes 147464 | tf_op jit(solution)/shard_map/ppermute | solution.py:273

commit v3 on v2

--- a/solution.py
+++ b/solution.py
@@ -51,23 +51,49 @@
     return mm(hit, tab)
 
 
-def down1_kernel(v_ref, w_ref, b_ref, tab_ref, out_ref, wd_ref, field_ref, cells_ref, sems):
-    z0 = v_ref.shape[1]
-    kz = C0 * z0
-    lanes = Z1 * C1
+def tissue_tables(t_ref):
+    n_y, n_z, n_x = t_ref.shape
+    here = lax.axis_index("gz")
+    layers = []
+    for k in (-1, 0, 1):
+        z = here + k
+        inside = jnp.where((z >= 0) & (z < n_z), 1.0, 0.0)
+        layers.append(t_ref[:, jnp.clip(z, 0, n_z - 1), :].astype(F32) * inside)
+    block = iota((128, n_y), 0)
+    hot_y = one_hot((block < YB * XB) & (lax.axis_index("gy") * 4 - 1 + block // XB == iota((128, n_y), 1)))
+    block = iota((128, 3 * n_x), 0)
+    hot_x = lax.axis_index("gx") * 8 - 1 + block % XB == iota((128, 3 * n_x), 1) % n_x
+    rows = jnp.where(hot_x, mm(hot_y, jnp.concatenate(layers, axis=1).astype(BF)), 0.0).astype(BF)
+    shape = (3 * n_x, 384)
+    layer, lane = iota(shape, 0) // n_x, iota(shape, 1)
+
+    def spread(first, last):
+        place = jnp.where(lane < first, 0, jnp.where(lane < last, 1, 2))
+        return mm(rows, one_hot(layer == place)).astype(BF)
+
+    return spread(64, 320), spread(128, 256)
+
+
+def down1_kernel(v_ref, w_ref, b_ref, t_ref, out_ref, tab_ref, tab2_ref, wd_ref, field_ref, cells_ref, sems):
+    half = v_ref.shape[2]
+    kz = C0 * half
+    lanes = Z1 // 2 * C1
     copies = []
     for n in range(sems.shape[0]):
-        cut = (slice(None), slice(None), slice(n * 256, n * 256 + 256))
+        cut = (slice(None), slice(None), slice(None), slice(n * 256, n * 256 + 256))
         copies.append(pltpu.make_async_copy(v_ref.at[cut], field_ref.at[cut], sems.at[n]))
         copies[-1].start()
 
+    tab, tab2 = tissue_tables(t_ref)
+    tab_ref[...] = tab
+    tab2_ref[...] = tab2
     r = iota((kz, 2 * C0), 0)
     l = iota((kz, 2 * C0), 1)
-    spread = one_hot((r // z0 == l % C0) & (r % 2 == l // C0))
-    keep = (iota((kz, lanes), 0) % z0) // 2 == iota((kz, lanes), 1) // C1
+    spread = one_hot((r // half == l % C0) & (r % 2 == l // C0))
+    keep = (iota((kz, lanes), 0) % half) // 2 == iota((kz, lanes), 1) // C1
     for ab in range(4):
         pair = w_ref[2 * ab : 2 * ab + 2].reshape(2 * C0, C1)
-        wide = jnp.concatenate([pair] * Z1, axis=1)
+        wide = jnp.concatenate([pair] * (Z1 // 2), axis=1)
         wd_ref[ab * kz : (ab + 1) * kz, :] = jnp.where(keep, mm(spread, wide), 0.0).astype(BF)
 
     shape = (4 * CX, 4 * CX)
@@ -76,16 +102,22 @@
     select = one_hot((2 * y + b) * CX + 2 * x + a == iota(shape, 1))
     for n, copy in enumerate(copies):
         copy.wait()
-        v = field_ref[:, :, n * 256 : n * 256 + 256].reshape(kz, 256)
-        cells = mm(select, v, NT).astype(BF)
-        for ab in range(4):
-            cells_ref[n * 64 : n * 64 + 64, ab * kz : (ab + 1) * kz] = cells[64 * ab : 64 * ab + 64]
-    mask = mask_rows(tab_ref[:, 128:256], 0, Y1, X1, lambda x: x, 4)
-    acc = mm(cells_ref[...], wd_ref[...])
-    for q in range(4):
-        cut = slice(q * 128, q * 128 + 128)
-        value = jnp.maximum(acc[:, cut] + b_ref[...], 0.0) * mask
-        out_ref[:, :, cut] = value.astype(BF).reshape(Y1, X1, 128)
+        for h in range(2):
+            v = field_ref[:, h, :, n * 256 : n * 256 + 256].reshape(kz, 256)
+            cells = mm(select, v, NT).astype(BF)
+            for ab in range(4):
+                cells_ref[h, n * 64 : n * 64 + 64, ab * kz : (ab + 1) * kz] = cells[64 * ab : 64 * ab + 64]
+    mask = mask_rows(tab[:, 128:256], 0, Y1, X1, lambda x: x, 4)
+    bias = twice(b_ref)
+    for h in range(2):
+        acc = mm(cells_ref[h], wd_ref[...])
+        for q in range(2):
+            value = finish(acc[:, q * 128 : q * 128 + 128], bias, mask, Y1)
+            out_ref[:, :, (2 * h + q) * 128 : (2 * h + q + 1) * 128] = value
+
+
+def twice(b_ref):
+    return jnp.concatenate([b_ref[...]] * 2, axis=1)
 
 
 def banded(weights, group, pad):
@@ -144,7 +176,7 @@
     acc = conv_group([[(ref, 128, 384)] for ref in (left_ref, win_ref, right_ref)], t_ref, 0, rows, 256, 384)
     for q in range(2):
         cut = slice(q * 128, q * 128 + 128)
-        out_ref[:, :, cut] = finish(acc[:, cut], b_ref[...], mask, rows)
+        out_ref[:, :, cut] = finish(acc[:, cut], twice(b_ref), mask, rows)
 
 
 def outer_kernel(win_ref, left_ref, right_ref, zl_ref, zr_ref, t_ref, b_ref, tab_ref, low_ref, high_ref, ll, lr, hl, hr):
@@ -157,10 +189,10 @@
     acc = conv_group(taps, t_ref, 0, rows, 256, 384)
     for q in range(2):
         cut = slice(q * 128, q * 128 + 128)
-        low_ref[:, :, cut] = finish(acc[:, cut], b_ref[...], mask[:, cut], rows)
+        low_ref[:, :, cut] = finish(acc[:, cut], twice(b_ref), mask[:, cut], rows)
     taps = [[(ref, 384, 128), (z, 0, 128)] for z, ref in zip((hl, zr_ref, hr), own)]
     acc = conv_group(taps, t_ref, 0, rows, 128, 384)
-    high_ref[...] = finish(acc, b_ref[...], mask[:, 256:384], rows)
+    high_ref[...] = finish(acc, twice(b_ref), mask[:, 256:384], rows)
 
 
 def fill_edges(copies, pieces):
@@ -186,7 +218,7 @@
         for q in range(out // 128):
             chunk = 2 * g + q
             which = 0 if chunk == 0 else (2 if chunk == 4 else 1)
-            edge = finish(acc[:, q * 128 : q * 128 + 128], ba_ref[...], mask[:, which * 128 : which * 128 + 128], rows)
+            edge = finish(acc[:, q * 128 : q * 128 + 128], twice(ba_ref), mask[:, which * 128 : which * 128 + 128], rows)
             inner = (g1_ref, g2_ref, g3_ref)[g][:, :, q * 128 : q * 128 + 128][:, 1:-1]
             cut = slice(chunk * 128, chunk * 128 + 128)
             i0[:, :, cut] = jnp.concatenate([edge[:, 0:2], inner], axis=1)
@@ -197,7 +229,7 @@
     for g in range(2):
         acc = conv_group([[(ref, 256 * g, 384)] for ref in (i0, i1, i2)], tb_ref, 0, Y1, 256, 384)
         for q in range(2):
-            value = jnp.maximum(acc[:, q * 128 : q * 128 + 128] + bb_ref[...], 0.0) * mask
+            value = jnp.maximum(acc[:, q * 128 : q * 128 + 128] + twice(bb_ref), 0.0) * mask
             feat_ref[:, (2 * g + q) * 128 : (2 * g + q + 1) * 128] = value.astype(BF)
 
     lanes = Z1 * C1
@@ -256,10 +288,16 @@
     out_ref[...] = mm(order, jnp.concatenate(feat, axis=1), NT).astype(BF)
 
 
-def swap_pairs(count, first):
-    pairs = [(i, i) for i in range(first)]
-    for i in range(first, count, 2):
-        pairs += [(i, i + 1), (i + 1, i)] if i + 1 < count else [(i, i)]
+def swap_pairs(count, cores, cores_first):
+    def place(y, i):
+        return y * count + i if cores_first else i * cores + y
+
+    pairs = []
+    for y in range(cores):
+        for i in range(count):
+            other = i + 1 if i % 2 else i - 1
+            target = place(y, other) if 0 <= other < count else place(y ^ 1, i)
+            pairs.append((place(y, i), target))
     return pairs
 
 
@@ -267,10 +305,15 @@
     count = lax.axis_size(axis)
     index = lax.axis_index(axis)
     even = index % 2 == 0
-    one = lax.ppermute(jnp.where(even, high_edge, low_edge), axis, swap_pairs(count, 0))
+    one = lax.ppermute(jnp.where(even, high_edge, low_edge), axis, [(i, i ^ 1) for i in range(count)])
     two = one
-    if count > 2:
-        two = lax.ppermute(jnp.where(even, low_edge, high_edge), axis, swap_pairs(count, 1))
+    if count > 2 and axis == "gy":
+        pairs = [(0, count - 1), (count - 1, 0)] + [(i, i - 1 + i % 2 * 2) for i in range(1, count - 1)]
+        two = lax.ppermute(jnp.where(even, low_edge, high_edge), axis, pairs)
+    elif count > 2:
+        axes = ("gx", "gy") if axis == "gx" else ("gy", "gz")
+        pairs = swap_pairs(count, lax.axis_size("gy"), axis == "gz")
+        two = lax.ppermute(jnp.where(even, low_edge, high_edge), axes, pairs)
     below = jnp.where(index > 0, jnp.where(even, two, one), jnp.zeros_like(one))
     above = jnp.where(index < count - 1, jnp.where(even, one, two), jnp.zeros_like(one))
     return below, above
@@ -290,20 +333,6 @@
 
 def pad_lanes(value):
     return jnp.pad(value, [(0, 0)] * (value.ndim - 1) + [(0, CP - value.shape[-1])])
-
-
-def tissue_tables(tissue):
-    flags = jnp.pad(tissue, 1)
-    start = (8 * lax.axis_index("gx"), 4 * lax.axis_index("gy"), lax.axis_index("gz"))
-    flags = lax.dynamic_slice(flags, start, (XB, YB, 3))
-    flags = flags.transpose(1, 0, 2).reshape(YB * XB, 3).astype(F32)
-    flags = jnp.pad(flags, ((0, 128 - YB * XB), (0, 0)))
-    lane = iota((128, 384), 1)
-
-    def spread(first, last):
-        return jnp.where(lane < first, flags[:, 0:1], jnp.where(lane < last, flags[:, 1:2], flags[:, 2:3])).astype(BF)
-
-    return spread(64, 320), spread(128, 256)
 
 
 def local(
@@ -313,26 +342,26 @@
     depth = volume.shape[1]
     kz = C0 * depth
     lanes1 = Z1 * C1
-    tab1, tab2 = tissue_tables(tissue)
-    own = pl.pallas_call(
+    half = depth // 2
+    own, tab1, tab2 = pl.pallas_call(
         down1_kernel,
         in_specs=[pl.BlockSpec(memory_space=pltpu.HBM)] + [pl.BlockSpec(memory_space=pltpu.VMEM)] * 3,
-        out_shape=shaped(Y1, X1, lanes1),
+        out_shape=[shaped(Y1, X1, lanes1), shaped(128, 384), shaped(128, 384)],
         scratch_shapes=[
-            pltpu.VMEM((4 * kz, lanes1), BF),
-            pltpu.VMEM(volume.shape, BF),
-            pltpu.VMEM((Y1 * X1, 4 * kz), BF),
+            pltpu.VMEM((2 * kz, lanes1 // 2), BF),
+            pltpu.VMEM((C0, 2, half, volume.shape[2]), BF),
+            pltpu.VMEM((2, Y1 * X1, 2 * kz), BF),
             pltpu.SemaphoreType.DMA((volume.shape[2] // 256,)),
         ],
-        compiler_params=params(),
+        compiler_params=pltpu.CompilerParams(vmem_limit_bytes=62 * 1024 * 1024),
         cost_estimate=cost(4e-6),
-    )(volume, jnp.swapaxes(w_down1, 1, 2), jnp.tile(b_down1, 2)[None], tab1)
+    )(volume.reshape(C0, 2, half, -1), jnp.swapaxes(w_down1, 1, 2), b_down1[None], tissue.transpose(1, 2, 0))
 
     t1a = banded(w_conv1a, 4, C1)
     t1b = banded(w_conv1b, 4, C1)
     t2a = banded(w_conv2a, 2, CP)
     t2b = banded(w_conv2b, 2, CP)
-    bias1a = jnp.tile(b_conv1a, 2)[None]
+    bias1a = b_conv1a[None]
 
     y_below, y_above = shift_along(own[:HALO], own[Y1 - HALO :], "gy")
     win = jnp.concatenate([y_below, own, y_above], axis=0)
@@ -365,7 +394,7 @@
         compiler_params=params(),
         cost_estimate=cost(6e-6),
     )(
-        x_below, low, high, x_above, g1, g2, g3, t1a, t1b, bias1a, jnp.tile(b_conv1b, 2)[None],
+        x_below, low, high, x_above, g1, g2, g3, t1a, t1b, bias1a, b_conv1b[None],
         pad_lanes(jnp.swapaxes(w_down2, 1, 2).reshape(8 * C1, C2)), pad_lanes(b_down2[None]), tab1, tab2,
     )
 

time: 59.7 us -> 49.5 us (0.83)
  the two profiles are of different devices: /device:TPU:10 before, /device:TPU:0 now
where the time goes in v3:
time: 49.5 us; the launch traced here: 49.1 us
  Pallas kernels  24.6 us (50%)
  starting transfers between devices  11.1 us (22%)
  waiting for transfers between devices  10 us (20%)
  other arithmetic  1.67 us (3%)
  between operations  1 us (2%)
  local copies, waits for them, and re-layouts  0.78 us (2%)
    ppermute x6, starting transfers between devices, shift_along(): lax.ppermute(jnp.where(even, high_edge, low_edge), axis, [(i, i ^ 1) for...  10.9 us
    ppermute x6, waiting for transfers between devices, shift_along(): lax.ppermute(jnp.where(even, high_edge, low_edge), axis, [(i, i ^ 1) for...  9.99 us
    pallas_call x1, Pallas kernels, local(): pl.pallas_call(level_one_kernel, out_shape=[shaped(lanes1, Y1 * X1), shap...  6.5 us
    pallas_call x1, Pallas kernels, local(): pl.pallas_call(down1_kernel, in_specs=[pl.BlockSpec(memory_space=pltpu.HB...  6.35 us
    pallas_call x1, Pallas kernels, local(): pl.pallas_call(level_two_kernel, out_shape=shaped(C2 * Z2, Y2 * X2), scra...  6.12 us
    pallas_call x1, Pallas kernels, local(): pl.pallas_call(outer_kernel, out_shape=[shaped(rows, X1, 256), shaped(row...  2.17 us
    pallas_call x4, Pallas kernels, banded(): pl.pallas_call(kernel, out_shape=jax.ShapeDtypeStruct((3, group * pad, 3...  1.89 us
    pallas_call x1, Pallas kernels, local(): pl.pallas_call(middle_kernel, out_shape=[shaped(ROWS1, X1, lanes1), shape...  1.53 us
  transfers between devices with their start and end apart: 10, of which 5 were waited for; matrix products, arithmetic and copies ran while one was open for 0% of the time, Pallas kernels for 11%

profile of v3, /device:TPU:0, one launch (start us, length us, event | category | flops | bytes accessed | tf_op | source)
XLA Modules:
  0.0 49.1 jit_solution(8378976908400382302)
XLA Ops:
  0.7 6.4 %shard_map.149 = (bf16[16,32,512]{2,1,0:T(8,128)(2,1)}, bf16[128,384]{1,0:T(8,128)(2,1)}, bf16[128,384]{1,0:T(8,128)(2,1)}) custom-call(bf16[48,2,8,2048]{3,2,1,0:T(8,128)(2,1)} %bitcast.25, bf16[8,48,64]{2,1,0:T(8,128)(2,1)} %bitcast.26, f32[1,64]{1,0:T(1,128)} %bitcast.28, s32[8,4,32]{2,1,0:T(4,128)} %bitcast.27), custom_call_target="tpu_custom_call" | custom-call | flops 4000000000 | tf_op jit(solution)/shard_map/pallas_call | solution.py:346
  7.1 0.9 %slice_select_fusion = bf16[2,32,512]{2,1,0:T(8,128)(2,1)S(1)} fusion(bf16[16,32,512]{2,1,0:T(8,128)(2,1)} %get-tuple-element.12, pred[]{:T(512)S(6)} %eq.21), kind=kLoop, calls=%fused_computation.22 | loop fusion | flops 32768 | bytes 196609 | tf_op jit(solution)/shard_map/jit(_where)/select_n | solution.py:308
  8.0 0.5 %collective-permute-start = (bf16[2,32,512]{2,1,0:T(8,128)(2,1)S(1)}, bf16[2,32,512]{2,1,0:T(8,128)(2,1)S(1)}, u32[]{:S(2)}, u32[]{:S(2)}) collective-permute-start(bf16[2,32,512]{2,1,0:T(8,128)(2,1)S(1)} %slice_select_fusion), channel_id=1, source_target_pairs={{0,4},{4,0},{1,5},{5,1},{2,6},{6,2},{3,7},{7,3},{8,12},{12,8},{9,1... | collective-permute-start | bytes 196616 | tf_op jit(solution)/shard_map/ppermute | solution.py:308
  8.5 0.6 %shard_map.150.t_ref.ta_ref = bf16[3,256,1152]{2,1,0:T(8,128)(2,1)S(1)} custom-call(bf16[27,64,64]{2,1,0:T(8,128)(2,1)S(1)} %copy-done.2), custom_call_target="tpu_custom_call" | custom-call | flops 1000000000 | tf_op jit(solution)/shard_map/pallas_call | solution.py:135
  9.3 0.6 %shard_map.153.tb_ref = bf16[3,256,1152]{2,1,0:T(8,128)(2,1)S(1)} custom-call(bf16[27,64,64]{2,1,0:T(8,128)(2,1)S(1)} %copy-done.3), custom_call_target="tpu_custom_call" | custom-call | flops 1000000000 | tf_op jit(solution)/shard_map/pallas_call | solution.py:135
  9.9 0.3 copy-done.8
  10.2 0.1 pad_maximum_fusion.win_ref
  10.3 0.1 collective-permute-start.1
  10.4 4.1 %collective-permute-start.2 = (bf16[20,32,128]{2,1,0:T(8,128)(2,1)S(1)}, bf16[20,32,128]{2,1,0:T(8,128)(2,1)S(1)}, u32[]{:S(2)}, u32[]{:S(2)}) collective-permute-start(bf16[20,32,128]{2,1,0:T(8,128)(2,1)S(1)} %get-tuple-element.28), channel_id=1, source_target_pairs={{0,1},{1,0},{2,3},{3,2},{4,5},{5,4},{6,7},{7,6},{8,9},{9,8},{10,11... | collective-permute-start | bytes 491528 | tf_op jit(solution)/shard_map/ppermute | solution.py:308
  14.6 1.5 %shard_map.151 = (bf16[20,32,512]{2,1,0:T(8,128)(2,1)S(1)}, bf16[20,32,512]{2,1,0:T(8,128)(2,1)S(1)}, bf16[18,32,256]{2,1,0:T(8,128)(2,1)S(1)}) custom-call(bf16[20,32,512]{2,1,0:T(8,128)(2,1)S(1)} %pad_maximum_fusion.win_ref, bf16[3,256,1152]{2,1,0:T(8,128)(2,1)S(1)} %shard_map.150.t_ref.ta_ref, f32[1,64]{1,0:T(1,128)S(1)} %bitcast.19, ...), custom_call_target="tpu_custom_call" | custom-call | flops 3000000000 | tf_op jit(solution)/shard_map/pallas_call | solution.py:370
  16.1 0.1 fusion
  16.2 2.9 %collective-permute-done.2 = bf16[20,32,128]{2,1,0:T(8,128)(2,1)S(1)} collective-permute-done((bf16[20,32,128]{2,1,0:T(8,128)(2,1)S(1)}, bf16[20,32,128]{2,1,0:T(8,128)(2,1)S(1)}, u32[]{:S(2)}, u32[]{:S(2)}) %collective-permute-start.2) | collective-permute-done | bytes 163872 | tf_op jit(solution)/shard_map/ppermute | solution.py:308
  19.2 0.1 broadcast_select_fusion.5
  19.4 0.1 collective-permute-start.3
  19.4 3.0 %collective-permute-start.4 = (bf16[20,2,768]{2,1,0:T(2,128)(2,1)S(1)}, bf16[20,2,768]{2,1,0:T(2,128)(2,1)S(1)}, u32[]{:S(2)}, u32[]{:S(2)}) collective-permute-start(bf16[20,2,768]{2,1,0:T(2,128)(2,1)S(1)} %get-tuple-element.22), channel_id=1, source_target_pairs={{0,8},{8,0},{16,24},{24,16},{1,9},{9,1},{17,25},{25,17},{2,10},{10... | collective-permute-start | bytes 184328 | tf_op jit(solution)/shard_map/ppermute | solution.py:308
  22.4 2.2 %shard_map.152 = (bf16[18,32,256]{2,1,0:T(8,128)(2,1)S(1)}, bf16[18,32,128]{2,1,0:T(8,128)(2,1)S(1)}) custom-call(bf16[20,32,512]{2,1,0:T(8,128)(2,1)S(1)} %pad_maximum_fusion.win_ref, bf16[20,32,512]{2,1,0:T(8,128)(2,1)S(1)} %get-tuple-element.14.left_ref, bf16[20,32,512]{2,1,0:T(8,128)(2,1)S(1)} %get-tuple-element.15.right_ref, ...), custom_call_target="tpu_custom_call" | custom-call | flops 4000000000 | tf_op jit(solution)/shard_map/pallas_call | solution.py:380
  24.6 0.7 %collective-permute-done.4 = bf16[20,2,768]{2,1,0:T(2,128)(2,1)S(1)} collective-permute-done((bf16[20,2,768]{2,1,0:T(2,128)(2,1)S(1)}, bf16[20,2,768]{2,1,0:T(2,128)(2,1)S(1)}, u32[]{:S(2)}, u32[]{:S(2)}) %collective-permute-start.4) | collective-permute-done | bytes 61472 | tf_op jit(solution)/shard_map/ppermute | solution.py:308
  25.3 0.1 broadcast_select_fusion.2
  25.4 6.5 %shard_map.154 = (bf16[512,512]{1,0:T(8,128)(2,1)}, bf16[8,16,512]{2,1,0:T(8,128)(2,1)S(1)}) custom-call(bf16[20,2,768]{2,1,0:T(2,128)(2,1)S(1)} %get-tuple-element.42.xl_ref, bf16[20,2,768]{2,1,0:T(2,128)(2,1)S(1)} %get-tuple-element.24.low_ref, bf16[20,2,768]{2,1,0:T(2,128)(2,1)S(1)} %get-tuple-element.23.high_ref, ...), custom_call_target="tpu_custom_call" | custom-call | flops 6000000000 | tf_op jit(solution)/shard_map/pallas_call | solution.py:388
  32.0 0.1 collective-permute-start.5
  32.1 0.3 shard_map.155.ta_ref
  32.4 0.2 copy-done.11
  32.6 0.0 copy-done.12
  32.6 0.6 %collective-permute-done.5 = bf16[2,16,512]{2,1,0:T(8,128)(2,1)S(1)} collective-permute-done((bf16[2,16,512]{2,1,0:T(8,128)(2,1)S(1)}, bf16[2,16,512]{2,1,0:T(8,128)(2,1)S(1)}, u32[]{:S(2)}, u32[]{:S(2)}) %collective-permute-start.5) | collective-permute-done | bytes 32800 | tf_op jit(solution)/shard_map/ppermute | solution.py:308
  33.3 1.8 %collective-permute-start.7 = (bf16[12,16,256]{2,1,0:T(8,128)(2,1)S(1)}, bf16[12,16,256]{2,1,0:T(8,128)(2,1)S(1)}, u32[]{:S(2)}, u32[]{:S(2)}) collective-permute-start(bf16[12,16,256]{2,1,0:T(8,128)(2,1)S(1)} %get-tuple-element.35), channel_id=1, source_target_pairs={{0,1},{1,0},{2,3},{3,2},{4,5},{5,4},{6,7},{7,6},{8,9},{9,8},{10,11... | collective-permute-start | bytes 294920 | tf_op jit(solution)/shard_map/ppermute | solution.py:308
  35.2 3.1 %collective-permute-done.7 = bf16[12,16,256]{2,1,0:T(8,128)(2,1)S(1)} collective-permute-done((bf16[12,16,256]{2,1,0:T(8,128)(2,1)S(1)}, bf16[12,16,256]{2,1,0:T(8,128)(2,1)S(1)}, u32[]{:S(2)}, u32[]{:S(2)}) %collective-permute-start.7) | collective-permute-done | bytes 98336 | tf_op jit(solution)/shard_map/ppermute | solution.py:308
  38.3 0.1 broadcast_select_fusion.11
  38.4 1.4 %collective-permute-start.9 = (bf16[12,2,1024]{2,1,0:T(2,128)(2,1)S(1)}, bf16[12,2,1024]{2,1,0:T(2,128)(2,1)S(1)}, u32[]{:S(2)}, u32[]{:S(2)}) collective-permute-start(bf16[12,2,1024]{2,1,0:T(2,128)(2,1)S(1)} %get-tuple-element.45), channel_id=1, source_target_pairs={{0,8},{8,0},{16,24},{24,16},{1,9},{9,1},{17,25},{25,17},{2,10},{10... | collective-permute-start | bytes 147464 | tf_op jit(solution)/shard_map/ppermute | solution.py:308
  39.9 0.3 shard_map.156.tb_ref
  40.2 2.7 %collective-permute-done.9 = bf16[12,2,1024]{2,1,0:T(2,128)(2,1)S(1)} collective-permute-done((bf16[12,2,1024]{2,1,0:T(2,128)(2,1)S(1)}, bf16[12,2,1024]{2,1,0:T(2,128)(2,1)S(1)}, u32[]{:S(2)}, u32[]{:S(2)}) %collective-permute-start.9) | collective-permute-done | bytes 49184 | tf_op jit(solution)/shard_map/ppermute | solution.py:308
  42.9 0.1 broadcast_select_fusion.8
  43.0 6.1 %shard_map.157 = bf16[384,128]{1,0:T(8,128)(2,1)} custom-call(bf16[12,16,512]{2,1,0:T(8,128)(2,1)S(1)} %pad_maximum_fusion.1.win_ref, bf16[12,16,256]{2,1,0:T(8,128)(2,1)S(1)} %get-tuple-element.34.zl_ref, bf16[12,16,256]{2,1,0:T(8,128)(2,1)S(1)} %get-tuple-element.33.zr_ref, bf16[12,2,1024]{2,1,0:T(2,128)(2,1)S(1)} %get-tuple-element.44.xl_ref, ...), custom_call_target="tpu_custom_call" | custom-call | flops 5000000000 | tf_op jit(solution)/shard_map/pallas_call | solution.py:407
  (47 shorter events, 0.4 us)
Async XLA Ops:
  0.6 7.9 %copy-start.2 = (bf16[27,64,64]{2,1,0:T(8,128)(2,1)S(1)}, bf16[27,64,64]{2,1,0:T(8,128)(2,1)}, u32[]{:S(2)}) copy-start(bf16[27,64,64]{2,1,0:T(8,128)(2,1)} %w_ref.4) | copy-start | bytes 663556
  7.0 2.1 %copy-start.10 = (f32[96]{0:T(128)S(1)}, f32[96]{0:T(128)}, u32[]{:S(2)}) copy-start(f32[96]{0:T(128)} %param.23) | copy-start | bytes 1156
  7.0 2.2 %copy-start.9 = (bf16[8,96,64]{1,2,0:T(8,128)(2,1)S(1)}, bf16[8,96,64]{1,2,0:T(8,128)(2,1)}, u32[]{:S(2)}) copy-start(bf16[8,96,64]{1,2,0:T(8,128)(2,1)} %param.22) | copy-start | bytes 294916
  7.0 2.2 %copy-start.3 = (bf16[27,64,64]{2,1,0:T(8,128)(2,1)S(1)}, bf16[27,64,64]{2,1,0:T(8,128)(2,1)}, u32[]{:S(2)}) copy-start(bf16[27,64,64]{2,1,0:T(8,128)(2,1)} %w_ref.5) | copy-start | bytes 663556
  8.0 1.9 %collective-permute-start = (bf16[2,32,512]{2,1,0:T(8,128)(2,1)S(1)}, bf16[2,32,512]{2,1,0:T(8,128)(2,1)S(1)}, u32[]{:S(2)}, u32[]{:S(2)}) collective-permute-start(bf16[2,32,512]{2,1,0:T(8,128)(2,1)S(1)} %slice_select_fusion), channel_id=1, source_target_pairs={{0,4},{4,0},{1,5},{5,1},{2,6},{6,2},{3,7},{7,3},{8,12},{12,8},{9,1... | collective-permute-start | bytes 196616 | tf_op jit(solution)/shard_map/ppermute | solution.py:308
  9.1 1.0 %copy-start.8 = (bf16[16,32,512]{2,1,0:T(8,128)(2,1)S(1)}, bf16[16,32,512]{2,1,0:T(8,128)(2,1)}, u32[]{:S(2)}) copy-start(bf16[16,32,512]{2,1,0:T(8,128)(2,1)} %get-tuple-element.12) | copy-start | bytes 1572868
  9.2 5.3 %copy-start.4 = (f32[64]{0:T(128)S(1)}, f32[64]{0:T(128)}, u32[]{:S(2)}) copy-start(f32[64]{0:T(128)} %param.19) | copy-start | bytes 772
  9.3 5.3 %copy-start.6 = (bf16[128,384]{1,0:T(8,128)(2,1)S(1)}, bf16[128,384]{1,0:T(8,128)(2,1)}, u32[]{:S(2)}) copy-start(bf16[128,384]{1,0:T(8,128)(2,1)} %get-tuple-element.13.tab_ref) | copy-start | bytes 294916
  10.3 5.9 %collective-permute-start.1 = (bf16[20,32,128]{2,1,0:T(8,128)(2,1)S(1)}, bf16[20,32,128]{2,1,0:T(8,128)(2,1)S(1)}, u32[]{:S(2)}, u32[]{:S(2)}) collective-permute-start(bf16[20,32,128]{2,1,0:T(8,128)(2,1)S(1)} %get-tuple-element.27), channel_id=1, source_target_pairs={{0,4},{1,2},{2,1},{3,7},{4,0},{5,6},{6,5},{7,3},{8,12},{9,10},{10,... | collective-permute-start | bytes 491528 | tf_op jit(solution)/shard_map/ppermute | solution.py:316
  10.4 8.7 %collective-permute-start.2 = (bf16[20,32,128]{2,1,0:T(8,128)(2,1)S(1)}, bf16[20,32,128]{2,1,0:T(8,128)(2,1)S(1)}, u32[]{:S(2)}, u32[]{:S(2)}) collective-permute-start(bf16[20,32,128]{2,1,0:T(8,128)(2,1)S(1)} %get-tuple-element.28), channel_id=1, source_target_pairs={{0,1},{1,0},{2,3},{3,2},{4,5},{5,4},{6,7},{7,6},{8,9},{9,8},{10,11... | collective-permute-start | bytes 491528 | tf_op jit(solution)/shard_map/ppermute | solution.py:308
  19.4 5.2 %collective-permute-start.3 = (bf16[20,2,768]{2,1,0:T(2,128)(2,1)S(1)}, bf16[20,2,768]{2,1,0:T(2,128)(2,1)S(1)}, u32[]{:S(2)}, u32[]{:S(2)}) collective-permute-start(bf16[20,2,768]{2,1,0:T(2,128)(2,1)S(1)} %bitcast.24), channel_id=1, source_target_pairs={{0,4},{8,16},{16,8},{24,28},{4,0},{12,20},{20,12},{28,24},{1,5},{9... | collective-permute-start | bytes 184328 | tf_op jit(solution)/shard_map/ppermute | solution.py:316
  19.4 5.8 %collective-permute-start.4 = (bf16[20,2,768]{2,1,0:T(2,128)(2,1)S(1)}, bf16[20,2,768]{2,1,0:T(2,128)(2,1)S(1)}, u32[]{:S(2)}, u32[]{:S(2)}) collective-permute-start(bf16[20,2,768]{2,1,0:T(2,128)(2,1)S(1)} %get-tuple-element.22), channel_id=1, source_target_pairs={{0,8},{8,0},{16,24},{24,16},{1,9},{9,1},{17,25},{25,17},{2,10},{10... | collective-permute-start | bytes 184328 | tf_op jit(solution)/shard_map/ppermute | solution.py:308
  22.4 3.0 %copy-start.5 = (f32[64]{0:T(128)S(1)}, f32[64]{0:T(128)}, u32[]{:S(2)}) copy-start(f32[64]{0:T(128)} %param.21) | copy-start | bytes 772
  22.4 3.0 %copy-start.7 = (bf16[128,384]{1,0:T(8,128)(2,1)S(1)}, bf16[128,384]{1,0:T(8,128)(2,1)}, u32[]{:S(2)}) copy-start(bf16[128,384]{1,0:T(8,128)(2,1)} %get-tuple-element.19.tab2_ref.tab_ref) | copy-start | bytes 294916
  25.4 6.6 %copy-start = (bf16[27,96,96]{2,1,0:T(8,128)(2,1)S(1)}, bf16[27,96,96]{2,1,0:T(8,128)(2,1)}, u32[]{:S(2)}) copy-start(bf16[27,96,96]{2,1,0:T(8,128)(2,1)} %w_ref.6) | copy-start | bytes 1492996
  31.9 0.7 %copy-start.11 = (f32[96]{0:T(128)S(1)}, f32[96]{0:T(128)}, u32[]{:S(2)}) copy-start(f32[96]{0:T(128)} %param.25) | copy-start | bytes 1156
  31.9 0.7 %copy-start.12 = (f32[96]{0:T(128)S(1)}, f32[96]{0:T(128)}, u32[]{:S(2)}) copy-start(f32[96]{0:T(128)} %param.27) | copy-start | bytes 1156
  32.0 7.9 %copy-start.1 = (bf16[27,96,96]{2,1,0:T(8,128)(2,1)S(1)}, bf16[27,96,96]{2,1,0:T(8,128)(2,1)}, u32[]{:S(2)}) copy-start(bf16[27,96,96]{2,1,0:T(8,128)(2,1)} %w_ref.7) | copy-start | bytes 1492996
  32.0 1.3 %collective-permute-start.5 = (bf16[2,16,512]{2,1,0:T(8,128)(2,1)S(1)}, bf16[2,16,512]{2,1,0:T(8,128)(2,1)S(1)}, u32[]{:S(2)}, u32[]{:S(2)}) collective-permute-start(bf16[2,16,512]{2,1,0:T(8,128)(2,1)S(1)} %slice_select_fusion.1), channel_id=1, source_target_pairs={{0,4},{4,0},{1,5},{5,1},{2,6},{6,2},{3,7},{7,3},{8,12},{12,8},{9,1... | collective-permute-start | bytes 98312 | tf_op jit(solution)/shard_map/ppermute | solution.py:308
  33.3 4.9 %collective-permute-start.7 = (bf16[12,16,256]{2,1,0:T(8,128)(2,1)S(1)}, bf16[12,16,256]{2,1,0:T(8,128)(2,1)S(1)}, u32[]{:S(2)}, u32[]{:S(2)}) collective-permute-start(bf16[12,16,256]{2,1,0:T(8,128)(2,1)S(1)} %get-tuple-element.35), channel_id=1, source_target_pairs={{0,1},{1,0},{2,3},{3,2},{4,5},{5,4},{6,7},{7,6},{8,9},{9,8},{10,11... | collective-permute-start | bytes 294920 | tf_op jit(solution)/shard_map/ppermute | solution.py:308
  35.1 3.1 %collective-permute-start.6 = (bf16[12,16,256]{2,1,0:T(8,128)(2,1)S(1)}, bf16[12,16,256]{2,1,0:T(8,128)(2,1)S(1)}, u32[]{:S(2)}, u32[]{:S(2)}) collective-permute-start(bf16[12,16,256]{2,1,0:T(8,128)(2,1)S(1)} %get-tuple-element.36), channel_id=1, source_target_pairs={{0,4},{1,2},{2,1},{3,7},{4,0},{5,6},{6,5},{7,3},{8,12},{9,10},{10,... | collective-permute-start | bytes 294920 | tf_op jit(solution)/shard_map/ppermute | solution.py:316
  38.4 4.5 %collective-permute-start.9 = (bf16[12,2,1024]{2,1,0:T(2,128)(2,1)S(1)}, bf16[12,2,1024]{2,1,0:T(2,128)(2,1)S(1)}, u32[]{:S(2)}, u32[]{:S(2)}) collective-permute-start(bf16[12,2,1024]{2,1,0:T(2,128)(2,1)S(1)} %get-tuple-element.45), channel_id=1, source_target_pairs={{0,8},{8,0},{16,24},{24,16},{1,9},{9,1},{17,25},{25,17},{2,10},{10... | collective-permute-start | bytes 147464 | tf_op jit(solution)/shard_map/ppermute | solution.py:308
  39.9 3.0 %collective-permute-start.8 = (bf16[12,2,1024]{2,1,0:T(2,128)(2,1)S(1)}, bf16[12,2,1024]{2,1,0:T(2,128)(2,1)S(1)}, u32[]{:S(2)}, u32[]{:S(2)}) collective-permute-start(bf16[12,2,1024]{2,1,0:T(2,128)(2,1)S(1)} %get-tuple-element.46), channel_id=1, source_target_pairs={{0,4},{8,16},{16,8},{24,28},{4,0},{12,20},{20,12},{28,24},{1,5},{9... | collective-permute-start | bytes 147464 | tf_op jit(solution)/shard_map/ppermute | solution.py:316

commit v4 on v3

--- a/solution.py
+++ b/solution.py
@@ -19,6 +19,7 @@
 CP = 128
 HALO = 2
 XB = 10
+XB_PITCH = 16
 YB = 6
 ROWS1 = Y1 + 2 * HALO
 ROWS2 = Y2 + 2 * HALO
@@ -43,11 +44,17 @@
     return jnp.where(flag, 1.0, 0.0).astype(BF)
 
 
+def one_hot_rows(key, lanes):
+    lane = iota(key.shape, 1)
+    return jnp.concatenate([one_hot(key == lane + q) for q in range(0, lanes, 128)], axis=1)
+
+
 def mask_rows(tab, y_start, rows, pitch, x_of, cell):
+    bits = cell.bit_length() - 1
     shape = (rows, pitch, 128)
-    y_block = lax.div(iota(shape, 0) + (y_start + cell), cell)
-    x_block = jnp.minimum(lax.div(x_of(iota(shape, 1)) + cell, cell), XB - 1)
-    hit = one_hot(y_block * XB + x_block == iota(shape, 2)).reshape(rows * pitch, 128)
+    y_block = (iota(shape, 0) + (y_start + cell)) >> bits
+    x_block = jnp.minimum((x_of(iota(shape, 1)) + cell) >> bits, XB - 1)
+    hit = one_hot(y_block * XB_PITCH + x_block == iota(shape, 2)).reshape(rows * pitch, 128)
     return mm(hit, tab)
 
 
@@ -60,12 +67,15 @@
         inside = jnp.where((z >= 0) & (z < n_z), 1.0, 0.0)
         layers.append(t_ref[:, jnp.clip(z, 0, n_z - 1), :].astype(F32) * inside)
     block = iota((128, n_y), 0)
-    hot_y = one_hot((block < YB * XB) & (lax.axis_index("gy") * 4 - 1 + block // XB == iota((128, n_y), 1)))
+    bits = XB_PITCH.bit_length() - 1
+    hot_y = one_hot(lax.axis_index("gy") * 4 - 1 + (block >> bits) == iota((128, n_y), 1))
     block = iota((128, 3 * n_x), 0)
-    hot_x = lax.axis_index("gx") * 8 - 1 + block % XB == iota((128, 3 * n_x), 1) % n_x
+    layer = sum((iota((128, 3 * n_x), 1) >= k * n_x).astype(jnp.int32) for k in (1, 2))
+    hot_x = lax.axis_index("gx") * 8 - 1 + (block & (XB_PITCH - 1)) == iota((128, 3 * n_x), 1) - layer * n_x
     rows = jnp.where(hot_x, mm(hot_y, jnp.concatenate(layers, axis=1).astype(BF)), 0.0).astype(BF)
     shape = (3 * n_x, 384)
-    layer, lane = iota(shape, 0) // n_x, iota(shape, 1)
+    layer = sum((iota(shape, 0) >= k * n_x).astype(jnp.int32) for k in (1, 2))
+    lane = iota(shape, 1)
 
     def spread(first, last):
         place = jnp.where(lane < first, 0, jnp.where(lane < last, 1, 2))
@@ -89,17 +99,16 @@
     tab2_ref[...] = tab2
     r = iota((kz, 2 * C0), 0)
     l = iota((kz, 2 * C0), 1)
-    spread = one_hot((r // half == l % C0) & (r % 2 == l // C0))
-    keep = (iota((kz, lanes), 0) % half) // 2 == iota((kz, lanes), 1) // C1
+    odd = l >= C0
+    spread = one_hot(((r >> 3) == jnp.where(odd, l - C0, l)) & ((r & 1) == odd.astype(jnp.int32)))
+    keep = (iota((kz, lanes), 0) & 7) >> 1 == iota((kz, lanes), 1) >> 6
     for ab in range(4):
         pair = w_ref[2 * ab : 2 * ab + 2].reshape(2 * C0, C1)
         wide = jnp.concatenate([pair] * (Z1 // 2), axis=1)
         wd_ref[ab * kz : (ab + 1) * kz, :] = jnp.where(keep, mm(spread, wide), 0.0).astype(BF)
 
-    shape = (4 * CX, 4 * CX)
-    r = iota(shape, 0)
-    a, b, y, x = r // 128, (r // 64) % 2, (r // 32) % 2, r % 32
-    select = one_hot((2 * y + b) * CX + 2 * x + a == iota(shape, 1))
+    r = iota((4 * CX, 128), 0)
+    select = one_hot_rows(((r & 32) << 2) | (r & 64) | ((r & 31) << 1) | (r >> 7), 4 * CX)
     for n, copy in enumerate(copies):
         copy.wait()
         for h in range(2):
@@ -120,23 +129,27 @@
     return jnp.concatenate([b_ref[...]] * 2, axis=1)
 
 
+def fill_banded(w_ref, t_ref, group, pad):
+    chan = w_ref.shape[1]
+    t_ref[...] = jnp.zeros_like(t_ref)
+    for j in range(3):
+        for i in range(3):
+            for zo in range(group):
+                for k in range(3):
+                    lane = i * (group + 2) * pad + (zo + k) * pad
+                    t_ref[j, zo * pad : zo * pad + chan, lane : lane + chan] = w_ref[9 * i + 3 * j + k]
+
+
+def banded_shape(group, pad):
+    return shaped(3, group * pad, 3 * (group + 2) * pad)
+
+
 def banded(weights, group, pad):
-    chan = weights.shape[1]
-
     def kernel(w_ref, t_ref):
-        t_ref[...] = jnp.zeros_like(t_ref)
-        for j in range(3):
-            for i in range(3):
-                for zo in range(group):
-                    for k in range(3):
-                        lane = i * (group + 2) * pad + (zo + k) * pad
-                        t_ref[j, zo * pad : zo * pad + chan, lane : lane + chan] = w_ref[9 * i + 3 * j + k]
+        fill_banded(w_ref, t_ref, group, pad)
 
     return pl.pallas_call(
-        kernel,
-        out_shape=jax.ShapeDtypeStruct((3, group * pad, 3 * (group + 2) * pad), BF),
-        compiler_params=params(),
-        cost_estimate=cost(1e-6),
+        kernel, out_shape=banded_shape(group, pad), compiler_params=params(), cost_estimate=cost(1e-6)
     )(weights)
 
 
@@ -168,7 +181,8 @@
     right[:, :, cut] = jnp.concatenate([inner[:, 1:], none], axis=1)
 
 
-def middle_kernel(win_ref, t_ref, b_ref, tab_ref, left_ref, right_ref, out_ref):
+def middle_kernel(win_ref, t_ref, b_ref, tab_ref, w_ref, left_ref, right_ref, out_ref, next_ref):
+    fill_banded(w_ref, next_ref, 4, C1)
     for q in range(4):
         fill_sides(left_ref, right_ref, q * 128, win_ref[:, :, q * 128 : q * 128 + 128])
     rows = Y1 + 2
@@ -235,10 +249,8 @@
     lanes = Z1 * C1
     size = 8 * X1
     quarter = size // 4
-    r = iota((size, size), 0)
-    ab = r // quarter
-    y = (r % quarter) // X2
-    select = one_hot((2 * y + ab % 2) * X1 + 2 * (r % X2) + ab // 2 == iota((size, size), 1))
+    r = iota((size, 128), 0)
+    select = one_hot_rows(((r & 48) << 2) | ((r & 64) >> 1) | ((r & 15) << 1) | (r >> 7), size)
     for n in range(Y1 // 8):
         cells = mm(select, feat_ref[n * size : n * size + size, :]).astype(BF)
         for q in range(4):
@@ -248,8 +260,8 @@
         left = jnp.concatenate([d_ref[q, :, z * 128 : z * 128 + 128] for q in range(4)], axis=1)
         down_ref[:, :, z * CP : z * CP + CP] = finish(mm(left, wd_ref[...]), bd_ref[...], mask, Y2)
 
-    r = iota((lanes, lanes), 0)
-    order = one_hot((r % Z1) * C1 + r // Z1 == iota((lanes, lanes), 1))
+    r = iota((lanes, 128), 0)
+    order = one_hot_rows(((r & 7) << 6) | (r >> 3), lanes)
     one_ref[...] = mm(order, feat_ref[...], NT).astype(BF)
 
 
@@ -282,9 +294,8 @@
         acc = conv_group([[(ref, 256 * g, 512)] for ref in (i0, i1, i2)], tb_ref, 0, Y2, 256, 512)
         for q in range(2):
             feat.append((jnp.maximum(acc[:, q * 128 : q * 128 + 128] + bb_ref[...], 0.0) * mask).astype(BF))
-    shape = (C2 * Z2, Z2 * CP)
-    r = iota(shape, 0)
-    order = one_hot((r % Z2) * CP + r // Z2 == iota(shape, 1))
+    r = iota((C2 * Z2, 128), 0)
+    order = one_hot_rows(((r & 3) << 7) | (r >> 2), Z2 * CP)
     out_ref[...] = mm(order, jnp.concatenate(feat, axis=1), NT).astype(BF)
 
 
@@ -353,12 +364,11 @@
             pltpu.VMEM((2, Y1 * X1, 2 * kz), BF),
             pltpu.SemaphoreType.DMA((volume.shape[2] // 256,)),
         ],
-        compiler_params=pltpu.CompilerParams(vmem_limit_bytes=62 * 1024 * 1024),
+        compiler_params=pltpu.CompilerParams(vmem_limit_bytes=123 * 512 * 1024),
         cost_estimate=cost(4e-6),
     )(volume.reshape(C0, 2, half, -1), jnp.swapaxes(w_down1, 1, 2), b_down1[None], tissue.transpose(1, 2, 0))
 
     t1a = banded(w_conv1a, 4, C1)
-    t1b = banded(w_conv1b, 4, C1)
     t2a = banded(w_conv2a, 2, CP)
     t2b = banded(w_conv2b, 2, CP)
     bias1a = b_conv1a[None]
@@ -367,12 +377,12 @@
     win = jnp.concatenate([y_below, own, y_above], axis=0)
     z_below, z_above = shift_along(win[:, :, :128], win[:, :, lanes1 - 128 :], "gz")
     rows = Y1 + 2
-    left, right, g2 = pl.pallas_call(
+    left, right, g2, t1b = pl.pallas_call(
         middle_kernel,
-        out_shape=[shaped(ROWS1, X1, lanes1), shaped(ROWS1, X1, lanes1), shaped(rows, X1, 256)],
+        out_shape=[shaped(ROWS1, X1, lanes1), shaped(ROWS1, X1, lanes1), shaped(rows, X1, 256), banded_shape(4, C1)],
         compiler_params=params(),
         cost_estimate=cost(3e-6),
-    )(win, t1a, bias1a, tab1)
+    )(win, t1a, bias1a, tab1, w_conv1b)
 
     low = jnp.concatenate([z_below[:, :2], win[:, :2], z_above[:, :2]], axis=2)
     high = jnp.concatenate([z_below[:, X1 - 2 :], win[:, X1 - 2 :], z_above[:, X1 - 2 :]], axis=2)

time: 49.5 us -> 49.9 us (level)
  starting transfers between devices: 11.1 us -> 13.3 us
  waiting for transfers between devices: 10 us -> 9.12 us
  Pallas kernels: 24.6 us -> 24.1 us
    ppermute x6, starting transfers between devices: 10.9 us -> 12.5 us  [shift_along(): lax.ppermute(jnp.where(even, high_edge, low_edge), axis, [(i, i ^ 1) for...]
    ppermute x6, waiting for transfers between devices: 9.99 us -> 9.11 us  [shift_along(): lax.ppermute(jnp.where(even, high_edge, low_edge), axis, [(i, i ^ 1) for...]
    pallas_call x4 -> x3, Pallas kernels: 1.89 us -> 1.27 us  [banded(): pl.pallas_call(kernel, out_shape=banded_shape(group, pad), compiler_param...]
    ppermute x4, starting transfers between devices: 0.2 us -> 0.79 us  [shift_along(): two = lax.ppermute(jnp.where(even, low_edge, high_edge), axes, pairs)]
  transfers between devices with their start and end apart: 10 -> 10, of which waited for: 5 -> 6; matrix products, arithmetic and copies ran while one was open for 0% -> 0% of each run, Pallas kernels for 11% -> 10%
where the time goes in v4:
time: 49.9 us; the launch traced here: 49.7 us
  Pallas kernels  24.1 us (48%)
  starting transfers between devices  13.3 us (27%)
  waiting for transfers between devices  9.12 us (18%)
  other arithmetic  1.68 us (3%)
  between operations  1 us (2%)
  local copies, waits for them, and re-layouts  0.52 us (1%)
    ppermute x6, starting transfers between devices, shift_along(): lax.ppermute(jnp.where(even, high_edge, low_edge), axis, [(i, i ^ 1) for...  12.5 us
    ppermute x6, waiting for transfers between devices, shift_along(): lax.ppermute(jnp.where(even, high_edge, low_edge), axis, [(i, i ^ 1) for...  9.11 us
    pallas_call x1, Pallas kernels, local(): pl.pallas_call(level_one_kernel, out_shape=[shaped(lanes1, Y1 * X1), shap...  6.5 us
    pallas_call x1, Pallas kernels, local(): pl.pallas_call(down1_kernel, in_specs=[pl.BlockSpec(memory_space=pltpu.HB...  6.36 us
    pallas_call x1, Pallas kernels, local(): pl.pallas_call(level_two_kernel, out_shape=shaped(C2 * Z2, Y2 * X2), scra...  6.12 us
    pallas_call x1, Pallas kernels, local(): pl.pallas_call(outer_kernel, out_shape=[shaped(rows, X1, 256), shaped(row...  2.16 us
    pallas_call x1, Pallas kernels, local(): pl.pallas_call(middle_kernel, out_shape=[shaped(ROWS1, X1, lanes1), shape...  1.69 us
    pallas_call x3, Pallas kernels, banded(): pl.pallas_call(kernel, out_shape=banded_shape(group, pad), compiler_param...  1.27 us
  transfers between devices with their start and end apart: 10, of which 6 were waited for; matrix products, arithmetic and copies ran while one was open for 0% of the time, Pallas kernels for 10%

profile of v4, /device:TPU:0, one launch (start us, length us, event | category | flops | bytes accessed | tf_op | source)
XLA Modules:
  0.0 49.7 jit_solution(11094526570448407898)
XLA Ops:
  0.7 6.4 %shard_map.149 = (bf16[16,32,512]{2,1,0:T(8,128)(2,1)}, bf16[128,384]{1,0:T(8,128)(2,1)}, bf16[128,384]{1,0:T(8,128)(2,1)}) custom-call(bf16[48,2,8,2048]{3,2,1,0:T(8,128)(2,1)} %bitcast.25, bf16[8,48,64]{2,1,0:T(8,128)(2,1)} %bitcast.26, f32[1,64]{1,0:T(1,128)} %bitcast.28, s32[8,4,32]{2,1,0:T(4,128)} %bitcast.27), custom_call_target="tpu_custom_call" | custom-call | flops 4000000000 | tf_op jit(solution)/shard_map/pallas_call | solution.py:357
  7.1 0.9 %slice_select_fusion = bf16[2,32,512]{2,1,0:T(8,128)(2,1)S(1)} fusion(bf16[16,32,512]{2,1,0:T(8,128)(2,1)} %get-tuple-element.13, pred[]{:T(512)S(6)} %eq.21), kind=kLoop, calls=%fused_computation.22 | loop fusion | flops 32768 | bytes 196609 | tf_op jit(solution)/shard_map/jit(_where)/select_n | solution.py:319
  8.0 0.5 %collective-permute-start = (bf16[2,32,512]{2,1,0:T(8,128)(2,1)S(1)}, bf16[2,32,512]{2,1,0:T(8,128)(2,1)S(1)}, u32[]{:S(2)}, u32[]{:S(2)}) collective-permute-start(bf16[2,32,512]{2,1,0:T(8,128)(2,1)S(1)} %slice_select_fusion), channel_id=1, source_target_pairs={{0,4},{4,0},{1,5},{5,1},{2,6},{6,2},{3,7},{7,3},{8,12},{12,8},{9,1... | collective-permute-start | bytes 196616 | tf_op jit(solution)/shard_map/ppermute | solution.py:319
  8.6 0.6 %shard_map.150.t_ref.ta_ref = bf16[3,256,1152]{2,1,0:T(8,128)(2,1)S(1)} custom-call(bf16[27,64,64]{2,1,0:T(8,128)(2,1)S(1)} %copy-done.2), custom_call_target="tpu_custom_call" | custom-call | flops 1000000000 | tf_op jit(solution)/shard_map/pallas_call | solution.py:151
  9.3 0.2 collective-permute-done
  9.4 0.1 pad_maximum_fusion.win_ref
  9.6 0.4 collective-permute-start.1
  10.0 4.2 %collective-permute-start.2 = (bf16[20,32,128]{2,1,0:T(8,128)(2,1)S(1)}, bf16[20,32,128]{2,1,0:T(8,128)(2,1)S(1)}, u32[]{:S(2)}, u32[]{:S(2)}) collective-permute-start(bf16[20,32,128]{2,1,0:T(8,128)(2,1)S(1)} %get-tuple-element.30), channel_id=1, source_target_pairs={{0,1},{1,0},{2,3},{3,2},{4,5},{5,4},{6,7},{7,6},{8,9},{9,8},{10,11... | collective-permute-start | bytes 491528 | tf_op jit(solution)/shard_map/ppermute | solution.py:319
  14.1 1.7 %shard_map.151 = (bf16[20,32,512]{2,1,0:T(8,128)(2,1)S(1)}, bf16[20,32,512]{2,1,0:T(8,128)(2,1)S(1)}, bf16[18,32,256]{2,1,0:T(8,128)(2,1)S(1)}, bf16[3,256,1152]{2,1,0:T(8,128)(2,1)S(1)}) custom-call(bf16[20,32,512]{2,1,0:T(8,128)(2,1)S(1)} %pad_maximum_fusion.win_ref, bf16[3,256,1152]{2,1,0:T(8,128)(2,1)S(1)} %shard_map.150.t_ref.ta_ref, ...), custom_call_target="tpu_custom_call" | custom-call | flops 3000000000 | tf_op jit(solution)/shard_map/pallas_call | solution.py:380
  15.8 0.1 fusion
  15.9 2.5 %collective-permute-done.2 = bf16[20,32,128]{2,1,0:T(8,128)(2,1)S(1)} collective-permute-done((bf16[20,32,128]{2,1,0:T(8,128)(2,1)S(1)}, bf16[20,32,128]{2,1,0:T(8,128)(2,1)S(1)}, u32[]{:S(2)}, u32[]{:S(2)}) %collective-permute-start.2) | collective-permute-done | bytes 163872 | tf_op jit(solution)/shard_map/ppermute | solution.py:319
  18.5 0.1 broadcast_select_fusion.5
  18.6 0.1 collective-permute-start.3
  18.7 3.0 %collective-permute-start.4 = (bf16[20,2,768]{2,1,0:T(2,128)(2,1)S(1)}, bf16[20,2,768]{2,1,0:T(2,128)(2,1)S(1)}, u32[]{:S(2)}, u32[]{:S(2)}) collective-permute-start(bf16[20,2,768]{2,1,0:T(2,128)(2,1)S(1)} %get-tuple-element.24), channel_id=1, source_target_pairs={{0,8},{8,0},{16,24},{24,16},{1,9},{9,1},{17,25},{25,17},{2,10},{10... | collective-permute-start | bytes 184328 | tf_op jit(solution)/shard_map/ppermute | solution.py:319
  21.7 2.2 %shard_map.152 = (bf16[18,32,256]{2,1,0:T(8,128)(2,1)S(1)}, bf16[18,32,128]{2,1,0:T(8,128)(2,1)S(1)}) custom-call(bf16[20,32,512]{2,1,0:T(8,128)(2,1)S(1)} %pad_maximum_fusion.win_ref, bf16[20,32,512]{2,1,0:T(8,128)(2,1)S(1)} %get-tuple-element.15.left_ref, bf16[20,32,512]{2,1,0:T(8,128)(2,1)S(1)} %get-tuple-element.16.right_ref, ...), custom_call_target="tpu_custom_call" | custom-call | flops 4000000000 | tf_op jit(solution)/shard_map/pallas_call | solution.py:390
  23.9 0.7 %collective-permute-done.4 = bf16[20,2,768]{2,1,0:T(2,128)(2,1)S(1)} collective-permute-done((bf16[20,2,768]{2,1,0:T(2,128)(2,1)S(1)}, bf16[20,2,768]{2,1,0:T(2,128)(2,1)S(1)}, u32[]{:S(2)}, u32[]{:S(2)}) %collective-permute-start.4) | collective-permute-done | bytes 61472 | tf_op jit(solution)/shard_map/ppermute | solution.py:319
  24.5 0.1 broadcast_select_fusion.2
  24.7 6.5 %shard_map.153 = (bf16[512,512]{1,0:T(8,128)(2,1)}, bf16[8,16,512]{2,1,0:T(8,128)(2,1)S(1)}) custom-call(bf16[20,2,768]{2,1,0:T(2,128)(2,1)S(1)} %get-tuple-element.44.xl_ref, bf16[20,2,768]{2,1,0:T(2,128)(2,1)S(1)} %get-tuple-element.26.low_ref, bf16[20,2,768]{2,1,0:T(2,128)(2,1)S(1)} %get-tuple-element.25.high_ref, ...), custom_call_target="tpu_custom_call" | custom-call | flops 6000000000 | tf_op jit(solution)/shard_map/pallas_call | solution.py:398
  31.2 0.1 collective-permute-start.5
  31.3 0.3 shard_map.154.ta_ref
  31.7 0.2 copy-done.11
  31.9 0.6 %collective-permute-done.5 = bf16[2,16,512]{2,1,0:T(8,128)(2,1)S(1)} collective-permute-done((bf16[2,16,512]{2,1,0:T(8,128)(2,1)S(1)}, bf16[2,16,512]{2,1,0:T(8,128)(2,1)S(1)}, u32[]{:S(2)}, u32[]{:S(2)}) %collective-permute-start.5) | collective-permute-done | bytes 32800 | tf_op jit(solution)/shard_map/ppermute | solution.py:319
  32.6 0.2 collective-permute-start.6
  32.8 2.0 %collective-permute-start.7 = (bf16[12,16,256]{2,1,0:T(8,128)(2,1)S(1)}, bf16[12,16,256]{2,1,0:T(8,128)(2,1)S(1)}, u32[]{:S(2)}, u32[]{:S(2)}) collective-permute-start(bf16[12,16,256]{2,1,0:T(8,128)(2,1)S(1)} %get-tuple-element.37), channel_id=1, source_target_pairs={{0,1},{1,0},{2,3},{3,2},{4,5},{5,4},{6,7},{7,6},{8,9},{9,8},{10,11... | collective-permute-start | bytes 294920 | tf_op jit(solution)/shard_map/ppermute | solution.py:319
  34.9 3.0 %collective-permute-done.7 = bf16[12,16,256]{2,1,0:T(8,128)(2,1)S(1)} collective-permute-done((bf16[12,16,256]{2,1,0:T(8,128)(2,1)S(1)}, bf16[12,16,256]{2,1,0:T(8,128)(2,1)S(1)}, u32[]{:S(2)}, u32[]{:S(2)}) %collective-permute-start.7) | collective-permute-done | bytes 98336 | tf_op jit(solution)/shard_map/ppermute | solution.py:319
  37.9 0.1 broadcast_select_fusion.11
  38.1 0.1 collective-permute-start.8
  38.1 2.8 %collective-permute-start.9 = (bf16[12,2,1024]{2,1,0:T(2,128)(2,1)S(1)}, bf16[12,2,1024]{2,1,0:T(2,128)(2,1)S(1)}, u32[]{:S(2)}, u32[]{:S(2)}) collective-permute-start(bf16[12,2,1024]{2,1,0:T(2,128)(2,1)S(1)} %get-tuple-element.47), channel_id=1, source_target_pairs={{0,8},{8,0},{16,24},{24,16},{1,9},{9,1},{17,25},{25,17},{2,10},{10... | collective-permute-start | bytes 147464 | tf_op jit(solution)/shard_map/ppermute | solution.py:319
  40.9 0.3 shard_map.155.tb_ref
  41.3 2.2 %collective-permute-done.9 = bf16[12,2,1024]{2,1,0:T(2,128)(2,1)S(1)} collective-permute-done((bf16[12,2,1024]{2,1,0:T(2,128)(2,1)S(1)}, bf16[12,2,1024]{2,1,0:T(2,128)(2,1)S(1)}, u32[]{:S(2)}, u32[]{:S(2)}) %collective-permute-start.9) | collective-permute-done | bytes 49184 | tf_op jit(solution)/shard_map/ppermute | solution.py:319
  43.5 0.1 broadcast_select_fusion.8
  43.6 6.1 %shard_map.156 = bf16[384,128]{1,0:T(8,128)(2,1)} custom-call(bf16[12,16,512]{2,1,0:T(8,128)(2,1)S(1)} %pad_maximum_fusion.1.win_ref, bf16[12,16,256]{2,1,0:T(8,128)(2,1)S(1)} %get-tuple-element.36.zl_ref, bf16[12,16,256]{2,1,0:T(8,128)(2,1)S(1)} %get-tuple-element.35.zr_ref, bf16[12,2,1024]{2,1,0:T(2,128)(2,1)S(1)} %get-tuple-element.46.xl_ref, ...), custom_call_target="tpu_custom_call" | custom-call | flops 5000000000 | tf_op jit(solution)/shard_map/pallas_call | solution.py:417
  (46 shorter events, 0.4 us)
Async XLA Ops:
  0.6 7.9 %copy-start.9 = (bf16[8,96,64]{1,2,0:T(8,128)(2,1)S(1)}, bf16[8,96,64]{1,2,0:T(8,128)(2,1)}, u32[]{:S(2)}) copy-start(bf16[8,96,64]{1,2,0:T(8,128)(2,1)} %param.22) | copy-start | bytes 294916
  0.7 7.9 %copy-start.10 = (f32[96]{0:T(128)S(1)}, f32[96]{0:T(128)}, u32[]{:S(2)}) copy-start(f32[96]{0:T(128)} %param.23) | copy-start | bytes 1156
  0.7 7.9 %copy-start.2 = (bf16[27,64,64]{2,1,0:T(8,128)(2,1)S(1)}, bf16[27,64,64]{2,1,0:T(8,128)(2,1)}, u32[]{:S(2)}) copy-start(bf16[27,64,64]{2,1,0:T(8,128)(2,1)} %w_ref.4) | copy-start | bytes 663556
  7.0 2.4 %copy-start.8 = (bf16[16,32,512]{2,1,0:T(8,128)(2,1)S(1)}, bf16[16,32,512]{2,1,0:T(8,128)(2,1)}, u32[]{:S(2)}) copy-start(bf16[16,32,512]{2,1,0:T(8,128)(2,1)} %get-tuple-element.13) | copy-start | bytes 1572868
  8.0 1.4 %collective-permute-start = (bf16[2,32,512]{2,1,0:T(8,128)(2,1)S(1)}, bf16[2,32,512]{2,1,0:T(8,128)(2,1)S(1)}, u32[]{:S(2)}, u32[]{:S(2)}) collective-permute-start(bf16[2,32,512]{2,1,0:T(8,128)(2,1)S(1)} %slice_select_fusion), channel_id=1, source_target_pairs={{0,4},{4,0},{1,5},{5,1},{2,6},{6,2},{3,7},{7,3},{8,12},{12,8},{9,1... | collective-permute-start | bytes 196616 | tf_op jit(solution)/shard_map/ppermute | solution.py:319
  8.6 5.6 %copy-start.3 = (bf16[27,64,64]{2,1,0:T(8,128)(2,1)S(1)}, bf16[27,64,64]{2,1,0:T(8,128)(2,1)}, u32[]{:S(2)}) copy-start(bf16[27,64,64]{2,1,0:T(8,128)(2,1)} %w_ref.5) | copy-start | bytes 663556
  8.6 5.5 %copy-start.4 = (f32[64]{0:T(128)S(1)}, f32[64]{0:T(128)}, u32[]{:S(2)}) copy-start(f32[64]{0:T(128)} %param.19) | copy-start | bytes 772
  8.6 5.5 %copy-start.6 = (bf16[128,384]{1,0:T(8,128)(2,1)S(1)}, bf16[128,384]{1,0:T(8,128)(2,1)}, u32[]{:S(2)}) copy-start(bf16[128,384]{1,0:T(8,128)(2,1)} %get-tuple-element.14.tab_ref) | copy-start | bytes 294916
  9.6 6.3 %collective-permute-start.1 = (bf16[20,32,128]{2,1,0:T(8,128)(2,1)S(1)}, bf16[20,32,128]{2,1,0:T(8,128)(2,1)S(1)}, u32[]{:S(2)}, u32[]{:S(2)}) collective-permute-start(bf16[20,32,128]{2,1,0:T(8,128)(2,1)S(1)} %get-tuple-element.29), channel_id=1, source_target_pairs={{0,4},{1,2},{2,1},{3,7},{4,0},{5,6},{6,5},{7,3},{8,12},{9,10},{10,... | collective-permute-start | bytes 491528 | tf_op jit(solution)/shard_map/ppermute | solution.py:327
  10.0 8.4 %collective-permute-start.2 = (bf16[20,32,128]{2,1,0:T(8,128)(2,1)S(1)}, bf16[20,32,128]{2,1,0:T(8,128)(2,1)S(1)}, u32[]{:S(2)}, u32[]{:S(2)}) collective-permute-start(bf16[20,32,128]{2,1,0:T(8,128)(2,1)S(1)} %get-tuple-element.30), channel_id=1, source_target_pairs={{0,1},{1,0},{2,3},{3,2},{4,5},{5,4},{6,7},{7,6},{8,9},{9,8},{10,11... | collective-permute-start | bytes 491528 | tf_op jit(solution)/shard_map/ppermute | solution.py:319
  18.6 5.2 %collective-permute-start.3 = (bf16[20,2,768]{2,1,0:T(2,128)(2,1)S(1)}, bf16[20,2,768]{2,1,0:T(2,128)(2,1)S(1)}, u32[]{:S(2)}, u32[]{:S(2)}) collective-permute-start(bf16[20,2,768]{2,1,0:T(2,128)(2,1)S(1)} %bitcast.24), channel_id=1, source_target_pairs={{0,4},{8,16},{16,8},{24,28},{4,0},{12,20},{20,12},{28,24},{1,5},{9... | collective-permute-start | bytes 184328 | tf_op jit(solution)/shard_map/ppermute | solution.py:327
  18.7 5.8 %collective-permute-start.4 = (bf16[20,2,768]{2,1,0:T(2,128)(2,1)S(1)}, bf16[20,2,768]{2,1,0:T(2,128)(2,1)S(1)}, u32[]{:S(2)}, u32[]{:S(2)}) collective-permute-start(bf16[20,2,768]{2,1,0:T(2,128)(2,1)S(1)} %get-tuple-element.24), channel_id=1, source_target_pairs={{0,8},{8,0},{16,24},{24,16},{1,9},{9,1},{17,25},{25,17},{2,10},{10... | collective-permute-start | bytes 184328 | tf_op jit(solution)/shard_map/ppermute | solution.py:319
  21.7 3.0 %copy-start.5 = (f32[64]{0:T(128)S(1)}, f32[64]{0:T(128)}, u32[]{:S(2)}) copy-start(f32[64]{0:T(128)} %param.21) | copy-start | bytes 772
  21.7 3.0 %copy-start.7 = (bf16[128,384]{1,0:T(8,128)(2,1)S(1)}, bf16[128,384]{1,0:T(8,128)(2,1)}, u32[]{:S(2)}) copy-start(bf16[128,384]{1,0:T(8,128)(2,1)} %get-tuple-element.21.tab2_ref.tab_ref) | copy-start | bytes 294916
  24.7 6.6 %copy-start = (bf16[27,96,96]{2,1,0:T(8,128)(2,1)S(1)}, bf16[27,96,96]{2,1,0:T(8,128)(2,1)}, u32[]{:S(2)}) copy-start(bf16[27,96,96]{2,1,0:T(8,128)(2,1)} %w_ref.6) | copy-start | bytes 1492996
  31.2 0.7 %copy-start.11 = (f32[96]{0:T(128)S(1)}, f32[96]{0:T(128)}, u32[]{:S(2)}) copy-start(f32[96]{0:T(128)} %param.25) | copy-start | bytes 1156
  31.2 0.7 %copy-start.12 = (f32[96]{0:T(128)S(1)}, f32[96]{0:T(128)}, u32[]{:S(2)}) copy-start(f32[96]{0:T(128)} %param.27) | copy-start | bytes 1156
  31.2 9.7 %copy-start.1 = (bf16[27,96,96]{2,1,0:T(8,128)(2,1)S(1)}, bf16[27,96,96]{2,1,0:T(8,128)(2,1)}, u32[]{:S(2)}) copy-start(bf16[27,96,96]{2,1,0:T(8,128)(2,1)} %w_ref.7) | copy-start | bytes 1492996
  31.2 1.3 %collective-permute-start.5 = (bf16[2,16,512]{2,1,0:T(8,128)(2,1)S(1)}, bf16[2,16,512]{2,1,0:T(8,128)(2,1)S(1)}, u32[]{:S(2)}, u32[]{:S(2)}) collective-permute-start(bf16[2,16,512]{2,1,0:T(8,128)(2,1)S(1)} %slice_select_fusion.1), channel_id=1, source_target_pairs={{0,4},{4,0},{1,5},{5,1},{2,6},{6,2},{3,7},{7,3},{8,12},{12,8},{9,1... | collective-permute-start | bytes 98312 | tf_op jit(solution)/shard_map/ppermute | solution.py:319
  32.6 2.3 %collective-permute-start.6 = (bf16[12,16,256]{2,1,0:T(8,128)(2,1)S(1)}, bf16[12,16,256]{2,1,0:T(8,128)(2,1)S(1)}, u32[]{:S(2)}, u32[]{:S(2)}) collective-permute-start(bf16[12,16,256]{2,1,0:T(8,128)(2,1)S(1)} %get-tuple-element.38), channel_id=1, source_target_pairs={{0,4},{1,2},{2,1},{3,7},{4,0},{5,6},{6,5},{7,3},{8,12},{9,10},{10,... | collective-permute-start | bytes 294920 | tf_op jit(solution)/shard_map/ppermute | solution.py:327
  32.8 5.0 %collective-permute-start.7 = (bf16[12,16,256]{2,1,0:T(8,128)(2,1)S(1)}, bf16[12,16,256]{2,1,0:T(8,128)(2,1)S(1)}, u32[]{:S(2)}, u32[]{:S(2)}) collective-permute-start(bf16[12,16,256]{2,1,0:T(8,128)(2,1)S(1)} %get-tuple-element.37), channel_id=1, source_target_pairs={{0,1},{1,0},{2,3},{3,2},{4,5},{5,4},{6,7},{7,6},{8,9},{9,8},{10,11... | collective-permute-start | bytes 294920 | tf_op jit(solution)/shard_map/ppermute | solution.py:319
  38.1 3.2 %collective-permute-start.8 = (bf16[12,2,1024]{2,1,0:T(2,128)(2,1)S(1)}, bf16[12,2,1024]{2,1,0:T(2,128)(2,1)S(1)}, u32[]{:S(2)}, u32[]{:S(2)}) collective-permute-start(bf16[12,2,1024]{2,1,0:T(2,128)(2,1)S(1)} %get-tuple-element.48), channel_id=1, source_target_pairs={{0,4},{8,16},{16,8},{24,28},{4,0},{12,20},{20,12},{28,24},{1,5},{9... | collective-permute-start | bytes 147464 | tf_op jit(solution)/shard_map/ppermute | solution.py:327
  38.1 5.4 %collective-permute-start.9 = (bf16[12,2,1024]{2,1,0:T(2,128)(2,1)S(1)}, bf16[12,2,1024]{2,1,0:T(2,128)(2,1)S(1)}, u32[]{:S(2)}, u32[]{:S(2)}) collective-permute-start(bf16[12,2,1024]{2,1,0:T(2,128)(2,1)S(1)} %get-tuple-element.47), channel_id=1, source_target_pairs={{0,8},{8,0},{16,24},{24,16},{1,9},{9,1},{17,25},{25,17},{2,10},{10... | collective-permute-start | bytes 147464 | tf_op jit(solution)/shard_map/ppermute | solution.py:319

commit v5 on v4

--- a/solution.py
+++ b/solution.py
@@ -30,6 +30,7 @@
 NN = (((1,), (0,)), ((), ()))
 NT = (((1,), (1,)), ((), ()))
 VMEM_BYTES = 40 * 1024 * 1024
+DOWN1_VMEM_BYTES = 52 * 1024 * 1024
 
 
 def mm(a, b, dims=NN):
@@ -90,7 +91,7 @@
     lanes = Z1 // 2 * C1
     copies = []
     for n in range(sems.shape[0]):
-        cut = (slice(None), slice(None), slice(None), slice(n * 256, n * 256 + 256))
+        cut = slice(n * 16, n * 16 + 16)
         copies.append(pltpu.make_async_copy(v_ref.at[cut], field_ref.at[cut], sems.at[n]))
         copies[-1].start()
 
@@ -109,13 +110,17 @@
 
     r = iota((4 * CX, 128), 0)
     select = one_hot_rows(((r & 32) << 2) | (r & 64) | ((r & 31) << 1) | (r >> 7), 4 * CX)
+    part = 16 * half
     for n, copy in enumerate(copies):
         copy.wait()
-        for h in range(2):
-            v = field_ref[:, h, :, n * 256 : n * 256 + 256].reshape(kz, 256)
-            cells = mm(select, v, NT).astype(BF)
+        for m in range(field_ref.shape[3] // 256):
+            v = [field_ref[n * 16 : n * 16 + 16, h, :, m * 256 : m * 256 + 256].reshape(part, 256) for h in range(2)]
+            cells = mm(select, jnp.concatenate(v, axis=0), NT).astype(BF)
             for ab in range(4):
-                cells_ref[h, n * 64 : n * 64 + 64, ab * kz : (ab + 1) * kz] = cells[64 * ab : 64 * ab + 64]
+                lane = ab * kz + n * part
+                for h in range(2):
+                    piece = cells[64 * ab : 64 * ab + 64, h * part : h * part + part]
+                    cells_ref[h, m * 64 : m * 64 + 64, lane : lane + part] = piece
     mask = mask_rows(tab[:, 128:256], 0, Y1, X1, lambda x: x, 4)
     bias = twice(b_ref)
     for h in range(2):
@@ -222,7 +227,7 @@
 
 def level_one_kernel(
     xl_ref, low_ref, high_ref, xr_ref, g1_ref, g2_ref, g3_ref, ta_ref, tb_ref, ba_ref, bb_ref, wd_ref, bd_ref, tab_ref, tab2_ref,
-    one_ref, down_ref, e0, e1, e2, i0, i1, i2, feat_ref, d_ref,
+    feat_ref, down_ref, e0, e1, e2, i0, i1, i2, d_ref,
 ):
     fill_edges((e0, e1, e2), (xl_ref, low_ref, high_ref, xr_ref))
     rows = Y1 + 2
@@ -246,7 +251,6 @@
             value = jnp.maximum(acc[:, q * 128 : q * 128 + 128] + twice(bb_ref), 0.0) * mask
             feat_ref[:, (2 * g + q) * 128 : (2 * g + q + 1) * 128] = value.astype(BF)
 
-    lanes = Z1 * C1
     size = 8 * X1
     quarter = size // 4
     r = iota((size, 128), 0)
@@ -260,9 +264,12 @@
         left = jnp.concatenate([d_ref[q, :, z * 128 : z * 128 + 128] for q in range(4)], axis=1)
         down_ref[:, :, z * CP : z * CP + CP] = finish(mm(left, wd_ref[...]), bd_ref[...], mask, Y2)
 
+
+def one_kernel(feat_ref, out_ref):
+    lanes = feat_ref.shape[1]
     r = iota((lanes, 128), 0)
     order = one_hot_rows(((r & 7) << 6) | (r >> 3), lanes)
-    one_ref[...] = mm(order, feat_ref[...], NT).astype(BF)
+    out_ref[...] = mm(order, feat_ref[...], NT).astype(BF)
 
 
 def level_two_kernel(
@@ -362,9 +369,9 @@
             pltpu.VMEM((2 * kz, lanes1 // 2), BF),
             pltpu.VMEM((C0, 2, half, volume.shape[2]), BF),
             pltpu.VMEM((2, Y1 * X1, 2 * kz), BF),
-            pltpu.SemaphoreType.DMA((volume.shape[2] // 256,)),
+            pltpu.SemaphoreType.DMA((C0 // 16,)),
         ],
-        compiler_params=pltpu.CompilerParams(vmem_limit_bytes=123 * 512 * 1024),
+        compiler_params=pltpu.CompilerParams(vmem_limit_bytes=DOWN1_VMEM_BYTES),
         cost_estimate=cost(4e-6),
     )(volume.reshape(C0, 2, half, -1), jnp.swapaxes(w_down1, 1, 2), b_down1[None], tissue.transpose(1, 2, 0))
 
@@ -395,18 +402,22 @@
         cost_estimate=cost(4e-6),
     )(win, left, right, z_below, z_above, t1a, bias1a, tab1)
 
-    one, down = pl.pallas_call(
+    feat, down = pl.pallas_call(
         level_one_kernel,
-        out_shape=[shaped(lanes1, Y1 * X1), shaped(Y2, X2, Z2 * CP)],
+        out_shape=[shaped(Y1 * X1, lanes1), shaped(Y2, X2, Z2 * CP)],
         scratch_shapes=[pltpu.VMEM((ROWS1, EDGE, (Z1 + 4) * C1), BF)] * 3
         + [pltpu.VMEM((rows, X1, (Z1 + 2) * C1), BF)] * 3
-        + [pltpu.VMEM((Y1 * X1, lanes1), BF), pltpu.VMEM((4, Y2 * X2, lanes1), BF)],
+        + [pltpu.VMEM((4, Y2 * X2, lanes1), BF)],
         compiler_params=params(),
         cost_estimate=cost(6e-6),
     )(
         x_below, low, high, x_above, g1, g2, g3, t1a, t1b, bias1a, b_conv1b[None],
         pad_lanes(jnp.swapaxes(w_down2, 1, 2).reshape(8 * C1, C2)), pad_lanes(b_down2[None]), tab1, tab2,
     )
+
+    one = pl.pallas_call(
+        one_kernel, out_shape=shaped(lanes1, Y1 * X1), compiler_params=params(), cost_estimate=cost(2e-6)
+    )(feat)
 
     y_below, y_above = shift_along(down[:HALO], down[Y2 - HALO :], "gy")
     win = jnp.concatenate([y_below, down, y_above], axis=0)

time: 49.9 us -> 50.9 us (1.020)
  local copies, waits for them, and re-layouts: 0.52 us -> 4.29 us
  Pallas kernels: 24.1 us -> 21.9 us
  waiting for transfers between devices: 9.12 us -> 8.49 us
  other arithmetic: 1.68 us -> 2.21 us
    unnamed x26 -> x28, local copies, waits for them, and re-layouts: 0.28 us -> 3.14 us
    pallas_call x1, Pallas kernels: 6.36 us -> 3.94 us  [local(): pl.pallas_call(down1_kernel, in_specs=[pl.BlockSpec(memory_space=pltpu.HB...]
    pad x4, local copies, waits for them, and re-layouts: 0.04 us -> 0.95 us  [pad_lanes(): jnp.pad(value, [(0, 0)] * (value.ndim - 1) + [(0, CP - value.shape[-1])])]
    select_n x3, other arithmetic: 0.06 us -> 0.89 us  [shift_along(): below = jnp.where(index > 0, jnp.where(even, two, one), jnp.zeros_like(one))]
    ppermute x6, waiting for transfers between devices: 9.11 us -> 8.48 us  [shift_along(): lax.ppermute(jnp.where(even, high_edge, low_edge), axis, [(i, i ^ 1) for...]
    pallas_call x1 -> x2, Pallas kernels: 6.5 us -> 6.67 us  [the longest x1 5.4 us: local(): pl.pallas_call(level_one_kernel, out_shape=[shaped(Y1 * X1, lanes1), shap...]
  transfers between devices with their start and end apart: 10 -> 10, of which waited for: 6 -> 5; matrix products, arithmetic and copies ran while one was open for 0% -> 2% of each run, Pallas kernels for 10% -> 13%
where the time goes in v5:
time: 50.9 us; the launch traced here: 50.6 us
  Pallas kernels  21.9 us (43%)
  starting transfers between devices  12.8 us (25%)
  waiting for transfers between devices  8.49 us (17%)
  local copies, waits for them, and re-layouts  4.29 us (8%)
  other arithmetic  2.21 us (4%)
  between operations  1 us (2%)
    ppermute x6, starting transfers between devices, shift_along(): lax.ppermute(jnp.where(even, high_edge, low_edge), axis, [(i, i ^ 1) for...  12.3 us
    ppermute x6, waiting for transfers between devices, shift_along(): lax.ppermute(jnp.where(even, high_edge, low_edge), axis, [(i, i ^ 1) for...  8.48 us
    pallas_call x1, Pallas kernels, local(): pl.pallas_call(level_two_kernel, out_shape=shaped(C2 * Z2, Y2 * X2), scra...  6.12 us
    pallas_call x1, Pallas kernels, local(): pl.pallas_call(level_one_kernel, out_shape=[shaped(Y1 * X1, lanes1), shap...  5.4 us
    pallas_call x1, Pallas kernels, local(): pl.pallas_call(down1_kernel, in_specs=[pl.BlockSpec(memory_space=pltpu.HB...  3.94 us
    unnamed x28, local copies, waits for them, and re-layouts  3.14 us
    pallas_call x1, Pallas kernels, local(): pl.pallas_call(outer_kernel, out_shape=[shaped(rows, X1, 256), shaped(row...  2.19 us
    pallas_call x1, Pallas kernels, local(): pl.pallas_call(middle_kernel, out_shape=[shaped(ROWS1, X1, lanes1), shape...  1.71 us
  transfers between devices with their start and end apart: 10, of which 5 were waited for; matrix products, arithmetic and copies ran while one was open for 2% of the time, Pallas kernels for 13%

profile of v5, /device:TPU:0, one launch (start us, length us, event | category | flops | bytes accessed | tf_op | source)
XLA Modules:
  0.0 50.6 jit_solution(12628445103684236887)
XLA Ops:
  0.7 0.9 %copy-done.4 = bf16[8,64,48]{1,2,0:T(8,128)(2,1)S(1)} copy-done((bf16[8,64,48]{1,2,0:T(8,128)(2,1)S(1)}, bf16[8,64,48]{1,2,0:T(8,128)(2,1)}, u32[]{:S(2)}) %copy-start.4) | copy-done | bytes 49176
  1.5 0.7 %copy-done.5 = s32[32,8,4]{0,2,1:T(4,128)S(1)} copy-done((s32[32,8,4]{0,2,1:T(4,128)S(1)}, s32[32,8,4]{0,2,1:T(4,128)}, u32[]{:S(2)}) %copy-start.5) | copy-done | bytes 4120
  2.3 0.7 %copy-done.6 = f32[64]{0:T(128)S(1)} copy-done((f32[64]{0:T(128)S(1)}, f32[64]{0:T(128)}, u32[]{:S(2)}) %copy-start.6) | copy-done | bytes 280
  2.9 3.9 %shard_map.149 = (bf16[16,32,512]{2,1,0:T(8,128)(2,1)S(1)}, bf16[128,384]{1,0:T(8,128)(2,1)S(1)}, bf16[128,384]{1,0:T(8,128)(2,1)S(1)}) custom-call(bf16[48,2,8,2048]{3,2,1,0:T(8,128)(2,1)} %bitcast.28, bf16[8,48,64]{2,1,0:T(8,128)(2,1)S(1)} %bitcast.19, f32[1,64]{1,0:T(1,128)S(1)} %bitcast.21, s32[8,4,32]{2,1,0:T(4,128)S(1)} %bitcast.20), custom_call_target="tpu_custom_call" | custom-call | flops 4000000000 | tf_op jit(solution)/shard_map/pallas_call | solution.py:364
  6.9 0.6 %copy-done.9 = bf16[128,384]{1,0:T(8,128)(2,1)} copy-done((bf16[128,384]{1,0:T(8,128)(2,1)}, bf16[128,384]{1,0:T(8,128)(2,1)S(1)}, u32[]{:S(2)}) %copy-start.9) | copy-done | bytes 98328
  7.5 0.6 %slice_select_fusion = bf16[2,32,512]{2,1,0:T(8,128)(2,1)} fusion(bf16[16,32,512]{2,1,0:T(8,128)(2,1)S(1)} %get-tuple-element.13, pred[]{:T(512)S(6)} %eq.21), kind=kLoop, calls=%fused_computation.22 | loop fusion | flops 32768 | bytes 196609 | tf_op jit(solution)/shard_map/jit(_where)/select_n | solution.py:326
  8.2 0.5 collective-permute-start
  8.6 0.6 %shard_map.150.t_ref.ta_ref = bf16[3,256,1152]{2,1,0:T(8,128)(2,1)S(1)} custom-call(bf16[27,64,64]{2,1,0:T(8,128)(2,1)S(1)} %copy-done.2), custom_call_target="tpu_custom_call" | custom-call | flops 1000000000 | tf_op jit(solution)/shard_map/pallas_call | solution.py:156
  9.3 0.9 %pad.14.wd_ref = bf16[512,128]{1,0:T(8,128)(2,1)S(1)} pad(bf16[512,96]{1,0:T(8,128)(2,1)} %bitcast.26, bf16[]{:T(256)} %constant.50.clone.1), padding=0_0x0_32 | pad | bytes 229378 | tf_op jit(solution)/shard_map/jit(_pad)/pad | solution.py:353
  10.3 0.3 shard_map.155.ta_ref
  10.6 0.9 %broadcast_select_fusion.17 = (bf16[2,32,512]{2,1,0:T(8,128)(2,1)S(1)}, bf16[2,32,512]{2,1,0:T(8,128)(2,1)S(1)}) fusion(bf16[2,32,512]{2,1,0:T(8,128)(2,1)} %collective-permute-done, pred[]{:T(512)S(6)} %gt.14, pred[]{:T(512)S(6)} %lt.35), kind=kLoop, calls=%fused_computation.24 | loop fusion | flops 65536 | bytes 196610 | tf_op jit(solution)/shard_map/jit(_where)/select_n | solution.py:335
  11.6 0.1 collective-permute-start.1
  11.7 4.1 %collective-permute-start.2 = (bf16[20,32,128]{2,1,0:T(8,128)(2,1)S(1)}, bf16[20,32,128]{2,1,0:T(8,128)(2,1)S(1)}, u32[]{:S(2)}, u32[]{:S(2)}) collective-permute-start(bf16[20,32,128]{2,1,0:T(8,128)(2,1)S(1)} %get-tuple-element.30), channel_id=1, source_target_pairs={{0,1},{1,0},{2,3},{3,2},{4,5},{5,4},{6,7},{7,6},{8,9},{9,8},{10,11... | collective-permute-start | bytes 491528 | tf_op jit(solution)/shard_map/ppermute | solution.py:326
  15.8 1.7 %shard_map.151 = (bf16[20,32,512]{2,1,0:T(8,128)(2,1)S(1)}, bf16[20,32,512]{2,1,0:T(8,128)(2,1)S(1)}, bf16[18,32,256]{2,1,0:T(8,128)(2,1)S(1)}, bf16[3,256,1152]{2,1,0:T(8,128)(2,1)S(1)}) custom-call(bf16[20,32,512]{2,1,0:T(8,128)(2,1)S(1)} %pad_maximum_fusion.win_ref, bf16[3,256,1152]{2,1,0:T(8,128)(2,1)S(1)} %shard_map.150.t_ref.ta_ref, ...), custom_call_target="tpu_custom_call" | custom-call | flops 3000000000 | tf_op jit(solution)/shard_map/pallas_call | solution.py:387
  17.6 2.8 %collective-permute-done.2 = bf16[20,32,128]{2,1,0:T(8,128)(2,1)S(1)} collective-permute-done((bf16[20,32,128]{2,1,0:T(8,128)(2,1)S(1)}, bf16[20,32,128]{2,1,0:T(8,128)(2,1)S(1)}, u32[]{:S(2)}, u32[]{:S(2)}) %collective-permute-start.2) | collective-permute-done | bytes 163872 | tf_op jit(solution)/shard_map/ppermute | solution.py:326
  20.5 0.1 broadcast_select_fusion.5
  20.7 3.0 %collective-permute-start.4 = (bf16[20,2,768]{2,1,0:T(2,128)(2,1)S(1)}, bf16[20,2,768]{2,1,0:T(2,128)(2,1)S(1)}, u32[]{:S(2)}, u32[]{:S(2)}) collective-permute-start(bf16[20,2,768]{2,1,0:T(2,128)(2,1)S(1)} %get-tuple-element.24), channel_id=1, source_target_pairs={{0,8},{8,0},{16,24},{24,16},{1,9},{9,1},{17,25},{25,17},{2,10},{10... | collective-permute-start | bytes 184328 | tf_op jit(solution)/shard_map/ppermute | solution.py:326
  23.7 2.2 %shard_map.152 = (bf16[18,32,256]{2,1,0:T(8,128)(2,1)S(1)}, bf16[18,32,128]{2,1,0:T(8,128)(2,1)S(1)}) custom-call(bf16[20,32,512]{2,1,0:T(8,128)(2,1)S(1)} %pad_maximum_fusion.win_ref, bf16[20,32,512]{2,1,0:T(8,128)(2,1)S(1)} %get-tuple-element.15.left_ref, bf16[20,32,512]{2,1,0:T(8,128)(2,1)S(1)} %get-tuple-element.16.right_ref, ...), custom_call_target="tpu_custom_call" | custom-call | flops 4000000000 | tf_op jit(solution)/shard_map/pallas_call | solution.py:397
  25.9 0.7 %collective-permute-done.4 = bf16[20,2,768]{2,1,0:T(2,128)(2,1)S(1)} collective-permute-done((bf16[20,2,768]{2,1,0:T(2,128)(2,1)S(1)}, bf16[20,2,768]{2,1,0:T(2,128)(2,1)S(1)}, u32[]{:S(2)}, u32[]{:S(2)}) %collective-permute-start.4) | collective-permute-done | bytes 61472 | tf_op jit(solution)/shard_map/ppermute | solution.py:326
  26.6 0.1 broadcast_select_fusion.2
  26.8 5.4 %shard_map.153 = (bf16[512,512]{1,0:T(8,128)(2,1)S(1)}, bf16[8,16,512]{2,1,0:T(8,128)(2,1)S(1)}) custom-call(bf16[20,2,768]{2,1,0:T(2,128)(2,1)S(1)} %get-tuple-element.44.xl_ref, bf16[20,2,768]{2,1,0:T(2,128)(2,1)S(1)} %get-tuple-element.26.low_ref, bf16[20,2,768]{2,1,0:T(2,128)(2,1)S(1)} %get-tuple-element.25.high_ref, ...), custom_call_target="tpu_custom_call" | custom-call | flops 6000000000 | tf_op jit(solution)/shard_map/pallas_call | solution.py:405
  32.3 0.3 shard_map.156.tb_ref
  32.6 0.2 copy-done.12
  32.8 0.6 %collective-permute-done.5 = bf16[2,16,512]{2,1,0:T(8,128)(2,1)S(1)} collective-permute-done((bf16[2,16,512]{2,1,0:T(8,128)(2,1)S(1)}, bf16[2,16,512]{2,1,0:T(8,128)(2,1)S(1)}, u32[]{:S(2)}, u32[]{:S(2)}) %collective-permute-start.5) | collective-permute-done | bytes 32800 | tf_op jit(solution)/shard_map/ppermute | solution.py:326
  33.6 0.2 collective-permute-start.6
  33.8 2.0 %collective-permute-start.7 = (bf16[12,16,256]{2,1,0:T(8,128)(2,1)S(1)}, bf16[12,16,256]{2,1,0:T(8,128)(2,1)S(1)}, u32[]{:S(2)}, u32[]{:S(2)}) collective-permute-start(bf16[12,16,256]{2,1,0:T(8,128)(2,1)S(1)} %get-tuple-element.37), channel_id=1, source_target_pairs={{0,1},{1,0},{2,3},{3,2},{4,5},{5,4},{6,7},{7,6},{8,9},{9,8},{10,11... | collective-permute-start | bytes 294920 | tf_op jit(solution)/shard_map/ppermute | solution.py:326
  35.8 3.0 %collective-permute-done.7 = bf16[12,16,256]{2,1,0:T(8,128)(2,1)S(1)} collective-permute-done((bf16[12,16,256]{2,1,0:T(8,128)(2,1)S(1)}, bf16[12,16,256]{2,1,0:T(8,128)(2,1)S(1)}, u32[]{:S(2)}, u32[]{:S(2)}) %collective-permute-start.7) | collective-permute-done | bytes 98336 | tf_op jit(solution)/shard_map/ppermute | solution.py:326
  38.9 0.1 broadcast_select_fusion.11
  39.1 2.7 %collective-permute-start.9 = (bf16[12,2,1024]{2,1,0:T(2,128)(2,1)S(1)}, bf16[12,2,1024]{2,1,0:T(2,128)(2,1)S(1)}, u32[]{:S(2)}, u32[]{:S(2)}) collective-permute-start(bf16[12,2,1024]{2,1,0:T(2,128)(2,1)S(1)} %get-tuple-element.47), channel_id=1, source_target_pairs={{0,8},{8,0},{16,24},{24,16},{1,9},{9,1},{17,25},{25,17},{2,10},{10... | collective-permute-start | bytes 147464 | tf_op jit(solution)/shard_map/ppermute | solution.py:326
  41.8 1.3 %shard_map.154 = bf16[512,512]{1,0:T(8,128)(2,1)} custom-call(bf16[512,512]{1,0:T(8,128)(2,1)S(1)} %get-tuple-element.22.feat_ref), custom_call_target="tpu_custom_call" | custom-call | flops 2000000000 | tf_op jit(solution)/shard_map/pallas_call | solution.py:418
  43.1 1.3 %collective-permute-done.9 = bf16[12,2,1024]{2,1,0:T(2,128)(2,1)S(1)} collective-permute-done((bf16[12,2,1024]{2,1,0:T(2,128)(2,1)S(1)}, bf16[12,2,1024]{2,1,0:T(2,128)(2,1)S(1)}, u32[]{:S(2)}, u32[]{:S(2)}) %collective-permute-start.9) | collective-permute-done | bytes 49184 | tf_op jit(solution)/shard_map/ppermute | solution.py:326
  44.5 6.1 %shard_map.157 = bf16[384,128]{1,0:T(8,128)(2,1)} custom-call(bf16[12,16,512]{2,1,0:T(8,128)(2,1)S(1)} %pad_maximum_fusion.1.win_ref, bf16[12,16,256]{2,1,0:T(8,128)(2,1)S(1)} %get-tuple-element.36.zl_ref, bf16[12,16,256]{2,1,0:T(8,128)(2,1)S(1)} %get-tuple-element.35.zr_ref, bf16[12,2,1024]{2,1,0:T(2,128)(2,1)S(1)} %get-tuple-element.46.xl_ref, ...), custom_call_target="tpu_custom_call" | custom-call | flops 5000000000 | tf_op jit(solution)/shard_map/pallas_call | solution.py:428
  (49 shorter events, 0.8 us)
Async XLA Ops:
  0.6 0.9 %copy-start.4 = (bf16[8,64,48]{1,2,0:T(8,128)(2,1)S(1)}, bf16[8,64,48]{1,2,0:T(8,128)(2,1)}, u32[]{:S(2)}) copy-start(bf16[8,64,48]{1,2,0:T(8,128)(2,1)} %param.16) | copy-start | bytes 147460
  1.5 0.7 %copy-start.5 = (s32[32,8,4]{0,2,1:T(4,128)S(1)}, s32[32,8,4]{0,2,1:T(4,128)}, u32[]{:S(2)}) copy-start(s32[32,8,4]{0,2,1:T(4,128)} %param.15) | copy-start | bytes 12292
  2.3 0.7 %copy-start.6 = (f32[64]{0:T(128)S(1)}, f32[64]{0:T(128)}, u32[]{:S(2)}) copy-start(f32[64]{0:T(128)} %param.17) | copy-start | bytes 772
  2.9 5.7 %copy-start.2 = (bf16[27,64,64]{2,1,0:T(8,128)(2,1)S(1)}, bf16[27,64,64]{2,1,0:T(8,128)(2,1)}, u32[]{:S(2)}) copy-start(bf16[27,64,64]{2,1,0:T(8,128)(2,1)} %w_ref.4) | copy-start | bytes 663556
  6.9 0.6 %copy-start.9 = (bf16[128,384]{1,0:T(8,128)(2,1)}, bf16[128,384]{1,0:T(8,128)(2,1)S(1)}, u32[]{:S(2)}) copy-start(bf16[128,384]{1,0:T(8,128)(2,1)S(1)} %get-tuple-element.21.tab2_ref.tab_ref) | copy-start | bytes 294916
  7.5 2.7 %copy-start.11 = (f32[96]{0:T(128)S(1)}, f32[96]{0:T(128)}, u32[]{:S(2)}) copy-start(f32[96]{0:T(128)} %param.23) | copy-start | bytes 1156
  7.5 2.7 %copy-start = (bf16[27,96,96]{2,1,0:T(8,128)(2,1)S(1)}, bf16[27,96,96]{2,1,0:T(8,128)(2,1)}, u32[]{:S(2)}) copy-start(bf16[27,96,96]{2,1,0:T(8,128)(2,1)} %w_ref.6) | copy-start | bytes 1492996
  8.2 2.4 %collective-permute-start = (bf16[2,32,512]{2,1,0:T(8,128)(2,1)}, bf16[2,32,512]{2,1,0:T(8,128)(2,1)}, u32[]{:S(2)}, u32[]{:S(2)}) collective-permute-start(bf16[2,32,512]{2,1,0:T(8,128)(2,1)} %slice_select_fusion), channel_id=1, source_target_pairs={{0,4},{4,0},{1,5},{5,1},{2,6},{6,2},{3,7},{7,3},{8,12},{12,8},{9,1... | collective-permute-start | bytes 196616 | tf_op jit(solution)/shard_map/ppermute | solution.py:326
  10.2 5.6 %copy-start.3 = (bf16[27,64,64]{2,1,0:T(8,128)(2,1)S(1)}, bf16[27,64,64]{2,1,0:T(8,128)(2,1)}, u32[]{:S(2)}) copy-start(bf16[27,64,64]{2,1,0:T(8,128)(2,1)} %w_ref.5) | copy-start | bytes 663556
  10.2 5.5 %copy-start.7 = (f32[64]{0:T(128)S(1)}, f32[64]{0:T(128)}, u32[]{:S(2)}) copy-start(f32[64]{0:T(128)} %param.19) | copy-start | bytes 772
  11.6 6.0 %collective-permute-start.1 = (bf16[20,32,128]{2,1,0:T(8,128)(2,1)S(1)}, bf16[20,32,128]{2,1,0:T(8,128)(2,1)S(1)}, u32[]{:S(2)}, u32[]{:S(2)}) collective-permute-start(bf16[20,32,128]{2,1,0:T(8,128)(2,1)S(1)} %get-tuple-element.29), channel_id=1, source_target_pairs={{0,4},{1,2},{2,1},{3,7},{4,0},{5,6},{6,5},{7,3},{8,12},{9,10},{10,... | collective-permute-start | bytes 491528 | tf_op jit(solution)/shard_map/ppermute | solution.py:334
  11.7 8.7 %collective-permute-start.2 = (bf16[20,32,128]{2,1,0:T(8,128)(2,1)S(1)}, bf16[20,32,128]{2,1,0:T(8,128)(2,1)S(1)}, u32[]{:S(2)}, u32[]{:S(2)}) collective-permute-start(bf16[20,32,128]{2,1,0:T(8,128)(2,1)S(1)} %get-tuple-element.30), channel_id=1, source_target_pairs={{0,1},{1,0},{2,3},{3,2},{4,5},{5,4},{6,7},{7,6},{8,9},{9,8},{10,11... | collective-permute-start | bytes 491528 | tf_op jit(solution)/shard_map/ppermute | solution.py:326
  20.6 5.3 %collective-permute-start.3 = (bf16[20,2,768]{2,1,0:T(2,128)(2,1)S(1)}, bf16[20,2,768]{2,1,0:T(2,128)(2,1)S(1)}, u32[]{:S(2)}, u32[]{:S(2)}) collective-permute-start(bf16[20,2,768]{2,1,0:T(2,128)(2,1)S(1)} %bitcast.27), channel_id=1, source_target_pairs={{0,4},{8,16},{16,8},{24,28},{4,0},{12,20},{20,12},{28,24},{1,5},{9... | collective-permute-start | bytes 184328 | tf_op jit(solution)/shard_map/ppermute | solution.py:334
  20.7 5.9 %collective-permute-start.4 = (bf16[20,2,768]{2,1,0:T(2,128)(2,1)S(1)}, bf16[20,2,768]{2,1,0:T(2,128)(2,1)S(1)}, u32[]{:S(2)}, u32[]{:S(2)}) collective-permute-start(bf16[20,2,768]{2,1,0:T(2,128)(2,1)S(1)} %get-tuple-element.24), channel_id=1, source_target_pairs={{0,8},{8,0},{16,24},{24,16},{1,9},{9,1},{17,25},{25,17},{2,10},{10... | collective-permute-start | bytes 184328 | tf_op jit(solution)/shard_map/ppermute | solution.py:326
  23.7 3.1 %copy-start.8 = (f32[64]{0:T(128)S(1)}, f32[64]{0:T(128)}, u32[]{:S(2)}) copy-start(f32[64]{0:T(128)} %param.21) | copy-start | bytes 772
  23.7 3.1 %copy-start.10 = (bf16[128,384]{1,0:T(8,128)(2,1)S(1)}, bf16[128,384]{1,0:T(8,128)(2,1)}, u32[]{:S(2)}) copy-start(bf16[128,384]{1,0:T(8,128)(2,1)} %copy-done.9) | copy-start | bytes 294916
  26.8 5.5 %copy-start.1 = (bf16[27,96,96]{2,1,0:T(8,128)(2,1)S(1)}, bf16[27,96,96]{2,1,0:T(8,128)(2,1)}, u32[]{:S(2)}) copy-start(bf16[27,96,96]{2,1,0:T(8,128)(2,1)} %w_ref.7) | copy-start | bytes 1492996
  32.2 0.7 %copy-start.12 = (f32[96]{0:T(128)S(1)}, f32[96]{0:T(128)}, u32[]{:S(2)}) copy-start(f32[96]{0:T(128)} %param.25) | copy-start | bytes 1156
  32.2 0.7 %copy-start.13 = (f32[96]{0:T(128)S(1)}, f32[96]{0:T(128)}, u32[]{:S(2)}) copy-start(f32[96]{0:T(128)} %param.27) | copy-start | bytes 1156
  32.2 1.3 %collective-permute-start.5 = (bf16[2,16,512]{2,1,0:T(8,128)(2,1)S(1)}, bf16[2,16,512]{2,1,0:T(8,128)(2,1)S(1)}, u32[]{:S(2)}, u32[]{:S(2)}) collective-permute-start(bf16[2,16,512]{2,1,0:T(8,128)(2,1)S(1)} %slice_select_fusion.1), channel_id=1, source_target_pairs={{0,4},{4,0},{1,5},{5,1},{2,6},{6,2},{3,7},{7,3},{8,12},{12,8},{9,1... | collective-permute-start | bytes 98312 | tf_op jit(solution)/shard_map/ppermute | solution.py:326
  33.6 2.2 %collective-permute-start.6 = (bf16[12,16,256]{2,1,0:T(8,128)(2,1)S(1)}, bf16[12,16,256]{2,1,0:T(8,128)(2,1)S(1)}, u32[]{:S(2)}, u32[]{:S(2)}) collective-permute-start(bf16[12,16,256]{2,1,0:T(8,128)(2,1)S(1)} %get-tuple-element.38), channel_id=1, source_target_pairs={{0,4},{1,2},{2,1},{3,7},{4,0},{5,6},{6,5},{7,3},{8,12},{9,10},{10,... | collective-permute-start | bytes 294920 | tf_op jit(solution)/shard_map/ppermute | solution.py:334
  33.8 5.0 %collective-permute-start.7 = (bf16[12,16,256]{2,1,0:T(8,128)(2,1)S(1)}, bf16[12,16,256]{2,1,0:T(8,128)(2,1)S(1)}, u32[]{:S(2)}, u32[]{:S(2)}) collective-permute-start(bf16[12,16,256]{2,1,0:T(8,128)(2,1)S(1)} %get-tuple-element.37), channel_id=1, source_target_pairs={{0,1},{1,0},{2,3},{3,2},{4,5},{5,4},{6,7},{7,6},{8,9},{9,8},{10,11... | collective-permute-start | bytes 294920 | tf_op jit(solution)/shard_map/ppermute | solution.py:326
  39.0 4.1 %collective-permute-start.8 = (bf16[12,2,1024]{2,1,0:T(2,128)(2,1)S(1)}, bf16[12,2,1024]{2,1,0:T(2,128)(2,1)S(1)}, u32[]{:S(2)}, u32[]{:S(2)}) collective-permute-start(bf16[12,2,1024]{2,1,0:T(2,128)(2,1)S(1)} %get-tuple-element.48), channel_id=1, source_target_pairs={{0,4},{8,16},{16,8},{24,28},{4,0},{12,20},{20,12},{28,24},{1,5},{9... | collective-permute-start | bytes 147464 | tf_op jit(solution)/shard_map/ppermute | solution.py:334
  39.1 5.3 %collective-permute-start.9 = (bf16[12,2,1024]{2,1,0:T(2,128)(2,1)S(1)}, bf16[12,2,1024]{2,1,0:T(2,128)(2,1)S(1)}, u32[]{:S(2)}, u32[]{:S(2)}) collective-permute-start(bf16[12,2,1024]{2,1,0:T(2,128)(2,1)S(1)} %get-tuple-element.47), channel_id=1, source_target_pairs={{0,8},{8,0},{16,24},{24,16},{1,9},{9,1},{17,25},{25,17},{2,10},{10... | collective-permute-start | bytes 147464 | tf_op jit(solution)/shard_map/ppermute | solution.py:326

commit v6 on v5

--- a/solution.py
+++ b/solution.py
@@ -30,7 +30,7 @@
 NN = (((1,), (0,)), ((), ()))
 NT = (((1,), (1,)), ((), ()))
 VMEM_BYTES = 40 * 1024 * 1024
-DOWN1_VMEM_BYTES = 52 * 1024 * 1024
+DOWN1_VMEM_BYTES = 60 * 1024 * 1024
 
 
 def mm(a, b, dims=NN):
@@ -85,7 +85,7 @@
     return spread(64, 320), spread(128, 256)
 
 
-def down1_kernel(v_ref, w_ref, b_ref, t_ref, out_ref, tab_ref, tab2_ref, wd_ref, field_ref, cells_ref, sems):
+def down1_kernel(v_ref, w_ref, b_ref, t_ref, out_ref, first_ref, second_ref, tab_ref, tab2_ref, wd_ref, field_ref, cells_ref, sems):
     half = v_ref.shape[2]
     kz = C0 * half
     lanes = Z1 // 2 * C1
@@ -128,6 +128,13 @@
         for q in range(2):
             value = finish(acc[:, q * 128 : q * 128 + 128], bias, mask, Y1)
             out_ref[:, :, (2 * h + q) * 128 : (2 * h + q + 1) * 128] = value
+    odd = lax.axis_index("gy") & 1
+    for parity, edges in enumerate(((second_ref, first_ref), (first_ref, second_ref))):
+
+        @pl.when(odd == parity)
+        def _(low=edges[0], high=edges[1]):
+            low[...] = out_ref[:HALO]
+            high[...] = out_ref[Y1 - HALO :]
 
 
 def twice(b_ref):
@@ -272,33 +279,52 @@
     out_ref[...] = mm(order, feat_ref[...], NT).astype(BF)
 
 
+def fill_pitch(copies, wide):
+    pitch = copies[0].shape[1]
+    for lane in range(0, wide.shape[2], 128):
+        line = wide[:, :, lane : lane + 128]
+        for i, copy in enumerate(copies):
+            spare = jnp.zeros((line.shape[0], pitch - line.shape[1] + i, 128), BF)
+            copy[:, :, lane : lane + 128] = jnp.concatenate([line[:, i:], spare], axis=1)
+
+
+def level_two_group(taps, t_ref, b_ref, masks, moved):
+    rows = Y2 + 2
+    acc = conv_group(taps, t_ref, 0, rows, 256, 512)
+    for q in range(2):
+        cut = slice(q * 128, q * 128 + 128)
+        value = finish(acc[:, cut], b_ref[...], masks[q], rows)
+        for i, ref in enumerate(moved):
+            ref[:, :, cut] = value[:, i : i + X2]
+
+
+def level_two_masks(tab_ref):
+    mask = mask_rows(tab_ref[...], -1, Y2 + 2, PITCH2, lambda x: x - 1, 2)
+    return [mask[:, q * 128 : q * 128 + 128] for q in range(3)]
+
+
+def level_two_middle_kernel(wide_ref, t_ref, b_ref, tab_ref, a0, a1, a2, m0, m1, m2):
+    fill_pitch((a0, a1, a2), wide_ref[...])
+    here = level_two_masks(tab_ref)[1]
+    level_two_group([[(a, 0, 512)] for a in (a0, a1, a2)], t_ref, b_ref, (here, here), (m0, m1, m2))
+
+
 def level_two_kernel(
-    win_ref, zl_ref, zr_ref, xl_ref, xr_ref, ta_ref, tb_ref, ba_ref, bb_ref, tab_ref, out_ref, a0, a1, a2, i0, i1, i2
+    a0, a1, a2, m0, m1, m2, zl_ref, zr_ref, ta_ref, tb_ref, ba_ref, bb_ref, tab_ref, out_ref,
+    l0, l1, l2, h0, h1, h2, i0, i1, i2, j0, j1, j2,
 ):
-    for chunk in range(8):
-        ref, lane = (zl_ref, chunk) if chunk < 2 else ((win_ref, chunk - 2) if chunk < 6 else (zr_ref, chunk - 6))
-        inner = ref[:, :, lane * 128 : lane * 128 + 128]
-        cut = slice(chunk * 128, chunk * 128 + 128)
-        left, right = xl_ref[:, :, cut], xr_ref[:, :, cut]
-        for i, copy in enumerate((a0, a1, a2)):
-            spare = jnp.zeros((ROWS2, PITCH2 - X2 - 4 + i, 128), BF)
-            line = [inner, right, spare] if i == 2 else [left[:, i:], inner, right, spare]
-            copy[:, :, cut] = jnp.concatenate(line, axis=1)
-    rows = Y2 + 2
-    mask = mask_rows(tab_ref[...], -1, rows, PITCH2, lambda x: x - 1, 2)
-    for g in range(3):
-        acc = conv_group([[(ref, 256 * g, 512)] for ref in (a0, a1, a2)], ta_ref, 0, rows, 256, 512)
-        for q in range(2):
-            chunk = 2 * g + q
-            which = 0 if chunk == 0 else (2 if chunk == 5 else 1)
-            value = finish(acc[:, q * 128 : q * 128 + 128], ba_ref[...], mask[:, which * 128 : which * 128 + 128], rows)
-            cut = slice(chunk * 128, chunk * 128 + 128)
-            for s, copy in enumerate((i0, i1, i2)):
-                copy[:, :, cut] = value[:, s : s + X2]
+    fill_pitch((l0, l1, l2), zl_ref[...])
+    fill_pitch((h0, h1, h2), zr_ref[...])
+    below, here, above = level_two_masks(tab_ref)
+    own, mid, low, high = (a0, a1, a2), (m0, m1, m2), (i0, i1, i2), (j0, j1, j2)
+    taps = [[(z, 0, 256), (a, 0, 256)] for z, a in zip((l0, l1, l2), own)]
+    level_two_group(taps, ta_ref, ba_ref, (below, here), low)
+    taps = [[(a, 256, 256), (z, 0, 256)] for z, a in zip((h0, h1, h2), own)]
+    level_two_group(taps, ta_ref, ba_ref, (here, above), high)
     mask = mask_rows(tab_ref[:, 128:256], 0, Y2, X2, lambda x: x, 2)
     feat = []
-    for g in range(2):
-        acc = conv_group([[(ref, 256 * g, 512)] for ref in (i0, i1, i2)], tb_ref, 0, Y2, 256, 512)
+    for pair in ((low, mid), (mid, high)):
+        acc = conv_group([[(a, 0, 256), (b, 0, 256)] for a, b in zip(*pair)], tb_ref, 0, Y2, 256, 512)
         for q in range(2):
             feat.append((jnp.maximum(acc[:, q * 128 : q * 128 + 128] + bb_ref[...], 0.0) * mask).astype(BF))
     r = iota((C2 * Z2, 128), 0)
@@ -319,22 +345,26 @@
     return pairs
 
 
-def shift_along(low_edge, high_edge, axis):
+def trade(first, second, axis):
     count = lax.axis_size(axis)
     index = lax.axis_index(axis)
     even = index % 2 == 0
-    one = lax.ppermute(jnp.where(even, high_edge, low_edge), axis, [(i, i ^ 1) for i in range(count)])
+    one = lax.ppermute(first, axis, [(i, i ^ 1) for i in range(count)])
     two = one
     if count > 2 and axis == "gy":
         pairs = [(0, count - 1), (count - 1, 0)] + [(i, i - 1 + i % 2 * 2) for i in range(1, count - 1)]
-        two = lax.ppermute(jnp.where(even, low_edge, high_edge), axis, pairs)
+        two = lax.ppermute(second, axis, pairs)
     elif count > 2:
         axes = ("gx", "gy") if axis == "gx" else ("gy", "gz")
-        pairs = swap_pairs(count, lax.axis_size("gy"), axis == "gz")
-        two = lax.ppermute(jnp.where(even, low_edge, high_edge), axes, pairs)
+        two = lax.ppermute(second, axes, swap_pairs(count, lax.axis_size("gy"), axis == "gz"))
     below = jnp.where(index > 0, jnp.where(even, two, one), jnp.zeros_like(one))
     above = jnp.where(index < count - 1, jnp.where(even, one, two), jnp.zeros_like(one))
     return below, above
+
+
+def shift_along(low_edge, high_edge, axis):
+    even = lax.axis_index(axis) % 2 == 0
+    return trade(jnp.where(even, high_edge, low_edge), jnp.where(even, low_edge, high_edge), axis)
 
 
 def params():
@@ -361,10 +391,10 @@
     kz = C0 * depth
     lanes1 = Z1 * C1
     half = depth // 2
-    own, tab1, tab2 = pl.pallas_call(
+    own, first, second, tab1, tab2 = pl.pallas_call(
         down1_kernel,
         in_specs=[pl.BlockSpec(memory_space=pltpu.HBM)] + [pl.BlockSpec(memory_space=pltpu.VMEM)] * 3,
-        out_shape=[shaped(Y1, X1, lanes1), shaped(128, 384), shaped(128, 384)],
+        out_shape=[shaped(Y1, X1, lanes1)] + [shaped(HALO, X1, lanes1)] * 2 + [shaped(128, 384)] * 2,
         scratch_shapes=[
             pltpu.VMEM((2 * kz, lanes1 // 2), BF),
             pltpu.VMEM((C0, 2, half, volume.shape[2]), BF),
@@ -380,7 +410,7 @@
     t2b = banded(w_conv2b, 2, CP)
     bias1a = b_conv1a[None]
 
-    y_below, y_above = shift_along(own[:HALO], own[Y1 - HALO :], "gy")
+    y_below, y_above = trade(first, second, "gy")
     win = jnp.concatenate([y_below, own, y_above], axis=0)
     z_below, z_above = shift_along(win[:, :, :128], win[:, :, lanes1 - 128 :], "gz")
     rows = Y1 + 2
@@ -421,18 +451,24 @@
 
     y_below, y_above = shift_along(down[:HALO], down[Y2 - HALO :], "gy")
     win = jnp.concatenate([y_below, down, y_above], axis=0)
-    z_below, z_above = shift_along(win[:, :, : 2 * CP], win[:, :, 2 * CP :], "gz")
-    low = jnp.concatenate([z_below[:, :2], win[:, :2], z_above[:, :2]], axis=2)
-    high = jnp.concatenate([z_below[:, X2 - 2 :], win[:, X2 - 2 :], z_above[:, X2 - 2 :]], axis=2)
-    x_below, x_above = shift_along(low, high, "gx")
+    x_below, x_above = shift_along(win[:, :HALO], win[:, X2 - HALO :], "gx")
+    wide = jnp.concatenate([x_below, win, x_above], axis=1)
+    z_below, z_above = shift_along(wide[:, :, : 2 * CP], wide[:, :, 2 * CP :], "gz")
+    bias2a = pad_lanes(b_conv2a[None])
+    moved = [shaped(Y2 + 2, X2, 2 * CP)] * 3
+    middle = pl.pallas_call(
+        level_two_middle_kernel,
+        out_shape=[shaped(ROWS2, PITCH2, Z2 * CP)] * 3 + moved,
+        compiler_params=params(),
+        cost_estimate=cost(3e-6),
+    )(wide, t2a, bias2a, tab2)
     two = pl.pallas_call(
         level_two_kernel,
         out_shape=shaped(C2 * Z2, Y2 * X2),
-        scratch_shapes=[pltpu.VMEM((ROWS2, PITCH2, (Z2 + 4) * CP), BF)] * 3
-        + [pltpu.VMEM((Y2 + 2, X2, (Z2 + 2) * CP), BF)] * 3,
+        scratch_shapes=[pltpu.VMEM((ROWS2, PITCH2, 2 * CP), BF)] * 6 + [pltpu.VMEM((Y2 + 2, X2, 2 * CP), BF)] * 6,
         compiler_params=params(),
         cost_estimate=cost(5e-6),
-    )(win, z_below, z_above, x_below, x_above, t2a, t2b, pad_lanes(b_conv2a[None]), pad_lanes(b_conv2b[None]), tab2)
+    )(*middle, z_below, z_above, t2a, t2b, bias2a, pad_lanes(b_conv2b[None]), tab2)
     return one.reshape(C1, Z1, Y1 * X1), two.reshape(C2, Z2, Y2 * X2)
 
 

time: 50.9 us -> 46.4 us (0.912)
  local copies, waits for them, and re-layouts: 4.29 us -> 0.43 us
  waiting for transfers between devices: 8.49 us -> 6.65 us
  starting transfers between devices: 12.8 us -> 14 us
  Pallas kernels: 21.9 us -> 22.6 us
  other arithmetic: 2.21 us -> 1.59 us
    unnamed x28 -> x26, local copies, waits for them, and re-layouts: 3.14 us -> 0.28 us
    pallas_call x1, Pallas kernels: 6.12 us -> 4.04 us  [local(): pl.pallas_call(level_two_kernel, out_shape=shaped(C2 * Z2, Y2 * X2), scra...]
    ppermute x10, waiting for transfers between devices: 8.49 us -> 6.65 us  [the longest x6 6.64 us: trade(): one = lax.ppermute(first, axis, [(i, i ^ 1) for i in range(count)])]
    pallas_call x1, Pallas kernels: 3.94 us -> 5.62 us  [local(): pl.pallas_call(down1_kernel, in_specs=[pl.BlockSpec(memory_space=pltpu.HB...]
    pallas_call x0 -> x1, Pallas kernels: none -> 1.25 us  [local(): pl.pallas_call(level_two_middle_kernel, out_shape=[shaped(ROWS2, PITCH2,...]
    ppermute x10, starting transfers between devices: 12.8 us -> 14 us  [the longest x6 13.3 us: trade(): one = lax.ppermute(first, axis, [(i, i ^ 1) for i in range(count)])]
    pad x4, local copies, waits for them, and re-layouts: 0.95 us -> 0.05 us  [pad_lanes(): jnp.pad(value, [(0, 0)] * (value.ndim - 1) + [(0, CP - value.shape[-1])])]
    select_n x5 -> x4, other arithmetic: 0.92 us -> 0.19 us  [shift_along(): jnp.where(even, high_edge, low_edge)]
  transfers between devices with their start and end apart: 10 -> 10, of which waited for: 5 -> 6; matrix products, arithmetic and copies ran while one was open for 2% -> 0% of each run, Pallas kernels for 13% -> 17%
where the time goes in v6:
time: 46.4 us; the launch traced here: 46.2 us
  Pallas kernels  22.6 us (49%)
  starting transfers between devices  14 us (30%)
  waiting for transfers between devices  6.65 us (14%)
  other arithmetic  1.59 us (3%)
  between operations  0.99 us (2%)
    ppermute x6, starting transfers between devices, trade(): one = lax.ppermute(first, axis, [(i, i ^ 1) for i in range(count)])  13.3 us
    ppermute x6, waiting for transfers between devices, trade(): one = lax.ppermute(first, axis, [(i, i ^ 1) for i in range(count)])  6.64 us
    pallas_call x1, Pallas kernels, local(): pl.pallas_call(down1_kernel, in_specs=[pl.BlockSpec(memory_space=pltpu.HB...  5.62 us
    pallas_call x1, Pallas kernels, local(): pl.pallas_call(level_one_kernel, out_shape=[shaped(Y1 * X1, lanes1), shap...  5.23 us
    pallas_call x1, Pallas kernels, local(): pl.pallas_call(level_two_kernel, out_shape=shaped(C2 * Z2, Y2 * X2), scra...  4.04 us
    pallas_call x1, Pallas kernels, local(): pl.pallas_call(outer_kernel, out_shape=[shaped(rows, X1, 256), shaped(row...  2.19 us
    pallas_call x1, Pallas kernels, local(): pl.pallas_call(middle_kernel, out_shape=[shaped(ROWS1, X1, lanes1), shape...  1.72 us
    pallas_call x3, Pallas kernels, banded(): pl.pallas_call(kernel, out_shape=banded_shape(group, pad), compiler_param...  1.27 us
  transfers between devices with their start and end apart: 10, of which 6 were waited for; matrix products, arithmetic and copies ran while one was open for 0% of the time, Pallas kernels for 17%

profile of v6, /device:TPU:0, one launch (start us, length us, event | category | flops | bytes accessed | tf_op | source)
XLA Modules:
  0.0 46.2 jit_solution(17853081175502088520)
XLA Ops:
  0.6 5.6 %shard_map.149 = (bf16[16,32,512]{2,1,0:T(8,128)(2,1)}, bf16[2,32,512]{2,1,0:T(8,128)(2,1)}, bf16[2,32,512]{2,1,0:T(8,128)(2,1)}, bf16[128,384]{1,0:T(8,128)(2,1)}, bf16[128,384]{1,0:T(8,128)(2,1)}) custom-call(bf16[48,2,8,2048]{3,2,1,0:T(8,128)(2,1)} %bitcast.31, bf16[8,48,64]{2,1,0:T(8,128)(2,1)} %bitcast.32, f32[1,64]{1,0:T(1,128)} %bitcast.34, ...), custom_call_target="tpu_custom_call" | custom-call | flops 4000000000 | tf_op jit(solution)/shard_map/pallas_call | solution.py:394
  6.3 0.5 %collective-permute-start = (bf16[2,32,512]{2,1,0:T(8,128)(2,1)}, bf16[2,32,512]{2,1,0:T(8,128)(2,1)}, u32[]{:S(2)}, u32[]{:S(2)}) collective-permute-start(bf16[2,32,512]{2,1,0:T(8,128)(2,1)} %get-tuple-element.20), channel_id=1, source_target_pairs={{0,4},{4,0},{1,5},{5,1},{2,6},{6,2},{3,7},{7,3},{8,12},{12,8},{9,1... | collective-permute-start | bytes 196616 | tf_op jit(solution)/shard_map/ppermute | solution.py:352
  6.8 0.6 %shard_map.150.t_ref.ta_ref = bf16[3,256,1152]{2,1,0:T(8,128)(2,1)S(1)} custom-call(bf16[27,64,64]{2,1,0:T(8,128)(2,1)S(1)} %copy-done.2), custom_call_target="tpu_custom_call" | custom-call | flops 1000000000 | tf_op jit(solution)/shard_map/pallas_call | solution.py:163
  7.6 0.3 shard_map.155.t_ref.ta_ref
  7.9 0.1 collective-permute-done
  8.1 0.9 %broadcast_select_fusion.11 = (bf16[2,32,512]{2,1,0:T(8,128)(2,1)S(1)}, bf16[2,32,512]{2,1,0:T(8,128)(2,1)S(1)}) fusion(bf16[2,32,512]{2,1,0:T(8,128)(2,1)} %collective-permute-done, pred[]{:T(512)S(6)} %gt.14, pred[]{:T(512)S(6)} %lt.44), kind=kLoop, calls=%fused_computation.17 | loop fusion | flops 65536 | bytes 196610 | tf_op jit(solution)/shard_map/jit(_where)/select_n | solution.py:360
  8.9 0.1 pad_maximum_fusion.win_ref
  9.1 0.4 collective-permute-start.1
  9.5 4.1 %collective-permute-start.2 = (bf16[20,32,128]{2,1,0:T(8,128)(2,1)S(1)}, bf16[20,32,128]{2,1,0:T(8,128)(2,1)S(1)}, u32[]{:S(2)}, u32[]{:S(2)}) collective-permute-start(bf16[20,32,128]{2,1,0:T(8,128)(2,1)S(1)} %get-tuple-element.47), channel_id=1, source_target_pairs={{0,1},{1,0},{2,3},{3,2},{4,5},{5,4},{6,7},{7,6},{8,9},{9,8},{10,11... | collective-permute-start | bytes 491528 | tf_op jit(solution)/shard_map/ppermute | solution.py:352
  13.6 1.7 %shard_map.151 = (bf16[20,32,512]{2,1,0:T(8,128)(2,1)S(1)}, bf16[20,32,512]{2,1,0:T(8,128)(2,1)S(1)}, bf16[18,32,256]{2,1,0:T(8,128)(2,1)S(1)}, bf16[3,256,1152]{2,1,0:T(8,128)(2,1)S(1)}) custom-call(bf16[20,32,512]{2,1,0:T(8,128)(2,1)S(1)} %pad_maximum_fusion.win_ref, bf16[3,256,1152]{2,1,0:T(8,128)(2,1)S(1)} %shard_map.150.t_ref.ta_ref, ...), custom_call_target="tpu_custom_call" | custom-call | flops 3000000000 | tf_op jit(solution)/shard_map/pallas_call | solution.py:417
  15.4 0.1 fusion
  15.4 2.4 %collective-permute-done.2 = bf16[20,32,128]{2,1,0:T(8,128)(2,1)S(1)} collective-permute-done((bf16[20,32,128]{2,1,0:T(8,128)(2,1)S(1)}, bf16[20,32,128]{2,1,0:T(8,128)(2,1)S(1)}, u32[]{:S(2)}, u32[]{:S(2)}) %collective-permute-start.2) | collective-permute-done | bytes 163872 | tf_op jit(solution)/shard_map/ppermute | solution.py:352
  17.9 0.1 broadcast_select_fusion.7
  18.1 1.6 %collective-permute-start.4 = (bf16[20,2,768]{2,1,0:T(2,128)(2,1)S(1)}, bf16[20,2,768]{2,1,0:T(2,128)(2,1)S(1)}, u32[]{:S(2)}, u32[]{:S(2)}) collective-permute-start(bf16[20,2,768]{2,1,0:T(2,128)(2,1)S(1)} %get-tuple-element.41), channel_id=1, source_target_pairs={{0,8},{8,0},{16,24},{24,16},{1,9},{9,1},{17,25},{25,17},{2,10},{10... | collective-permute-start | bytes 184328 | tf_op jit(solution)/shard_map/ppermute | solution.py:352
  19.7 0.1 collective-permute-start.3
  19.8 2.2 %shard_map.152 = (bf16[18,32,256]{2,1,0:T(8,128)(2,1)S(1)}, bf16[18,32,128]{2,1,0:T(8,128)(2,1)S(1)}) custom-call(bf16[20,32,512]{2,1,0:T(8,128)(2,1)S(1)} %pad_maximum_fusion.win_ref, bf16[20,32,512]{2,1,0:T(8,128)(2,1)S(1)} %get-tuple-element.23.left_ref, bf16[20,32,512]{2,1,0:T(8,128)(2,1)S(1)} %get-tuple-element.24.right_ref, ...), custom_call_target="tpu_custom_call" | custom-call | flops 4000000000 | tf_op jit(solution)/shard_map/pallas_call | solution.py:427
  22.0 0.5 %collective-permute-done.4 = bf16[20,2,768]{2,1,0:T(2,128)(2,1)S(1)} collective-permute-done((bf16[20,2,768]{2,1,0:T(2,128)(2,1)S(1)}, bf16[20,2,768]{2,1,0:T(2,128)(2,1)S(1)}, u32[]{:S(2)}, u32[]{:S(2)}) %collective-permute-start.4) | collective-permute-done | bytes 61472 | tf_op jit(solution)/shard_map/ppermute | solution.py:352
  22.5 0.1 broadcast_select_fusion.4
  22.6 5.2 %shard_map.153 = (bf16[512,512]{1,0:T(8,128)(2,1)S(1)}, bf16[8,16,512]{2,1,0:T(8,128)(2,1)S(1)}) custom-call(bf16[20,2,768]{2,1,0:T(2,128)(2,1)S(1)} %get-tuple-element.59.xl_ref, bf16[20,2,768]{2,1,0:T(2,128)(2,1)S(1)} %get-tuple-element.43.low_ref, bf16[20,2,768]{2,1,0:T(2,128)(2,1)S(1)} %get-tuple-element.42.high_ref, ...), custom_call_target="tpu_custom_call" | custom-call | flops 6000000000 | tf_op jit(solution)/shard_map/pallas_call | solution.py:435
  27.9 0.1 collective-permute-start.5
  28.0 0.3 shard_map.157.tb_ref
  28.3 0.2 copy-done.11
  28.6 0.6 %collective-permute-done.5 = bf16[2,16,512]{2,1,0:T(8,128)(2,1)S(1)} collective-permute-done((bf16[2,16,512]{2,1,0:T(8,128)(2,1)S(1)}, bf16[2,16,512]{2,1,0:T(8,128)(2,1)S(1)}, u32[]{:S(2)}, u32[]{:S(2)}) %collective-permute-start.5) | collective-permute-done | bytes 32800 | tf_op jit(solution)/shard_map/ppermute | solution.py:352
  29.3 0.2 collective-permute-start.6
  29.5 5.2 %collective-permute-start.7 = (bf16[12,2,512]{2,1,0:T(2,128)(2,1)S(1)}, bf16[12,2,512]{2,1,0:T(2,128)(2,1)S(1)}, u32[]{:S(2)}, u32[]{:S(2)}) collective-permute-start(bf16[12,2,512]{2,1,0:T(2,128)(2,1)S(1)} %bitcast.30), channel_id=1, source_target_pairs={{0,8},{8,0},{16,24},{24,16},{1,9},{9,1},{17,25},{25,17},{2,10},{10... | collective-permute-start | bytes 73736 | tf_op jit(solution)/shard_map/ppermute | solution.py:352
  34.7 1.3 %shard_map.154 = bf16[512,512]{1,0:T(8,128)(2,1)} custom-call(bf16[512,512]{1,0:T(8,128)(2,1)S(1)} %get-tuple-element.30.feat_ref), custom_call_target="tpu_custom_call" | custom-call | flops 2000000000 | tf_op jit(solution)/shard_map/pallas_call | solution.py:448
  36.0 0.8 %collective-permute-done.7 = bf16[12,2,512]{2,1,0:T(2,128)(2,1)S(1)} collective-permute-done((bf16[12,2,512]{2,1,0:T(2,128)(2,1)S(1)}, bf16[12,2,512]{2,1,0:T(2,128)(2,1)S(1)}, u32[]{:S(2)}, u32[]{:S(2)}) %collective-permute-start.7) | collective-permute-done | bytes 24608 | tf_op jit(solution)/shard_map/ppermute | solution.py:352
  36.8 0.1 pad_maximum_fusion.1.wide_ref
  37.0 1.8 %collective-permute-start.9 = (bf16[12,20,256]{2,1,0:T(8,128)(2,1)S(1)}, bf16[12,20,256]{2,1,0:T(8,128)(2,1)S(1)}, u32[]{:S(2)}, u32[]{:S(2)}) collective-permute-start(bf16[12,20,256]{2,1,0:T(8,128)(2,1)S(1)} %get-tuple-element.52), channel_id=1, source_target_pairs={{0,1},{1,0},{2,3},{3,2},{4,5},{5,4},{6,7},{7,6},{8,9},{9,8},{10,11... | collective-permute-start | bytes 368648 | tf_op jit(solution)/shard_map/ppermute | solution.py:352
  38.8 1.3 %shard_map.156 = (bf16[12,32,512]{2,1,0:T(8,128)(2,1)S(1)}, bf16[12,32,512]{2,1,0:T(8,128)(2,1)S(1)}, bf16[12,32,512]{2,1,0:T(8,128)(2,1)S(1)}, bf16[10,16,256]{...) custom-call(bf16[12,20,512]{2,1,0:T(8,128)(2,1)S(1)} %pad_maximum_fusion.1.wide_ref, ...), custom_call_target="tpu_custom_call" | custom-call | flops 3000000000 | tf_op jit(solution)/shard_map/pallas_call | solution.py:459
  40.0 2.1 %collective-permute-done.9 = bf16[12,20,256]{2,1,0:T(8,128)(2,1)S(1)} collective-permute-done((bf16[12,20,256]{2,1,0:T(8,128)(2,1)S(1)}, bf16[12,20,256]{2,1,0:T(8,128)(2,1)S(1)}, u32[]{:S(2)}, u32[]{:S(2)}) %collective-permute-start.9) | collective-permute-done | bytes 122912 | tf_op jit(solution)/shard_map/ppermute | solution.py:352
  42.2 4.0 %shard_map.158 = bf16[384,128]{1,0:T(8,128)(2,1)} custom-call(bf16[12,32,512]{2,1,0:T(8,128)(2,1)S(1)} %get-tuple-element.32.a0, bf16[12,32,512]{2,1,0:T(8,128)(2,1)S(1)} %get-tuple-element.33.a1, bf16[12,32,512]{2,1,0:T(8,128)(2,1)S(1)} %get-tuple-element.34.a2, bf16[10,16,256]{2,1,0:T(8,128)(2,1)S(1)} %get-tuple-element.35.m0, ...), custom_call_target="tpu_custom_call" | custom-call | flops 5000000000 | tf_op jit(solution)/shard_map/pallas_call | solution.py:465
  (45 shorter events, 0.4 us)
Async XLA Ops:
  0.6 6.2 %copy-start.2 = (bf16[27,64,64]{2,1,0:T(8,128)(2,1)S(1)}, bf16[27,64,64]{2,1,0:T(8,128)(2,1)}, u32[]{:S(2)}) copy-start(bf16[27,64,64]{2,1,0:T(8,128)(2,1)} %w_ref.4) | copy-start | bytes 663556
  6.3 1.2 %copy-start.9 = (bf16[8,96,64]{1,2,0:T(8,128)(2,1)S(1)}, bf16[8,96,64]{1,2,0:T(8,128)(2,1)}, u32[]{:S(2)}) copy-start(bf16[8,96,64]{1,2,0:T(8,128)(2,1)} %param.22) | copy-start | bytes 294916
  6.3 1.2 %copy-start.10 = (f32[96]{0:T(128)S(1)}, f32[96]{0:T(128)}, u32[]{:S(2)}) copy-start(f32[96]{0:T(128)} %param.23) | copy-start | bytes 1156
  6.3 1.3 %copy-start = (bf16[27,96,96]{2,1,0:T(8,128)(2,1)S(1)}, bf16[27,96,96]{2,1,0:T(8,128)(2,1)}, u32[]{:S(2)}) copy-start(bf16[27,96,96]{2,1,0:T(8,128)(2,1)} %w_ref.6) | copy-start | bytes 1492996
  6.3 1.8 %collective-permute-start = (bf16[2,32,512]{2,1,0:T(8,128)(2,1)}, bf16[2,32,512]{2,1,0:T(8,128)(2,1)}, u32[]{:S(2)}, u32[]{:S(2)}) collective-permute-start(bf16[2,32,512]{2,1,0:T(8,128)(2,1)} %get-tuple-element.20), channel_id=1, source_target_pairs={{0,4},{4,0},{1,5},{5,1},{2,6},{6,2},{3,7},{7,3},{8,12},{12,8},{9,1... | collective-permute-start | bytes 196616 | tf_op jit(solution)/shard_map/ppermute | solution.py:352
  7.4 1.5 %copy-start.8 = (bf16[16,32,512]{2,1,0:T(8,128)(2,1)S(1)}, bf16[16,32,512]{2,1,0:T(8,128)(2,1)}, u32[]{:S(2)}) copy-start(bf16[16,32,512]{2,1,0:T(8,128)(2,1)} %get-tuple-element.21) | copy-start | bytes 1572868
  7.6 6.1 %copy-start.3 = (bf16[27,64,64]{2,1,0:T(8,128)(2,1)S(1)}, bf16[27,64,64]{2,1,0:T(8,128)(2,1)}, u32[]{:S(2)}) copy-start(bf16[27,64,64]{2,1,0:T(8,128)(2,1)} %w_ref.5) | copy-start | bytes 663556
  7.6 6.1 %copy-start.4 = (f32[64]{0:T(128)S(1)}, f32[64]{0:T(128)}, u32[]{:S(2)}) copy-start(f32[64]{0:T(128)} %param.19) | copy-start | bytes 772
  7.6 6.0 %copy-start.6 = (bf16[128,384]{1,0:T(8,128)(2,1)S(1)}, bf16[128,384]{1,0:T(8,128)(2,1)}, u32[]{:S(2)}) copy-start(bf16[128,384]{1,0:T(8,128)(2,1)} %get-tuple-element.22.tab_ref) | copy-start | bytes 294916
  9.1 6.4 %collective-permute-start.1 = (bf16[20,32,128]{2,1,0:T(8,128)(2,1)S(1)}, bf16[20,32,128]{2,1,0:T(8,128)(2,1)S(1)}, u32[]{:S(2)}, u32[]{:S(2)}) collective-permute-start(bf16[20,32,128]{2,1,0:T(8,128)(2,1)S(1)} %get-tuple-element.46), channel_id=1, source_target_pairs={{0,4},{1,2},{2,1},{3,7},{4,0},{5,6},{6,5},{7,3},{8,12},{9,10},{10,... | collective-permute-start | bytes 491528 | tf_op jit(solution)/shard_map/ppermute | solution.py:359
  9.5 8.4 %collective-permute-start.2 = (bf16[20,32,128]{2,1,0:T(8,128)(2,1)S(1)}, bf16[20,32,128]{2,1,0:T(8,128)(2,1)S(1)}, u32[]{:S(2)}, u32[]{:S(2)}) collective-permute-start(bf16[20,32,128]{2,1,0:T(8,128)(2,1)S(1)} %get-tuple-element.47), channel_id=1, source_target_pairs={{0,1},{1,0},{2,3},{3,2},{4,5},{5,4},{6,7},{7,6},{8,9},{9,8},{10,11... | collective-permute-start | bytes 491528 | tf_op jit(solution)/shard_map/ppermute | solution.py:352
  18.1 4.4 %collective-permute-start.4 = (bf16[20,2,768]{2,1,0:T(2,128)(2,1)S(1)}, bf16[20,2,768]{2,1,0:T(2,128)(2,1)S(1)}, u32[]{:S(2)}, u32[]{:S(2)}) collective-permute-start(bf16[20,2,768]{2,1,0:T(2,128)(2,1)S(1)} %get-tuple-element.41), channel_id=1, source_target_pairs={{0,8},{8,0},{16,24},{24,16},{1,9},{9,1},{17,25},{25,17},{2,10},{10... | collective-permute-start | bytes 184328 | tf_op jit(solution)/shard_map/ppermute | solution.py:352
  19.7 2.8 %collective-permute-start.3 = (bf16[20,2,768]{2,1,0:T(2,128)(2,1)S(1)}, bf16[20,2,768]{2,1,0:T(2,128)(2,1)S(1)}, u32[]{:S(2)}, u32[]{:S(2)}) collective-permute-start(bf16[20,2,768]{2,1,0:T(2,128)(2,1)S(1)} %bitcast.29), channel_id=1, source_target_pairs={{0,4},{8,16},{16,8},{24,28},{4,0},{12,20},{20,12},{28,24},{1,5},{9... | collective-permute-start | bytes 184328 | tf_op jit(solution)/shard_map/ppermute | solution.py:359
  19.7 2.9 %copy-start.5 = (f32[64]{0:T(128)S(1)}, f32[64]{0:T(128)}, u32[]{:S(2)}) copy-start(f32[64]{0:T(128)} %param.21) | copy-start | bytes 772
  19.8 2.9 %copy-start.7 = (bf16[128,384]{1,0:T(8,128)(2,1)S(1)}, bf16[128,384]{1,0:T(8,128)(2,1)}, u32[]{:S(2)}) copy-start(bf16[128,384]{1,0:T(8,128)(2,1)} %get-tuple-element.29.tab2_ref.tab_ref) | copy-start | bytes 294916
  22.6 5.4 %copy-start.1 = (bf16[27,96,96]{2,1,0:T(8,128)(2,1)S(1)}, bf16[27,96,96]{2,1,0:T(8,128)(2,1)}, u32[]{:S(2)}) copy-start(bf16[27,96,96]{2,1,0:T(8,128)(2,1)} %w_ref.7) | copy-start | bytes 1492996
  27.9 0.7 %copy-start.11 = (f32[96]{0:T(128)S(1)}, f32[96]{0:T(128)}, u32[]{:S(2)}) copy-start(f32[96]{0:T(128)} %param.25) | copy-start | bytes 1156
  27.9 0.7 %copy-start.12 = (f32[96]{0:T(128)S(1)}, f32[96]{0:T(128)}, u32[]{:S(2)}) copy-start(f32[96]{0:T(128)} %param.27) | copy-start | bytes 1156
  27.9 1.3 %collective-permute-start.5 = (bf16[2,16,512]{2,1,0:T(8,128)(2,1)S(1)}, bf16[2,16,512]{2,1,0:T(8,128)(2,1)S(1)}, u32[]{:S(2)}, u32[]{:S(2)}) collective-permute-start(bf16[2,16,512]{2,1,0:T(8,128)(2,1)S(1)} %slice_select_fusion), channel_id=1, source_target_pairs={{0,4},{4,0},{1,5},{5,1},{2,6},{6,2},{3,7},{7,3},{8,12},{12,8},{9,1... | collective-permute-start | bytes 98312 | tf_op jit(solution)/shard_map/ppermute | solution.py:352
  29.3 6.7 %collective-permute-start.6 = (bf16[12,2,512]{2,1,0:T(2,128)(2,1)S(1)}, bf16[12,2,512]{2,1,0:T(2,128)(2,1)S(1)}, u32[]{:S(2)}, u32[]{:S(2)}) collective-permute-start(bf16[12,2,512]{2,1,0:T(2,128)(2,1)S(1)} %get-tuple-element.38), channel_id=1, source_target_pairs={{0,4},{8,16},{16,8},{24,28},{4,0},{12,20},{20,12},{28,24},{1,5},{9... | collective-permute-start | bytes 73736 | tf_op jit(solution)/shard_map/ppermute | solution.py:359
  29.5 7.2 %collective-permute-start.7 = (bf16[12,2,512]{2,1,0:T(2,128)(2,1)S(1)}, bf16[12,2,512]{2,1,0:T(2,128)(2,1)S(1)}, u32[]{:S(2)}, u32[]{:S(2)}) collective-permute-start(bf16[12,2,512]{2,1,0:T(2,128)(2,1)S(1)} %bitcast.30), channel_id=1, source_target_pairs={{0,8},{8,0},{16,24},{24,16},{1,9},{9,1},{17,25},{25,17},{2,10},{10... | collective-permute-start | bytes 73736 | tf_op jit(solution)/shard_map/ppermute | solution.py:352
  37.0 5.2 %collective-permute-start.9 = (bf16[12,20,256]{2,1,0:T(8,128)(2,1)S(1)}, bf16[12,20,256]{2,1,0:T(8,128)(2,1)S(1)}, u32[]{:S(2)}, u32[]{:S(2)}) collective-permute-start(bf16[12,20,256]{2,1,0:T(8,128)(2,1)S(1)} %get-tuple-element.52), channel_id=1, source_target_pairs={{0,1},{1,0},{2,3},{3,2},{4,5},{5,4},{6,7},{7,6},{8,9},{9,8},{10,11... | collective-permute-start | bytes 368648 | tf_op jit(solution)/shard_map/ppermute | solution.py:352
  38.8 3.4 %collective-permute-start.8 = (bf16[12,20,256]{2,1,0:T(8,128)(2,1)S(1)}, bf16[12,20,256]{2,1,0:T(8,128)(2,1)S(1)}, u32[]{:S(2)}, u32[]{:S(2)}) collective-permute-start(bf16[12,20,256]{2,1,0:T(8,128)(2,1)S(1)} %get-tuple-element.53), channel_id=1, source_target_pairs={{0,4},{1,2},{2,1},{3,7},{4,0},{5,6},{6,5},{7,3},{8,12},{9,10},{10,... | collective-permute-start | bytes 368648 | tf_op jit(solution)/shard_map/ppermute | solution.py:359

commit v7 on v6

--- a/solution.py
+++ b/solution.py
@@ -30,7 +30,6 @@
 NN = (((1,), (0,)), ((), ()))
 NT = (((1,), (1,)), ((), ()))
 VMEM_BYTES = 40 * 1024 * 1024
-DOWN1_VMEM_BYTES = 60 * 1024 * 1024
 
 
 def mm(a, b, dims=NN):
@@ -85,16 +84,11 @@
     return spread(64, 320), spread(128, 256)
 
 
-def down1_kernel(v_ref, w_ref, b_ref, t_ref, out_ref, first_ref, second_ref, tab_ref, tab2_ref, wd_ref, field_ref, cells_ref, sems):
+def down1_kernel(v_ref, w_ref, b_ref, t_ref, order_ref, out_ref, tab_ref, tab2_ref, wd_ref, cells_ref):
+    del order_ref
     half = v_ref.shape[2]
     kz = C0 * half
     lanes = Z1 // 2 * C1
-    copies = []
-    for n in range(sems.shape[0]):
-        cut = slice(n * 16, n * 16 + 16)
-        copies.append(pltpu.make_async_copy(v_ref.at[cut], field_ref.at[cut], sems.at[n]))
-        copies[-1].start()
-
     tab, tab2 = tissue_tables(t_ref)
     tab_ref[...] = tab
     tab2_ref[...] = tab2
@@ -111,10 +105,10 @@
     r = iota((4 * CX, 128), 0)
     select = one_hot_rows(((r & 32) << 2) | (r & 64) | ((r & 31) << 1) | (r >> 7), 4 * CX)
     part = 16 * half
-    for n, copy in enumerate(copies):
-        copy.wait()
-        for m in range(field_ref.shape[3] // 256):
-            v = [field_ref[n * 16 : n * 16 + 16, h, :, m * 256 : m * 256 + 256].reshape(part, 256) for h in range(2)]
+    part = 16 * half
+    for n in range(C0 // 16):
+        for m in range(v_ref.shape[3] // 256):
+            v = [v_ref[n * 16 : n * 16 + 16, h, :, m * 256 : m * 256 + 256].reshape(part, 256) for h in range(2)]
             cells = mm(select, jnp.concatenate(v, axis=0), NT).astype(BF)
             for ab in range(4):
                 lane = ab * kz + n * part
@@ -128,13 +122,6 @@
         for q in range(2):
             value = finish(acc[:, q * 128 : q * 128 + 128], bias, mask, Y1)
             out_ref[:, :, (2 * h + q) * 128 : (2 * h + q + 1) * 128] = value
-    odd = lax.axis_index("gy") & 1
-    for parity, edges in enumerate(((second_ref, first_ref), (first_ref, second_ref))):
-
-        @pl.when(odd == parity)
-        def _(low=edges[0], high=edges[1]):
-            low[...] = out_ref[:HALO]
-            high[...] = out_ref[Y1 - HALO :]
 
 
 def twice(b_ref):
@@ -391,28 +378,27 @@
     kz = C0 * depth
     lanes1 = Z1 * C1
     half = depth // 2
-    own, first, second, tab1, tab2 = pl.pallas_call(
+    t1a = banded(w_conv1a, 4, C1)
+    own, tab1, tab2 = pl.pallas_call(
         down1_kernel,
-        in_specs=[pl.BlockSpec(memory_space=pltpu.HBM)] + [pl.BlockSpec(memory_space=pltpu.VMEM)] * 3,
-        out_shape=[shaped(Y1, X1, lanes1)] + [shaped(HALO, X1, lanes1)] * 2 + [shaped(128, 384)] * 2,
+        in_specs=[pl.BlockSpec(memory_space=pltpu.VMEM)] * 4 + [pl.BlockSpec(memory_space=pl.ANY)],
+        out_shape=[shaped(Y1, X1, lanes1), shaped(128, 384), shaped(128, 384)],
         scratch_shapes=[
             pltpu.VMEM((2 * kz, lanes1 // 2), BF),
-            pltpu.VMEM((C0, 2, half, volume.shape[2]), BF),
             pltpu.VMEM((2, Y1 * X1, 2 * kz), BF),
-            pltpu.SemaphoreType.DMA((C0 // 16,)),
         ],
-        compiler_params=pltpu.CompilerParams(vmem_limit_bytes=DOWN1_VMEM_BYTES),
+        compiler_params=params(),
         cost_estimate=cost(4e-6),
-    )(volume.reshape(C0, 2, half, -1), jnp.swapaxes(w_down1, 1, 2), b_down1[None], tissue.transpose(1, 2, 0))
-
-    t1a = banded(w_conv1a, 4, C1)
+    )(volume.reshape(C0, 2, half, -1), jnp.swapaxes(w_down1, 1, 2), b_down1[None], tissue.transpose(1, 2, 0), t1a)
+
     t2a = banded(w_conv2a, 2, CP)
     t2b = banded(w_conv2b, 2, CP)
     bias1a = b_conv1a[None]
 
-    y_below, y_above = trade(first, second, "gy")
+    y_below, y_above = shift_along(own[:HALO], own[Y1 - HALO :], "gy")
     win = jnp.concatenate([y_below, own, y_above], axis=0)
     z_below, z_above = shift_along(win[:, :, :128], win[:, :, lanes1 - 128 :], "gz")
+    x_below, x_above = shift_along(win[:, :HALO], win[:, X1 - HALO :], "gx")
     rows = Y1 + 2
     left, right, g2, t1b = pl.pallas_call(
         middle_kernel,
@@ -421,9 +407,13 @@
         cost_estimate=cost(3e-6),
     )(win, t1a, bias1a, tab1, w_conv1b)
 
+    corner = jnp.concatenate([x_below, x_above], axis=1)
+    corner, z_below, z_above, g2 = lax.optimization_barrier((corner, z_below, z_above, g2))
+    corner_below, corner_above = shift_along(corner[:, :, :128], corner[:, :, lanes1 - 128 :], "gz")
+    x_below = jnp.concatenate([corner_below[:, :HALO], x_below, corner_above[:, :HALO]], axis=2)
+    x_above = jnp.concatenate([corner_below[:, HALO:], x_above, corner_above[:, HALO:]], axis=2)
     low = jnp.concatenate([z_below[:, :2], win[:, :2], z_above[:, :2]], axis=2)
     high = jnp.concatenate([z_below[:, X1 - 2 :], win[:, X1 - 2 :], z_above[:, X1 - 2 :]], axis=2)
-    x_below, x_above = shift_along(low, high, "gx")
     g1, g3 = pl.pallas_call(
         outer_kernel,
         out_shape=[shaped(rows, X1, 256), shaped(rows, X1, 128)],

time: 46.4 us -> 46.5 us (level)
  Pallas kernels: 22.6 us -> 19.1 us
  local copies, waits for them, and re-layouts: 0.43 us -> 3.51 us
  starting transfers between devices: 14 us -> 14.8 us
  other arithmetic: 1.59 us -> 1.06 us
    pallas_call x1, Pallas kernels: 5.62 us -> 2.3 us  [local(): pl.pallas_call(down1_kernel, in_specs=[pl.BlockSpec(memory_space=pltpu.VM...]
    unnamed x26 -> x28, local copies, waits for them, and re-layouts: 0.28 us -> 3.39 us
    ppermute x6 -> x7, starting transfers between devices: 13.3 us -> 14.1 us  [trade(): one = lax.ppermute(first, axis, [(i, i ^ 1) for i in range(count)])]
    select_n x4 -> x5, other arithmetic: 0.95 us -> 0.19 us  [trade(): below = jnp.where(index > 0, jnp.where(even, two, one), jnp.zeros_like(one))]
    ppermute x6 -> x7, waiting for transfers between devices: 6.64 us -> 6.75 us  [trade(): one = lax.ppermute(first, axis, [(i, i ^ 1) for i in range(count)])]
  transfers between devices with their start and end apart: 10 -> 12, of which waited for: 6 -> 5; matrix products, arithmetic and copies ran while one was open for 0% -> 1% of each run, Pallas kernels for 17% -> 15%
where the time goes in v7:
time: 46.5 us; the launch traced here: 46.3 us
  Pallas kernels  19.1 us (41%)
  starting transfers between devices  14.8 us (32%)
  waiting for transfers between devices  6.77 us (15%)
  local copies, waits for them, and re-layouts  3.51 us (8%)
  other arithmetic  1.06 us (2%)
  between operations  1.04 us (2%)
    ppermute x7, starting transfers between devices, trade(): one = lax.ppermute(first, axis, [(i, i ^ 1) for i in range(count)])  14.1 us
    ppermute x7, waiting for transfers between devices, trade(): one = lax.ppermute(first, axis, [(i, i ^ 1) for i in range(count)])  6.75 us
    pallas_call x1, Pallas kernels, local(): pl.pallas_call(level_one_kernel, out_shape=[shaped(Y1 * X1, lanes1), shap...  5.36 us
    pallas_call x1, Pallas kernels, local(): pl.pallas_call(level_two_kernel, out_shape=shaped(C2 * Z2, Y2 * X2), scra...  4.03 us
    unnamed x28, local copies, waits for them, and re-layouts  3.39 us
    pallas_call x1, Pallas kernels, local(): pl.pallas_call(down1_kernel, in_specs=[pl.BlockSpec(memory_space=pltpu.VM...  2.3 us
    pallas_call x1, Pallas kernels, local(): pl.pallas_call(outer_kernel, out_shape=[shaped(rows, X1, 256), shaped(row...  2.15 us
    pallas_call x1, Pallas kernels, local(): pl.pallas_call(middle_kernel, out_shape=[shaped(ROWS1, X1, lanes1), shape...  1.72 us
  transfers between devices with their start and end apart: 12, of which 5 were waited for; matrix products, arithmetic and copies ran while one was open for 1% of the time, Pallas kernels for 15%

profile of v7, /device:TPU:0, one launch (start us, length us, event | category | flops | bytes accessed | tf_op | source)
XLA Modules:
  0.0 46.3 jit_solution(2281661410027332384)
XLA Ops:
  0.7 1.0 %copy-done.3 = bf16[27,64,64]{2,1,0:T(8,128)(2,1)S(1)} copy-done((bf16[27,64,64]{2,1,0:T(8,128)(2,1)S(1)}, bf16[27,64,64]{2,1,0:T(8,128)(2,1)}, u32[]{:S(2)}) %copy-start.3) | copy-done | bytes 221208
  1.7 0.6 %shard_map.149.order_ref.t_ref.ta_ref = bf16[3,256,1152]{2,1,0:T(8,128)(2,1)S(1)} custom-call(bf16[27,64,64]{2,1,0:T(8,128)(2,1)S(1)} %copy-done.3), custom_call_target="tpu_custom_call" | custom-call | flops 1000000000 | tf_op jit(solution)/shard_map/pallas_call | solution.py:150
  2.3 0.2 copy-done.5
  2.6 1.9 %copy-done = bf16[48,16,2048]{2,1,0:T(8,128)(2,1)S(1)} copy-done((bf16[48,16,2048]{2,1,0:T(8,128)(2,1)S(1)}, bf16[48,16,2048]{2,1,0:T(8,128)(2,1)}, u32[]{:S(2)}) %copy-start) | copy-done | bytes 3145752
  4.5 2.3 %shard_map.150 = (bf16[16,32,512]{2,1,0:T(8,128)(2,1)S(1)}, bf16[128,384]{1,0:T(8,128)(2,1)S(1)}, bf16[128,384]{1,0:T(8,128)(2,1)S(1)}) custom-call(bf16[48,2,8,2048]{3,2,1,0:T(8,128)(2,1)S(1)} %bitcast.17, bf16[8,48,64]{2,1,0:T(8,128)(2,1)S(1)} %bitcast.18, f32[1,64]{1,0:T(1,128)S(1)} %bitcast.20, s32[8,4,32]{2,1,0:T(4,128)S(1)} %bitcast.19, ...), custom_call_target="tpu_custom_call" | custom-call | flops 4000000000 | tf_op jit(solution)/shard_map/pallas_call | solution.py:382
  6.8 0.5 %collective-permute-start = (bf16[2,32,512]{2,1,0:T(8,128)(2,1)S(1)}, bf16[2,32,512]{2,1,0:T(8,128)(2,1)S(1)}, u32[]{:S(2)}, u32[]{:S(2)}) collective-permute-start(bf16[2,32,512]{2,1,0:T(8,128)(2,1)S(1)} %slice_select_fusion), channel_id=1, source_target_pairs={{0,4},{4,0},{1,5},{5,1},{2,6},{6,2},{3,7},{7,3},{8,12},{12,8},{9,1... | collective-permute-start | bytes 196616 | tf_op jit(solution)/shard_map/ppermute | solution.py:339
  7.4 0.3 shard_map.155.t_ref.ta_ref
  7.7 0.5 %collective-permute-done = bf16[2,32,512]{2,1,0:T(8,128)(2,1)S(1)} collective-permute-done((bf16[2,32,512]{2,1,0:T(8,128)(2,1)S(1)}, bf16[2,32,512]{2,1,0:T(8,128)(2,1)S(1)}, u32[]{:S(2)}, u32[]{:S(2)}) %collective-permute-start) | collective-permute-done | bytes 65568 | tf_op jit(solution)/shard_map/ppermute | solution.py:339
  8.3 0.1 fusion
  8.5 0.4 collective-permute-start.1
  8.9 4.0 %collective-permute-start.2 = (bf16[20,2,512]{2,1,0:T(2,128)(2,1)S(1)}, bf16[20,2,512]{2,1,0:T(2,128)(2,1)S(1)}, u32[]{:S(2)}, u32[]{:S(2)}) collective-permute-start(bf16[20,2,512]{2,1,0:T(2,128)(2,1)S(1)} %get-tuple-element.49), channel_id=1, source_target_pairs={{0,8},{8,0},{16,24},{24,16},{1,9},{9,1},{17,25},{25,17},{2,10},{10... | collective-permute-start | bytes 122888 | tf_op jit(solution)/shard_map/ppermute | solution.py:339
  12.9 1.6 %collective-permute-start.4 = (bf16[20,32,128]{2,1,0:T(8,128)(2,1)S(1)}, bf16[20,32,128]{2,1,0:T(8,128)(2,1)S(1)}, u32[]{:S(2)}, u32[]{:S(2)}) collective-permute-start(bf16[20,32,128]{2,1,0:T(8,128)(2,1)S(1)} %get-tuple-element.51), channel_id=1, source_target_pairs={{0,1},{1,0},{2,3},{3,2},{4,5},{5,4},{6,7},{7,6},{8,9},{9,8},{10,11... | collective-permute-start | bytes 491528 | tf_op jit(solution)/shard_map/ppermute | solution.py:339
  14.5 1.7 %shard_map.151 = (bf16[20,32,512]{2,1,0:T(8,128)(2,1)S(1)}, bf16[20,32,512]{2,1,0:T(8,128)(2,1)S(1)}, bf16[18,32,256]{2,1,0:T(8,128)(2,1)S(1)}, bf16[3,256,1152]{2,1,0:T(8,128)(2,1)S(1)}) custom-call(bf16[20,32,512]{2,1,0:T(8,128)(2,1)S(1)} %pad_maximum_fusion.win_ref, bf16[3,256,1152]{2,1,0:T(8,128)(2,1)S(1)} %shard_map.149.order_ref.t_ref.ta_ref, ...), custom_call_target="tpu_custom_call" | custom-call | flops 3000000000 | tf_op jit(solution)/shard_map/pallas_call | solution.py:403
  16.4 0.1 pad_maximum_fusion.2
  16.5 2.2 %collective-permute-done.4 = bf16[20,32,128]{2,1,0:T(8,128)(2,1)S(1)} collective-permute-done((bf16[20,32,128]{2,1,0:T(8,128)(2,1)S(1)}, bf16[20,32,128]{2,1,0:T(8,128)(2,1)S(1)}, u32[]{:S(2)}, u32[]{:S(2)}) %collective-permute-start.4) | collective-permute-done | bytes 163872 | tf_op jit(solution)/shard_map/ppermute | solution.py:339
  18.8 4.4 %collective-permute-start.6 = (bf16[20,4,128]{2,1,0:T(4,128)(2,1)S(1)}, bf16[20,4,128]{2,1,0:T(4,128)(2,1)S(1)}, u32[]{:S(2)}, u32[]{:S(2)}) collective-permute-start(bf16[20,4,128]{2,1,0:T(4,128)(2,1)S(1)} %get-tuple-element.64), channel_id=1, source_target_pairs={{0,1},{1,0},{2,3},{3,2},{4,5},{5,4},{6,7},{7,6},{8,9},{9,8},{10,11... | collective-permute-start | bytes 61448 | tf_op jit(solution)/shard_map/ppermute | solution.py:339
  23.3 2.2 %shard_map.152 = (bf16[18,32,256]{2,1,0:T(8,128)(2,1)S(1)}, bf16[18,32,128]{2,1,0:T(8,128)(2,1)S(1)}) custom-call(bf16[20,32,512]{2,1,0:T(8,128)(2,1)S(1)} %pad_maximum_fusion.win_ref, bf16[20,32,512]{2,1,0:T(8,128)(2,1)S(1)} %get-tuple-element.29.left_ref, bf16[20,32,512]{2,1,0:T(8,128)(2,1)S(1)} %get-tuple-element.30.right_ref, ...), custom_call_target="tpu_custom_call" | custom-call | flops 4000000000 | tf_op jit(solution)/shard_map/pallas_call | solution.py:417
  25.5 0.1 pad_maximum_fusion.4
  25.7 0.1 pad_maximum_fusion.3
  25.8 5.4 %shard_map.153 = (bf16[512,512]{1,0:T(8,128)(2,1)S(1)}, bf16[8,16,512]{2,1,0:T(8,128)(2,1)S(1)}) custom-call(bf16[20,2,768]{2,1,0:T(2,128)(2,1)S(1)} %get-tuple-element.81.xl_ref, bf16[20,2,768]{2,1,0:T(2,128)(2,1)S(1)} %get-tuple-element.79.low_ref, bf16[20,2,768]{2,1,0:T(2,128)(2,1)S(1)} %get-tuple-element.80.high_ref, ...), custom_call_target="tpu_custom_call" | custom-call | flops 6000000000 | tf_op jit(solution)/shard_map/pallas_call | solution.py:425
  31.3 0.3 shard_map.157.tb_ref
  31.6 0.2 copy-done.12
  31.9 0.6 %collective-permute-done.7 = bf16[2,16,512]{2,1,0:T(8,128)(2,1)S(1)} collective-permute-done((bf16[2,16,512]{2,1,0:T(8,128)(2,1)S(1)}, bf16[2,16,512]{2,1,0:T(8,128)(2,1)S(1)}, u32[]{:S(2)}, u32[]{:S(2)}) %collective-permute-start.7) | collective-permute-done | bytes 32800 | tf_op jit(solution)/shard_map/ppermute | solution.py:339
  32.6 0.2 collective-permute-start.8
  32.8 2.0 %collective-permute-start.9 = (bf16[12,2,512]{2,1,0:T(2,128)(2,1)S(1)}, bf16[12,2,512]{2,1,0:T(2,128)(2,1)S(1)}, u32[]{:S(2)}, u32[]{:S(2)}) collective-permute-start(bf16[12,2,512]{2,1,0:T(2,128)(2,1)S(1)} %bitcast.28), channel_id=1, source_target_pairs={{0,8},{8,0},{16,24},{24,16},{1,9},{9,1},{17,25},{25,17},{2,10},{10... | collective-permute-start | bytes 73736 | tf_op jit(solution)/shard_map/ppermute | solution.py:339
  34.8 1.3 %shard_map.154 = bf16[512,512]{1,0:T(8,128)(2,1)} custom-call(bf16[512,512]{1,0:T(8,128)(2,1)S(1)} %get-tuple-element.36.feat_ref), custom_call_target="tpu_custom_call" | custom-call | flops 2000000000 | tf_op jit(solution)/shard_map/pallas_call | solution.py:438
  36.0 0.8 %collective-permute-done.9 = bf16[12,2,512]{2,1,0:T(2,128)(2,1)S(1)} collective-permute-done((bf16[12,2,512]{2,1,0:T(2,128)(2,1)S(1)}, bf16[12,2,512]{2,1,0:T(2,128)(2,1)S(1)}, u32[]{:S(2)}, u32[]{:S(2)}) %collective-permute-start.9) | collective-permute-done | bytes 24608 | tf_op jit(solution)/shard_map/ppermute | solution.py:339
  36.9 0.1 pad_maximum_fusion.1.wide_ref
  37.0 1.5 %collective-permute-start.11 = (bf16[12,20,256]{2,1,0:T(8,128)(2,1)S(1)}, bf16[12,20,256]{2,1,0:T(8,128)(2,1)S(1)}, u32[]{:S(2)}, u32[]{:S(2)}) collective-permute-start(bf16[12,20,256]{2,1,0:T(8,128)(2,1)S(1)} %get-tuple-element.57), channel_id=1, source_target_pairs={{0,1},{1,0},{2,3},{3,2},{4,5},{5,4},{6,7},{7,6},{8,9},{9,8},{10,11... | collective-permute-start | bytes 368648 | tf_op jit(solution)/shard_map/ppermute | solution.py:339
  38.5 1.0 %shard_map.156 = (bf16[12,32,512]{2,1,0:T(8,128)(2,1)S(1)}, bf16[12,32,512]{2,1,0:T(8,128)(2,1)S(1)}, bf16[12,32,512]{2,1,0:T(8,128)(2,1)S(1)}, bf16[10,16,256]{...) custom-call(bf16[12,20,512]{2,1,0:T(8,128)(2,1)S(1)} %pad_maximum_fusion.1.wide_ref, ...), custom_call_target="tpu_custom_call" | custom-call | flops 3000000000 | tf_op jit(solution)/shard_map/pallas_call | solution.py:449
  39.6 2.7 %collective-permute-done.11 = bf16[12,20,256]{2,1,0:T(8,128)(2,1)S(1)} collective-permute-done((bf16[12,20,256]{2,1,0:T(8,128)(2,1)S(1)}, bf16[12,20,256]{2,1,0:T(8,128)(2,1)S(1)}, u32[]{:S(2)}, u32[]{:S(2)}) %collective-permute-start.11) | collective-permute-done | bytes 122912 | tf_op jit(solution)/shard_map/ppermute | solution.py:339
  42.3 4.0 %shard_map.158 = bf16[384,128]{1,0:T(8,128)(2,1)} custom-call(bf16[12,32,512]{2,1,0:T(8,128)(2,1)S(1)} %get-tuple-element.38.a0, bf16[12,32,512]{2,1,0:T(8,128)(2,1)S(1)} %get-tuple-element.39.a1, bf16[12,32,512]{2,1,0:T(8,128)(2,1)S(1)} %get-tuple-element.40.a2, bf16[10,16,256]{2,1,0:T(8,128)(2,1)S(1)} %get-tuple-element.41.m0, ...), custom_call_target="tpu_custom_call" | custom-call | flops 5000000000 | tf_op jit(solution)/shard_map/pallas_call | solution.py:455
  (58 shorter events, 0.8 us)
Async XLA Ops:
  0.6 1.7 %copy-start.7 = (f32[64]{0:T(128)S(1)}, f32[64]{0:T(128)}, u32[]{:S(2)}) copy-start(f32[64]{0:T(128)} %param.17) | copy-start | bytes 772
  0.6 1.7 %copy-start.6 = (s32[32,8,4]{0,2,1:T(4,128)S(1)}, s32[32,8,4]{0,2,1:T(4,128)}, u32[]{:S(2)}) copy-start(s32[32,8,4]{0,2,1:T(4,128)} %param.15) | copy-start | bytes 12292
  0.7 1.0 %copy-start.3 = (bf16[27,64,64]{2,1,0:T(8,128)(2,1)S(1)}, bf16[27,64,64]{2,1,0:T(8,128)(2,1)}, u32[]{:S(2)}) copy-start(bf16[27,64,64]{2,1,0:T(8,128)(2,1)} %w_ref.4) | copy-start | bytes 663556
  1.7 0.9 %copy-start.5 = (bf16[8,64,48]{1,2,0:T(8,128)(2,1)S(1)}, bf16[8,64,48]{1,2,0:T(8,128)(2,1)}, u32[]{:S(2)}) copy-start(bf16[8,64,48]{1,2,0:T(8,128)(2,1)} %param.16) | copy-start | bytes 147460
  2.6 1.9 %copy-start = (bf16[48,16,2048]{2,1,0:T(8,128)(2,1)S(1)}, bf16[48,16,2048]{2,1,0:T(8,128)(2,1)}, u32[]{:S(2)}) copy-start(bf16[48,16,2048]{2,1,0:T(8,128)(2,1)} %param.14) | copy-start | bytes 9437188
  4.5 2.8 %copy-start.10 = (bf16[8,96,64]{1,2,0:T(8,128)(2,1)S(1)}, bf16[8,96,64]{1,2,0:T(8,128)(2,1)}, u32[]{:S(2)}) copy-start(bf16[8,96,64]{1,2,0:T(8,128)(2,1)} %param.22) | copy-start | bytes 294916
  4.5 2.9 %copy-start.11 = (f32[96]{0:T(128)S(1)}, f32[96]{0:T(128)}, u32[]{:S(2)}) copy-start(f32[96]{0:T(128)} %param.23) | copy-start | bytes 1156
  4.5 2.9 %copy-start.1 = (bf16[27,96,96]{2,1,0:T(8,128)(2,1)S(1)}, bf16[27,96,96]{2,1,0:T(8,128)(2,1)}, u32[]{:S(2)}) copy-start(bf16[27,96,96]{2,1,0:T(8,128)(2,1)} %w_ref.6) | copy-start | bytes 1492996
  6.8 1.4 %collective-permute-start = (bf16[2,32,512]{2,1,0:T(8,128)(2,1)S(1)}, bf16[2,32,512]{2,1,0:T(8,128)(2,1)S(1)}, u32[]{:S(2)}, u32[]{:S(2)}) collective-permute-start(bf16[2,32,512]{2,1,0:T(8,128)(2,1)S(1)} %slice_select_fusion), channel_id=1, source_target_pairs={{0,4},{4,0},{1,5},{5,1},{2,6},{6,2},{3,7},{7,3},{8,12},{12,8},{9,1... | collective-permute-start | bytes 196616 | tf_op jit(solution)/shard_map/ppermute | solution.py:339
  7.4 7.1 %copy-start.4 = (bf16[27,64,64]{2,1,0:T(8,128)(2,1)S(1)}, bf16[27,64,64]{2,1,0:T(8,128)(2,1)}, u32[]{:S(2)}) copy-start(bf16[27,64,64]{2,1,0:T(8,128)(2,1)} %w_ref.5) | copy-start | bytes 663556
  7.4 7.1 %copy-start.8 = (f32[64]{0:T(128)S(1)}, f32[64]{0:T(128)}, u32[]{:S(2)}) copy-start(f32[64]{0:T(128)} %param.19) | copy-start | bytes 772
  8.5 7.8 %collective-permute-start.1 = (bf16[20,2,512]{2,1,0:T(2,128)(2,1)S(1)}, bf16[20,2,512]{2,1,0:T(2,128)(2,1)S(1)}, u32[]{:S(2)}, u32[]{:S(2)}) collective-permute-start(bf16[20,2,512]{2,1,0:T(2,128)(2,1)S(1)} %get-tuple-element.48), channel_id=1, source_target_pairs={{0,4},{8,16},{16,8},{24,28},{4,0},{12,20},{20,12},{28,24},{1,5},{9... | collective-permute-start | bytes 122888 | tf_op jit(solution)/shard_map/ppermute | solution.py:346
  8.9 7.4 %collective-permute-start.2 = (bf16[20,2,512]{2,1,0:T(2,128)(2,1)S(1)}, bf16[20,2,512]{2,1,0:T(2,128)(2,1)S(1)}, u32[]{:S(2)}, u32[]{:S(2)}) collective-permute-start(bf16[20,2,512]{2,1,0:T(2,128)(2,1)S(1)} %get-tuple-element.49), channel_id=1, source_target_pairs={{0,8},{8,0},{16,24},{24,16},{1,9},{9,1},{17,25},{25,17},{2,10},{10... | collective-permute-start | bytes 122888 | tf_op jit(solution)/shard_map/ppermute | solution.py:339
  12.9 5.8 %collective-permute-start.4 = (bf16[20,32,128]{2,1,0:T(8,128)(2,1)S(1)}, bf16[20,32,128]{2,1,0:T(8,128)(2,1)S(1)}, u32[]{:S(2)}, u32[]{:S(2)}) collective-permute-start(bf16[20,32,128]{2,1,0:T(8,128)(2,1)S(1)} %get-tuple-element.51), channel_id=1, source_target_pairs={{0,1},{1,0},{2,3},{3,2},{4,5},{5,4},{6,7},{7,6},{8,9},{9,8},{10,11... | collective-permute-start | bytes 491528 | tf_op jit(solution)/shard_map/ppermute | solution.py:339
  14.5 4.1 %collective-permute-start.3 = (bf16[20,32,128]{2,1,0:T(8,128)(2,1)S(1)}, bf16[20,32,128]{2,1,0:T(8,128)(2,1)S(1)}, u32[]{:S(2)}, u32[]{:S(2)}) collective-permute-start(bf16[20,32,128]{2,1,0:T(8,128)(2,1)S(1)} %get-tuple-element.52), channel_id=1, source_target_pairs={{0,4},{1,2},{2,1},{3,7},{4,0},{5,6},{6,5},{7,3},{8,12},{9,10},{10,... | collective-permute-start | bytes 491528 | tf_op jit(solution)/shard_map/ppermute | solution.py:346
  18.7 6.9 %collective-permute-start.5 = (bf16[20,4,128]{2,1,0:T(4,128)(2,1)S(1)}, bf16[20,4,128]{2,1,0:T(4,128)(2,1)S(1)}, u32[]{:S(2)}, u32[]{:S(2)}) collective-permute-start(bf16[20,4,128]{2,1,0:T(4,128)(2,1)S(1)} %get-tuple-element.63), channel_id=1, source_target_pairs={{0,4},{1,2},{2,1},{3,7},{4,0},{5,6},{6,5},{7,3},{8,12},{9,10},{10,... | collective-permute-start | bytes 61448 | tf_op jit(solution)/shard_map/ppermute | solution.py:346
  18.8 6.8 %collective-permute-start.6 = (bf16[20,4,128]{2,1,0:T(4,128)(2,1)S(1)}, bf16[20,4,128]{2,1,0:T(4,128)(2,1)S(1)}, u32[]{:S(2)}, u32[]{:S(2)}) collective-permute-start(bf16[20,4,128]{2,1,0:T(4,128)(2,1)S(1)} %get-tuple-element.64), channel_id=1, source_target_pairs={{0,1},{1,0},{2,3},{3,2},{4,5},{5,4},{6,7},{7,6},{8,9},{9,8},{10,11... | collective-permute-start | bytes 61448 | tf_op jit(solution)/shard_map/ppermute | solution.py:339
  23.3 2.5 %copy-start.9 = (f32[64]{0:T(128)S(1)}, f32[64]{0:T(128)}, u32[]{:S(2)}) copy-start(f32[64]{0:T(128)} %param.21) | copy-start | bytes 772
  25.8 5.5 %copy-start.2 = (bf16[27,96,96]{2,1,0:T(8,128)(2,1)S(1)}, bf16[27,96,96]{2,1,0:T(8,128)(2,1)}, u32[]{:S(2)}) copy-start(bf16[27,96,96]{2,1,0:T(8,128)(2,1)} %w_ref.7) | copy-start | bytes 1492996
  31.2 0.7 %copy-start.12 = (f32[96]{0:T(128)S(1)}, f32[96]{0:T(128)}, u32[]{:S(2)}) copy-start(f32[96]{0:T(128)} %param.25) | copy-start | bytes 1156
  31.2 0.7 %copy-start.13 = (f32[96]{0:T(128)S(1)}, f32[96]{0:T(128)}, u32[]{:S(2)}) copy-start(f32[96]{0:T(128)} %param.27) | copy-start | bytes 1156
  31.2 1.3 %collective-permute-start.7 = (bf16[2,16,512]{2,1,0:T(8,128)(2,1)S(1)}, bf16[2,16,512]{2,1,0:T(8,128)(2,1)S(1)}, u32[]{:S(2)}, u32[]{:S(2)}) collective-permute-start(bf16[2,16,512]{2,1,0:T(8,128)(2,1)S(1)} %slice_select_fusion.1), channel_id=1, source_target_pairs={{0,4},{4,0},{1,5},{5,1},{2,6},{6,2},{3,7},{7,3},{8,12},{12,8},{9,1... | collective-permute-start | bytes 98312 | tf_op jit(solution)/shard_map/ppermute | solution.py:339
  32.6 3.5 %collective-permute-start.8 = (bf16[12,2,512]{2,1,0:T(2,128)(2,1)S(1)}, bf16[12,2,512]{2,1,0:T(2,128)(2,1)S(1)}, u32[]{:S(2)}, u32[]{:S(2)}) collective-permute-start(bf16[12,2,512]{2,1,0:T(2,128)(2,1)S(1)} %get-tuple-element.44), channel_id=1, source_target_pairs={{0,4},{8,16},{16,8},{24,28},{4,0},{12,20},{20,12},{28,24},{1,5},{9... | collective-permute-start | bytes 73736 | tf_op jit(solution)/shard_map/ppermute | solution.py:346
  32.8 4.0 %collective-permute-start.9 = (bf16[12,2,512]{2,1,0:T(2,128)(2,1)S(1)}, bf16[12,2,512]{2,1,0:T(2,128)(2,1)S(1)}, u32[]{:S(2)}, u32[]{:S(2)}) collective-permute-start(bf16[12,2,512]{2,1,0:T(2,128)(2,1)S(1)} %bitcast.28), channel_id=1, source_target_pairs={{0,8},{8,0},{16,24},{24,16},{1,9},{9,1},{17,25},{25,17},{2,10},{10... | collective-permute-start | bytes 73736 | tf_op jit(solution)/shard_map/ppermute | solution.py:339
  37.0 5.2 %collective-permute-start.11 = (bf16[12,20,256]{2,1,0:T(8,128)(2,1)S(1)}, bf16[12,20,256]{2,1,0:T(8,128)(2,1)S(1)}, u32[]{:S(2)}, u32[]{:S(2)}) collective-permute-start(bf16[12,20,256]{2,1,0:T(8,128)(2,1)S(1)} %get-tuple-element.57), channel_id=1, source_target_pairs={{0,1},{1,0},{2,3},{3,2},{4,5},{5,4},{6,7},{7,6},{8,9},{9,8},{10,11... | collective-permute-start | bytes 368648 | tf_op jit(solution)/shard_map/ppermute | solution.py:339
  38.5 3.7 %collective-permute-start.10 = (bf16[12,20,256]{2,1,0:T(8,128)(2,1)S(1)}, bf16[12,20,256]{2,1,0:T(8,128)(2,1)S(1)}, u32[]{:S(2)}, u32[]{:S(2)}) collective-permute-start(bf16[12,20,256]{2,1,0:T(8,128)(2,1)S(1)} %get-tuple-element.58), channel_id=1, source_target_pairs={{0,4},{1,2},{2,1},{3,7},{4,0},{5,6},{6,5},{7,3},{8,12},{9,10},{10,... | collective-permute-start | bytes 368648 | tf_op jit(solution)/shard_map/ppermute | solution.py:346

commit v8 on v7

--- a/solution.py
+++ b/solution.py
@@ -18,7 +18,10 @@
 C2 = 96
 CP = 128
 HALO = 2
-XB = 10
+HALO_X = 6
+HALO_X2 = 2
+XB = 12
+XB_BELOW = 2
 XB_PITCH = 16
 YB = 6
 ROWS1 = Y1 + 2 * HALO
@@ -53,7 +56,7 @@
     bits = cell.bit_length() - 1
     shape = (rows, pitch, 128)
     y_block = (iota(shape, 0) + (y_start + cell)) >> bits
-    x_block = jnp.minimum((x_of(iota(shape, 1)) + cell) >> bits, XB - 1)
+    x_block = jnp.minimum((x_of(iota(shape, 1)) + XB_BELOW * cell) >> bits, XB - 1)
     hit = one_hot(y_block * XB_PITCH + x_block == iota(shape, 2)).reshape(rows * pitch, 128)
     return mm(hit, tab)
 
@@ -71,7 +74,7 @@
     hot_y = one_hot(lax.axis_index("gy") * 4 - 1 + (block >> bits) == iota((128, n_y), 1))
     block = iota((128, 3 * n_x), 0)
     layer = sum((iota((128, 3 * n_x), 1) >= k * n_x).astype(jnp.int32) for k in (1, 2))
-    hot_x = lax.axis_index("gx") * 8 - 1 + (block & (XB_PITCH - 1)) == iota((128, 3 * n_x), 1) - layer * n_x
+    hot_x = lax.axis_index("gx") * 8 - XB_BELOW + (block & (XB_PITCH - 1)) == iota((128, 3 * n_x), 1) - layer * n_x
     rows = jnp.where(hot_x, mm(hot_y, jnp.concatenate(layers, axis=1).astype(BF)), 0.0).astype(BF)
     shape = (3 * n_x, 384)
     layer = sum((iota(shape, 0) >= k * n_x).astype(jnp.int32) for k in (1, 2))
@@ -84,14 +87,27 @@
     return spread(64, 320), spread(128, 256)
 
 
-def down1_kernel(v_ref, w_ref, b_ref, t_ref, order_ref, out_ref, tab_ref, tab2_ref, wd_ref, cells_ref):
-    del order_ref
+def down1_kernel(
+    v_hbm, wd_hbm, b_hbm, t_hbm, wa_hbm, out_ref, ta_ref, tab_ref, tab2_ref,
+    v_ref, w_ref, b_ref, t_ref, wa_ref, wd_ref, cells_ref, sems,
+):
     half = v_ref.shape[2]
     kz = C0 * half
     lanes = Z1 // 2 * C1
+    small = ((t_hbm, t_ref), (wd_hbm, w_ref), (b_hbm, b_ref), (wa_hbm, wa_ref))
+    copies = [pltpu.make_async_copy(src, dst, sems.at[n]) for n, (src, dst) in enumerate(small)]
+    for n in range(C0 // 16):
+        cut = slice(n * 16, n * 16 + 16)
+        copies.append(pltpu.make_async_copy(v_hbm.at[cut], v_ref.at[cut], sems.at[len(small) + n]))
+    for copy in copies:
+        copy.start()
+
+    copies[0].wait()
     tab, tab2 = tissue_tables(t_ref)
     tab_ref[...] = tab
     tab2_ref[...] = tab2
+    copies[1].wait()
+    copies[2].wait()
     r = iota((kz, 2 * C0), 0)
     l = iota((kz, 2 * C0), 1)
     odd = l >= C0
@@ -102,11 +118,14 @@
         wide = jnp.concatenate([pair] * (Z1 // 2), axis=1)
         wd_ref[ab * kz : (ab + 1) * kz, :] = jnp.where(keep, mm(spread, wide), 0.0).astype(BF)
 
+    copies[3].wait()
+    fill_banded(wa_ref, ta_ref, 4, C1)
     r = iota((4 * CX, 128), 0)
     select = one_hot_rows(((r & 32) << 2) | (r & 64) | ((r & 31) << 1) | (r >> 7), 4 * CX)
     part = 16 * half
     part = 16 * half
-    for n in range(C0 // 16):
+    for n, copy in enumerate(copies[4:]):
+        copy.wait()
         for m in range(v_ref.shape[3] // 256):
             v = [v_ref[n * 16 : n * 16 + 16, h, :, m * 256 : m * 256 + 256].reshape(part, 256) for h in range(2)]
             cells = mm(select, jnp.concatenate(v, axis=0), NT).astype(BF)
@@ -215,17 +234,17 @@
         used = sum(p.shape[1] for p in line)
         for i, copy in enumerate(copies):
             moved = [line[0][:, i:]] + line[1:] if i < line[0].shape[1] else line[1:]
-            spare = jnp.zeros((rows, pitch - used + i, 128), BF)
-            copy[:, :, lane : lane + 128] = jnp.concatenate(moved + [spare], axis=1)
+            spare = [jnp.zeros((rows, pitch - used + i, 128), BF)] if pitch - used + i else []
+            copy[:, :, lane : lane + 128] = jnp.concatenate(moved + spare, axis=1)
 
 
 def level_one_kernel(
     xl_ref, low_ref, high_ref, xr_ref, g1_ref, g2_ref, g3_ref, ta_ref, tb_ref, ba_ref, bb_ref, wd_ref, bd_ref, tab_ref, tab2_ref,
-    feat_ref, down_ref, e0, e1, e2, i0, i1, i2, d_ref,
+    feat_ref, down_ref, e0, e1, e2, i0, i1, i2, side_ref, d_ref,
 ):
     fill_edges((e0, e1, e2), (xl_ref, low_ref, high_ref, xr_ref))
     rows = Y1 + 2
-    mask = mask_rows(tab_ref[...], -1, rows, EDGE, lambda r: jnp.where(r < 4, r - 1, r + X1 - 5), 4)
+    mask = mask_rows(tab_ref[...], -1, rows, EDGE, lambda r: jnp.where(r < 8, r - 5, r + X1 - 9), 4)
     for g, (lane, width, out) in enumerate(((0, 384, 256), (256, 384, 256), (512, 256, 128))):
         acc = conv_group([[(e, lane, width)] for e in (e0, e1, e2)], ta_ref, 0, rows, out, 384)
         for q in range(out // 128):
@@ -234,16 +253,24 @@
             edge = finish(acc[:, q * 128 : q * 128 + 128], twice(ba_ref), mask[:, which * 128 : which * 128 + 128], rows)
             inner = (g1_ref, g2_ref, g3_ref)[g][:, :, q * 128 : q * 128 + 128][:, 1:-1]
             cut = slice(chunk * 128, chunk * 128 + 128)
-            i0[:, :, cut] = jnp.concatenate([edge[:, 0:2], inner], axis=1)
-            i1[:, :, cut] = jnp.concatenate([edge[:, 1:2], inner, edge[:, 4:5]], axis=1)
-            i2[:, :, cut] = jnp.concatenate([inner, edge[:, 4:6]], axis=1)
-
-    mask = mask_rows(tab_ref[:, 128:256], 0, Y1, X1, lambda x: x, 4)
+            i0[:, :X1, cut] = jnp.concatenate([edge[:, 4:6], inner], axis=1)
+            i1[:, :X1, cut] = jnp.concatenate([edge[:, 5:6], inner, edge[:, 8:9]], axis=1)
+            i2[:, :X1, cut] = jnp.concatenate([inner, edge[:, 8:10]], axis=1)
+            i0[:, X1:, cut] = edge
+            for i, copy in ((1, i1), (2, i2)):
+                copy[:, X1:, cut] = jnp.concatenate([edge[:, i:], jnp.zeros((rows, i, 128), BF)], axis=1)
+
+    def cell_of(r):
+        return jnp.where(r < X1, r, jnp.where(r < X1 + 8, r - X1 - 4, r - 8))
+
+    mask = mask_rows(tab_ref[:, 128:256], 0, Y1, X1 + EDGE, cell_of, 4)
     for g in range(2):
         acc = conv_group([[(ref, 256 * g, 384)] for ref in (i0, i1, i2)], tb_ref, 0, Y1, 256, 384)
         for q in range(2):
-            value = jnp.maximum(acc[:, q * 128 : q * 128 + 128] + twice(bb_ref), 0.0) * mask
-            feat_ref[:, (2 * g + q) * 128 : (2 * g + q + 1) * 128] = value.astype(BF)
+            value = finish(acc[:, q * 128 : q * 128 + 128], twice(bb_ref), mask, Y1)
+            cut = slice((2 * g + q) * 128, (2 * g + q + 1) * 128)
+            feat_ref[:, cut] = value[:, :X1].reshape(Y1 * X1, 128)
+            side_ref[:, cut] = value[:, X1:].reshape(Y1 * EDGE, 128)
 
     size = 8 * X1
     quarter = size // 4
@@ -253,10 +280,18 @@
         cells = mm(select, feat_ref[n * size : n * size + size, :]).astype(BF)
         for q in range(4):
             d_ref[q, n * quarter : n * quarter + quarter, :] = cells[q * quarter : (q + 1) * quarter]
-    mask = mask_rows(tab2_ref[:, 128:256], 0, Y2, X2, lambda x: x, 2)
+    select = one_hot_rows(((r & 56) << 2) | ((r & 64) >> 2) | ((r & 7) << 1) | (r >> 7), size)
+    cells = mm(select, side_ref[...]).astype(BF)
+    for q in range(4):
+        d_ref[q, Y2 * X2 :, :] = cells[q * quarter : (q + 1) * quarter]
+    inner_mask = mask_rows(tab2_ref[:, 128:256], 0, Y2, X2, lambda x: x, 2)
+    side_mask = mask_rows(tab2_ref[:, 128:256], 0, Y2, EDGE // 2, lambda r: jnp.where(r < 4, r - 2, r + X2 - 4), 2)
     for z in range(Z2):
         left = jnp.concatenate([d_ref[q, :, z * 128 : z * 128 + 128] for q in range(4)], axis=1)
-        down_ref[:, :, z * CP : z * CP + CP] = finish(mm(left, wd_ref[...]), bd_ref[...], mask, Y2)
+        acc = mm(left, wd_ref[...])
+        inner = finish(acc[: Y2 * X2], bd_ref[...], inner_mask, Y2)
+        side = finish(acc[Y2 * X2 :], bd_ref[...], side_mask, Y2)
+        down_ref[:, :, z * CP : z * CP + CP] = jnp.concatenate([side[:, 0:2], inner, side[:, 4:6]], axis=1)
 
 
 def one_kernel(feat_ref, out_ref):
@@ -378,18 +413,21 @@
     kz = C0 * depth
     lanes1 = Z1 * C1
     half = depth // 2
-    t1a = banded(w_conv1a, 4, C1)
-    own, tab1, tab2 = pl.pallas_call(
+    operands = [volume.reshape(C0, 2, half, -1), jnp.swapaxes(w_down1, 1, 2), b_down1[None], tissue.transpose(1, 2, 0), w_conv1a]
+    operands = [pltpu.with_memory_space_constraint(x, pltpu.HBM) for x in operands]
+    own, t1a, tab1, tab2 = pl.pallas_call(
         down1_kernel,
-        in_specs=[pl.BlockSpec(memory_space=pltpu.VMEM)] * 4 + [pl.BlockSpec(memory_space=pl.ANY)],
-        out_shape=[shaped(Y1, X1, lanes1), shaped(128, 384), shaped(128, 384)],
-        scratch_shapes=[
+        in_specs=[pl.BlockSpec(memory_space=pltpu.HBM)] * 5,
+        out_shape=[shaped(Y1, X1, lanes1), banded_shape(4, C1), shaped(128, 384), shaped(128, 384)],
+        scratch_shapes=[pltpu.VMEM(x.shape, x.dtype) for x in operands]
+        + [
             pltpu.VMEM((2 * kz, lanes1 // 2), BF),
             pltpu.VMEM((2, Y1 * X1, 2 * kz), BF),
+            pltpu.SemaphoreType.DMA((4 + C0 // 16,)),
         ],
         compiler_params=params(),
         cost_estimate=cost(4e-6),
-    )(volume.reshape(C0, 2, half, -1), jnp.swapaxes(w_down1, 1, 2), b_down1[None], tissue.transpose(1, 2, 0), t1a)
+    )(*operands)
 
     t2a = banded(w_conv2a, 2, CP)
     t2b = banded(w_conv2b, 2, CP)
@@ -398,7 +436,7 @@
     y_below, y_above = shift_along(own[:HALO], own[Y1 - HALO :], "gy")
     win = jnp.concatenate([y_below, own, y_above], axis=0)
     z_below, z_above = shift_along(win[:, :, :128], win[:, :, lanes1 - 128 :], "gz")
-    x_below, x_above = shift_along(win[:, :HALO], win[:, X1 - HALO :], "gx")
+    x_below, x_above = shift_along(win[:, :HALO_X], win[:, X1 - HALO_X :], "gx")
     rows = Y1 + 2
     left, right, g2, t1b = pl.pallas_call(
         middle_kernel,
@@ -410,8 +448,8 @@
     corner = jnp.concatenate([x_below, x_above], axis=1)
     corner, z_below, z_above, g2 = lax.optimization_barrier((corner, z_below, z_above, g2))
     corner_below, corner_above = shift_along(corner[:, :, :128], corner[:, :, lanes1 - 128 :], "gz")
-    x_below = jnp.concatenate([corner_below[:, :HALO], x_below, corner_above[:, :HALO]], axis=2)
-    x_above = jnp.concatenate([corner_below[:, HALO:], x_above, corner_above[:, HALO:]], axis=2)
+    x_below = jnp.concatenate([corner_below[:, :HALO_X], x_below, corner_above[:, :HALO_X]], axis=2)
+    x_above = jnp.concatenate([corner_below[:, HALO_X:], x_above, corner_above[:, HALO_X:]], axis=2)
     low = jnp.concatenate([z_below[:, :2], win[:, :2], z_above[:, :2]], axis=2)
     high = jnp.concatenate([z_below[:, X1 - 2 :], win[:, X1 - 2 :], z_above[:, X1 - 2 :]], axis=2)
     g1, g3 = pl.pallas_call(
@@ -424,10 +462,10 @@
 
     feat, down = pl.pallas_call(
         level_one_kernel,
-        out_shape=[shaped(Y1 * X1, lanes1), shaped(Y2, X2, Z2 * CP)],
+        out_shape=[shaped(Y1 * X1, lanes1), shaped(Y2, X2 + 2 * HALO_X2, Z2 * CP)],
         scratch_shapes=[pltpu.VMEM((ROWS1, EDGE, (Z1 + 4) * C1), BF)] * 3
-        + [pltpu.VMEM((rows, X1, (Z1 + 2) * C1), BF)] * 3
-        + [pltpu.VMEM((4, Y2 * X2, lanes1), BF)],
+        + [pltpu.VMEM((rows, X1 + EDGE, (Z1 + 2) * C1), BF)] * 3
+        + [pltpu.VMEM((Y1 * EDGE, lanes1), BF), pltpu.VMEM((4, Y2 * (X2 + EDGE // 2), lanes1), BF)],
         compiler_params=params(),
         cost_estimate=cost(6e-6),
     )(
@@ -435,14 +473,12 @@
         pad_lanes(jnp.swapaxes(w_down2, 1, 2).reshape(8 * C1, C2)), pad_lanes(b_down2[None]), tab1, tab2,
     )
 
+    y_below, y_above = shift_along(down[:HALO], down[Y2 - HALO :], "gy")
+    wide = jnp.concatenate([y_below, down, y_above], axis=0)
+    feat, wide = lax.optimization_barrier((feat, wide))
     one = pl.pallas_call(
         one_kernel, out_shape=shaped(lanes1, Y1 * X1), compiler_params=params(), cost_estimate=cost(2e-6)
     )(feat)
-
-    y_below, y_above = shift_along(down[:HALO], down[Y2 - HALO :], "gy")
-    win = jnp.concatenate([y_below, down, y_above], axis=0)
-    x_below, x_above = shift_along(win[:, :HALO], win[:, X2 - HALO :], "gx")
-    wide = jnp.concatenate([x_below, win, x_above], axis=1)
     z_below, z_above = shift_along(wide[:, :, : 2 * CP], wide[:, :, 2 * CP :], "gz")
     bias2a = pad_lanes(b_conv2a[None])
     moved = [shaped(Y2 + 2, X2, 2 * CP)] * 3

time: 46.5 us -> 43.8 us (0.942)
  Pallas kernels: 19.1 us -> 22.3 us
  local copies, waits for them, and re-layouts: 3.51 us -> 0.44 us
  starting transfers between devices: 14.8 us -> 11.8 us
  waiting for transfers between devices: 6.77 us -> 7.35 us
    unnamed x28 -> x18, local copies, waits for them, and re-layouts: 3.39 us -> 0.25 us
    ppermute x7 -> x6, starting transfers between devices: 14.1 us -> 11.4 us  [trade(): one = lax.ppermute(first, axis, [(i, i ^ 1) for i in range(count)])]
    pallas_call x1, Pallas kernels: 2.3 us -> 4.75 us  [local(): pl.pallas_call(down1_kernel, in_specs=[pl.BlockSpec(memory_space=pltpu.HB...]
    pallas_call x1, Pallas kernels: 5.36 us -> 6.67 us  [local(): pl.pallas_call(level_one_kernel, out_shape=[shaped(Y1 * X1, lanes1), shap...]
    pallas_call x3 -> x2, Pallas kernels: 1.27 us -> 0.65 us  [banded(): pl.pallas_call(kernel, out_shape=banded_shape(group, pad), compiler_param...]
    ppermute x7 -> x6, waiting for transfers between devices: 6.75 us -> 7.34 us  [trade(): one = lax.ppermute(first, axis, [(i, i ^ 1) for i in range(count)])]
  transfers between devices with their start and end apart: 12 -> 10, of which waited for: 5 -> 5; matrix products, arithmetic and copies ran while one was open for 1% -> 1% of each run, Pallas kernels for 15% -> 16%
where the time goes in v8:
time: 43.8 us; the launch traced here: 43.7 us
  Pallas kernels  22.3 us (51%)
  starting transfers between devices  11.8 us (27%)
  waiting for transfers between devices  7.35 us (17%)
  between operations  1.01 us (2%)
  other arithmetic  0.72 us (2%)
  local copies, waits for them, and re-layouts  0.44 us (1%)
    ppermute x6, starting transfers between devices, trade(): one = lax.ppermute(first, axis, [(i, i ^ 1) for i in range(count)])  11.4 us
    ppermute x6, waiting for transfers between devices, trade(): one = lax.ppermute(first, axis, [(i, i ^ 1) for i in range(count)])  7.34 us
    pallas_call x1, Pallas kernels, local(): pl.pallas_call(level_one_kernel, out_shape=[shaped(Y1 * X1, lanes1), shap...  6.67 us
    pallas_call x1, Pallas kernels, local(): pl.pallas_call(down1_kernel, in_specs=[pl.BlockSpec(memory_space=pltpu.HB...  4.75 us
    pallas_call x1, Pallas kernels, local(): pl.pallas_call(level_two_kernel, out_shape=shaped(C2 * Z2, Y2 * X2), scra...  4.04 us
    pallas_call x1, Pallas kernels, local(): pl.pallas_call(outer_kernel, out_shape=[shaped(rows, X1, 256), shaped(row...  2.16 us
    pallas_call x1, Pallas kernels, local(): pl.pallas_call(middle_kernel, out_shape=[shaped(ROWS1, X1, lanes1), shape...  1.71 us
    pallas_call x1, Pallas kernels, local(): pl.pallas_call(one_kernel, out_shape=shaped(lanes1, Y1 * X1), compiler_pa...  1.27 us
  transfers between devices with their start and end apart: 10, of which 5 were waited for; matrix products, arithmetic and copies ran while one was open for 1% of the time, Pallas kernels for 16%

profile of v8, /device:TPU:0, one launch (start us, length us, event | category | flops | bytes accessed | tf_op | source)
XLA Modules:
  0.0 43.7 jit_solution(5701194469881689120)
XLA Ops:
  0.7 4.8 %shard_map.149 = (bf16[16,32,512]{2,1,0:T(8,128)(2,1)S(1)}, bf16[3,256,1152]{2,1,0:T(8,128)(2,1)S(1)}, bf16[128,384]{1,0:T(8,128)(2,1)S(1)}, bf16[128,384]{1,0:T(8,128)(2,1)S(1)}) custom-call(bf16[48,2,8,2048]{3,2,1,0:T(8,128)(2,1)} %bitcast.19, bf16[8,48,64]{2,1,0:T(8,128)(2,1)} %bitcast.20, f32[1,64]{1,0:T(1,128)} %bitcast.22, s32[8,4,32]{2,1,0:T(4,128)} %bitcast.21, ...), custom_call_target="tpu_custom_call" | custom-call | flops 4000000000 | tf_op jit(solution)/shard_map/pallas_call | solution.py:418
  5.5 0.5 %collective-permute-start = (bf16[2,32,512]{2,1,0:T(8,128)(2,1)S(1)}, bf16[2,32,512]{2,1,0:T(8,128)(2,1)S(1)}, u32[]{:S(2)}, u32[]{:S(2)}) collective-permute-start(bf16[2,32,512]{2,1,0:T(8,128)(2,1)S(1)} %slice_select_fusion), channel_id=1, source_target_pairs={{0,4},{4,0},{1,5},{5,1},{2,6},{6,2},{3,7},{7,3},{8,12},{12,8},{9,1... | collective-permute-start | bytes 196616 | tf_op jit(solution)/shard_map/ppermute | solution.py:374
  6.0 0.0 copy-start.2
  6.0 0.3 shard_map.154.t_ref.ta_ref
  6.4 0.5 %collective-permute-done = bf16[2,32,512]{2,1,0:T(8,128)(2,1)S(1)} collective-permute-done((bf16[2,32,512]{2,1,0:T(8,128)(2,1)S(1)}, bf16[2,32,512]{2,1,0:T(8,128)(2,1)S(1)}, u32[]{:S(2)}, u32[]{:S(2)}) %collective-permute-start) | collective-permute-done | bytes 65568 | tf_op jit(solution)/shard_map/ppermute | solution.py:374
  6.9 0.1 pad_maximum_fusion.win_ref
  6.9 0.1 broadcast_select_fusion.3
  7.0 0.4 collective-permute-start.1
  7.4 4.0 %collective-permute-start.2 = (bf16[20,6,512]{2,1,0:T(8,128)(2,1)S(1)}, bf16[20,6,512]{2,1,0:T(8,128)(2,1)S(1)}, u32[]{:S(2)}, u32[]{:S(2)}) collective-permute-start(bf16[20,6,512]{2,1,0:T(8,128)(2,1)S(1)} %get-tuple-element.55), channel_id=1, source_target_pairs={{0,8},{8,0},{16,24},{24,16},{1,9},{9,1},{17,25},{25,17},{2,10},{10... | collective-permute-start | bytes 368648 | tf_op jit(solution)/shard_map/ppermute | solution.py:374
  11.5 1.6 %collective-permute-start.4 = (bf16[20,32,128]{2,1,0:T(8,128)(2,1)S(1)}, bf16[20,32,128]{2,1,0:T(8,128)(2,1)S(1)}, u32[]{:S(2)}, u32[]{:S(2)}) collective-permute-start(bf16[20,32,128]{2,1,0:T(8,128)(2,1)S(1)} %get-tuple-element.52), channel_id=1, source_target_pairs={{0,1},{1,0},{2,3},{3,2},{4,5},{5,4},{6,7},{7,6},{8,9},{9,8},{10,11... | collective-permute-start | bytes 491528 | tf_op jit(solution)/shard_map/ppermute | solution.py:374
  13.1 1.7 %shard_map.150 = (bf16[20,32,512]{2,1,0:T(8,128)(2,1)S(1)}, bf16[20,32,512]{2,1,0:T(8,128)(2,1)S(1)}, bf16[18,32,256]{2,1,0:T(8,128)(2,1)S(1)}, bf16[3,256,1152]{2,1,0:T(8,128)(2,1)S(1)}) custom-call(bf16[20,32,512]{2,1,0:T(8,128)(2,1)S(1)} %pad_maximum_fusion.win_ref, bf16[3,256,1152]{2,1,0:T(8,128)(2,1)S(1)} %get-tuple-element.27.t_ref.ta_ref, ...), custom_call_target="tpu_custom_call" | custom-call | flops 3000000000 | tf_op jit(solution)/shard_map/pallas_call | solution.py:441
  14.8 0.1 fusion
  14.9 4.3 %collective-permute-done.2 = bf16[20,6,512]{2,1,0:T(8,128)(2,1)S(1)} collective-permute-done((bf16[20,6,512]{2,1,0:T(8,128)(2,1)S(1)}, bf16[20,6,512]{2,1,0:T(8,128)(2,1)S(1)}, u32[]{:S(2)}, u32[]{:S(2)}) %collective-permute-start.2) | collective-permute-done | bytes 122912 | tf_op jit(solution)/shard_map/ppermute | solution.py:374
  19.2 0.1 pad_maximum_fusion.1
  19.4 0.1 collective-permute-start.5
  19.5 3.1 %collective-permute-start.6 = (bf16[20,12,128]{2,1,0:T(8,128)(2,1)S(1)}, bf16[20,12,128]{2,1,0:T(8,128)(2,1)S(1)}, u32[]{:S(2)}, u32[]{:S(2)}) collective-permute-start(bf16[20,12,128]{2,1,0:T(8,128)(2,1)S(1)} %get-tuple-element.57), channel_id=1, source_target_pairs={{0,1},{1,0},{2,3},{3,2},{4,5},{5,4},{6,7},{7,6},{8,9},{9,8},{10,11... | collective-permute-start | bytes 184328 | tf_op jit(solution)/shard_map/ppermute | solution.py:374
  22.7 2.2 %shard_map.151 = (bf16[18,32,256]{2,1,0:T(8,128)(2,1)S(1)}, bf16[18,32,128]{2,1,0:T(8,128)(2,1)S(1)}) custom-call(bf16[20,32,512]{2,1,0:T(8,128)(2,1)S(1)} %pad_maximum_fusion.win_ref, bf16[20,32,512]{2,1,0:T(8,128)(2,1)S(1)} %get-tuple-element.33.left_ref, bf16[20,32,512]{2,1,0:T(8,128)(2,1)S(1)} %get-tuple-element.34.right_ref, ...), custom_call_target="tpu_custom_call" | custom-call | flops 4000000000 | tf_op jit(solution)/shard_map/pallas_call | solution.py:455
  24.8 0.1 pad_maximum_fusion.5.low_ref
  24.9 0.1 pad_maximum_fusion.6.high_ref
  25.0 0.1 collective-permute-done.6
  25.1 0.1 pad_maximum_fusion.3
  25.2 6.7 %shard_map.152 = (bf16[512,512]{1,0:T(8,128)(2,1)S(1)}, bf16[8,20,512]{2,1,0:T(8,128)(2,1)S(1)}) custom-call(bf16[20,6,768]{2,1,0:T(8,128)(2,1)S(1)} %get-tuple-element.80.xl_ref, bf16[20,2,768]{2,1,0:T(2,128)(2,1)S(1)} %pad_maximum_fusion.5.low_ref, bf16[20,2,768]{2,1,0:T(2,128)(2,1)S(1)} %pad_maximum_fusion.6.high_ref, ...), custom_call_target="tpu_custom_call" | custom-call | flops 6000000000 | tf_op jit(solution)/shard_map/pallas_call | solution.py:463
  31.9 0.1 collective-permute-start.7
  32.0 0.3 shard_map.156.tb_ref
  32.4 0.2 copy-done.7
  32.6 0.0 copy-done.8
  32.6 0.7 %collective-permute-done.7 = bf16[2,20,512]{2,1,0:T(8,128)(2,1)S(1)} collective-permute-done((bf16[2,20,512]{2,1,0:T(8,128)(2,1)S(1)}, bf16[2,20,512]{2,1,0:T(8,128)(2,1)S(1)}, u32[]{:S(2)}, u32[]{:S(2)}) %collective-permute-start.7) | collective-permute-done | bytes 40992 | tf_op jit(solution)/shard_map/ppermute | solution.py:374
  33.3 2.1 %collective-permute-start.9 = (bf16[12,20,256]{2,1,0:T(8,128)(2,1)S(1)}, bf16[12,20,256]{2,1,0:T(8,128)(2,1)S(1)}, u32[]{:S(2)}, u32[]{:S(2)}) collective-permute-start(bf16[12,20,256]{2,1,0:T(8,128)(2,1)S(1)} %get-tuple-element.64), channel_id=1, source_target_pairs={{0,1},{1,0},{2,3},{3,2},{4,5},{5,4},{6,7},{7,6},{8,9},{9,8},{10,11... | collective-permute-start | bytes 368648 | tf_op jit(solution)/shard_map/ppermute | solution.py:374
  35.4 1.0 %shard_map.155 = (bf16[12,32,512]{2,1,0:T(8,128)(2,1)S(1)}, bf16[12,32,512]{2,1,0:T(8,128)(2,1)S(1)}, bf16[12,32,512]{2,1,0:T(8,128)(2,1)S(1)}, bf16[10,16,256]{...) custom-call(bf16[12,20,512]{2,1,0:T(8,128)(2,1)S(1)} %pad_maximum_fusion.2.wide_ref, ...), custom_call_target="tpu_custom_call" | custom-call | flops 3000000000 | tf_op jit(solution)/shard_map/pallas_call | solution.py:485
  36.5 1.3 %shard_map.153 = bf16[512,512]{1,0:T(8,128)(2,1)} custom-call(bf16[512,512]{1,0:T(8,128)(2,1)S(1)} %get-tuple-element.42.feat_ref), custom_call_target="tpu_custom_call" | custom-call | flops 2000000000 | tf_op jit(solution)/shard_map/pallas_call | solution.py:479
  37.8 1.8 %collective-permute-done.9 = bf16[12,20,256]{2,1,0:T(8,128)(2,1)S(1)} collective-permute-done((bf16[12,20,256]{2,1,0:T(8,128)(2,1)S(1)}, bf16[12,20,256]{2,1,0:T(8,128)(2,1)S(1)}, u32[]{:S(2)}, u32[]{:S(2)}) %collective-permute-start.9) | collective-permute-done | bytes 122912 | tf_op jit(solution)/shard_map/ppermute | solution.py:374
  39.6 4.0 %shard_map.157 = bf16[384,128]{1,0:T(8,128)(2,1)} custom-call(bf16[12,32,512]{2,1,0:T(8,128)(2,1)S(1)} %get-tuple-element.44.a0, bf16[12,32,512]{2,1,0:T(8,128)(2,1)S(1)} %get-tuple-element.45.a1, bf16[12,32,512]{2,1,0:T(8,128)(2,1)S(1)} %get-tuple-element.46.a2, bf16[10,16,256]{2,1,0:T(8,128)(2,1)S(1)} %get-tuple-element.47.m0, ...), custom_call_target="tpu_custom_call" | custom-call | flops 5000000000 | tf_op jit(solution)/shard_map/pallas_call | solution.py:491
  (41 shorter events, 0.5 us)
Async XLA Ops:
  0.6 5.3 %copy-start.5 = (bf16[8,96,64]{1,2,0:T(8,128)(2,1)S(1)}, bf16[8,96,64]{1,2,0:T(8,128)(2,1)}, u32[]{:S(2)}) copy-start(bf16[8,96,64]{1,2,0:T(8,128)(2,1)} %param.22) | copy-start | bytes 294916
  0.7 5.3 %copy-start.6 = (f32[96]{0:T(128)S(1)}, f32[96]{0:T(128)}, u32[]{:S(2)}) copy-start(f32[96]{0:T(128)} %param.23) | copy-start | bytes 1156
  0.7 5.3 %copy-start = (bf16[27,96,96]{2,1,0:T(8,128)(2,1)S(1)}, bf16[27,96,96]{2,1,0:T(8,128)(2,1)}, u32[]{:S(2)}) copy-start(bf16[27,96,96]{2,1,0:T(8,128)(2,1)} %w_ref.4) | copy-start | bytes 1492996
  5.5 1.4 %collective-permute-start = (bf16[2,32,512]{2,1,0:T(8,128)(2,1)S(1)}, bf16[2,32,512]{2,1,0:T(8,128)(2,1)S(1)}, u32[]{:S(2)}, u32[]{:S(2)}) collective-permute-start(bf16[2,32,512]{2,1,0:T(8,128)(2,1)S(1)} %slice_select_fusion), channel_id=1, source_target_pairs={{0,4},{4,0},{1,5},{5,1},{2,6},{6,2},{3,7},{7,3},{8,12},{12,8},{9,1... | collective-permute-start | bytes 196616 | tf_op jit(solution)/shard_map/ppermute | solution.py:374
  6.0 7.1 %copy-start.2 = (bf16[27,64,64]{2,1,0:T(8,128)(2,1)S(1)}, bf16[27,64,64]{2,1,0:T(8,128)(2,1)}, u32[]{:S(2)}) copy-start(bf16[27,64,64]{2,1,0:T(8,128)(2,1)} %w_ref.3) | copy-start | bytes 663556
  6.0 7.1 %copy-start.3 = (f32[64]{0:T(128)S(1)}, f32[64]{0:T(128)}, u32[]{:S(2)}) copy-start(f32[64]{0:T(128)} %param.19) | copy-start | bytes 772
  7.0 7.9 %collective-permute-start.1 = (bf16[20,6,512]{2,1,0:T(8,128)(2,1)S(1)}, bf16[20,6,512]{2,1,0:T(8,128)(2,1)S(1)}, u32[]{:S(2)}, u32[]{:S(2)}) collective-permute-start(bf16[20,6,512]{2,1,0:T(8,128)(2,1)S(1)} %get-tuple-element.54), channel_id=1, source_target_pairs={{0,4},{8,16},{16,8},{24,28},{4,0},{12,20},{20,12},{28,24},{1,5},{9... | collective-permute-start | bytes 368648 | tf_op jit(solution)/shard_map/ppermute | solution.py:381
  7.4 11.8 %collective-permute-start.2 = (bf16[20,6,512]{2,1,0:T(8,128)(2,1)S(1)}, bf16[20,6,512]{2,1,0:T(8,128)(2,1)S(1)}, u32[]{:S(2)}, u32[]{:S(2)}) collective-permute-start(bf16[20,6,512]{2,1,0:T(8,128)(2,1)S(1)} %get-tuple-element.55), channel_id=1, source_target_pairs={{0,8},{8,0},{16,24},{24,16},{1,9},{9,1},{17,25},{25,17},{2,10},{10... | collective-permute-start | bytes 368648 | tf_op jit(solution)/shard_map/ppermute | solution.py:374
  11.5 7.9 %collective-permute-start.4 = (bf16[20,32,128]{2,1,0:T(8,128)(2,1)S(1)}, bf16[20,32,128]{2,1,0:T(8,128)(2,1)S(1)}, u32[]{:S(2)}, u32[]{:S(2)}) collective-permute-start(bf16[20,32,128]{2,1,0:T(8,128)(2,1)S(1)} %get-tuple-element.52), channel_id=1, source_target_pairs={{0,1},{1,0},{2,3},{3,2},{4,5},{5,4},{6,7},{7,6},{8,9},{9,8},{10,11... | collective-permute-start | bytes 491528 | tf_op jit(solution)/shard_map/ppermute | solution.py:374
  13.1 6.3 %collective-permute-start.3 = (bf16[20,32,128]{2,1,0:T(8,128)(2,1)S(1)}, bf16[20,32,128]{2,1,0:T(8,128)(2,1)S(1)}, u32[]{:S(2)}, u32[]{:S(2)}) collective-permute-start(bf16[20,32,128]{2,1,0:T(8,128)(2,1)S(1)} %get-tuple-element.53), channel_id=1, source_target_pairs={{0,4},{1,2},{2,1},{3,7},{4,0},{5,6},{6,5},{7,3},{8,12},{9,10},{10,... | collective-permute-start | bytes 491528 | tf_op jit(solution)/shard_map/ppermute | solution.py:381
  19.4 5.5 %collective-permute-start.5 = (bf16[20,12,128]{2,1,0:T(8,128)(2,1)S(1)}, bf16[20,12,128]{2,1,0:T(8,128)(2,1)S(1)}, u32[]{:S(2)}, u32[]{:S(2)}) collective-permute-start(bf16[20,12,128]{2,1,0:T(8,128)(2,1)S(1)} %get-tuple-element.56), channel_id=1, source_target_pairs={{0,4},{1,2},{2,1},{3,7},{4,0},{5,6},{6,5},{7,3},{8,12},{9,10},{10,... | collective-permute-start | bytes 184328 | tf_op jit(solution)/shard_map/ppermute | solution.py:381
  19.5 5.5 %collective-permute-start.6 = (bf16[20,12,128]{2,1,0:T(8,128)(2,1)S(1)}, bf16[20,12,128]{2,1,0:T(8,128)(2,1)S(1)}, u32[]{:S(2)}, u32[]{:S(2)}) collective-permute-start(bf16[20,12,128]{2,1,0:T(8,128)(2,1)S(1)} %get-tuple-element.57), channel_id=1, source_target_pairs={{0,1},{1,0},{2,3},{3,2},{4,5},{5,4},{6,7},{7,6},{8,9},{9,8},{10,11... | collective-permute-start | bytes 184328 | tf_op jit(solution)/shard_map/ppermute | solution.py:374
  22.6 2.6 %copy-start.4 = (f32[64]{0:T(128)S(1)}, f32[64]{0:T(128)}, u32[]{:S(2)}) copy-start(f32[64]{0:T(128)} %param.21) | copy-start | bytes 772
  25.2 6.8 %copy-start.1 = (bf16[27,96,96]{2,1,0:T(8,128)(2,1)S(1)}, bf16[27,96,96]{2,1,0:T(8,128)(2,1)}, u32[]{:S(2)}) copy-start(bf16[27,96,96]{2,1,0:T(8,128)(2,1)} %w_ref.5) | copy-start | bytes 1492996
  31.9 0.7 %copy-start.7 = (f32[96]{0:T(128)S(1)}, f32[96]{0:T(128)}, u32[]{:S(2)}) copy-start(f32[96]{0:T(128)} %param.25) | copy-start | bytes 1156
  31.9 0.7 %copy-start.8 = (f32[96]{0:T(128)S(1)}, f32[96]{0:T(128)}, u32[]{:S(2)}) copy-start(f32[96]{0:T(128)} %param.27) | copy-start | bytes 1156
  31.9 1.3 %collective-permute-start.7 = (bf16[2,20,512]{2,1,0:T(8,128)(2,1)S(1)}, bf16[2,20,512]{2,1,0:T(8,128)(2,1)S(1)}, u32[]{:S(2)}, u32[]{:S(2)}) collective-permute-start(bf16[2,20,512]{2,1,0:T(8,128)(2,1)S(1)} %slice_select_fusion.1), channel_id=1, source_target_pairs={{0,4},{4,0},{1,5},{5,1},{2,6},{6,2},{3,7},{7,3},{8,12},{12,8},{9,1... | collective-permute-start | bytes 122888 | tf_op jit(solution)/shard_map/ppermute | solution.py:374
  33.3 6.3 %collective-permute-start.9 = (bf16[12,20,256]{2,1,0:T(8,128)(2,1)S(1)}, bf16[12,20,256]{2,1,0:T(8,128)(2,1)S(1)}, u32[]{:S(2)}, u32[]{:S(2)}) collective-permute-start(bf16[12,20,256]{2,1,0:T(8,128)(2,1)S(1)} %get-tuple-element.64), channel_id=1, source_target_pairs={{0,1},{1,0},{2,3},{3,2},{4,5},{5,4},{6,7},{7,6},{8,9},{9,8},{10,11... | collective-permute-start | bytes 368648 | tf_op jit(solution)/shard_map/ppermute | solution.py:374
  35.4 4.2 %collective-permute-start.8 = (bf16[12,20,256]{2,1,0:T(8,128)(2,1)S(1)}, bf16[12,20,256]{2,1,0:T(8,128)(2,1)S(1)}, u32[]{:S(2)}, u32[]{:S(2)}) collective-permute-start(bf16[12,20,256]{2,1,0:T(8,128)(2,1)S(1)} %get-tuple-element.65), channel_id=1, source_target_pairs={{0,4},{1,2},{2,1},{3,7},{4,0},{5,6},{6,5},{7,3},{8,12},{9,10},{10,... | collective-permute-start | bytes 368648 | tf_op jit(solution)/shard_map/ppermute | solution.py:381

commit v9 on v8

--- a/solution.py
+++ b/solution.py
@@ -93,6 +93,7 @@
 ):
     half = v_ref.shape[2]
     kz = C0 * half
+    part = 16 * half
     lanes = Z1 // 2 * C1
     small = ((t_hbm, t_ref), (wd_hbm, w_ref), (b_hbm, b_ref), (wa_hbm, wa_ref))
     copies = [pltpu.make_async_copy(src, dst, sems.at[n]) for n, (src, dst) in enumerate(small)]
@@ -116,30 +117,31 @@
     for ab in range(4):
         pair = w_ref[2 * ab : 2 * ab + 2].reshape(2 * C0, C1)
         wide = jnp.concatenate([pair] * (Z1 // 2), axis=1)
-        wd_ref[ab * kz : (ab + 1) * kz, :] = jnp.where(keep, mm(spread, wide), 0.0).astype(BF)
+        block = jnp.where(keep, mm(spread, wide), 0.0).astype(BF)
+        for n in range(C0 // 16):
+            wd_ref[n, ab * part : ab * part + part, :] = block[n * part : n * part + part]
 
     copies[3].wait()
     fill_banded(wa_ref, ta_ref, 4, C1)
     r = iota((4 * CX, 128), 0)
     select = one_hot_rows(((r & 32) << 2) | (r & 64) | ((r & 31) << 1) | (r >> 7), 4 * CX)
     part = 16 * half
-    part = 16 * half
+    acc = [0.0, 0.0]
     for n, copy in enumerate(copies[4:]):
         copy.wait()
         for m in range(v_ref.shape[3] // 256):
             v = [v_ref[n * 16 : n * 16 + 16, h, :, m * 256 : m * 256 + 256].reshape(part, 256) for h in range(2)]
             cells = mm(select, jnp.concatenate(v, axis=0), NT).astype(BF)
             for ab in range(4):
-                lane = ab * kz + n * part
                 for h in range(2):
                     piece = cells[64 * ab : 64 * ab + 64, h * part : h * part + part]
-                    cells_ref[h, m * 64 : m * 64 + 64, lane : lane + part] = piece
+                    cells_ref[n, h, m * 64 : m * 64 + 64, ab * part : ab * part + part] = piece
+        acc = [acc[h] + mm(cells_ref[n, h], wd_ref[n]) for h in range(2)]
     mask = mask_rows(tab[:, 128:256], 0, Y1, X1, lambda x: x, 4)
     bias = twice(b_ref)
     for h in range(2):
-        acc = mm(cells_ref[h], wd_ref[...])
         for q in range(2):
-            value = finish(acc[:, q * 128 : q * 128 + 128], bias, mask, Y1)
+            value = finish(acc[h][:, q * 128 : q * 128 + 128], bias, mask, Y1)
             out_ref[:, :, (2 * h + q) * 128 : (2 * h + q + 1) * 128] = value
 
 
@@ -228,44 +230,67 @@
 
 
 def fill_edges(copies, pieces):
-    rows, pitch, lanes = copies[0].shape
-    for lane in range(0, lanes, 128):
-        line = [p[:, :, lane : lane + 128] for p in pieces]
-        used = sum(p.shape[1] for p in line)
-        for i, copy in enumerate(copies):
-            moved = [line[0][:, i:]] + line[1:] if i < line[0].shape[1] else line[1:]
-            spare = [jnp.zeros((rows, pitch - used + i, 128), BF)] if pitch - used + i else []
-            copy[:, :, lane : lane + 128] = jnp.concatenate(moved + spare, axis=1)
+    pitch = copies[0].shape[1]
+    for i, copy in enumerate(copies):
+        line = [pieces[0][:, i:]] + pieces[1:]
+        if i:
+            line.append(jnp.zeros((copy.shape[0], i, pieces[0].shape[2]), BF))
+        copy[...] = jnp.concatenate(line, axis=1)
+
+
+def edge_masks(tab_ref):
+    mask = mask_rows(tab_ref[...], -1, Y1 + 2, EDGE, lambda r: jnp.where(r < 8, r - 5, r + X1 - 9), 4)
+    return [mask[:, q * 128 : q * 128 + 128] for q in range(3)]
+
+
+def edge_group(taps, t_ref, b_ref, masks, inner_ref, moved):
+    rows = Y1 + 2
+    acc = conv_group(taps, t_ref, 0, rows, 128 * len(masks), 384)
+    i0, i1, i2 = moved
+    for q, mask in enumerate(masks):
+        cut = slice(q * 128, q * 128 + 128)
+        edge = finish(acc[:, cut], twice(b_ref), mask, rows)
+        inner = inner_ref[:, :, cut][:, 1:-1]
+        i0[:, :X1, cut] = jnp.concatenate([edge[:, 4:6], inner], axis=1)
+        i1[:, :X1, cut] = jnp.concatenate([edge[:, 5:6], inner, edge[:, 8:9]], axis=1)
+        i2[:, :X1, cut] = jnp.concatenate([inner, edge[:, 8:10]], axis=1)
+        i0[:, X1:, cut] = edge
+        for i, copy in ((1, i1), (2, i2)):
+            copy[:, X1:, cut] = jnp.concatenate([edge[:, i:], jnp.zeros((rows, i, 128), BF)], axis=1)
+
+
+def edge_middle_kernel(xl_ref, win_ref, xr_ref, g_ref, t_ref, b_ref, tab_ref, e0, e1, e2, m0, m1, m2):
+    for lane in range(0, Z1 * C1, 128):
+        cut = slice(lane, lane + 128)
+        inner = win_ref[:, :, cut]
+        pieces = [xl_ref[:, :, cut], inner[:, :2], inner[:, X1 - 2 :], xr_ref[:, :, cut]]
+        fill_edges([e.at[:, :, cut] for e in (e0, e1, e2)], pieces)
+    here = edge_masks(tab_ref)[1]
+    edge_group([[(e, 128, 384)] for e in (e0, e1, e2)], t_ref, b_ref, (here, here), g_ref, (m0, m1, m2))
 
 
 def level_one_kernel(
-    xl_ref, low_ref, high_ref, xr_ref, g1_ref, g2_ref, g3_ref, ta_ref, tb_ref, ba_ref, bb_ref, wd_ref, bd_ref, tab_ref, tab2_ref,
-    feat_ref, down_ref, e0, e1, e2, i0, i1, i2, side_ref, d_ref,
+    zl_ref, zr_ref, cl_ref, cr_ref, e0, e1, e2, m0, m1, m2, g1_ref, g3_ref, ta_ref, tb_ref, ba_ref, bb_ref, wd_ref, bd_ref, tab_ref,
+    tab2_ref, feat_ref, down_ref, l0, l1, l2, h0, h1, h2, i0, i1, i2, j0, j1, j2, side_ref, d_ref,
 ):
-    fill_edges((e0, e1, e2), (xl_ref, low_ref, high_ref, xr_ref))
-    rows = Y1 + 2
-    mask = mask_rows(tab_ref[...], -1, rows, EDGE, lambda r: jnp.where(r < 8, r - 5, r + X1 - 9), 4)
-    for g, (lane, width, out) in enumerate(((0, 384, 256), (256, 384, 256), (512, 256, 128))):
-        acc = conv_group([[(e, lane, width)] for e in (e0, e1, e2)], ta_ref, 0, rows, out, 384)
-        for q in range(out // 128):
-            chunk = 2 * g + q
-            which = 0 if chunk == 0 else (2 if chunk == 4 else 1)
-            edge = finish(acc[:, q * 128 : q * 128 + 128], twice(ba_ref), mask[:, which * 128 : which * 128 + 128], rows)
-            inner = (g1_ref, g2_ref, g3_ref)[g][:, :, q * 128 : q * 128 + 128][:, 1:-1]
-            cut = slice(chunk * 128, chunk * 128 + 128)
-            i0[:, :X1, cut] = jnp.concatenate([edge[:, 4:6], inner], axis=1)
-            i1[:, :X1, cut] = jnp.concatenate([edge[:, 5:6], inner, edge[:, 8:9]], axis=1)
-            i2[:, :X1, cut] = jnp.concatenate([inner, edge[:, 8:10]], axis=1)
-            i0[:, X1:, cut] = edge
-            for i, copy in ((1, i1), (2, i2)):
-                copy[:, X1:, cut] = jnp.concatenate([edge[:, i:], jnp.zeros((rows, i, 128), BF)], axis=1)
+    own, mid, low, high = (e0, e1, e2), (m0, m1, m2), (i0, i1, i2), (j0, j1, j2)
+    for z_ref, c_ref, copies in ((zl_ref, cl_ref, (l0, l1, l2)), (zr_ref, cr_ref, (h0, h1, h2))):
+        inner, corner = z_ref[...], c_ref[...]
+        fill_edges(copies, [corner[:, :HALO_X], inner[:, :2], inner[:, X1 - 2 :], corner[:, HALO_X:]])
+    below, here, above = edge_masks(tab_ref)
+    taps = [[(z, 0, 128), (e, 0, 256)] for z, e in zip((l0, l1, l2), own)]
+    edge_group(taps, ta_ref, ba_ref, (below, here), g1_ref, low)
+    taps = [[(e, 384, 128), (z, 0, 128)] for z, e in zip((h0, h1, h2), own)]
+    edge_group(taps, ta_ref, ba_ref, (above,), g3_ref, high)
 
     def cell_of(r):
         return jnp.where(r < X1, r, jnp.where(r < X1 + 8, r - X1 - 4, r - 8))
 
     mask = mask_rows(tab_ref[:, 128:256], 0, Y1, X1 + EDGE, cell_of, 4)
-    for g in range(2):
-        acc = conv_group([[(ref, 256 * g, 384)] for ref in (i0, i1, i2)], tb_ref, 0, Y1, 256, 384)
+    first = [[(a, 0, 256), (b, 0, 128)] for a, b in zip(low, mid)]
+    second = [[(a, 0, 256), (b, 0, 128)] for a, b in zip(mid, high)]
+    for g, taps in enumerate((first, second)):
+        acc = conv_group(taps, tb_ref, 0, Y1, 256, 384)
         for q in range(2):
             value = finish(acc[:, q * 128 : q * 128 + 128], twice(bb_ref), mask, Y1)
             cut = slice((2 * g + q) * 128, (2 * g + q + 1) * 128)
@@ -385,8 +410,11 @@
 
 
 def shift_along(low_edge, high_edge, axis):
+    shape = low_edge.shape
+    low, high = (edge.reshape(-1, shape[-1]) for edge in (low_edge, high_edge))
     even = lax.axis_index(axis) % 2 == 0
-    return trade(jnp.where(even, high_edge, low_edge), jnp.where(even, low_edge, high_edge), axis)
+    below, above = trade(jnp.where(even, high, low), jnp.where(even, low, high), axis)
+    return below.reshape(shape), above.reshape(shape)
 
 
 def params():
@@ -410,7 +438,6 @@
     w_down2, b_down2, w_conv2a, b_conv2a, w_conv2b, b_conv2b,
 ):
     depth = volume.shape[1]
-    kz = C0 * depth
     lanes1 = Z1 * C1
     half = depth // 2
     operands = [volume.reshape(C0, 2, half, -1), jnp.swapaxes(w_down1, 1, 2), b_down1[None], tissue.transpose(1, 2, 0), w_conv1a]
@@ -421,8 +448,8 @@
         out_shape=[shaped(Y1, X1, lanes1), banded_shape(4, C1), shaped(128, 384), shaped(128, 384)],
         scratch_shapes=[pltpu.VMEM(x.shape, x.dtype) for x in operands]
         + [
-            pltpu.VMEM((2 * kz, lanes1 // 2), BF),
-            pltpu.VMEM((2, Y1 * X1, 2 * kz), BF),
+            pltpu.VMEM((C0 // 16, 64 * half, lanes1 // 2), BF),
+            pltpu.VMEM((C0 // 16, 2, Y1 * X1, 64 * half), BF),
             pltpu.SemaphoreType.DMA((4 + C0 // 16,)),
         ],
         compiler_params=params(),
@@ -448,10 +475,6 @@
     corner = jnp.concatenate([x_below, x_above], axis=1)
     corner, z_below, z_above, g2 = lax.optimization_barrier((corner, z_below, z_above, g2))
     corner_below, corner_above = shift_along(corner[:, :, :128], corner[:, :, lanes1 - 128 :], "gz")
-    x_below = jnp.concatenate([corner_below[:, :HALO_X], x_below, corner_above[:, :HALO_X]], axis=2)
-    x_above = jnp.concatenate([corner_below[:, HALO_X:], x_above, corner_above[:, HALO_X:]], axis=2)
-    low = jnp.concatenate([z_below[:, :2], win[:, :2], z_above[:, :2]], axis=2)
-    high = jnp.concatenate([z_below[:, X1 - 2 :], win[:, X1 - 2 :], z_above[:, X1 - 2 :]], axis=2)
     g1, g3 = pl.pallas_call(
         outer_kernel,
         out_shape=[shaped(rows, X1, 256), shaped(rows, X1, 128)],
@@ -460,16 +483,24 @@
         cost_estimate=cost(4e-6),
     )(win, left, right, z_below, z_above, t1a, bias1a, tab1)
 
+    wide_x = X1 + EDGE
+    edges = pl.pallas_call(
+        edge_middle_kernel,
+        out_shape=[shaped(ROWS1, EDGE, lanes1)] * 3 + [shaped(rows, wide_x, 256)] * 3,
+        compiler_params=params(),
+        cost_estimate=cost(3e-6),
+    )(x_below, win, x_above, g2, t1a, bias1a, tab1)
     feat, down = pl.pallas_call(
         level_one_kernel,
         out_shape=[shaped(Y1 * X1, lanes1), shaped(Y2, X2 + 2 * HALO_X2, Z2 * CP)],
-        scratch_shapes=[pltpu.VMEM((ROWS1, EDGE, (Z1 + 4) * C1), BF)] * 3
-        + [pltpu.VMEM((rows, X1 + EDGE, (Z1 + 2) * C1), BF)] * 3
+        scratch_shapes=[pltpu.VMEM((ROWS1, EDGE, 128), BF)] * 6
+        + [pltpu.VMEM((rows, wide_x, 256), BF)] * 3
+        + [pltpu.VMEM((rows, wide_x, 128), BF)] * 3
         + [pltpu.VMEM((Y1 * EDGE, lanes1), BF), pltpu.VMEM((4, Y2 * (X2 + EDGE // 2), lanes1), BF)],
         compiler_params=params(),
         cost_estimate=cost(6e-6),
     )(
-        x_below, low, high, x_above, g1, g2, g3, t1a, t1b, bias1a, b_conv1b[None],
+        z_below, z_above, corner_below, corner_above, *edges, g1, g3, t1a, t1b, bias1a, b_conv1b[None],
         pad_lanes(jnp.swapaxes(w_down2, 1, 2).reshape(8 * C1, C2)), pad_lanes(b_down2[None]), tab1, tab2,
     )
 

time: 43.8 us -> 72.8 us (1.66)
  local copies, waits for them, and re-layouts: 0.44 us -> 32.2 us
  waiting for transfers between devices: 7.35 us -> 2.35 us
  other arithmetic: 0.72 us -> 3.15 us
  starting transfers between devices: 11.8 us -> 10.7 us
    unnamed x18 -> x94, local copies, waits for them, and re-layouts: 0.25 us -> 30.5 us
    ppermute x6, waiting for transfers between devices: 7.34 us -> 2.34 us  [trade(): one = lax.ppermute(first, axis, [(i, i ^ 1) for i in range(count)])]
    select_n x2 -> x3, other arithmetic: 0.05 us -> 1.96 us  [trade(): jnp.where(index < count - 1, jnp.where(even, one, two), jnp.zeros_like(one))]
    select_n x0 -> x7, local copies, waits for them, and re-layouts: none -> 1.51 us  [the longest x4 0.76 us: shift_along(): jnp.where(even, high, low)]
    ppermute x6, starting transfers between devices: 11.4 us -> 10 us  [trade(): one = lax.ppermute(first, axis, [(i, i ^ 1) for i in range(count)])]
    pallas_call x0 -> x1, Pallas kernels: none -> 1.3 us  [local(): pl.pallas_call(edge_middle_kernel, out_shape=[shaped(ROWS1, EDGE, lanes1)...]
    pallas_call x1, Pallas kernels: 6.67 us -> 5.55 us  [local(): pl.pallas_call(level_one_kernel, out_shape=[shaped(Y1 * X1, lanes1), shap...]
    select_n x6, other arithmetic: 0.14 us -> 0.89 us  [the longest x5 0.84 us: shift_along(): jnp.where(even, high, low)]
  transfers between devices with their start and end apart: 10 -> 10, of which waited for: 5 -> 2; matrix products, arithmetic and copies ran while one was open for 1% -> 2% of each run, Pallas kernels for 16% -> 11%
where the time goes in v9:
time: 72.8 us; the launch traced here: 72 us
  local copies, waits for them, and re-layouts  32.2 us (44%)
  Pallas kernels  22.3 us (31%)
  starting transfers between devices  10.7 us (15%)
  other arithmetic  3.15 us (4%)
  waiting for transfers between devices  2.35 us (3%)
  between operations  1.21 us (2%)
    unnamed x94, local copies, waits for them, and re-layouts  30.5 us
    ppermute x6, starting transfers between devices, trade(): one = lax.ppermute(first, axis, [(i, i ^ 1) for i in range(count)])  10 us
    pallas_call x1, Pallas kernels, local(): pl.pallas_call(level_one_kernel, out_shape=[shaped(Y1 * X1, lanes1), shap...  5.55 us
    pallas_call x1, Pallas kernels, local(): pl.pallas_call(down1_kernel, in_specs=[pl.BlockSpec(memory_space=pltpu.HB...  4.73 us
    pallas_call x1, Pallas kernels, local(): pl.pallas_call(level_two_kernel, out_shape=shaped(C2 * Z2, Y2 * X2), scra...  4.02 us
    ppermute x6, waiting for transfers between devices, trade(): one = lax.ppermute(first, axis, [(i, i ^ 1) for i in range(count)])  2.34 us
    pallas_call x1, Pallas kernels, local(): pl.pallas_call(outer_kernel, out_shape=[shaped(rows, X1, 256), shaped(row...  2.13 us
    select_n x3, other arithmetic, trade(): jnp.where(index < count - 1, jnp.where(even, one, two), jnp.zeros_like(one))  1.96 us
  transfers between devices with their start and end apart: 10, of which 2 were waited for; matrix products, arithmetic and copies ran while one was open for 2% of the time, Pallas kernels for 11%

profile of v9, /device:TPU:0, one launch (start us, length us, event | category | flops | bytes accessed | tf_op | source)
XLA Modules:
  0.0 72.0 jit_solution(14052114988084819993)
XLA Ops:
  0.7 4.7 %shard_map.149 = (bf16[16,32,512]{2,1,0:T(8,128)(2,1)S(1)}, bf16[3,256,1152]{2,1,0:T(8,128)(2,1)S(1)}, bf16[128,384]{1,0:T(8,128)(2,1)S(1)}, bf16[128,384]{1,0:T(8,128)(2,1)S(1)}) custom-call(bf16[48,2,8,2048]{3,2,1,0:T(8,128)(2,1)} %bitcast.34, bf16[8,48,64]{2,1,0:T(8,128)(2,1)} %bitcast.35, f32[1,64]{1,0:T(1,128)} %bitcast.37, s32[8,4,32]{2,1,0:T(4,128)} %bitcast.36, ...), custom_call_target="tpu_custom_call" | custom-call | flops 4000000000 | tf_op jit(solution)/shard_map/pallas_call | solution.py:445
  5.4 1.2 %copy-done.10 = bf16[3,256,1152]{2,1,0:T(8,128)(2,1)} copy-done((bf16[3,256,1152]{2,1,0:T(8,128)(2,1)}, bf16[3,256,1152]{2,1,0:T(8,128)(2,1)S(1)}, u32[]{:S(2)}) %copy-start.10) | copy-done | bytes 1769496
  7.6 1.4 %copy-done.5 = bf16[3,256,1536]{2,1,0:T(8,128)(2,1)} copy-done((bf16[3,256,1536]{2,1,0:T(8,128)(2,1)}, bf16[3,256,1536]{2,1,0:T(8,128)(2,1)S(1)}, u32[]{:S(2)}) %copy-start.5) | copy-done | bytes 2359320
  9.9 4.2 %collective-permute-start.4 = (bf16[640,128]{1,0:T(8,128)(2,1)}, bf16[640,128]{1,0:T(8,128)(2,1)}, u32[]{:S(2)}, u32[]{:S(2)}) collective-permute-start(bf16[640,128]{1,0:T(8,128)(2,1)} %bitcast.8), channel_id=1, source_target_pairs={{0,1},{1,0},{2,3},{3,2},{4,5},{5,4},{6,7},{7,6},{8,9},{9,8},{10,11... | collective-permute-start | bytes 491528 | tf_op jit(solution)/shard_map/ppermute | solution.py:399
  14.3 3.0 %collective-permute-start.2 = (bf16[120,512]{1,0:T(8,128)(2,1)S(1)}, bf16[120,512]{1,0:T(8,128)(2,1)S(1)}, u32[]{:S(2)}, u32[]{:S(2)}) collective-permute-start(bf16[120,512]{1,0:T(8,128)(2,1)S(1)} %select_n.262), channel_id=1, source_target_pairs={{0,8},{8,0},{16,24},{24,16},{1,9},{9,1},{17,25},{25,17},{2,10},{10... | collective-permute-start | bytes 368648 | tf_op jit(solution)/shard_map/ppermute | solution.py:399
  17.4 1.5 %copy-done.11 = bf16[3,256,1152]{2,1,0:T(8,128)(2,1)S(1)} copy-done((bf16[3,256,1152]{2,1,0:T(8,128)(2,1)S(1)}, bf16[3,256,1152]{2,1,0:T(8,128)(2,1)}, u32[]{:S(2)}) %copy-start.11) | copy-done | bytes 1769496
  18.9 1.7 %shard_map.150 = (bf16[20,32,512]{2,1,0:T(8,128)(2,1)S(1)}, bf16[20,32,512]{2,1,0:T(8,128)(2,1)S(1)}, bf16[18,32,256]{2,1,0:T(8,128)(2,1)S(1)}, bf16[3,256,1152]{2,1,0:T(8,128)(2,1)S(1)}) custom-call(bf16[20,32,512]{2,1,0:T(8,128)(2,1)S(1)} %pad_maximum_fusion.win_ref, bf16[3,256,1152]{2,1,0:T(8,128)(2,1)S(1)} %copy-done.11, f32[1,64]{1,0:T(1,128)S(1)} %bitcast.25, ...), custom_call_target="tpu_custom_call" | custom-call | flops 3000000000 | tf_op jit(solution)/shard_map/pallas_call | solution.py:468
  20.5 1.2 %copy-done.14 = bf16[3,256,1152]{2,1,0:T(8,128)(2,1)} copy-done((bf16[3,256,1152]{2,1,0:T(8,128)(2,1)}, bf16[3,256,1152]{2,1,0:T(8,128)(2,1)S(1)}, u32[]{:S(2)}) %copy-start.14) | copy-done | bytes 1769496
  21.8 1.2 %collective-permute-done.2 = bf16[120,512]{1,0:T(8,128)(2,1)S(1)} collective-permute-done((bf16[120,512]{1,0:T(8,128)(2,1)S(1)}, bf16[120,512]{1,0:T(8,128)(2,1)S(1)}, u32[]{:S(2)}, u32[]{:S(2)}) %collective-permute-start.2) | collective-permute-done | bytes 122912 | tf_op jit(solution)/shard_map/ppermute | solution.py:399
  23.3 1.0 %select_select_fusion = (bf16[640,128]{1,0:T(8,128)(2,1)S(1)}, bf16[640,128]{1,0:T(8,128)(2,1)S(1)}) fusion(bf16[640,128]{1,0:T(8,128)(2,1)} %collective-permute-done.4, bf16[640,128]{1,0:T(8,128)(2,1)} %collective-permute-done.3, pred[]{:T(512)S(6)} %lt.49, pred[]{:T(512)S(6)} %eq.33, pred[]{:T(512)S(6)} %gt.14), kind=kLoop, calls=%fused_computation.3 | loop fusion | flops 327680 | bytes 655363 | tf_op jit(solution)/shard_map/jit(_where)/select_n | solution.py:408
  24.4 2.0 %collective-permute-start.6 = (bf16[240,128]{1,0:T(8,128)(2,1)S(1)}, bf16[240,128]{1,0:T(8,128)(2,1)S(1)}, u32[]{:S(2)}, u32[]{:S(2)}) collective-permute-start(bf16[240,128]{1,0:T(8,128)(2,1)S(1)} %select_n.287), channel_id=1, source_target_pairs={{0,1},{1,0},{2,3},{3,2},{4,5},{5,4},{6,7},{7,6},{8,9},{9,8},{10,11... | collective-permute-start | bytes 184328 | tf_op jit(solution)/shard_map/ppermute | solution.py:399
  26.4 1.5 %copy-done.12 = bf16[3,256,1152]{2,1,0:T(8,128)(2,1)S(1)} copy-done((bf16[3,256,1152]{2,1,0:T(8,128)(2,1)S(1)}, bf16[3,256,1152]{2,1,0:T(8,128)(2,1)}, u32[]{:S(2)}) %copy-start.12) | copy-done | bytes 1769496
  27.9 2.1 %shard_map.152 = (bf16[18,32,256]{2,1,0:T(8,128)(2,1)S(1)}, bf16[18,32,128]{2,1,0:T(8,128)(2,1)S(1)}) custom-call(bf16[20,32,512]{2,1,0:T(8,128)(2,1)S(1)} %pad_maximum_fusion.win_ref, bf16[20,32,512]{2,1,0:T(8,128)(2,1)S(1)} %get-tuple-element.46.left_ref, bf16[20,32,512]{2,1,0:T(8,128)(2,1)S(1)} %get-tuple-element.47.right_ref, ...), custom_call_target="tpu_custom_call" | custom-call | flops 4000000000 | tf_op jit(solution)/shard_map/pallas_call | solution.py:478
  30.7 1.3 %shard_map.151 = (bf16[20,16,512]{2,1,0:T(8,128)(2,1)S(1)}, bf16[20,16,512]{2,1,0:T(8,128)(2,1)S(1)}, bf16[20,16,512]{2,1,0:T(8,128)(2,1)S(1)}, bf16[18,48,256]{...) custom-call(bf16[20,6,512]{2,1,0:T(8,128)(2,1)S(1)} %reshape.87.xl_ref, ...), custom_call_target="tpu_custom_call" | custom-call | flops 3000000000 | tf_op jit(solution)/shard_map/pallas_call | solution.py:487
  35.8 1.5 %copy-done.13 = bf16[3,256,1152]{2,1,0:T(8,128)(2,1)S(1)} copy-done((bf16[3,256,1152]{2,1,0:T(8,128)(2,1)S(1)}, bf16[3,256,1152]{2,1,0:T(8,128)(2,1)}, u32[]{:S(2)}) %copy-start.13) | copy-done | bytes 1769496
  37.2 1.5 %copy-done.15 = bf16[3,256,1152]{2,1,0:T(8,128)(2,1)S(1)} copy-done((bf16[3,256,1152]{2,1,0:T(8,128)(2,1)S(1)}, bf16[3,256,1152]{2,1,0:T(8,128)(2,1)}, u32[]{:S(2)}) %copy-start.15) | copy-done | bytes 1769496
  38.7 1.0 %copy-done.17 = bf16[18,48,256]{2,1,0:T(8,128)(2,1)S(1)} copy-done((bf16[18,48,256]{2,1,0:T(8,128)(2,1)S(1)}, bf16[18,48,256]{2,1,0:T(8,128)(2,1)}, u32[]{:S(2)}) %copy-start.17) | copy-done | bytes 442392
  39.7 1.0 %copy-done.19 = bf16[18,48,256]{2,1,0:T(8,128)(2,1)S(1)} copy-done((bf16[18,48,256]{2,1,0:T(8,128)(2,1)S(1)}, bf16[18,48,256]{2,1,0:T(8,128)(2,1)}, u32[]{:S(2)}) %copy-start.19) | copy-done | bytes 442392
  40.7 1.0 %copy-done.27 = bf16[20,16,512]{2,1,0:T(8,128)(2,1)S(1)} copy-done((bf16[20,16,512]{2,1,0:T(8,128)(2,1)S(1)}, bf16[20,16,512]{2,1,0:T(8,128)(2,1)}, u32[]{:S(2)}) %copy-start.27) | copy-done | bytes 327704
  41.7 1.0 %copy-done.29 = bf16[20,16,512]{2,1,0:T(8,128)(2,1)S(1)} copy-done((bf16[20,16,512]{2,1,0:T(8,128)(2,1)S(1)}, bf16[20,16,512]{2,1,0:T(8,128)(2,1)}, u32[]{:S(2)}) %copy-start.29) | copy-done | bytes 327704
  42.7 1.0 %copy-done.31 = bf16[20,16,512]{2,1,0:T(8,128)(2,1)S(1)} copy-done((bf16[20,16,512]{2,1,0:T(8,128)(2,1)S(1)}, bf16[20,16,512]{2,1,0:T(8,128)(2,1)}, u32[]{:S(2)}) %copy-start.31) | copy-done | bytes 327704
  46.4 5.5 %shard_map.153 = (bf16[512,512]{1,0:T(8,128)(2,1)S(1)}, bf16[8,20,512]{2,1,0:T(8,128)(2,1)S(1)}) custom-call(bf16[20,32,128]{2,1,0:T(8,128)(2,1)S(1)} %bitcast.24, bf16[20,32,128]{2,1,0:T(8,128)(2,1)S(1)} %bitcast.22, bf16[20,12,128]{2,1,0:T(8,128)(2,1)S(1)} %reshape.91.cl_ref, bf16[20,12,128]{2,1,0:T(8,128)(2,1)S(1)} %reshape.92.cr_ref, ...), custom_call_target="tpu_custom_call" | custom-call | flops 6000000000 | tf_op jit(solution)/shard_map/pallas_call | solution.py:493
  52.5 1.4 %copy-done.8 = bf16[3,256,1536]{2,1,0:T(8,128)(2,1)} copy-done((bf16[3,256,1536]{2,1,0:T(8,128)(2,1)}, bf16[3,256,1536]{2,1,0:T(8,128)(2,1)S(1)}, u32[]{:S(2)}) %copy-start.8) | copy-done | bytes 2359320
  56.2 1.7 %copy-done.6 = bf16[3,256,1536]{2,1,0:T(8,128)(2,1)S(1)} copy-done((bf16[3,256,1536]{2,1,0:T(8,128)(2,1)S(1)}, bf16[3,256,1536]{2,1,0:T(8,128)(2,1)}, u32[]{:S(2)}) %copy-start.6) | copy-done | bytes 2359320
  57.9 1.0 %shard_map.156 = (bf16[12,32,512]{2,1,0:T(8,128)(2,1)S(1)}, bf16[12,32,512]{2,1,0:T(8,128)(2,1)S(1)}, bf16[12,32,512]{2,1,0:T(8,128)(2,1)S(1)}, bf16[10,16,256]{...) custom-call(bf16[12,20,512]{2,1,0:T(8,128)(2,1)S(1)} %pad_maximum_fusion.2.wide_ref, ...), custom_call_target="tpu_custom_call" | custom-call | flops 3000000000 | tf_op jit(solution)/shard_map/pallas_call | solution.py:516
  59.0 1.3 %shard_map.154 = bf16[512,512]{1,0:T(8,128)(2,1)} custom-call(bf16[512,512]{1,0:T(8,128)(2,1)S(1)} %get-tuple-element.54.feat_ref), custom_call_target="tpu_custom_call" | custom-call | flops 2000000000 | tf_op jit(solution)/shard_map/pallas_call | solution.py:510
  60.3 1.1 %collective-permute-done.9 = bf16[240,256]{1,0:T(8,128)(2,1)S(1)} collective-permute-done((bf16[240,256]{1,0:T(8,128)(2,1)}, bf16[240,256]{1,0:T(8,128)(2,1)S(1)}, u32[]{:S(2)}, u32[]{:S(2)}) %collective-permute-start.9) | collective-permute-done | bytes 122912 | tf_op jit(solution)/shard_map/ppermute | solution.py:399
  62.4 1.7 %copy-done.9 = bf16[3,256,1536]{2,1,0:T(8,128)(2,1)S(1)} copy-done((bf16[3,256,1536]{2,1,0:T(8,128)(2,1)S(1)}, bf16[3,256,1536]{2,1,0:T(8,128)(2,1)}, u32[]{:S(2)}) %copy-start.9) | copy-done | bytes 2359320
  64.1 1.0 %copy-done.21 = bf16[12,32,512]{2,1,0:T(8,128)(2,1)S(1)} copy-done((bf16[12,32,512]{2,1,0:T(8,128)(2,1)S(1)}, bf16[12,32,512]{2,1,0:T(8,128)(2,1)}, u32[]{:S(2)}) %copy-start.21) | copy-done | bytes 393240
  65.1 1.0 %copy-done.23 = bf16[12,32,512]{2,1,0:T(8,128)(2,1)S(1)} copy-done((bf16[12,32,512]{2,1,0:T(8,128)(2,1)S(1)}, bf16[12,32,512]{2,1,0:T(8,128)(2,1)}, u32[]{:S(2)}) %copy-start.23) | copy-done | bytes 393240
  66.1 1.0 %copy-done.25 = bf16[12,32,512]{2,1,0:T(8,128)(2,1)S(1)} copy-done((bf16[12,32,512]{2,1,0:T(8,128)(2,1)S(1)}, bf16[12,32,512]{2,1,0:T(8,128)(2,1)}, u32[]{:S(2)}) %copy-start.25) | copy-done | bytes 393240
  68.0 4.0 %shard_map.158 = bf16[384,128]{1,0:T(8,128)(2,1)} custom-call(bf16[12,32,512]{2,1,0:T(8,128)(2,1)S(1)} %copy-done.21, bf16[12,32,512]{2,1,0:T(8,128)(2,1)S(1)} %copy-done.23, bf16[12,32,512]{2,1,0:T(8,128)(2,1)S(1)} %copy-done.25, bf16[10,16,256]{2,1,0:T(8,128)(2,1)S(1)} %get-tuple-element.59.m0, bf16[10,16,256]{2,1,0:T(8,128)(2,1)S(1)} %get-tuple-element.60.m1, ...), custom_call_target="tpu_custom_call" | custom-call | flops 5000000000 | tf_op jit(solution)/shard_map/pallas_call | solution.py:522
  (126 shorter events, 14.2 us)
Async XLA Ops:
  0.6 6.5 %copy-start.43 = (bf16[8,96,64]{1,2,0:T(8,128)(2,1)S(1)}, bf16[8,96,64]{1,2,0:T(8,128)(2,1)}, u32[]{:S(2)}) copy-start(bf16[8,96,64]{1,2,0:T(8,128)(2,1)} %param.22) | copy-start | bytes 294916
  0.7 6.6 %copy-start.44 = (f32[96]{0:T(128)S(1)}, f32[96]{0:T(128)}, u32[]{:S(2)}) copy-start(f32[96]{0:T(128)} %param.23) | copy-start | bytes 1156
  0.7 6.6 %copy-start = (bf16[27,96,96]{2,1,0:T(8,128)(2,1)S(1)}, bf16[27,96,96]{2,1,0:T(8,128)(2,1)}, u32[]{:S(2)}) copy-start(bf16[27,96,96]{2,1,0:T(8,128)(2,1)} %w_ref.4) | copy-start | bytes 1492996
  6.6 2.4 %copy-start.36 = (bf16[128,384]{1,0:T(8,128)(2,1)}, bf16[128,384]{1,0:T(8,128)(2,1)S(1)}, u32[]{:S(2)}) copy-start(bf16[128,384]{1,0:T(8,128)(2,1)S(1)} %get-tuple-element.51.tab2_ref.tab_ref) | copy-start | bytes 294916
  6.7 2.3 %collective-permute-start = (bf16[64,512]{1,0:T(8,128)(2,1)S(1)}, bf16[64,512]{1,0:T(8,128)(2,1)S(1)}, u32[]{:S(2)}, u32[]{:S(2)}) collective-permute-start(bf16[64,512]{1,0:T(8,128)(2,1)S(1)} %bitcast.33), channel_id=1, source_target_pairs={{0,4},{4,0},{1,5},{5,1},{2,6},{6,2},{3,7},{7,3},{8,12},{12,8},{9,1... | collective-permute-start | bytes 196616 | tf_op jit(solution)/shard_map/ppermute | solution.py:399
  7.6 1.4 %copy-start.5 = (bf16[3,256,1536]{2,1,0:T(8,128)(2,1)}, bf16[3,256,1536]{2,1,0:T(8,128)(2,1)S(1)}, u32[]{:S(2)}) copy-start(bf16[3,256,1536]{2,1,0:T(8,128)(2,1)S(1)} %shard_map.155.t_ref.ta_ref) | copy-start | bytes 7077892
  9.0 8.4 %copy-start.2 = (bf16[27,64,64]{2,1,0:T(8,128)(2,1)S(1)}, bf16[27,64,64]{2,1,0:T(8,128)(2,1)}, u32[]{:S(2)}) copy-start(bf16[27,64,64]{2,1,0:T(8,128)(2,1)} %w_ref.3) | copy-start | bytes 663556
  9.0 8.4 %copy-start.3 = (f32[64]{0:T(128)S(1)}, f32[64]{0:T(128)}, u32[]{:S(2)}) copy-start(f32[64]{0:T(128)} %param.19) | copy-start | bytes 772
  9.9 13.4 %collective-permute-start.3 = (bf16[640,128]{1,0:T(8,128)(2,1)}, bf16[640,128]{1,0:T(8,128)(2,1)}, u32[]{:S(2)}, u32[]{:S(2)}) collective-permute-start(bf16[640,128]{1,0:T(8,128)(2,1)} %bitcast.7), channel_id=1, source_target_pairs={{0,4},{1,2},{2,1},{3,7},{4,0},{5,6},{6,5},{7,3},{8,12},{9,10},{10,... | collective-permute-start | bytes 491528 | tf_op jit(solution)/shard_map/ppermute | solution.py:406
  9.9 13.3 %collective-permute-start.4 = (bf16[640,128]{1,0:T(8,128)(2,1)}, bf16[640,128]{1,0:T(8,128)(2,1)}, u32[]{:S(2)}, u32[]{:S(2)}) collective-permute-start(bf16[640,128]{1,0:T(8,128)(2,1)} %bitcast.8), channel_id=1, source_target_pairs={{0,1},{1,0},{2,3},{3,2},{4,5},{5,4},{6,7},{7,6},{8,9},{9,8},{10,11... | collective-permute-start | bytes 491528 | tf_op jit(solution)/shard_map/ppermute | solution.py:399
  14.2 7.6 %collective-permute-start.1 = (bf16[120,512]{1,0:T(8,128)(2,1)S(1)}, bf16[120,512]{1,0:T(8,128)(2,1)S(1)}, u32[]{:S(2)}, u32[]{:S(2)}) collective-permute-start(bf16[120,512]{1,0:T(8,128)(2,1)S(1)} %select_n.260), channel_id=1, source_target_pairs={{0,4},{8,16},{16,8},{24,28},{4,0},{12,20},{20,12},{28,24},{1,5},{9... | collective-permute-start | bytes 368648 | tf_op jit(solution)/shard_map/ppermute | solution.py:406
  14.3 8.6 %collective-permute-start.2 = (bf16[120,512]{1,0:T(8,128)(2,1)S(1)}, bf16[120,512]{1,0:T(8,128)(2,1)S(1)}, u32[]{:S(2)}, u32[]{:S(2)}) collective-permute-start(bf16[120,512]{1,0:T(8,128)(2,1)S(1)} %select_n.262), channel_id=1, source_target_pairs={{0,8},{8,0},{16,24},{24,16},{1,9},{9,1},{17,25},{25,17},{2,10},{10... | collective-permute-start | bytes 368648 | tf_op jit(solution)/shard_map/ppermute | solution.py:399
  17.4 1.5 %copy-start.11 = (bf16[3,256,1152]{2,1,0:T(8,128)(2,1)S(1)}, bf16[3,256,1152]{2,1,0:T(8,128)(2,1)}, u32[]{:S(2)}) copy-start(bf16[3,256,1152]{2,1,0:T(8,128)(2,1)} %copy-done.10) | copy-start | bytes 5308420
  24.3 10.7 %collective-permute-start.5 = (bf16[240,128]{1,0:T(8,128)(2,1)S(1)}, bf16[240,128]{1,0:T(8,128)(2,1)S(1)}, u32[]{:S(2)}, u32[]{:S(2)}) collective-permute-start(bf16[240,128]{1,0:T(8,128)(2,1)S(1)} %select_n.285), channel_id=1, source_target_pairs={{0,4},{1,2},{2,1},{3,7},{4,0},{5,6},{6,5},{7,3},{8,12},{9,10},{10,... | collective-permute-start | bytes 184328 | tf_op jit(solution)/shard_map/ppermute | solution.py:406
  24.4 10.6 %collective-permute-start.6 = (bf16[240,128]{1,0:T(8,128)(2,1)S(1)}, bf16[240,128]{1,0:T(8,128)(2,1)S(1)}, u32[]{:S(2)}, u32[]{:S(2)}) collective-permute-start(bf16[240,128]{1,0:T(8,128)(2,1)S(1)} %select_n.287), channel_id=1, source_target_pairs={{0,1},{1,0},{2,3},{3,2},{4,5},{5,4},{6,7},{7,6},{8,9},{9,8},{10,11... | collective-permute-start | bytes 184328 | tf_op jit(solution)/shard_map/ppermute | solution.py:399
  26.4 1.5 %copy-start.12 = (bf16[3,256,1152]{2,1,0:T(8,128)(2,1)S(1)}, bf16[3,256,1152]{2,1,0:T(8,128)(2,1)}, u32[]{:S(2)}) copy-start(bf16[3,256,1152]{2,1,0:T(8,128)(2,1)} %copy-done.10) | copy-start | bytes 5308420
  27.9 2.8 %copy-start.33 = (bf16[18,32,256]{2,1,0:T(8,128)(2,1)S(1)}, bf16[18,32,256]{2,1,0:T(8,128)(2,1)}, u32[]{:S(2)}) copy-start(bf16[18,32,256]{2,1,0:T(8,128)(2,1)} %copy-done.32) | copy-start | bytes 884740
  30.7 5.1 %copy-start.4 = (f32[64]{0:T(128)S(1)}, f32[64]{0:T(128)}, u32[]{:S(2)}) copy-start(f32[64]{0:T(128)} %param.21) | copy-start | bytes 772
  35.8 1.5 %copy-start.13 = (bf16[3,256,1152]{2,1,0:T(8,128)(2,1)S(1)}, bf16[3,256,1152]{2,1,0:T(8,128)(2,1)}, u32[]{:S(2)}) copy-start(bf16[3,256,1152]{2,1,0:T(8,128)(2,1)} %copy-done.10) | copy-start | bytes 5308420
  37.2 1.5 %copy-start.15 = (bf16[3,256,1152]{2,1,0:T(8,128)(2,1)S(1)}, bf16[3,256,1152]{2,1,0:T(8,128)(2,1)}, u32[]{:S(2)}) copy-start(bf16[3,256,1152]{2,1,0:T(8,128)(2,1)} %copy-done.14) | copy-start | bytes 5308420
  46.4 5.7 %copy-start.1 = (bf16[27,96,96]{2,1,0:T(8,128)(2,1)S(1)}, bf16[27,96,96]{2,1,0:T(8,128)(2,1)}, u32[]{:S(2)}) copy-start(bf16[27,96,96]{2,1,0:T(8,128)(2,1)} %w_ref.5) | copy-start | bytes 1492996
  52.0 1.9 %copy-start.45 = (f32[96]{0:T(128)S(1)}, f32[96]{0:T(128)}, u32[]{:S(2)}) copy-start(f32[96]{0:T(128)} %param.25) | copy-start | bytes 1156
  52.0 1.9 %copy-start.46 = (f32[96]{0:T(128)S(1)}, f32[96]{0:T(128)}, u32[]{:S(2)}) copy-start(f32[96]{0:T(128)} %param.27) | copy-start | bytes 1156
  52.0 4.2 %copy-start.38 = (bf16[128,384]{1,0:T(8,128)(2,1)S(1)}, bf16[128,384]{1,0:T(8,128)(2,1)}, u32[]{:S(2)}) copy-start(bf16[128,384]{1,0:T(8,128)(2,1)} %copy-done.36) | copy-start | bytes 294916
  52.1 1.9 %collective-permute-start.7 = (bf16[40,512]{1,0:T(8,128)(2,1)S(1)}, bf16[40,512]{1,0:T(8,128)(2,1)S(1)}, u32[]{:S(2)}, u32[]{:S(2)}) collective-permute-start(bf16[40,512]{1,0:T(8,128)(2,1)S(1)} %select_n.296), channel_id=1, source_target_pairs={{0,4},{4,0},{1,5},{5,1},{2,6},{6,2},{3,7},{7,3},{8,12},{12,8},{9,1... | collective-permute-start | bytes 122888 | tf_op jit(solution)/shard_map/ppermute | solution.py:399
  52.5 1.4 %copy-start.8 = (bf16[3,256,1536]{2,1,0:T(8,128)(2,1)}, bf16[3,256,1536]{2,1,0:T(8,128)(2,1)S(1)}, u32[]{:S(2)}) copy-start(bf16[3,256,1536]{2,1,0:T(8,128)(2,1)S(1)} %shard_map.157.tb_ref) | copy-start | bytes 7077892
  54.8 5.5 %collective-permute-start.8 = (bf16[240,256]{1,0:T(8,128)(2,1)}, bf16[240,256]{1,0:T(8,128)(2,1)}, u32[]{:S(2)}, u32[]{:S(2)}) collective-permute-start(bf16[240,256]{1,0:T(8,128)(2,1)} %select_n.304), channel_id=1, source_target_pairs={{0,4},{1,2},{2,1},{3,7},{4,0},{5,6},{6,5},{7,3},{8,12},{9,10},{10,... | collective-permute-start | bytes 368648 | tf_op jit(solution)/shard_map/ppermute | solution.py:406
  55.9 5.5 %collective-permute-start.9 = (bf16[240,256]{1,0:T(8,128)(2,1)}, bf16[240,256]{1,0:T(8,128)(2,1)S(1)}, u32[]{:S(2)}, u32[]{:S(2)}) collective-permute-start(bf16[240,256]{1,0:T(8,128)(2,1)} %select_n.306), channel_id=1, source_target_pairs={{0,1},{1,0},{2,3},{3,2},{4,5},{5,4},{6,7},{7,6},{8,9},{9,8},{10,11... | collective-permute-start | bytes 368648 | tf_op jit(solution)/shard_map/ppermute | solution.py:399
  56.2 1.7 %copy-start.6 = (bf16[3,256,1536]{2,1,0:T(8,128)(2,1)S(1)}, bf16[3,256,1536]{2,1,0:T(8,128)(2,1)}, u32[]{:S(2)}) copy-start(bf16[3,256,1536]{2,1,0:T(8,128)(2,1)} %copy-done.5) | copy-start | bytes 7077892
  58.9 1.3 %copy-start.20 = (bf16[12,32,512]{2,1,0:T(8,128)(2,1)}, bf16[12,32,512]{2,1,0:T(8,128)(2,1)S(1)}, u32[]{:S(2)}) copy-start(bf16[12,32,512]{2,1,0:T(8,128)(2,1)S(1)} %get-tuple-element.56.a0) | copy-start | bytes 1179652
  59.0 3.4 %copy-start.7 = (bf16[3,256,1536]{2,1,0:T(8,128)(2,1)S(1)}, bf16[3,256,1536]{2,1,0:T(8,128)(2,1)}, u32[]{:S(2)}) copy-start(bf16[3,256,1536]{2,1,0:T(8,128)(2,1)} %copy-done.5) | copy-start | bytes 7077892
  62.4 1.7 %copy-start.9 = (bf16[3,256,1536]{2,1,0:T(8,128)(2,1)S(1)}, bf16[3,256,1536]{2,1,0:T(8,128)(2,1)}, u32[]{:S(2)}) copy-start(bf16[3,256,1536]{2,1,0:T(8,128)(2,1)} %copy-done.8) | copy-start | bytes 7077892
  (25 other events, 24.9 us)

commit v10 on v9

--- a/solution.py
+++ b/solution.py
@@ -32,7 +32,7 @@
 F32 = jnp.float32
 NN = (((1,), (0,)), ((), ()))
 NT = (((1,), (1,)), ((), ()))
-VMEM_BYTES = 40 * 1024 * 1024
+VMEM_BYTES = 20 * 1024 * 1024
 
 
 def mm(a, b, dims=NN):

time: 72.8 us -> 72.8 us (level)
  no operation moved by 1% of the time
where the time goes in v10:
time: 72.8 us; the launch traced here: 72 us
  local copies, waits for them, and re-layouts  32.2 us (44%)
  Pallas kernels  22.3 us (31%)
  starting transfers between devices  10.7 us (15%)
  other arithmetic  3.15 us (4%)
  waiting for transfers between devices  2.35 us (3%)
  between operations  1.21 us (2%)
    unnamed x94, local copies, waits for them, and re-layouts  30.5 us
    ppermute x6, starting transfers between devices, trade(): one = lax.ppermute(first, axis, [(i, i ^ 1) for i in range(count)])  10 us
    pallas_call x1, Pallas kernels, local(): pl.pallas_call(level_one_kernel, out_shape=[shaped(Y1 * X1, lanes1), shap...  5.55 us
    pallas_call x1, Pallas kernels, local(): pl.pallas_call(down1_kernel, in_specs=[pl.BlockSpec(memory_space=pltpu.HB...  4.73 us
    pallas_call x1, Pallas kernels, local(): pl.pallas_call(level_two_kernel, out_shape=shaped(C2 * Z2, Y2 * X2), scra...  4.02 us
    ppermute x6, waiting for transfers between devices, trade(): one = lax.ppermute(first, axis, [(i, i ^ 1) for i in range(count)])  2.34 us
    pallas_call x1, Pallas kernels, local(): pl.pallas_call(outer_kernel, out_shape=[shaped(rows, X1, 256), shaped(row...  2.13 us
    select_n x3, other arithmetic, trade(): jnp.where(index < count - 1, jnp.where(even, one, two), jnp.zeros_like(one))  1.96 us
  transfers between devices with their start and end apart: 10, of which 2 were waited for; matrix products, arithmetic and copies ran while one was open for 2% of the time, Pallas kernels for 11%

profile of v10, /device:TPU:0, one launch (start us, length us, event | category | flops | bytes accessed | tf_op | source)
XLA Modules:
  0.0 72.0 jit_solution(522609913981846817)
XLA Ops:
  0.7 4.7 %shard_map.149 = (bf16[16,32,512]{2,1,0:T(8,128)(2,1)S(1)}, bf16[3,256,1152]{2,1,0:T(8,128)(2,1)S(1)}, bf16[128,384]{1,0:T(8,128)(2,1)S(1)}, bf16[128,384]{1,0:T(8,128)(2,1)S(1)}) custom-call(bf16[48,2,8,2048]{3,2,1,0:T(8,128)(2,1)} %bitcast.34, bf16[8,48,64]{2,1,0:T(8,128)(2,1)} %bitcast.35, f32[1,64]{1,0:T(1,128)} %bitcast.37, s32[8,4,32]{2,1,0:T(4,128)} %bitcast.36, ...), custom_call_target="tpu_custom_call" | custom-call | flops 4000000000 | tf_op jit(solution)/shard_map/pallas_call | solution.py:445
  5.4 1.2 %copy-done.10 = bf16[3,256,1152]{2,1,0:T(8,128)(2,1)} copy-done((bf16[3,256,1152]{2,1,0:T(8,128)(2,1)}, bf16[3,256,1152]{2,1,0:T(8,128)(2,1)S(1)}, u32[]{:S(2)}) %copy-start.10) | copy-done | bytes 1769496
  7.6 1.4 %copy-done.5 = bf16[3,256,1536]{2,1,0:T(8,128)(2,1)} copy-done((bf16[3,256,1536]{2,1,0:T(8,128)(2,1)}, bf16[3,256,1536]{2,1,0:T(8,128)(2,1)S(1)}, u32[]{:S(2)}) %copy-start.5) | copy-done | bytes 2359320
  9.9 4.2 %collective-permute-start.4 = (bf16[640,128]{1,0:T(8,128)(2,1)}, bf16[640,128]{1,0:T(8,128)(2,1)}, u32[]{:S(2)}, u32[]{:S(2)}) collective-permute-start(bf16[640,128]{1,0:T(8,128)(2,1)} %bitcast.8), channel_id=1, source_target_pairs={{0,1},{1,0},{2,3},{3,2},{4,5},{5,4},{6,7},{7,6},{8,9},{9,8},{10,11... | collective-permute-start | bytes 491528 | tf_op jit(solution)/shard_map/ppermute | solution.py:399
  14.3 3.0 %collective-permute-start.2 = (bf16[120,512]{1,0:T(8,128)(2,1)S(1)}, bf16[120,512]{1,0:T(8,128)(2,1)S(1)}, u32[]{:S(2)}, u32[]{:S(2)}) collective-permute-start(bf16[120,512]{1,0:T(8,128)(2,1)S(1)} %select_n.262), channel_id=1, source_target_pairs={{0,8},{8,0},{16,24},{24,16},{1,9},{9,1},{17,25},{25,17},{2,10},{10... | collective-permute-start | bytes 368648 | tf_op jit(solution)/shard_map/ppermute | solution.py:399
  17.4 1.5 %copy-done.11 = bf16[3,256,1152]{2,1,0:T(8,128)(2,1)S(1)} copy-done((bf16[3,256,1152]{2,1,0:T(8,128)(2,1)S(1)}, bf16[3,256,1152]{2,1,0:T(8,128)(2,1)}, u32[]{:S(2)}) %copy-start.11) | copy-done | bytes 1769496
  18.9 1.7 %shard_map.150 = (bf16[20,32,512]{2,1,0:T(8,128)(2,1)S(1)}, bf16[20,32,512]{2,1,0:T(8,128)(2,1)S(1)}, bf16[18,32,256]{2,1,0:T(8,128)(2,1)S(1)}, bf16[3,256,1152]{2,1,0:T(8,128)(2,1)S(1)}) custom-call(bf16[20,32,512]{2,1,0:T(8,128)(2,1)S(1)} %pad_maximum_fusion.win_ref, bf16[3,256,1152]{2,1,0:T(8,128)(2,1)S(1)} %copy-done.11, f32[1,64]{1,0:T(1,128)S(1)} %bitcast.25, ...), custom_call_target="tpu_custom_call" | custom-call | flops 3000000000 | tf_op jit(solution)/shard_map/pallas_call | solution.py:468
  20.5 1.2 %copy-done.14 = bf16[3,256,1152]{2,1,0:T(8,128)(2,1)} copy-done((bf16[3,256,1152]{2,1,0:T(8,128)(2,1)}, bf16[3,256,1152]{2,1,0:T(8,128)(2,1)S(1)}, u32[]{:S(2)}) %copy-start.14) | copy-done | bytes 1769496
  21.8 1.2 %collective-permute-done.2 = bf16[120,512]{1,0:T(8,128)(2,1)S(1)} collective-permute-done((bf16[120,512]{1,0:T(8,128)(2,1)S(1)}, bf16[120,512]{1,0:T(8,128)(2,1)S(1)}, u32[]{:S(2)}, u32[]{:S(2)}) %collective-permute-start.2) | collective-permute-done | bytes 122912 | tf_op jit(solution)/shard_map/ppermute | solution.py:399
  23.3 1.0 %select_select_fusion = (bf16[640,128]{1,0:T(8,128)(2,1)S(1)}, bf16[640,128]{1,0:T(8,128)(2,1)S(1)}) fusion(bf16[640,128]{1,0:T(8,128)(2,1)} %collective-permute-done.4, bf16[640,128]{1,0:T(8,128)(2,1)} %collective-permute-done.3, pred[]{:T(512)S(6)} %lt.49, pred[]{:T(512)S(6)} %eq.33, pred[]{:T(512)S(6)} %gt.14), kind=kLoop, calls=%fused_computation.3 | loop fusion | flops 327680 | bytes 655363 | tf_op jit(solution)/shard_map/jit(_where)/select_n | solution.py:408
  24.4 2.0 %collective-permute-start.6 = (bf16[240,128]{1,0:T(8,128)(2,1)S(1)}, bf16[240,128]{1,0:T(8,128)(2,1)S(1)}, u32[]{:S(2)}, u32[]{:S(2)}) collective-permute-start(bf16[240,128]{1,0:T(8,128)(2,1)S(1)} %select_n.287), channel_id=1, source_target_pairs={{0,1},{1,0},{2,3},{3,2},{4,5},{5,4},{6,7},{7,6},{8,9},{9,8},{10,11... | collective-permute-start | bytes 184328 | tf_op jit(solution)/shard_map/ppermute | solution.py:399
  26.4 1.5 %copy-done.12 = bf16[3,256,1152]{2,1,0:T(8,128)(2,1)S(1)} copy-done((bf16[3,256,1152]{2,1,0:T(8,128)(2,1)S(1)}, bf16[3,256,1152]{2,1,0:T(8,128)(2,1)}, u32[]{:S(2)}) %copy-start.12) | copy-done | bytes 1769496
  27.9 2.1 %shard_map.152 = (bf16[18,32,256]{2,1,0:T(8,128)(2,1)S(1)}, bf16[18,32,128]{2,1,0:T(8,128)(2,1)S(1)}) custom-call(bf16[20,32,512]{2,1,0:T(8,128)(2,1)S(1)} %pad_maximum_fusion.win_ref, bf16[20,32,512]{2,1,0:T(8,128)(2,1)S(1)} %get-tuple-element.46.left_ref, bf16[20,32,512]{2,1,0:T(8,128)(2,1)S(1)} %get-tuple-element.47.right_ref, ...), custom_call_target="tpu_custom_call" | custom-call | flops 4000000000 | tf_op jit(solution)/shard_map/pallas_call | solution.py:478
  30.7 1.3 %shard_map.151 = (bf16[20,16,512]{2,1,0:T(8,128)(2,1)S(1)}, bf16[20,16,512]{2,1,0:T(8,128)(2,1)S(1)}, bf16[20,16,512]{2,1,0:T(8,128)(2,1)S(1)}, bf16[18,48,256]{...) custom-call(bf16[20,6,512]{2,1,0:T(8,128)(2,1)S(1)} %reshape.87.xl_ref, ...), custom_call_target="tpu_custom_call" | custom-call | flops 3000000000 | tf_op jit(solution)/shard_map/pallas_call | solution.py:487
  35.8 1.5 %copy-done.13 = bf16[3,256,1152]{2,1,0:T(8,128)(2,1)S(1)} copy-done((bf16[3,256,1152]{2,1,0:T(8,128)(2,1)S(1)}, bf16[3,256,1152]{2,1,0:T(8,128)(2,1)}, u32[]{:S(2)}) %copy-start.13) | copy-done | bytes 1769496
  37.2 1.5 %copy-done.15 = bf16[3,256,1152]{2,1,0:T(8,128)(2,1)S(1)} copy-done((bf16[3,256,1152]{2,1,0:T(8,128)(2,1)S(1)}, bf16[3,256,1152]{2,1,0:T(8,128)(2,1)}, u32[]{:S(2)}) %copy-start.15) | copy-done | bytes 1769496
  38.7 1.0 %copy-done.17 = bf16[18,48,256]{2,1,0:T(8,128)(2,1)S(1)} copy-done((bf16[18,48,256]{2,1,0:T(8,128)(2,1)S(1)}, bf16[18,48,256]{2,1,0:T(8,128)(2,1)}, u32[]{:S(2)}) %copy-start.17) | copy-done | bytes 442392
  39.7 1.0 %copy-done.19 = bf16[18,48,256]{2,1,0:T(8,128)(2,1)S(1)} copy-done((bf16[18,48,256]{2,1,0:T(8,128)(2,1)S(1)}, bf16[18,48,256]{2,1,0:T(8,128)(2,1)}, u32[]{:S(2)}) %copy-start.19) | copy-done | bytes 442392
  40.7 1.0 %copy-done.27 = bf16[20,16,512]{2,1,0:T(8,128)(2,1)S(1)} copy-done((bf16[20,16,512]{2,1,0:T(8,128)(2,1)S(1)}, bf16[20,16,512]{2,1,0:T(8,128)(2,1)}, u32[]{:S(2)}) %copy-start.27) | copy-done | bytes 327704
  41.7 1.0 %copy-done.29 = bf16[20,16,512]{2,1,0:T(8,128)(2,1)S(1)} copy-done((bf16[20,16,512]{2,1,0:T(8,128)(2,1)S(1)}, bf16[20,16,512]{2,1,0:T(8,128)(2,1)}, u32[]{:S(2)}) %copy-start.29) | copy-done | bytes 327704
  42.7 1.0 %copy-done.31 = bf16[20,16,512]{2,1,0:T(8,128)(2,1)S(1)} copy-done((bf16[20,16,512]{2,1,0:T(8,128)(2,1)S(1)}, bf16[20,16,512]{2,1,0:T(8,128)(2,1)}, u32[]{:S(2)}) %copy-start.31) | copy-done | bytes 327704
  46.4 5.5 %shard_map.153 = (bf16[512,512]{1,0:T(8,128)(2,1)S(1)}, bf16[8,20,512]{2,1,0:T(8,128)(2,1)S(1)}) custom-call(bf16[20,32,128]{2,1,0:T(8,128)(2,1)S(1)} %bitcast.24, bf16[20,32,128]{2,1,0:T(8,128)(2,1)S(1)} %bitcast.22, bf16[20,12,128]{2,1,0:T(8,128)(2,1)S(1)} %reshape.91.cl_ref, bf16[20,12,128]{2,1,0:T(8,128)(2,1)S(1)} %reshape.92.cr_ref, ...), custom_call_target="tpu_custom_call" | custom-call | flops 6000000000 | tf_op jit(solution)/shard_map/pallas_call | solution.py:493
  52.5 1.4 %copy-done.8 = bf16[3,256,1536]{2,1,0:T(8,128)(2,1)} copy-done((bf16[3,256,1536]{2,1,0:T(8,128)(2,1)}, bf16[3,256,1536]{2,1,0:T(8,128)(2,1)S(1)}, u32[]{:S(2)}) %copy-start.8) | copy-done | bytes 2359320
  56.2 1.7 %copy-done.6 = bf16[3,256,1536]{2,1,0:T(8,128)(2,1)S(1)} copy-done((bf16[3,256,1536]{2,1,0:T(8,128)(2,1)S(1)}, bf16[3,256,1536]{2,1,0:T(8,128)(2,1)}, u32[]{:S(2)}) %copy-start.6) | copy-done | bytes 2359320
  57.9 1.0 %shard_map.156 = (bf16[12,32,512]{2,1,0:T(8,128)(2,1)S(1)}, bf16[12,32,512]{2,1,0:T(8,128)(2,1)S(1)}, bf16[12,32,512]{2,1,0:T(8,128)(2,1)S(1)}, bf16[10,16,256]{...) custom-call(bf16[12,20,512]{2,1,0:T(8,128)(2,1)S(1)} %pad_maximum_fusion.2.wide_ref, ...), custom_call_target="tpu_custom_call" | custom-call | flops 3000000000 | tf_op jit(solution)/shard_map/pallas_call | solution.py:516
  59.0 1.3 %shard_map.154 = bf16[512,512]{1,0:T(8,128)(2,1)} custom-call(bf16[512,512]{1,0:T(8,128)(2,1)S(1)} %get-tuple-element.54.feat_ref), custom_call_target="tpu_custom_call" | custom-call | flops 2000000000 | tf_op jit(solution)/shard_map/pallas_call | solution.py:510
  60.3 1.1 %collective-permute-done.9 = bf16[240,256]{1,0:T(8,128)(2,1)S(1)} collective-permute-done((bf16[240,256]{1,0:T(8,128)(2,1)}, bf16[240,256]{1,0:T(8,128)(2,1)S(1)}, u32[]{:S(2)}, u32[]{:S(2)}) %collective-permute-start.9) | collective-permute-done | bytes 122912 | tf_op jit(solution)/shard_map/ppermute | solution.py:399
  62.4 1.7 %copy-done.9 = bf16[3,256,1536]{2,1,0:T(8,128)(2,1)S(1)} copy-done((bf16[3,256,1536]{2,1,0:T(8,128)(2,1)S(1)}, bf16[3,256,1536]{2,1,0:T(8,128)(2,1)}, u32[]{:S(2)}) %copy-start.9) | copy-done | bytes 2359320
  64.1 1.0 %copy-done.21 = bf16[12,32,512]{2,1,0:T(8,128)(2,1)S(1)} copy-done((bf16[12,32,512]{2,1,0:T(8,128)(2,1)S(1)}, bf16[12,32,512]{2,1,0:T(8,128)(2,1)}, u32[]{:S(2)}) %copy-start.21) | copy-done | bytes 393240
  65.1 1.0 %copy-done.23 = bf16[12,32,512]{2,1,0:T(8,128)(2,1)S(1)} copy-done((bf16[12,32,512]{2,1,0:T(8,128)(2,1)S(1)}, bf16[12,32,512]{2,1,0:T(8,128)(2,1)}, u32[]{:S(2)}) %copy-start.23) | copy-done | bytes 393240
  66.1 1.0 %copy-done.25 = bf16[12,32,512]{2,1,0:T(8,128)(2,1)S(1)} copy-done((bf16[12,32,512]{2,1,0:T(8,128)(2,1)S(1)}, bf16[12,32,512]{2,1,0:T(8,128)(2,1)}, u32[]{:S(2)}) %copy-start.25) | copy-done | bytes 393240
  68.0 4.0 %shard_map.158 = bf16[384,128]{1,0:T(8,128)(2,1)} custom-call(bf16[12,32,512]{2,1,0:T(8,128)(2,1)S(1)} %copy-done.21, bf16[12,32,512]{2,1,0:T(8,128)(2,1)S(1)} %copy-done.23, bf16[12,32,512]{2,1,0:T(8,128)(2,1)S(1)} %copy-done.25, bf16[10,16,256]{2,1,0:T(8,128)(2,1)S(1)} %get-tuple-element.59.m0, bf16[10,16,256]{2,1,0:T(8,128)(2,1)S(1)} %get-tuple-element.60.m1, ...), custom_call_target="tpu_custom_call" | custom-call | flops 5000000000 | tf_op jit(solution)/shard_map/pallas_call | solution.py:522
  (126 shorter events, 14.2 us)
Async XLA Ops:
  0.6 6.5 %copy-start.43 = (bf16[8,96,64]{1,2,0:T(8,128)(2,1)S(1)}, bf16[8,96,64]{1,2,0:T(8,128)(2,1)}, u32[]{:S(2)}) copy-start(bf16[8,96,64]{1,2,0:T(8,128)(2,1)} %param.22) | copy-start | bytes 294916
  0.7 6.6 %copy-start.44 = (f32[96]{0:T(128)S(1)}, f32[96]{0:T(128)}, u32[]{:S(2)}) copy-start(f32[96]{0:T(128)} %param.23) | copy-start | bytes 1156
  0.7 6.6 %copy-start = (bf16[27,96,96]{2,1,0:T(8,128)(2,1)S(1)}, bf16[27,96,96]{2,1,0:T(8,128)(2,1)}, u32[]{:S(2)}) copy-start(bf16[27,96,96]{2,1,0:T(8,128)(2,1)} %w_ref.4) | copy-start | bytes 1492996
  6.6 2.4 %copy-start.36 = (bf16[128,384]{1,0:T(8,128)(2,1)}, bf16[128,384]{1,0:T(8,128)(2,1)S(1)}, u32[]{:S(2)}) copy-start(bf16[128,384]{1,0:T(8,128)(2,1)S(1)} %get-tuple-element.51.tab2_ref.tab_ref) | copy-start | bytes 294916
  6.7 2.3 %collective-permute-start = (bf16[64,512]{1,0:T(8,128)(2,1)S(1)}, bf16[64,512]{1,0:T(8,128)(2,1)S(1)}, u32[]{:S(2)}, u32[]{:S(2)}) collective-permute-start(bf16[64,512]{1,0:T(8,128)(2,1)S(1)} %bitcast.33), channel_id=1, source_target_pairs={{0,4},{4,0},{1,5},{5,1},{2,6},{6,2},{3,7},{7,3},{8,12},{12,8},{9,1... | collective-permute-start | bytes 196616 | tf_op jit(solution)/shard_map/ppermute | solution.py:399
  7.6 1.4 %copy-start.5 = (bf16[3,256,1536]{2,1,0:T(8,128)(2,1)}, bf16[3,256,1536]{2,1,0:T(8,128)(2,1)S(1)}, u32[]{:S(2)}) copy-start(bf16[3,256,1536]{2,1,0:T(8,128)(2,1)S(1)} %shard_map.155.t_ref.ta_ref) | copy-start | bytes 7077892
  9.0 8.4 %copy-start.2 = (bf16[27,64,64]{2,1,0:T(8,128)(2,1)S(1)}, bf16[27,64,64]{2,1,0:T(8,128)(2,1)}, u32[]{:S(2)}) copy-start(bf16[27,64,64]{2,1,0:T(8,128)(2,1)} %w_ref.3) | copy-start | bytes 663556
  9.0 8.4 %copy-start.3 = (f32[64]{0:T(128)S(1)}, f32[64]{0:T(128)}, u32[]{:S(2)}) copy-start(f32[64]{0:T(128)} %param.19) | copy-start | bytes 772
  9.9 13.4 %collective-permute-start.3 = (bf16[640,128]{1,0:T(8,128)(2,1)}, bf16[640,128]{1,0:T(8,128)(2,1)}, u32[]{:S(2)}, u32[]{:S(2)}) collective-permute-start(bf16[640,128]{1,0:T(8,128)(2,1)} %bitcast.7), channel_id=1, source_target_pairs={{0,4},{1,2},{2,1},{3,7},{4,0},{5,6},{6,5},{7,3},{8,12},{9,10},{10,... | collective-permute-start | bytes 491528 | tf_op jit(solution)/shard_map/ppermute | solution.py:406
  9.9 13.3 %collective-permute-start.4 = (bf16[640,128]{1,0:T(8,128)(2,1)}, bf16[640,128]{1,0:T(8,128)(2,1)}, u32[]{:S(2)}, u32[]{:S(2)}) collective-permute-start(bf16[640,128]{1,0:T(8,128)(2,1)} %bitcast.8), channel_id=1, source_target_pairs={{0,1},{1,0},{2,3},{3,2},{4,5},{5,4},{6,7},{7,6},{8,9},{9,8},{10,11... | collective-permute-start | bytes 491528 | tf_op jit(solution)/shard_map/ppermute | solution.py:399
  14.2 7.6 %collective-permute-start.1 = (bf16[120,512]{1,0:T(8,128)(2,1)S(1)}, bf16[120,512]{1,0:T(8,128)(2,1)S(1)}, u32[]{:S(2)}, u32[]{:S(2)}) collective-permute-start(bf16[120,512]{1,0:T(8,128)(2,1)S(1)} %select_n.260), channel_id=1, source_target_pairs={{0,4},{8,16},{16,8},{24,28},{4,0},{12,20},{20,12},{28,24},{1,5},{9... | collective-permute-start | bytes 368648 | tf_op jit(solution)/shard_map/ppermute | solution.py:406
  14.3 8.6 %collective-permute-start.2 = (bf16[120,512]{1,0:T(8,128)(2,1)S(1)}, bf16[120,512]{1,0:T(8,128)(2,1)S(1)}, u32[]{:S(2)}, u32[]{:S(2)}) collective-permute-start(bf16[120,512]{1,0:T(8,128)(2,1)S(1)} %select_n.262), channel_id=1, source_target_pairs={{0,8},{8,0},{16,24},{24,16},{1,9},{9,1},{17,25},{25,17},{2,10},{10... | collective-permute-start | bytes 368648 | tf_op jit(solution)/shard_map/ppermute | solution.py:399
  17.4 1.5 %copy-start.11 = (bf16[3,256,1152]{2,1,0:T(8,128)(2,1)S(1)}, bf16[3,256,1152]{2,1,0:T(8,128)(2,1)}, u32[]{:S(2)}) copy-start(bf16[3,256,1152]{2,1,0:T(8,128)(2,1)} %copy-done.10) | copy-start | bytes 5308420
  24.3 10.7 %collective-permute-start.5 = (bf16[240,128]{1,0:T(8,128)(2,1)S(1)}, bf16[240,128]{1,0:T(8,128)(2,1)S(1)}, u32[]{:S(2)}, u32[]{:S(2)}) collective-permute-start(bf16[240,128]{1,0:T(8,128)(2,1)S(1)} %select_n.285), channel_id=1, source_target_pairs={{0,4},{1,2},{2,1},{3,7},{4,0},{5,6},{6,5},{7,3},{8,12},{9,10},{10,... | collective-permute-start | bytes 184328 | tf_op jit(solution)/shard_map/ppermute | solution.py:406
  24.4 10.6 %collective-permute-start.6 = (bf16[240,128]{1,0:T(8,128)(2,1)S(1)}, bf16[240,128]{1,0:T(8,128)(2,1)S(1)}, u32[]{:S(2)}, u32[]{:S(2)}) collective-permute-start(bf16[240,128]{1,0:T(8,128)(2,1)S(1)} %select_n.287), channel_id=1, source_target_pairs={{0,1},{1,0},{2,3},{3,2},{4,5},{5,4},{6,7},{7,6},{8,9},{9,8},{10,11... | collective-permute-start | bytes 184328 | tf_op jit(solution)/shard_map/ppermute | solution.py:399
  26.4 1.5 %copy-start.12 = (bf16[3,256,1152]{2,1,0:T(8,128)(2,1)S(1)}, bf16[3,256,1152]{2,1,0:T(8,128)(2,1)}, u32[]{:S(2)}) copy-start(bf16[3,256,1152]{2,1,0:T(8,128)(2,1)} %copy-done.10) | copy-start | bytes 5308420
  27.9 2.8 %copy-start.33 = (bf16[18,32,256]{2,1,0:T(8,128)(2,1)S(1)}, bf16[18,32,256]{2,1,0:T(8,128)(2,1)}, u32[]{:S(2)}) copy-start(bf16[18,32,256]{2,1,0:T(8,128)(2,1)} %copy-done.32) | copy-start | bytes 884740
  30.7 5.1 %copy-start.4 = (f32[64]{0:T(128)S(1)}, f32[64]{0:T(128)}, u32[]{:S(2)}) copy-start(f32[64]{0:T(128)} %param.21) | copy-start | bytes 772
  35.8 1.5 %copy-start.13 = (bf16[3,256,1152]{2,1,0:T(8,128)(2,1)S(1)}, bf16[3,256,1152]{2,1,0:T(8,128)(2,1)}, u32[]{:S(2)}) copy-start(bf16[3,256,1152]{2,1,0:T(8,128)(2,1)} %copy-done.10) | copy-start | bytes 5308420
  37.2 1.5 %copy-start.15 = (bf16[3,256,1152]{2,1,0:T(8,128)(2,1)S(1)}, bf16[3,256,1152]{2,1,0:T(8,128)(2,1)}, u32[]{:S(2)}) copy-start(bf16[3,256,1152]{2,1,0:T(8,128)(2,1)} %copy-done.14) | copy-start | bytes 5308420
  46.4 5.7 %copy-start.1 = (bf16[27,96,96]{2,1,0:T(8,128)(2,1)S(1)}, bf16[27,96,96]{2,1,0:T(8,128)(2,1)}, u32[]{:S(2)}) copy-start(bf16[27,96,96]{2,1,0:T(8,128)(2,1)} %w_ref.5) | copy-start | bytes 1492996
  52.0 1.9 %copy-start.45 = (f32[96]{0:T(128)S(1)}, f32[96]{0:T(128)}, u32[]{:S(2)}) copy-start(f32[96]{0:T(128)} %param.25) | copy-start | bytes 1156
  52.0 1.9 %copy-start.46 = (f32[96]{0:T(128)S(1)}, f32[96]{0:T(128)}, u32[]{:S(2)}) copy-start(f32[96]{0:T(128)} %param.27) | copy-start | bytes 1156
  52.0 4.2 %copy-start.38 = (bf16[128,384]{1,0:T(8,128)(2,1)S(1)}, bf16[128,384]{1,0:T(8,128)(2,1)}, u32[]{:S(2)}) copy-start(bf16[128,384]{1,0:T(8,128)(2,1)} %copy-done.36) | copy-start | bytes 294916
  52.1 1.9 %collective-permute-start.7 = (bf16[40,512]{1,0:T(8,128)(2,1)S(1)}, bf16[40,512]{1,0:T(8,128)(2,1)S(1)}, u32[]{:S(2)}, u32[]{:S(2)}) collective-permute-start(bf16[40,512]{1,0:T(8,128)(2,1)S(1)} %select_n.296), channel_id=1, source_target_pairs={{0,4},{4,0},{1,5},{5,1},{2,6},{6,2},{3,7},{7,3},{8,12},{12,8},{9,1... | collective-permute-start | bytes 122888 | tf_op jit(solution)/shard_map/ppermute | solution.py:399
  52.5 1.4 %copy-start.8 = (bf16[3,256,1536]{2,1,0:T(8,128)(2,1)}, bf16[3,256,1536]{2,1,0:T(8,128)(2,1)S(1)}, u32[]{:S(2)}) copy-start(bf16[3,256,1536]{2,1,0:T(8,128)(2,1)S(1)} %shard_map.157.tb_ref) | copy-start | bytes 7077892
  54.8 5.5 %collective-permute-start.8 = (bf16[240,256]{1,0:T(8,128)(2,1)}, bf16[240,256]{1,0:T(8,128)(2,1)}, u32[]{:S(2)}, u32[]{:S(2)}) collective-permute-start(bf16[240,256]{1,0:T(8,128)(2,1)} %select_n.304), channel_id=1, source_target_pairs={{0,4},{1,2},{2,1},{3,7},{4,0},{5,6},{6,5},{7,3},{8,12},{9,10},{10,... | collective-permute-start | bytes 368648 | tf_op jit(solution)/shard_map/ppermute | solution.py:406
  55.9 5.5 %collective-permute-start.9 = (bf16[240,256]{1,0:T(8,128)(2,1)}, bf16[240,256]{1,0:T(8,128)(2,1)S(1)}, u32[]{:S(2)}, u32[]{:S(2)}) collective-permute-start(bf16[240,256]{1,0:T(8,128)(2,1)} %select_n.306), channel_id=1, source_target_pairs={{0,1},{1,0},{2,3},{3,2},{4,5},{5,4},{6,7},{7,6},{8,9},{9,8},{10,11... | collective-permute-start | bytes 368648 | tf_op jit(solution)/shard_map/ppermute | solution.py:399
  56.2 1.7 %copy-start.6 = (bf16[3,256,1536]{2,1,0:T(8,128)(2,1)S(1)}, bf16[3,256,1536]{2,1,0:T(8,128)(2,1)}, u32[]{:S(2)}) copy-start(bf16[3,256,1536]{2,1,0:T(8,128)(2,1)} %copy-done.5) | copy-start | bytes 7077892
  58.9 1.3 %copy-start.20 = (bf16[12,32,512]{2,1,0:T(8,128)(2,1)}, bf16[12,32,512]{2,1,0:T(8,128)(2,1)S(1)}, u32[]{:S(2)}) copy-start(bf16[12,32,512]{2,1,0:T(8,128)(2,1)S(1)} %get-tuple-element.56.a0) | copy-start | bytes 1179652
  59.0 3.4 %copy-start.7 = (bf16[3,256,1536]{2,1,0:T(8,128)(2,1)S(1)}, bf16[3,256,1536]{2,1,0:T(8,128)(2,1)}, u32[]{:S(2)}) copy-start(bf16[3,256,1536]{2,1,0:T(8,128)(2,1)} %copy-done.5) | copy-start | bytes 7077892
  62.4 1.7 %copy-start.9 = (bf16[3,256,1536]{2,1,0:T(8,128)(2,1)S(1)}, bf16[3,256,1536]{2,1,0:T(8,128)(2,1)}, u32[]{:S(2)}) copy-start(bf16[3,256,1536]{2,1,0:T(8,128)(2,1)} %copy-done.8) | copy-start | bytes 7077892
  (25 other events, 24.9 us)

commit v11 on v10

--- a/solution.py
+++ b/solution.py
@@ -410,11 +410,8 @@
 
 
 def shift_along(low_edge, high_edge, axis):
-    shape = low_edge.shape
-    low, high = (edge.reshape(-1, shape[-1]) for edge in (low_edge, high_edge))
     even = lax.axis_index(axis) % 2 == 0
-    below, above = trade(jnp.where(even, high, low), jnp.where(even, low, high), axis)
-    return below.reshape(shape), above.reshape(shape)
+    return trade(jnp.where(even, high_edge, low_edge), jnp.where(even, low_edge, high_edge), axis)
 
 
 def params():

time: 72.8 us -> 45.6 us (0.63)
  local copies, waits for them, and re-layouts: 32.2 us -> 0.3 us
  waiting for transfers between devices: 2.35 us -> 9.57 us
  other arithmetic: 3.15 us -> 0.52 us
  starting transfers between devices: 10.7 us -> 11.5 us
    unnamed x94 -> x18, local copies, waits for them, and re-layouts: 30.5 us -> 0.25 us
    ppermute x6, waiting for transfers between devices: 2.34 us -> 9.56 us  [trade(): one = lax.ppermute(first, axis, [(i, i ^ 1) for i in range(count)])]
    select_n x3, other arithmetic: 1.96 us -> 0.07 us  [trade(): jnp.where(index < count - 1, jnp.where(even, one, two), jnp.zeros_like(one))]
    select_n x7 -> x0, local copies, waits for them, and re-layouts: 1.51 us -> none  [the longest x4 0.76 us: shift_along(): jnp.where(even, high, low)]
    select_n x6, other arithmetic: 0.89 us -> 0.14 us  [the longest x5 0.09 us: shift_along(): jnp.where(even, high_edge, low_edge)]
  transfers between devices with their start and end apart: 10 -> 10, of which waited for: 2 -> 4; matrix products, arithmetic and copies ran while one was open for 2% -> 1% of each run, Pallas kernels for 11% -> 18%
where the time goes in v11:
time: 45.6 us; the launch traced here: 45.4 us
  Pallas kernels  22.6 us (50%)
  starting transfers between devices  11.5 us (25%)
  waiting for transfers between devices  9.57 us (21%)
  between operations  0.99 us (2%)
  other arithmetic  0.52 us (1%)
    ppermute x6, starting transfers between devices, trade(): one = lax.ppermute(first, axis, [(i, i ^ 1) for i in range(count)])  10.7 us
    ppermute x6, waiting for transfers between devices, trade(): one = lax.ppermute(first, axis, [(i, i ^ 1) for i in range(count)])  9.56 us
    pallas_call x1, Pallas kernels, local(): pl.pallas_call(level_one_kernel, out_shape=[shaped(Y1 * X1, lanes1), shap...  5.62 us
    pallas_call x1, Pallas kernels, local(): pl.pallas_call(down1_kernel, in_specs=[pl.BlockSpec(memory_space=pltpu.HB...  4.73 us
    pallas_call x1, Pallas kernels, local(): pl.pallas_call(level_two_kernel, out_shape=shaped(C2 * Z2, Y2 * X2), scra...  4.04 us
    pallas_call x1, Pallas kernels, local(): pl.pallas_call(outer_kernel, out_shape=[shaped(rows, X1, 256), shaped(row...  2.18 us
    pallas_call x1, Pallas kernels, local(): pl.pallas_call(middle_kernel, out_shape=[shaped(ROWS1, X1, lanes1), shape...  1.71 us
    pallas_call x1, Pallas kernels, local(): pl.pallas_call(edge_middle_kernel, out_shape=[shaped(ROWS1, EDGE, lanes1)...  1.32 us
  transfers between devices with their start and end apart: 10, of which 4 were waited for; matrix products, arithmetic and copies ran while one was open for 1% of the time, Pallas kernels for 18%

profile of v11, /device:TPU:0, one launch (start us, length us, event | category | flops | bytes accessed | tf_op | source)
XLA Modules:
  0.0 45.4 jit_solution(14864560995939866987)
XLA Ops:
  0.7 4.7 %shard_map.149 = (bf16[16,32,512]{2,1,0:T(8,128)(2,1)S(1)}, bf16[3,256,1152]{2,1,0:T(8,128)(2,1)S(1)}, bf16[128,384]{1,0:T(8,128)(2,1)S(1)}, bf16[128,384]{1,0:T(8,128)(2,1)S(1)}) custom-call(bf16[48,2,8,2048]{3,2,1,0:T(8,128)(2,1)} %bitcast.20, bf16[8,48,64]{2,1,0:T(8,128)(2,1)} %bitcast.21, f32[1,64]{1,0:T(1,128)} %bitcast.23, s32[8,4,32]{2,1,0:T(4,128)} %bitcast.22, ...), custom_call_target="tpu_custom_call" | custom-call | flops 4000000000 | tf_op jit(solution)/shard_map/pallas_call | solution.py:442
  5.4 0.5 %collective-permute-start = (bf16[2,32,512]{2,1,0:T(8,128)(2,1)S(1)}, bf16[2,32,512]{2,1,0:T(8,128)(2,1)S(1)}, u32[]{:S(2)}, u32[]{:S(2)}) collective-permute-start(bf16[2,32,512]{2,1,0:T(8,128)(2,1)S(1)} %slice_select_fusion), channel_id=1, source_target_pairs={{0,4},{4,0},{1,5},{5,1},{2,6},{6,2},{3,7},{7,3},{8,12},{12,8},{9,1... | collective-permute-start | bytes 196616 | tf_op jit(solution)/shard_map/ppermute | solution.py:399
  6.0 0.0 copy-start.2
  6.0 0.0 copy-start.3
  6.0 0.3 shard_map.155.t_ref.ta_ref
  6.4 0.5 %collective-permute-done = bf16[2,32,512]{2,1,0:T(8,128)(2,1)S(1)} collective-permute-done((bf16[2,32,512]{2,1,0:T(8,128)(2,1)S(1)}, bf16[2,32,512]{2,1,0:T(8,128)(2,1)S(1)}, u32[]{:S(2)}, u32[]{:S(2)}) %collective-permute-start) | collective-permute-done | bytes 65568 | tf_op jit(solution)/shard_map/ppermute | solution.py:399
  6.9 0.1 pad_maximum_fusion.win_ref
  7.0 0.4 collective-permute-start.3
  7.4 4.2 %collective-permute-start.4 = (bf16[20,32,128]{2,1,0:T(8,128)(2,1)S(1)}, bf16[20,32,128]{2,1,0:T(8,128)(2,1)S(1)}, u32[]{:S(2)}, u32[]{:S(2)}) collective-permute-start(bf16[20,32,128]{2,1,0:T(8,128)(2,1)S(1)} %get-tuple-element.62), channel_id=1, source_target_pairs={{0,1},{1,0},{2,3},{3,2},{4,5},{5,4},{6,7},{7,6},{8,9},{9,8},{10,11... | collective-permute-start | bytes 491528 | tf_op jit(solution)/shard_map/ppermute | solution.py:399
  11.6 0.1 broadcast_select_fusion.3
  11.6 0.1 collective-permute-start.1
  11.7 3.0 %collective-permute-start.2 = (bf16[20,6,512]{2,1,0:T(8,128)(2,1)S(1)}, bf16[20,6,512]{2,1,0:T(8,128)(2,1)S(1)}, u32[]{:S(2)}, u32[]{:S(2)}) collective-permute-start(bf16[20,6,512]{2,1,0:T(8,128)(2,1)S(1)} %get-tuple-element.65), channel_id=1, source_target_pairs={{0,8},{8,0},{16,24},{24,16},{1,9},{9,1},{17,25},{25,17},{2,10},{10... | collective-permute-start | bytes 368648 | tf_op jit(solution)/shard_map/ppermute | solution.py:399
  14.7 1.7 %shard_map.150 = (bf16[20,32,512]{2,1,0:T(8,128)(2,1)S(1)}, bf16[20,32,512]{2,1,0:T(8,128)(2,1)S(1)}, bf16[18,32,256]{2,1,0:T(8,128)(2,1)S(1)}, bf16[3,256,1152]{2,1,0:T(8,128)(2,1)S(1)}) custom-call(bf16[20,32,512]{2,1,0:T(8,128)(2,1)S(1)} %pad_maximum_fusion.win_ref, bf16[3,256,1152]{2,1,0:T(8,128)(2,1)S(1)} %get-tuple-element.33.t_ref.ta_ref, ...), custom_call_target="tpu_custom_call" | custom-call | flops 3000000000 | tf_op jit(solution)/shard_map/pallas_call | solution.py:465
  16.4 5.5 %collective-permute-done.2 = bf16[20,6,512]{2,1,0:T(8,128)(2,1)S(1)} collective-permute-done((bf16[20,6,512]{2,1,0:T(8,128)(2,1)S(1)}, bf16[20,6,512]{2,1,0:T(8,128)(2,1)S(1)}, u32[]{:S(2)}, u32[]{:S(2)}) %collective-permute-start.2) | collective-permute-done | bytes 122912 | tf_op jit(solution)/shard_map/ppermute | solution.py:399
  21.9 0.1 pad_maximum_fusion.1
  22.1 0.1 collective-permute-start.5
  22.2 2.2 %collective-permute-start.6 = (bf16[20,12,128]{2,1,0:T(8,128)(2,1)S(1)}, bf16[20,12,128]{2,1,0:T(8,128)(2,1)S(1)}, u32[]{:S(2)}, u32[]{:S(2)}) collective-permute-start(bf16[20,12,128]{2,1,0:T(8,128)(2,1)S(1)} %get-tuple-element.66), channel_id=1, source_target_pairs={{0,1},{1,0},{2,3},{3,2},{4,5},{5,4},{6,7},{7,6},{8,9},{9,8},{10,11... | collective-permute-start | bytes 184328 | tf_op jit(solution)/shard_map/ppermute | solution.py:399
  24.4 2.2 %shard_map.152 = (bf16[18,32,256]{2,1,0:T(8,128)(2,1)S(1)}, bf16[18,32,128]{2,1,0:T(8,128)(2,1)S(1)}) custom-call(bf16[20,32,512]{2,1,0:T(8,128)(2,1)S(1)} %pad_maximum_fusion.win_ref, bf16[20,32,512]{2,1,0:T(8,128)(2,1)S(1)} %get-tuple-element.46.left_ref, bf16[20,32,512]{2,1,0:T(8,128)(2,1)S(1)} %get-tuple-element.47.right_ref, ...), custom_call_target="tpu_custom_call" | custom-call | flops 4000000000 | tf_op jit(solution)/shard_map/pallas_call | solution.py:475
  26.6 0.0 copy-start.4
  26.6 1.3 %shard_map.151 = (bf16[20,16,512]{2,1,0:T(8,128)(2,1)S(1)}, bf16[20,16,512]{2,1,0:T(8,128)(2,1)S(1)}, bf16[20,16,512]{2,1,0:T(8,128)(2,1)S(1)}, bf16[18,48,256]{...) custom-call(bf16[20,6,512]{2,1,0:T(8,128)(2,1)S(1)} %get-tuple-element.70.xl_ref, ...), custom_call_target="tpu_custom_call" | custom-call | flops 3000000000 | tf_op jit(solution)/shard_map/pallas_call | solution.py:484
  28.0 5.6 %shard_map.153 = (bf16[512,512]{1,0:T(8,128)(2,1)S(1)}, bf16[8,20,512]{2,1,0:T(8,128)(2,1)S(1)}) custom-call(bf16[20,32,128]{2,1,0:T(8,128)(2,1)S(1)} %get-tuple-element.36.zl_ref, bf16[20,32,128]{2,1,0:T(8,128)(2,1)S(1)} %get-tuple-element.37.zr_ref, bf16[20,12,128]{2,1,0:T(8,128)(2,1)S(1)} %get-tuple-element.77.cl_ref, ...), custom_call_target="tpu_custom_call" | custom-call | flops 6000000000 | tf_op jit(solution)/shard_map/pallas_call | solution.py:490
  33.7 0.1 collective-permute-start.7
  33.7 0.3 shard_map.157.tb_ref
  34.1 0.2 copy-done.7
  34.3 0.0 copy-done.8
  34.3 0.7 %collective-permute-done.7 = bf16[2,20,512]{2,1,0:T(8,128)(2,1)S(1)} collective-permute-done((bf16[2,20,512]{2,1,0:T(8,128)(2,1)S(1)}, bf16[2,20,512]{2,1,0:T(8,128)(2,1)S(1)}, u32[]{:S(2)}, u32[]{:S(2)}) %collective-permute-start.7) | collective-permute-done | bytes 40992 | tf_op jit(solution)/shard_map/ppermute | solution.py:399
  35.0 0.2 collective-permute-start.8
  35.3 0.8 %collective-permute-start.9 = (bf16[12,20,256]{2,1,0:T(8,128)(2,1)S(1)}, bf16[12,20,256]{2,1,0:T(8,128)(2,1)S(1)}, u32[]{:S(2)}, u32[]{:S(2)}) collective-permute-start(bf16[12,20,256]{2,1,0:T(8,128)(2,1)S(1)} %get-tuple-element.74), channel_id=1, source_target_pairs={{0,1},{1,0},{2,3},{3,2},{4,5},{5,4},{6,7},{7,6},{8,9},{9,8},{10,11... | collective-permute-start | bytes 368648 | tf_op jit(solution)/shard_map/ppermute | solution.py:399
  36.1 1.0 %shard_map.156 = (bf16[12,32,512]{2,1,0:T(8,128)(2,1)S(1)}, bf16[12,32,512]{2,1,0:T(8,128)(2,1)S(1)}, bf16[12,32,512]{2,1,0:T(8,128)(2,1)S(1)}, bf16[10,16,256]{...) custom-call(bf16[12,20,512]{2,1,0:T(8,128)(2,1)S(1)} %pad_maximum_fusion.2.wide_ref, ...), custom_call_target="tpu_custom_call" | custom-call | flops 3000000000 | tf_op jit(solution)/shard_map/pallas_call | solution.py:513
  37.1 1.3 %shard_map.154 = bf16[512,512]{1,0:T(8,128)(2,1)} custom-call(bf16[512,512]{1,0:T(8,128)(2,1)S(1)} %get-tuple-element.54.feat_ref), custom_call_target="tpu_custom_call" | custom-call | flops 2000000000 | tf_op jit(solution)/shard_map/pallas_call | solution.py:507
  38.4 3.0 %collective-permute-done.9 = bf16[12,20,256]{2,1,0:T(8,128)(2,1)S(1)} collective-permute-done((bf16[12,20,256]{2,1,0:T(8,128)(2,1)S(1)}, bf16[12,20,256]{2,1,0:T(8,128)(2,1)S(1)}, u32[]{:S(2)}, u32[]{:S(2)}) %collective-permute-start.9) | collective-permute-done | bytes 122912 | tf_op jit(solution)/shard_map/ppermute | solution.py:399
  41.4 4.0 %shard_map.158 = bf16[384,128]{1,0:T(8,128)(2,1)} custom-call(bf16[12,32,512]{2,1,0:T(8,128)(2,1)S(1)} %get-tuple-element.56.a0, bf16[12,32,512]{2,1,0:T(8,128)(2,1)S(1)} %get-tuple-element.57.a1, bf16[12,32,512]{2,1,0:T(8,128)(2,1)S(1)} %get-tuple-element.58.a2, bf16[10,16,256]{2,1,0:T(8,128)(2,1)S(1)} %get-tuple-element.59.m0, ...), custom_call_target="tpu_custom_call" | custom-call | flops 5000000000 | tf_op jit(solution)/shard_map/pallas_call | solution.py:519
  (35 shorter events, 0.4 us)
Async XLA Ops:
  0.6 5.3 %copy-start.5 = (bf16[8,96,64]{1,2,0:T(8,128)(2,1)S(1)}, bf16[8,96,64]{1,2,0:T(8,128)(2,1)}, u32[]{:S(2)}) copy-start(bf16[8,96,64]{1,2,0:T(8,128)(2,1)} %param.22) | copy-start | bytes 294916
  0.7 5.3 %copy-start.6 = (f32[96]{0:T(128)S(1)}, f32[96]{0:T(128)}, u32[]{:S(2)}) copy-start(f32[96]{0:T(128)} %param.23) | copy-start | bytes 1156
  0.7 5.3 %copy-start = (bf16[27,96,96]{2,1,0:T(8,128)(2,1)S(1)}, bf16[27,96,96]{2,1,0:T(8,128)(2,1)}, u32[]{:S(2)}) copy-start(bf16[27,96,96]{2,1,0:T(8,128)(2,1)} %w_ref.4) | copy-start | bytes 1492996
  5.4 1.4 %collective-permute-start = (bf16[2,32,512]{2,1,0:T(8,128)(2,1)S(1)}, bf16[2,32,512]{2,1,0:T(8,128)(2,1)S(1)}, u32[]{:S(2)}, u32[]{:S(2)}) collective-permute-start(bf16[2,32,512]{2,1,0:T(8,128)(2,1)S(1)} %slice_select_fusion), channel_id=1, source_target_pairs={{0,4},{4,0},{1,5},{5,1},{2,6},{6,2},{3,7},{7,3},{8,12},{12,8},{9,1... | collective-permute-start | bytes 196616 | tf_op jit(solution)/shard_map/ppermute | solution.py:399
  6.0 8.7 %copy-start.2 = (bf16[27,64,64]{2,1,0:T(8,128)(2,1)S(1)}, bf16[27,64,64]{2,1,0:T(8,128)(2,1)}, u32[]{:S(2)}) copy-start(bf16[27,64,64]{2,1,0:T(8,128)(2,1)} %w_ref.3) | copy-start | bytes 663556
  6.0 8.6 %copy-start.3 = (f32[64]{0:T(128)S(1)}, f32[64]{0:T(128)}, u32[]{:S(2)}) copy-start(f32[64]{0:T(128)} %param.19) | copy-start | bytes 772
  7.0 15.0 %collective-permute-start.3 = (bf16[20,32,128]{2,1,0:T(8,128)(2,1)S(1)}, bf16[20,32,128]{2,1,0:T(8,128)(2,1)S(1)}, u32[]{:S(2)}, u32[]{:S(2)}) collective-permute-start(bf16[20,32,128]{2,1,0:T(8,128)(2,1)S(1)} %get-tuple-element.63), channel_id=1, source_target_pairs={{0,4},{1,2},{2,1},{3,7},{4,0},{5,6},{6,5},{7,3},{8,12},{9,10},{10,... | collective-permute-start | bytes 491528 | tf_op jit(solution)/shard_map/ppermute | solution.py:406
  7.4 14.6 %collective-permute-start.4 = (bf16[20,32,128]{2,1,0:T(8,128)(2,1)S(1)}, bf16[20,32,128]{2,1,0:T(8,128)(2,1)S(1)}, u32[]{:S(2)}, u32[]{:S(2)}) collective-permute-start(bf16[20,32,128]{2,1,0:T(8,128)(2,1)S(1)} %get-tuple-element.62), channel_id=1, source_target_pairs={{0,1},{1,0},{2,3},{3,2},{4,5},{5,4},{6,7},{7,6},{8,9},{9,8},{10,11... | collective-permute-start | bytes 491528 | tf_op jit(solution)/shard_map/ppermute | solution.py:399
  11.6 4.8 %collective-permute-start.1 = (bf16[20,6,512]{2,1,0:T(8,128)(2,1)S(1)}, bf16[20,6,512]{2,1,0:T(8,128)(2,1)S(1)}, u32[]{:S(2)}, u32[]{:S(2)}) collective-permute-start(bf16[20,6,512]{2,1,0:T(8,128)(2,1)S(1)} %get-tuple-element.64), channel_id=1, source_target_pairs={{0,4},{8,16},{16,8},{24,28},{4,0},{12,20},{20,12},{28,24},{1,5},{9... | collective-permute-start | bytes 368648 | tf_op jit(solution)/shard_map/ppermute | solution.py:406
  11.7 10.1 %collective-permute-start.2 = (bf16[20,6,512]{2,1,0:T(8,128)(2,1)S(1)}, bf16[20,6,512]{2,1,0:T(8,128)(2,1)S(1)}, u32[]{:S(2)}, u32[]{:S(2)}) collective-permute-start(bf16[20,6,512]{2,1,0:T(8,128)(2,1)S(1)} %get-tuple-element.65), channel_id=1, source_target_pairs={{0,8},{8,0},{16,24},{24,16},{1,9},{9,1},{17,25},{25,17},{2,10},{10... | collective-permute-start | bytes 368648 | tf_op jit(solution)/shard_map/ppermute | solution.py:399
  22.1 5.8 %collective-permute-start.5 = (bf16[20,12,128]{2,1,0:T(8,128)(2,1)S(1)}, bf16[20,12,128]{2,1,0:T(8,128)(2,1)S(1)}, u32[]{:S(2)}, u32[]{:S(2)}) collective-permute-start(bf16[20,12,128]{2,1,0:T(8,128)(2,1)S(1)} %get-tuple-element.67), channel_id=1, source_target_pairs={{0,4},{1,2},{2,1},{3,7},{4,0},{5,6},{6,5},{7,3},{8,12},{9,10},{10,... | collective-permute-start | bytes 184328 | tf_op jit(solution)/shard_map/ppermute | solution.py:406
  22.2 5.8 %collective-permute-start.6 = (bf16[20,12,128]{2,1,0:T(8,128)(2,1)S(1)}, bf16[20,12,128]{2,1,0:T(8,128)(2,1)S(1)}, u32[]{:S(2)}, u32[]{:S(2)}) collective-permute-start(bf16[20,12,128]{2,1,0:T(8,128)(2,1)S(1)} %get-tuple-element.66), channel_id=1, source_target_pairs={{0,1},{1,0},{2,3},{3,2},{4,5},{5,4},{6,7},{7,6},{8,9},{9,8},{10,11... | collective-permute-start | bytes 184328 | tf_op jit(solution)/shard_map/ppermute | solution.py:399
  26.6 1.4 %copy-start.4 = (f32[64]{0:T(128)S(1)}, f32[64]{0:T(128)}, u32[]{:S(2)}) copy-start(f32[64]{0:T(128)} %param.21) | copy-start | bytes 772
  28.0 5.8 %copy-start.1 = (bf16[27,96,96]{2,1,0:T(8,128)(2,1)S(1)}, bf16[27,96,96]{2,1,0:T(8,128)(2,1)}, u32[]{:S(2)}) copy-start(bf16[27,96,96]{2,1,0:T(8,128)(2,1)} %w_ref.5) | copy-start | bytes 1492996
  33.6 0.7 %copy-start.7 = (f32[96]{0:T(128)S(1)}, f32[96]{0:T(128)}, u32[]{:S(2)}) copy-start(f32[96]{0:T(128)} %param.25) | copy-start | bytes 1156
  33.6 0.7 %copy-start.8 = (f32[96]{0:T(128)S(1)}, f32[96]{0:T(128)}, u32[]{:S(2)}) copy-start(f32[96]{0:T(128)} %param.27) | copy-start | bytes 1156
  33.7 1.3 %collective-permute-start.7 = (bf16[2,20,512]{2,1,0:T(8,128)(2,1)S(1)}, bf16[2,20,512]{2,1,0:T(8,128)(2,1)S(1)}, u32[]{:S(2)}, u32[]{:S(2)}) collective-permute-start(bf16[2,20,512]{2,1,0:T(8,128)(2,1)S(1)} %slice_select_fusion.1), channel_id=1, source_target_pairs={{0,4},{4,0},{1,5},{5,1},{2,6},{6,2},{3,7},{7,3},{8,12},{12,8},{9,1... | collective-permute-start | bytes 122888 | tf_op jit(solution)/shard_map/ppermute | solution.py:399
  35.0 3.4 %collective-permute-start.8 = (bf16[12,20,256]{2,1,0:T(8,128)(2,1)S(1)}, bf16[12,20,256]{2,1,0:T(8,128)(2,1)S(1)}, u32[]{:S(2)}, u32[]{:S(2)}) collective-permute-start(bf16[12,20,256]{2,1,0:T(8,128)(2,1)S(1)} %get-tuple-element.75), channel_id=1, source_target_pairs={{0,4},{1,2},{2,1},{3,7},{4,0},{5,6},{6,5},{7,3},{8,12},{9,10},{10,... | collective-permute-start | bytes 368648 | tf_op jit(solution)/shard_map/ppermute | solution.py:406
  35.3 6.1 %collective-permute-start.9 = (bf16[12,20,256]{2,1,0:T(8,128)(2,1)S(1)}, bf16[12,20,256]{2,1,0:T(8,128)(2,1)S(1)}, u32[]{:S(2)}, u32[]{:S(2)}) collective-permute-start(bf16[12,20,256]{2,1,0:T(8,128)(2,1)S(1)} %get-tuple-element.74), channel_id=1, source_target_pairs={{0,1},{1,0},{2,3},{3,2},{4,5},{5,4},{6,7},{7,6},{8,9},{9,8},{10,11... | collective-permute-start | bytes 368648 | tf_op jit(solution)/shard_map/ppermute | solution.py:399

commit v12 on v11

--- a/solution.py
+++ b/solution.py
@@ -1,3 +1,5 @@
+import itertools
+
 import jax
 import jax.numpy as jnp
 from jax import lax
@@ -230,9 +232,8 @@
 
 
 def fill_edges(copies, pieces):
-    pitch = copies[0].shape[1]
     for i, copy in enumerate(copies):
-        line = [pieces[0][:, i:]] + pieces[1:]
+        line = [pieces[0][:, i:]] + pieces[1:] if i < 2 else pieces[1:]
         if i:
             line.append(jnp.zeros((copy.shape[0], i, pieces[0].shape[2]), BF))
         copy[...] = jnp.concatenate(line, axis=1)
@@ -259,11 +260,16 @@
             copy[:, X1:, cut] = jnp.concatenate([edge[:, i:], jnp.zeros((rows, i, 128), BF)], axis=1)
 
 
+def column_lanes(field, lane, stride=Z1 * C1):
+    return [field[:, :, first : first + 128] for first in range(lane, field.shape[2], stride)]
+
+
 def edge_middle_kernel(xl_ref, win_ref, xr_ref, g_ref, t_ref, b_ref, tab_ref, e0, e1, e2, m0, m1, m2):
     for lane in range(0, Z1 * C1, 128):
         cut = slice(lane, lane + 128)
         inner = win_ref[:, :, cut]
-        pieces = [xl_ref[:, :, cut], inner[:, :2], inner[:, X1 - 2 :], xr_ref[:, :, cut]]
+        left, right = (column_lanes(ref, lane) for ref in (xl_ref, xr_ref))
+        pieces = left + [inner[:, :2], inner[:, X1 - 2 :]] + right
         fill_edges([e.at[:, :, cut] for e in (e0, e1, e2)], pieces)
     here = edge_masks(tab_ref)[1]
     edge_group([[(e, 128, 384)] for e in (e0, e1, e2)], t_ref, b_ref, (here, here), g_ref, (m0, m1, m2))
@@ -275,8 +281,9 @@
 ):
     own, mid, low, high = (e0, e1, e2), (m0, m1, m2), (i0, i1, i2), (j0, j1, j2)
     for z_ref, c_ref, copies in ((zl_ref, cl_ref, (l0, l1, l2)), (zr_ref, cr_ref, (h0, h1, h2))):
-        inner, corner = z_ref[...], c_ref[...]
-        fill_edges(copies, [corner[:, :HALO_X], inner[:, :2], inner[:, X1 - 2 :], corner[:, HALO_X:]])
+        inner = z_ref[...]
+        corner = column_lanes(c_ref, 0, 128)
+        fill_edges(copies, corner[:3] + [inner[:, :2], inner[:, X1 - 2 :]] + corner[3:])
     below, here, above = edge_masks(tab_ref)
     taps = [[(z, 0, 128), (e, 0, 256)] for z, e in zip((l0, l1, l2), own)]
     edge_group(taps, ta_ref, ba_ref, (below, here), g1_ref, low)
@@ -379,39 +386,45 @@
     out_ref[...] = mm(order, jnp.concatenate(feat, axis=1), NT).astype(BF)
 
 
-def swap_pairs(count, cores, cores_first):
-    def place(y, i):
-        return y * count + i if cores_first else i * cores + y
-
+def partner(index, second, count):
+    other = index + 1 if index % 2 == second else index - 1
+    return other if 0 <= other < count else None
+
+
+def swap(value, moves):
+    axes = ("gx", "gy", "gz")
+    sizes = [lax.axis_size(axis) for axis in axes]
     pairs = []
-    for y in range(cores):
-        for i in range(count):
-            other = i + 1 if i % 2 else i - 1
-            target = place(y, other) if 0 <= other < count else place(y ^ 1, i)
-            pairs.append((place(y, i), target))
-    return pairs
-
-
-def trade(first, second, axis):
-    count = lax.axis_size(axis)
+    for source in itertools.product(*(range(size) for size in sizes)):
+        target = [partner(i, moves[axis], size) if axis in moves else i for i, axis, size in zip(source, axes, sizes)]
+        if None in target:
+            other = sizes[1] - 1 - source[1] if "gy" in moves else source[1] ^ 1
+            target = [source[0], other, source[2]]
+        pairs.append(tuple((x * sizes[1] + y) * sizes[2] + z for x, y, z in (source, target)))
+    return lax.ppermute(value, axes, pairs)
+
+
+def parity(axis):
+    return lax.axis_index(axis) % 2 == 0
+
+
+def sides(first, second, axis):
     index = lax.axis_index(axis)
-    even = index % 2 == 0
-    one = lax.ppermute(first, axis, [(i, i ^ 1) for i in range(count)])
-    two = one
-    if count > 2 and axis == "gy":
-        pairs = [(0, count - 1), (count - 1, 0)] + [(i, i - 1 + i % 2 * 2) for i in range(1, count - 1)]
-        two = lax.ppermute(second, axis, pairs)
-    elif count > 2:
-        axes = ("gx", "gy") if axis == "gx" else ("gy", "gz")
-        two = lax.ppermute(second, axes, swap_pairs(count, lax.axis_size("gy"), axis == "gz"))
-    below = jnp.where(index > 0, jnp.where(even, two, one), jnp.zeros_like(one))
-    above = jnp.where(index < count - 1, jnp.where(even, one, two), jnp.zeros_like(one))
+    even = parity(axis)
+    below = jnp.where(index > 0, jnp.where(even, second, first), jnp.zeros_like(first))
+    above = jnp.where(index < lax.axis_size(axis) - 1, jnp.where(even, first, second), jnp.zeros_like(first))
     return below, above
 
 
 def shift_along(low_edge, high_edge, axis):
-    even = lax.axis_index(axis) % 2 == 0
-    return trade(jnp.where(even, high_edge, low_edge), jnp.where(even, low_edge, high_edge), axis)
+    even = parity(axis)
+    first = swap(jnp.where(even, high_edge, low_edge), {axis: 0})
+    second = swap(jnp.where(even, low_edge, high_edge), {axis: 1}) if lax.axis_size(axis) > 2 else first
+    return sides(first, second, axis)
+
+
+def column_pairs(field):
+    return jnp.concatenate([field[:, i : i + 2] for i in range(0, field.shape[1], 2)], axis=2)
 
 
 def params():
@@ -460,18 +473,20 @@
     y_below, y_above = shift_along(own[:HALO], own[Y1 - HALO :], "gy")
     win = jnp.concatenate([y_below, own, y_above], axis=0)
     z_below, z_above = shift_along(win[:, :, :128], win[:, :, lanes1 - 128 :], "gz")
-    x_below, x_above = shift_along(win[:, :HALO_X], win[:, X1 - HALO_X :], "gx")
+    low, high = win[:, :HALO_X], win[:, X1 - HALO_X :]
+    x_below, x_above = shift_along(column_pairs(low), column_pairs(high), "gx")
     rows = Y1 + 2
     left, right, g2, t1b = pl.pallas_call(
         middle_kernel,
         out_shape=[shaped(ROWS1, X1, lanes1), shaped(ROWS1, X1, lanes1), shaped(rows, X1, 256), banded_shape(4, C1)],
         compiler_params=params(),
-        cost_estimate=cost(3e-6),
+        cost_estimate=cost(1e-7),
     )(win, t1a, bias1a, tab1, w_conv1b)
 
-    corner = jnp.concatenate([x_below, x_above], axis=1)
-    corner, z_below, z_above, g2 = lax.optimization_barrier((corner, z_below, z_above, g2))
-    corner_below, corner_above = shift_along(corner[:, :, :128], corner[:, :, lanes1 - 128 :], "gz")
+    corner = [jnp.concatenate(column_lanes(x, at), axis=2) for at in (0, lanes1 - 128) for x in (x_below, x_above)]
+    low, high = jnp.concatenate(corner[:2], axis=2), jnp.concatenate(corner[2:], axis=2)
+    low, high, g2 = lax.optimization_barrier((low, high, g2))
+    corner_below, corner_above = shift_along(low, high, "gz")
     g1, g3 = pl.pallas_call(
         outer_kernel,
         out_shape=[shaped(rows, X1, 256), shaped(rows, X1, 128)],

time: 45.6 us -> 43.9 us (0.963)
  waiting for transfers between devices: 9.57 us -> 4.42 us
  starting transfers between devices: 11.5 us -> 13.1 us
  Pallas kernels: 22.6 us -> 23.5 us
    ppermute x10, waiting for transfers between devices: 9.57 us -> 4.42 us  [swap(): return lax.ppermute(value, axes, pairs)]
    ppermute x10, starting transfers between devices: 11.5 us -> 13.1 us  [swap(): return lax.ppermute(value, axes, pairs)]
    pallas_call x1, Pallas kernels: 1.32 us -> 2.07 us  [local(): pl.pallas_call(edge_middle_kernel, out_shape=[shaped(ROWS1, EDGE, lanes1)...]
    select_n x12, other arithmetic: 0.28 us -> 0.81 us  [the longest x4 0.43 us: sides(): jnp.where(index < lax.axis_size(axis) - 1, jnp.where(even, first, second)...]
  transfers between devices with their start and end apart: 10 -> 10, of which waited for: 4 -> 4; matrix products, arithmetic and copies ran while one was open for 1% -> 1% of each run, Pallas kernels for 18% -> 20%
where the time goes in v12:
time: 43.9 us; the launch traced here: 43.7 us
  Pallas kernels  23.5 us (54%)
  starting transfers between devices  13.1 us (30%)
  waiting for transfers between devices  4.42 us (10%)
  between operations  1.03 us (2%)
  other arithmetic  0.94 us (2%)
  local copies, waits for them, and re-layouts  0.66 us (2%)
    ppermute x10, starting transfers between devices, swap(): return lax.ppermute(value, axes, pairs)  13.1 us
    pallas_call x1, Pallas kernels, local(): pl.pallas_call(level_one_kernel, out_shape=[shaped(Y1 * X1, lanes1), shap...  5.84 us
    pallas_call x1, Pallas kernels, local(): pl.pallas_call(down1_kernel, in_specs=[pl.BlockSpec(memory_space=pltpu.HB...  4.73 us
    ppermute x10, waiting for transfers between devices, swap(): return lax.ppermute(value, axes, pairs)  4.42 us
    pallas_call x1, Pallas kernels, local(): pl.pallas_call(level_two_kernel, out_shape=shaped(C2 * Z2, Y2 * X2), scra...  4.04 us
    pallas_call x1, Pallas kernels, local(): pl.pallas_call(outer_kernel, out_shape=[shaped(rows, X1, 256), shaped(row...  2.15 us
    pallas_call x1, Pallas kernels, local(): pl.pallas_call(edge_middle_kernel, out_shape=[shaped(ROWS1, EDGE, lanes1)...  2.07 us
    pallas_call x1, Pallas kernels, local(): pl.pallas_call(middle_kernel, out_shape=[shaped(ROWS1, X1, lanes1), shape...  1.71 us
  transfers between devices with their start and end apart: 10, of which 4 were waited for; matrix products, arithmetic and copies ran while one was open for 1% of the time, Pallas kernels for 20%

profile of v12, /device:TPU:0, one launch (start us, length us, event | category | flops | bytes accessed | tf_op | source)
XLA Modules:
  0.0 43.7 jit_solution(10393630845949087613)
XLA Ops:
  0.7 4.7 %shard_map.149 = (bf16[16,32,512]{2,1,0:T(8,128)(2,1)S(1)}, bf16[3,256,1152]{2,1,0:T(8,128)(2,1)S(1)}, bf16[128,384]{1,0:T(8,128)(2,1)S(1)}, bf16[128,384]{1,0:T(8,128)(2,1)S(1)}) custom-call(bf16[48,2,8,2048]{3,2,1,0:T(8,128)(2,1)} %bitcast.28, bf16[8,48,64]{2,1,0:T(8,128)(2,1)} %bitcast.29, f32[1,64]{1,0:T(1,128)} %bitcast.31, s32[8,4,32]{2,1,0:T(4,128)} %bitcast.30, ...), custom_call_target="tpu_custom_call" | custom-call | flops 4000000000 | tf_op jit(solution)/shard_map/pallas_call | solution.py:455
  5.4 0.5 %collective-permute-start = (bf16[2,32,512]{2,1,0:T(8,128)(2,1)S(1)}, bf16[2,32,512]{2,1,0:T(8,128)(2,1)S(1)}, u32[]{:S(2)}, u32[]{:S(2)}) collective-permute-start(bf16[2,32,512]{2,1,0:T(8,128)(2,1)S(1)} %slice_select_fusion), channel_id=1, source_target_pairs={{0,4},{1,5},{2,6},{3,7},{4,0},{5,1},{6,2},{7,3},{8,12},{9,13},{10,... | collective-permute-start | bytes 196616 | tf_op jit(solution)/shard_map/ppermute | solution.py:404
  6.0 0.3 shard_map.155.t_ref.ta_ref
  6.3 0.0 copy-start
  6.4 0.5 %collective-permute-done = bf16[2,32,512]{2,1,0:T(8,128)(2,1)S(1)} collective-permute-done((bf16[2,32,512]{2,1,0:T(8,128)(2,1)S(1)}, bf16[2,32,512]{2,1,0:T(8,128)(2,1)S(1)}, u32[]{:S(2)}, u32[]{:S(2)}) %collective-permute-start) | collective-permute-done | bytes 65568 | tf_op jit(solution)/shard_map/ppermute | solution.py:404
  6.9 0.1 pad_maximum_fusion.win_ref
  7.0 0.2 fusion
  7.2 0.3 broadcast_select_fusion.3
  7.4 0.4 collective-permute-start.3
  7.8 4.0 %collective-permute-start.4 = (bf16[20,2,1536]{2,1,0:T(2,128)(2,1)S(1)}, bf16[20,2,1536]{2,1,0:T(2,128)(2,1)S(1)}, u32[]{:S(2)}, u32[]{:S(2)}) collective-permute-start(bf16[20,2,1536]{2,1,0:T(2,128)(2,1)S(1)} %get-tuple-element.76), channel_id=1, source_target_pairs={{0,8},{1,9},{2,10},{3,11},{4,12},{5,13},{6,14},{7,15},{8,0},{9,1},... | collective-permute-start | bytes 368648 | tf_op jit(solution)/shard_map/ppermute | solution.py:404
  11.9 0.1 collective-permute-start.1
  11.9 3.1 %collective-permute-start.2 = (bf16[20,32,128]{2,1,0:T(8,128)(2,1)S(1)}, bf16[20,32,128]{2,1,0:T(8,128)(2,1)S(1)}, u32[]{:S(2)}, u32[]{:S(2)}) collective-permute-start(bf16[20,32,128]{2,1,0:T(8,128)(2,1)S(1)} %get-tuple-element.66), channel_id=1, source_target_pairs={{0,1},{1,0},{2,3},{3,2},{4,5},{5,4},{6,7},{7,6},{8,9},{9,8},{10,11... | collective-permute-start | bytes 491528 | tf_op jit(solution)/shard_map/ppermute | solution.py:404
  15.1 1.7 %shard_map.150 = (bf16[20,32,512]{2,1,0:T(8,128)(2,1)S(1)}, bf16[20,32,512]{2,1,0:T(8,128)(2,1)S(1)}, bf16[18,32,256]{2,1,0:T(8,128)(2,1)S(1)}, bf16[3,256,1152]{2,1,0:T(8,128)(2,1)S(1)}) custom-call(bf16[20,32,512]{2,1,0:T(8,128)(2,1)S(1)} %pad_maximum_fusion.win_ref, bf16[3,256,1152]{2,1,0:T(8,128)(2,1)S(1)} %get-tuple-element.32.t_ref.ta_ref, ...), custom_call_target="tpu_custom_call" | custom-call | flops 100000000 | tf_op jit(solution)/shard_map/pallas_call | solution.py:479
  16.8 1.0 %collective-permute-done.4 = bf16[20,2,1536]{2,1,0:T(2,128)(2,1)S(1)} collective-permute-done((bf16[20,2,1536]{2,1,0:T(2,128)(2,1)S(1)}, bf16[20,2,1536]{2,1,0:T(2,128)(2,1)S(1)}, u32[]{:S(2)}, u32[]{:S(2)}) %collective-permute-start.4) | collective-permute-done | bytes 122912 | tf_op jit(solution)/shard_map/ppermute | solution.py:404
  17.8 0.2 broadcast_select_fusion
  18.3 0.1 collective-permute-start.5
  18.4 3.1 %collective-permute-start.6 = (bf16[20,2,768]{2,1,0:T(2,128)(2,1)S(1)}, bf16[20,2,768]{2,1,0:T(2,128)(2,1)S(1)}, u32[]{:S(2)}, u32[]{:S(2)}) collective-permute-start(bf16[20,2,768]{2,1,0:T(2,128)(2,1)S(1)} %bitcast.26), channel_id=1, source_target_pairs={{0,1},{1,0},{2,3},{3,2},{4,5},{5,4},{6,7},{7,6},{8,9},{9,8},{10,11... | collective-permute-start | bytes 184328 | tf_op jit(solution)/shard_map/ppermute | solution.py:404
  21.5 2.1 %shard_map.151 = (bf16[20,16,512]{2,1,0:T(8,128)(2,1)S(1)}, bf16[20,16,512]{2,1,0:T(8,128)(2,1)S(1)}, bf16[20,16,512]{2,1,0:T(8,128)(2,1)S(1)}, bf16[18,48,256]{...) custom-call(bf16[20,2,1536]{2,1,0:T(2,128)(2,1)S(1)} %get-tuple-element.75.xl_ref, ...), custom_call_target="tpu_custom_call" | custom-call | flops 3000000000 | tf_op jit(solution)/shard_map/pallas_call | solution.py:499
  23.7 2.2 %shard_map.152 = (bf16[18,32,256]{2,1,0:T(8,128)(2,1)S(1)}, bf16[18,32,128]{2,1,0:T(8,128)(2,1)S(1)}) custom-call(bf16[20,32,512]{2,1,0:T(8,128)(2,1)S(1)} %pad_maximum_fusion.win_ref, bf16[20,32,512]{2,1,0:T(8,128)(2,1)S(1)} %get-tuple-element.44.left_ref, bf16[20,32,512]{2,1,0:T(8,128)(2,1)S(1)} %get-tuple-element.45.right_ref, ...), custom_call_target="tpu_custom_call" | custom-call | flops 4000000000 | tf_op jit(solution)/shard_map/pallas_call | solution.py:490
  25.9 0.1 broadcast_select_fusion.10
  26.0 5.8 %shard_map.153 = (bf16[512,512]{1,0:T(8,128)(2,1)S(1)}, bf16[8,20,512]{2,1,0:T(8,128)(2,1)S(1)}) custom-call(bf16[20,32,128]{2,1,0:T(8,128)(2,1)S(1)} %get-tuple-element.69.zl_ref, bf16[20,32,128]{2,1,0:T(8,128)(2,1)S(1)} %get-tuple-element.68.zr_ref, bf16[20,2,768]{2,1,0:T(2,128)(2,1)S(1)} %get-tuple-element.79.cl_ref, ...), custom_call_target="tpu_custom_call" | custom-call | flops 6000000000 | tf_op jit(solution)/shard_map/pallas_call | solution.py:505
  31.9 0.1 collective-permute-start.7
  32.0 0.3 shard_map.157.tb_ref
  32.3 0.2 copy-done.7
  32.5 0.0 copy-done.8
  32.5 0.7 %collective-permute-done.7 = bf16[2,20,512]{2,1,0:T(8,128)(2,1)S(1)} collective-permute-done((bf16[2,20,512]{2,1,0:T(8,128)(2,1)S(1)}, bf16[2,20,512]{2,1,0:T(8,128)(2,1)S(1)}, u32[]{:S(2)}, u32[]{:S(2)}) %collective-permute-start.7) | collective-permute-done | bytes 40992 | tf_op jit(solution)/shard_map/ppermute | solution.py:404
  33.3 0.2 collective-permute-start.8
  33.5 1.5 %collective-permute-start.9 = (bf16[12,20,256]{2,1,0:T(8,128)(2,1)S(1)}, bf16[12,20,256]{2,1,0:T(8,128)(2,1)S(1)}, u32[]{:S(2)}, u32[]{:S(2)}) collective-permute-start(bf16[12,20,256]{2,1,0:T(8,128)(2,1)S(1)} %get-tuple-element.72), channel_id=1, source_target_pairs={{0,1},{1,0},{2,3},{3,2},{4,5},{5,4},{6,7},{7,6},{8,9},{9,8},{10,11... | collective-permute-start | bytes 368648 | tf_op jit(solution)/shard_map/ppermute | solution.py:404
  35.1 1.0 %shard_map.156 = (bf16[12,32,512]{2,1,0:T(8,128)(2,1)S(1)}, bf16[12,32,512]{2,1,0:T(8,128)(2,1)S(1)}, bf16[12,32,512]{2,1,0:T(8,128)(2,1)S(1)}, bf16[10,16,256]{...) custom-call(bf16[12,20,512]{2,1,0:T(8,128)(2,1)S(1)} %pad_maximum_fusion.1.wide_ref, ...), custom_call_target="tpu_custom_call" | custom-call | flops 3000000000 | tf_op jit(solution)/shard_map/pallas_call | solution.py:528
  36.1 1.3 %shard_map.154 = bf16[512,512]{1,0:T(8,128)(2,1)} custom-call(bf16[512,512]{1,0:T(8,128)(2,1)S(1)} %get-tuple-element.52.feat_ref), custom_call_target="tpu_custom_call" | custom-call | flops 2000000000 | tf_op jit(solution)/shard_map/pallas_call | solution.py:522
  37.4 2.3 %collective-permute-done.9 = bf16[12,20,256]{2,1,0:T(8,128)(2,1)S(1)} collective-permute-done((bf16[12,20,256]{2,1,0:T(8,128)(2,1)S(1)}, bf16[12,20,256]{2,1,0:T(8,128)(2,1)S(1)}, u32[]{:S(2)}, u32[]{:S(2)}) %collective-permute-start.9) | collective-permute-done | bytes 122912 | tf_op jit(solution)/shard_map/ppermute | solution.py:404
  39.7 4.0 %shard_map.158 = bf16[384,128]{1,0:T(8,128)(2,1)} custom-call(bf16[12,32,512]{2,1,0:T(8,128)(2,1)S(1)} %get-tuple-element.54.a0, bf16[12,32,512]{2,1,0:T(8,128)(2,1)S(1)} %get-tuple-element.55.a1, bf16[12,32,512]{2,1,0:T(8,128)(2,1)S(1)} %get-tuple-element.56.a2, bf16[10,16,256]{2,1,0:T(8,128)(2,1)S(1)} %get-tuple-element.57.m0, ...), custom_call_target="tpu_custom_call" | custom-call | flops 5000000000 | tf_op jit(solution)/shard_map/pallas_call | solution.py:534
  (41 shorter events, 0.5 us)
Async XLA Ops:
  0.6 5.3 %copy-start.5 = (bf16[8,96,64]{1,2,0:T(8,128)(2,1)S(1)}, bf16[8,96,64]{1,2,0:T(8,128)(2,1)}, u32[]{:S(2)}) copy-start(bf16[8,96,64]{1,2,0:T(8,128)(2,1)} %param.22) | copy-start | bytes 294916
  0.7 5.3 %copy-start.6 = (f32[96]{0:T(128)S(1)}, f32[96]{0:T(128)}, u32[]{:S(2)}) copy-start(f32[96]{0:T(128)} %param.23) | copy-start | bytes 1156
  0.7 5.3 %copy-start.2 = (bf16[27,96,96]{2,1,0:T(8,128)(2,1)S(1)}, bf16[27,96,96]{2,1,0:T(8,128)(2,1)}, u32[]{:S(2)}) copy-start(bf16[27,96,96]{2,1,0:T(8,128)(2,1)} %w_ref.4) | copy-start | bytes 1492996
  5.4 1.4 %collective-permute-start = (bf16[2,32,512]{2,1,0:T(8,128)(2,1)S(1)}, bf16[2,32,512]{2,1,0:T(8,128)(2,1)S(1)}, u32[]{:S(2)}, u32[]{:S(2)}) collective-permute-start(bf16[2,32,512]{2,1,0:T(8,128)(2,1)S(1)} %slice_select_fusion), channel_id=1, source_target_pairs={{0,4},{1,5},{2,6},{3,7},{4,0},{5,1},{6,2},{7,3},{8,12},{9,13},{10,... | collective-permute-start | bytes 196616 | tf_op jit(solution)/shard_map/ppermute | solution.py:404
  6.3 8.7 %copy-start = (bf16[27,64,64]{2,1,0:T(8,128)(2,1)S(1)}, bf16[27,64,64]{2,1,0:T(8,128)(2,1)}, u32[]{:S(2)}) copy-start(bf16[27,64,64]{2,1,0:T(8,128)(2,1)} %w_ref.3) | copy-start | bytes 663556
  6.4 8.7 %copy-start.1 = (f32[64]{0:T(128)S(1)}, f32[64]{0:T(128)}, u32[]{:S(2)}) copy-start(f32[64]{0:T(128)} %param.19) | copy-start | bytes 772
  7.4 9.4 %collective-permute-start.3 = (bf16[20,2,1536]{2,1,0:T(2,128)(2,1)S(1)}, bf16[20,2,1536]{2,1,0:T(2,128)(2,1)S(1)}, u32[]{:S(2)}, u32[]{:S(2)}) collective-permute-start(bf16[20,2,1536]{2,1,0:T(2,128)(2,1)S(1)} %get-tuple-element.77), channel_id=1, source_target_pairs={{0,4},{1,5},{2,6},{3,7},{4,0},{5,1},{6,2},{7,3},{8,16},{9,17},{10,... | collective-permute-start | bytes 368648 | tf_op jit(solution)/shard_map/ppermute | solution.py:404
  7.8 10.0 %collective-permute-start.4 = (bf16[20,2,1536]{2,1,0:T(2,128)(2,1)S(1)}, bf16[20,2,1536]{2,1,0:T(2,128)(2,1)S(1)}, u32[]{:S(2)}, u32[]{:S(2)}) collective-permute-start(bf16[20,2,1536]{2,1,0:T(2,128)(2,1)S(1)} %get-tuple-element.76), channel_id=1, source_target_pairs={{0,8},{1,9},{2,10},{3,11},{4,12},{5,13},{6,14},{7,15},{8,0},{9,1},... | collective-permute-start | bytes 368648 | tf_op jit(solution)/shard_map/ppermute | solution.py:404
  11.9 11.8 %collective-permute-start.1 = (bf16[20,32,128]{2,1,0:T(8,128)(2,1)S(1)}, bf16[20,32,128]{2,1,0:T(8,128)(2,1)S(1)}, u32[]{:S(2)}, u32[]{:S(2)}) collective-permute-start(bf16[20,32,128]{2,1,0:T(8,128)(2,1)S(1)} %get-tuple-element.67), channel_id=1, source_target_pairs={{0,4},{1,2},{2,1},{3,7},{4,0},{5,6},{6,5},{7,3},{8,12},{9,10},{10,... | collective-permute-start | bytes 491528 | tf_op jit(solution)/shard_map/ppermute | solution.py:404
  11.9 11.7 %collective-permute-start.2 = (bf16[20,32,128]{2,1,0:T(8,128)(2,1)S(1)}, bf16[20,32,128]{2,1,0:T(8,128)(2,1)S(1)}, u32[]{:S(2)}, u32[]{:S(2)}) collective-permute-start(bf16[20,32,128]{2,1,0:T(8,128)(2,1)S(1)} %get-tuple-element.66), channel_id=1, source_target_pairs={{0,1},{1,0},{2,3},{3,2},{4,5},{5,4},{6,7},{7,6},{8,9},{9,8},{10,11... | collective-permute-start | bytes 491528 | tf_op jit(solution)/shard_map/ppermute | solution.py:404
  18.3 7.5 %collective-permute-start.5 = (bf16[20,2,768]{2,1,0:T(2,128)(2,1)S(1)}, bf16[20,2,768]{2,1,0:T(2,128)(2,1)S(1)}, u32[]{:S(2)}, u32[]{:S(2)}) collective-permute-start(bf16[20,2,768]{2,1,0:T(2,128)(2,1)S(1)} %bitcast.27), channel_id=1, source_target_pairs={{0,4},{1,2},{2,1},{3,7},{4,0},{5,6},{6,5},{7,3},{8,12},{9,10},{10,... | collective-permute-start | bytes 184328 | tf_op jit(solution)/shard_map/ppermute | solution.py:404
  18.4 7.5 %collective-permute-start.6 = (bf16[20,2,768]{2,1,0:T(2,128)(2,1)S(1)}, bf16[20,2,768]{2,1,0:T(2,128)(2,1)S(1)}, u32[]{:S(2)}, u32[]{:S(2)}) collective-permute-start(bf16[20,2,768]{2,1,0:T(2,128)(2,1)S(1)} %bitcast.26), channel_id=1, source_target_pairs={{0,1},{1,0},{2,3},{3,2},{4,5},{5,4},{6,7},{7,6},{8,9},{9,8},{10,11... | collective-permute-start | bytes 184328 | tf_op jit(solution)/shard_map/ppermute | solution.py:404
  23.7 2.3 %copy-start.4 = (f32[64]{0:T(128)S(1)}, f32[64]{0:T(128)}, u32[]{:S(2)}) copy-start(f32[64]{0:T(128)} %param.21) | copy-start | bytes 772
  26.0 6.0 %copy-start.3 = (bf16[27,96,96]{2,1,0:T(8,128)(2,1)S(1)}, bf16[27,96,96]{2,1,0:T(8,128)(2,1)}, u32[]{:S(2)}) copy-start(bf16[27,96,96]{2,1,0:T(8,128)(2,1)} %w_ref.5) | copy-start | bytes 1492996
  31.9 0.7 %copy-start.7 = (f32[96]{0:T(128)S(1)}, f32[96]{0:T(128)}, u32[]{:S(2)}) copy-start(f32[96]{0:T(128)} %param.25) | copy-start | bytes 1156
  31.9 0.7 %copy-start.8 = (f32[96]{0:T(128)S(1)}, f32[96]{0:T(128)}, u32[]{:S(2)}) copy-start(f32[96]{0:T(128)} %param.27) | copy-start | bytes 1156
  31.9 1.3 %collective-permute-start.7 = (bf16[2,20,512]{2,1,0:T(8,128)(2,1)S(1)}, bf16[2,20,512]{2,1,0:T(8,128)(2,1)S(1)}, u32[]{:S(2)}, u32[]{:S(2)}) collective-permute-start(bf16[2,20,512]{2,1,0:T(8,128)(2,1)S(1)} %slice_select_fusion.1), channel_id=1, source_target_pairs={{0,4},{1,5},{2,6},{3,7},{4,0},{5,1},{6,2},{7,3},{8,12},{9,13},{10,... | collective-permute-start | bytes 122888 | tf_op jit(solution)/shard_map/ppermute | solution.py:404
  33.3 4.1 %collective-permute-start.8 = (bf16[12,20,256]{2,1,0:T(8,128)(2,1)S(1)}, bf16[12,20,256]{2,1,0:T(8,128)(2,1)S(1)}, u32[]{:S(2)}, u32[]{:S(2)}) collective-permute-start(bf16[12,20,256]{2,1,0:T(8,128)(2,1)S(1)} %get-tuple-element.73), channel_id=1, source_target_pairs={{0,4},{1,2},{2,1},{3,7},{4,0},{5,6},{6,5},{7,3},{8,12},{9,10},{10,... | collective-permute-start | bytes 368648 | tf_op jit(solution)/shard_map/ppermute | solution.py:404
  33.5 6.1 %collective-permute-start.9 = (bf16[12,20,256]{2,1,0:T(8,128)(2,1)S(1)}, bf16[12,20,256]{2,1,0:T(8,128)(2,1)S(1)}, u32[]{:S(2)}, u32[]{:S(2)}) collective-permute-start(bf16[12,20,256]{2,1,0:T(8,128)(2,1)S(1)} %get-tuple-element.72), channel_id=1, source_target_pairs={{0,1},{1,0},{2,3},{3,2},{4,5},{5,4},{6,7},{7,6},{8,9},{9,8},{10,11... | collective-permute-start | bytes 368648 | tf_op jit(solution)/shard_map/ppermute | solution.py:404

commit v13 on v12

--- a/solution.py
+++ b/solution.py
@@ -90,14 +90,13 @@
 
 
 def down1_kernel(
-    v_hbm, wd_hbm, b_hbm, t_hbm, wa_hbm, out_ref, ta_ref, tab_ref, tab2_ref,
-    v_ref, w_ref, b_ref, t_ref, wa_ref, wd_ref, cells_ref, sems,
+    v_hbm, wd_hbm, b_hbm, t_hbm, out_ref, tab_ref, tab2_ref, v_ref, w_ref, b_ref, t_ref, wd_ref, cells_ref, sems
 ):
     half = v_ref.shape[2]
     kz = C0 * half
     part = 16 * half
     lanes = Z1 // 2 * C1
-    small = ((t_hbm, t_ref), (wd_hbm, w_ref), (b_hbm, b_ref), (wa_hbm, wa_ref))
+    small = ((t_hbm, t_ref), (wd_hbm, w_ref), (b_hbm, b_ref))
     copies = [pltpu.make_async_copy(src, dst, sems.at[n]) for n, (src, dst) in enumerate(small)]
     for n in range(C0 // 16):
         cut = slice(n * 16, n * 16 + 16)
@@ -123,13 +122,11 @@
         for n in range(C0 // 16):
             wd_ref[n, ab * part : ab * part + part, :] = block[n * part : n * part + part]
 
-    copies[3].wait()
-    fill_banded(wa_ref, ta_ref, 4, C1)
     r = iota((4 * CX, 128), 0)
     select = one_hot_rows(((r & 32) << 2) | (r & 64) | ((r & 31) << 1) | (r >> 7), 4 * CX)
     part = 16 * half
     acc = [0.0, 0.0]
-    for n, copy in enumerate(copies[4:]):
+    for n, copy in enumerate(copies[3:]):
         copy.wait()
         for m in range(v_ref.shape[3] // 256):
             v = [v_ref[n * 16 : n * 16 + 16, h, :, m * 256 : m * 256 + 256].reshape(part, 256) for h in range(2)]
@@ -175,20 +172,27 @@
     )(weights)
 
 
-def conv_group(taps, t_ref, y_first, rows, group_out, group_full):
-    pitch = taps[0][0][0].shape[1]
-    width = sum(piece[2] for piece in taps[0])
+def conv_groups(groups, t_ref, rows, group_out, group_full):
+    pitch = groups[0][0][0][0].shape[1]
+    width = sum(piece[2] for piece in groups[0][0])
     total = None
     for j in range(3):
-        parts = [ref[y_first + j : y_first + j + rows, :, lane : lane + n] for tap in taps for ref, lane, n in tap]
-        left = jnp.concatenate([p.reshape(rows * pitch, p.shape[2]) for p in parts], axis=1)
+        left = []
+        for taps in groups:
+            parts = [ref[j : j + rows, :, lane : lane + n] for tap in taps for ref, lane, n in tap]
+            left.append(jnp.concatenate([p.reshape(rows * pitch, p.shape[2]) for p in parts], axis=1))
         if width == group_full:
             right = t_ref[j, 0:group_out, :]
         else:
             right = jnp.concatenate([t_ref[j, 0:group_out, i * group_full : i * group_full + width] for i in range(3)], axis=1)
-        term = mm(left, right, NT)
+        term = mm(jnp.concatenate(left, axis=0), right, NT)
         total = term if total is None else total + term
-    return total
+    size = rows * pitch
+    return [total[g * size : g * size + size] for g in range(len(groups))]
+
+
+def conv_group(taps, t_ref, rows, group_out, group_full):
+    return conv_groups([taps], t_ref, rows, group_out, group_full)[0]
 
 
 def finish(acc, bias, mask, rows):
@@ -209,7 +213,7 @@
         fill_sides(left_ref, right_ref, q * 128, win_ref[:, :, q * 128 : q * 128 + 128])
     rows = Y1 + 2
     mask = mask_rows(tab_ref[:, 128:256], -1, rows, X1, lambda x: x, 4)
-    acc = conv_group([[(ref, 128, 384)] for ref in (left_ref, win_ref, right_ref)], t_ref, 0, rows, 256, 384)
+    acc = conv_group([[(ref, 128, 384)] for ref in (left_ref, win_ref, right_ref)], t_ref, rows, 256, 384)
     for q in range(2):
         cut = slice(q * 128, q * 128 + 128)
         out_ref[:, :, cut] = finish(acc[:, cut], twice(b_ref), mask, rows)
@@ -222,21 +226,20 @@
     rows = Y1 + 2
     mask = mask_rows(tab_ref[...], -1, rows, X1, lambda x: x, 4)
     taps = [[(z, 0, 128), (ref, 0, 256)] for z, ref in zip((ll, zl_ref, lr), own)]
-    acc = conv_group(taps, t_ref, 0, rows, 256, 384)
+    acc = conv_group(taps, t_ref, rows, 256, 384)
     for q in range(2):
         cut = slice(q * 128, q * 128 + 128)
         low_ref[:, :, cut] = finish(acc[:, cut], twice(b_ref), mask[:, cut], rows)
     taps = [[(ref, 384, 128), (z, 0, 128)] for z, ref in zip((hl, zr_ref, hr), own)]
-    acc = conv_group(taps, t_ref, 0, rows, 128, 384)
+    acc = conv_group(taps, t_ref, rows, 128, 384)
     high_ref[...] = finish(acc, twice(b_ref), mask[:, 256:384], rows)
 
 
 def fill_edges(copies, pieces):
-    for i, copy in enumerate(copies):
-        line = [pieces[0][:, i:]] + pieces[1:] if i < 2 else pieces[1:]
-        if i:
-            line.append(jnp.zeros((copy.shape[0], i, pieces[0].shape[2]), BF))
-        copy[...] = jnp.concatenate(line, axis=1)
+    line = jnp.concatenate(pieces, axis=1)
+    copies[0][...] = line
+    for i in (1, 2):
+        copies[i][...] = jnp.concatenate([line[:, i:], jnp.zeros_like(line[:, :i])], axis=1)
 
 
 def edge_masks(tab_ref):
@@ -246,7 +249,7 @@
 
 def edge_group(taps, t_ref, b_ref, masks, inner_ref, moved):
     rows = Y1 + 2
-    acc = conv_group(taps, t_ref, 0, rows, 128 * len(masks), 384)
+    acc = conv_group(taps, t_ref, rows, 128 * len(masks), 384)
     i0, i1, i2 = moved
     for q, mask in enumerate(masks):
         cut = slice(q * 128, q * 128 + 128)
@@ -297,7 +300,7 @@
     first = [[(a, 0, 256), (b, 0, 128)] for a, b in zip(low, mid)]
     second = [[(a, 0, 256), (b, 0, 128)] for a, b in zip(mid, high)]
     for g, taps in enumerate((first, second)):
-        acc = conv_group(taps, tb_ref, 0, Y1, 256, 384)
+        acc = conv_group(taps, tb_ref, Y1, 256, 384)
         for q in range(2):
             value = finish(acc[:, q * 128 : q * 128 + 128], twice(bb_ref), mask, Y1)
             cut = slice((2 * g + q) * 128, (2 * g + q + 1) * 128)
@@ -342,14 +345,14 @@
             copy[:, :, lane : lane + 128] = jnp.concatenate([line[:, i:], spare], axis=1)
 
 
-def level_two_group(taps, t_ref, b_ref, masks, moved):
+def level_two_groups(groups, t_ref, b_ref, masks, moved):
     rows = Y2 + 2
-    acc = conv_group(taps, t_ref, 0, rows, 256, 512)
-    for q in range(2):
-        cut = slice(q * 128, q * 128 + 128)
-        value = finish(acc[:, cut], b_ref[...], masks[q], rows)
-        for i, ref in enumerate(moved):
-            ref[:, :, cut] = value[:, i : i + X2]
+    for g, acc in enumerate(conv_groups(groups, t_ref, rows, 256, 512)):
+        for q in range(2):
+            cut = slice(q * 128, q * 128 + 128)
+            value = finish(acc[:, cut], b_ref[...], masks[g][q], rows)
+            for i, ref in enumerate(moved[g]):
+                ref[:, :, cut] = value[:, i : i + X2]
 
 
 def level_two_masks(tab_ref):
@@ -360,7 +363,7 @@
 def level_two_middle_kernel(wide_ref, t_ref, b_ref, tab_ref, a0, a1, a2, m0, m1, m2):
     fill_pitch((a0, a1, a2), wide_ref[...])
     here = level_two_masks(tab_ref)[1]
-    level_two_group([[(a, 0, 512)] for a in (a0, a1, a2)], t_ref, b_ref, (here, here), (m0, m1, m2))
+    level_two_groups([[[(a, 0, 512)] for a in (a0, a1, a2)]], t_ref, b_ref, [(here, here)], [(m0, m1, m2)])
 
 
 def level_two_kernel(
@@ -371,14 +374,13 @@
     fill_pitch((h0, h1, h2), zr_ref[...])
     below, here, above = level_two_masks(tab_ref)
     own, mid, low, high = (a0, a1, a2), (m0, m1, m2), (i0, i1, i2), (j0, j1, j2)
-    taps = [[(z, 0, 256), (a, 0, 256)] for z, a in zip((l0, l1, l2), own)]
-    level_two_group(taps, ta_ref, ba_ref, (below, here), low)
-    taps = [[(a, 256, 256), (z, 0, 256)] for z, a in zip((h0, h1, h2), own)]
-    level_two_group(taps, ta_ref, ba_ref, (here, above), high)
+    first = [[(z, 0, 256), (a, 0, 256)] for z, a in zip((l0, l1, l2), own)]
+    second = [[(a, 256, 256), (z, 0, 256)] for z, a in zip((h0, h1, h2), own)]
+    level_two_groups([first, second], ta_ref, ba_ref, [(below, here), (here, above)], [low, high])
     mask = mask_rows(tab_ref[:, 128:256], 0, Y2, X2, lambda x: x, 2)
+    groups = [[[(a, 0, 256), (b, 0, 256)] for a, b in zip(*pair)] for pair in ((low, mid), (mid, high))]
     feat = []
-    for pair in ((low, mid), (mid, high)):
-        acc = conv_group([[(a, 0, 256), (b, 0, 256)] for a, b in zip(*pair)], tb_ref, 0, Y2, 256, 512)
+    for acc in conv_groups(groups, tb_ref, Y2, 256, 512):
         for q in range(2):
             feat.append((jnp.maximum(acc[:, q * 128 : q * 128 + 128] + bb_ref[...], 0.0) * mask).astype(BF))
     r = iota((C2 * Z2, 128), 0)
@@ -450,24 +452,23 @@
     depth = volume.shape[1]
     lanes1 = Z1 * C1
     half = depth // 2
-    operands = [volume.reshape(C0, 2, half, -1), jnp.swapaxes(w_down1, 1, 2), b_down1[None], tissue.transpose(1, 2, 0), w_conv1a]
+    operands = [volume.reshape(C0, 2, half, -1), jnp.swapaxes(w_down1, 1, 2), b_down1[None], tissue.transpose(1, 2, 0)]
     operands = [pltpu.with_memory_space_constraint(x, pltpu.HBM) for x in operands]
-    own, t1a, tab1, tab2 = pl.pallas_call(
+    own, tab1, tab2 = pl.pallas_call(
         down1_kernel,
-        in_specs=[pl.BlockSpec(memory_space=pltpu.HBM)] * 5,
-        out_shape=[shaped(Y1, X1, lanes1), banded_shape(4, C1), shaped(128, 384), shaped(128, 384)],
+        in_specs=[pl.BlockSpec(memory_space=pltpu.HBM)] * 4,
+        out_shape=[shaped(Y1, X1, lanes1), shaped(128, 384), shaped(128, 384)],
         scratch_shapes=[pltpu.VMEM(x.shape, x.dtype) for x in operands]
         + [
             pltpu.VMEM((C0 // 16, 64 * half, lanes1 // 2), BF),
             pltpu.VMEM((C0 // 16, 2, Y1 * X1, 64 * half), BF),
-            pltpu.SemaphoreType.DMA((4 + C0 // 16,)),
+            pltpu.SemaphoreType.DMA((3 + C0 // 16,)),
         ],
         compiler_params=params(),
         cost_estimate=cost(4e-6),
     )(*operands)
 
-    t2a = banded(w_conv2a, 2, CP)
-    t2b = banded(w_conv2b, 2, CP)
+    t1a = banded(w_conv1a, 4, C1)
     bias1a = b_conv1a[None]
 
     y_below, y_above = shift_along(own[:HALO], own[Y1 - HALO :], "gy")
@@ -516,9 +517,12 @@
         pad_lanes(jnp.swapaxes(w_down2, 1, 2).reshape(8 * C1, C2)), pad_lanes(b_down2[None]), tab1, tab2,
     )
 
+    down, w_conv2a = lax.optimization_barrier((down, w_conv2a))
+    t2a = banded(w_conv2a, 2, CP)
     y_below, y_above = shift_along(down[:HALO], down[Y2 - HALO :], "gy")
     wide = jnp.concatenate([y_below, down, y_above], axis=0)
-    feat, wide = lax.optimization_barrier((feat, wide))
+    feat, wide, w_conv2b = lax.optimization_barrier((feat, wide, w_conv2b))
+    t2b = banded(w_conv2b, 2, CP)
     one = pl.pallas_call(
         one_kernel, out_shape=shaped(lanes1, Y1 * X1), compiler_params=params(), cost_estimate=cost(2e-6)
     )(feat)

time: 43.9 us -> 42.8 us (0.975)
    pallas_call x1, Pallas kernels: 2.07 us -> 1.27 us  [local(): pl.pallas_call(edge_middle_kernel, out_shape=[shaped(ROWS1, EDGE, lanes1)...]
    pallas_call x1, Pallas kernels: 4.73 us -> 4.02 us  [local(): pl.pallas_call(down1_kernel, in_specs=[pl.BlockSpec(memory_space=pltpu.HB...]
    pallas_call x1, Pallas kernels: 4.04 us -> 4.74 us  [local(): pl.pallas_call(level_two_kernel, out_shape=shaped(C2 * Z2, Y2 * X2), scra...]
    pallas_call x2 -> x3, Pallas kernels: 0.65 us -> 1.27 us  [banded(): pl.pallas_call(kernel, out_shape=banded_shape(group, pad), compiler_param...]
where the time goes in v13:
time: 42.8 us; the launch traced here: 42.7 us
  Pallas kernels  23.1 us (54%)
  starting transfers between devices  13.1 us (31%)
  waiting for transfers between devices  4 us (9%)
  between operations  1.07 us (2%)
  other arithmetic  0.93 us (2%)
  local copies, waits for them, and re-layouts  0.47 us (1%)
    ppermute x10, starting transfers between devices, swap(): return lax.ppermute(value, axes, pairs)  13.1 us
    pallas_call x1, Pallas kernels, local(): pl.pallas_call(level_one_kernel, out_shape=[shaped(Y1 * X1, lanes1), shap...  5.59 us
    pallas_call x1, Pallas kernels, local(): pl.pallas_call(level_two_kernel, out_shape=shaped(C2 * Z2, Y2 * X2), scra...  4.74 us
    pallas_call x1, Pallas kernels, local(): pl.pallas_call(down1_kernel, in_specs=[pl.BlockSpec(memory_space=pltpu.HB...  4.02 us
    ppermute x10, waiting for transfers between devices, swap(): return lax.ppermute(value, axes, pairs)  4 us
    pallas_call x1, Pallas kernels, local(): pl.pallas_call(outer_kernel, out_shape=[shaped(rows, X1, 256), shaped(row...  2.17 us
    pallas_call x1, Pallas kernels, local(): pl.pallas_call(middle_kernel, out_shape=[shaped(ROWS1, X1, lanes1), shape...  1.68 us
    pallas_call x1, Pallas kernels, local(): pl.pallas_call(edge_middle_kernel, out_shape=[shaped(ROWS1, EDGE, lanes1)...  1.27 us
  transfers between devices with their start and end apart: 10, of which 4 were waited for; matrix products, arithmetic and copies ran while one was open for 1% of the time, Pallas kernels for 20%

profile of v13, /device:TPU:0, one launch (start us, length us, event | category | flops | bytes accessed | tf_op | source)
XLA Modules:
  0.0 42.7 jit_solution(12763713994007648060)
XLA Ops:
  0.7 4.0 %shard_map.149 = (bf16[16,32,512]{2,1,0:T(8,128)(2,1)S(1)}, bf16[128,384]{1,0:T(8,128)(2,1)S(1)}, bf16[128,384]{1,0:T(8,128)(2,1)S(1)}) custom-call(bf16[48,2,8,2048]{3,2,1,0:T(8,128)(2,1)} %bitcast.28, bf16[8,48,64]{2,1,0:T(8,128)(2,1)} %bitcast.29, f32[1,64]{1,0:T(1,128)} %bitcast.31, s32[8,4,32]{2,1,0:T(4,128)} %bitcast.30), custom_call_target="tpu_custom_call" | custom-call | flops 4000000000 | tf_op jit(solution)/shard_map/pallas_call | solution.py:457
  4.7 0.5 %collective-permute-start = (bf16[2,32,512]{2,1,0:T(8,128)(2,1)S(1)}, bf16[2,32,512]{2,1,0:T(8,128)(2,1)S(1)}, u32[]{:S(2)}, u32[]{:S(2)}) collective-permute-start(bf16[2,32,512]{2,1,0:T(8,128)(2,1)S(1)} %slice_select_fusion), channel_id=1, source_target_pairs={{0,4},{1,5},{2,6},{3,7},{4,0},{5,1},{6,2},{7,3},{8,12},{9,13},{10,... | collective-permute-start | bytes 196616 | tf_op jit(solution)/shard_map/ppermute | solution.py:406
  5.4 0.6 %shard_map.150.t_ref.ta_ref = bf16[3,256,1152]{2,1,0:T(8,128)(2,1)S(1)} custom-call(bf16[27,64,64]{2,1,0:T(8,128)(2,1)S(1)} %copy-done.4), custom_call_target="tpu_custom_call" | custom-call | flops 1000000000 | tf_op jit(solution)/shard_map/pallas_call | solution.py:170
  6.0 0.0 copy-start
  6.0 0.1 collective-permute-done
  6.2 0.1 pad_maximum_fusion.win_ref
  6.3 0.2 fusion
  6.5 0.3 broadcast_select_fusion.3
  6.7 0.4 collective-permute-start.3
  7.2 4.0 %collective-permute-start.4 = (bf16[20,2,1536]{2,1,0:T(2,128)(2,1)S(1)}, bf16[20,2,1536]{2,1,0:T(2,128)(2,1)S(1)}, u32[]{:S(2)}, u32[]{:S(2)}) collective-permute-start(bf16[20,2,1536]{2,1,0:T(2,128)(2,1)S(1)} %get-tuple-element.80), channel_id=1, source_target_pairs={{0,8},{1,9},{2,10},{3,11},{4,12},{5,13},{6,14},{7,15},{8,0},{9,1},... | collective-permute-start | bytes 368648 | tf_op jit(solution)/shard_map/ppermute | solution.py:406
  11.2 0.1 collective-permute-start.1
  11.2 3.1 %collective-permute-start.2 = (bf16[20,32,128]{2,1,0:T(8,128)(2,1)S(1)}, bf16[20,32,128]{2,1,0:T(8,128)(2,1)S(1)}, u32[]{:S(2)}, u32[]{:S(2)}) collective-permute-start(bf16[20,32,128]{2,1,0:T(8,128)(2,1)S(1)} %get-tuple-element.70), channel_id=1, source_target_pairs={{0,1},{1,0},{2,3},{3,2},{4,5},{5,4},{6,7},{7,6},{8,9},{9,8},{10,11... | collective-permute-start | bytes 491528 | tf_op jit(solution)/shard_map/ppermute | solution.py:406
  14.4 1.7 %shard_map.151 = (bf16[20,32,512]{2,1,0:T(8,128)(2,1)S(1)}, bf16[20,32,512]{2,1,0:T(8,128)(2,1)S(1)}, bf16[18,32,256]{2,1,0:T(8,128)(2,1)S(1)}, bf16[3,256,1152]{2,1,0:T(8,128)(2,1)S(1)}) custom-call(bf16[20,32,512]{2,1,0:T(8,128)(2,1)S(1)} %pad_maximum_fusion.win_ref, bf16[3,256,1152]{2,1,0:T(8,128)(2,1)S(1)} %shard_map.150.t_ref.ta_ref, ...), custom_call_target="tpu_custom_call" | custom-call | flops 100000000 | tf_op jit(solution)/shard_map/pallas_call | solution.py:480
  16.1 1.0 %collective-permute-done.4 = bf16[20,2,1536]{2,1,0:T(2,128)(2,1)S(1)} collective-permute-done((bf16[20,2,1536]{2,1,0:T(2,128)(2,1)S(1)}, bf16[20,2,1536]{2,1,0:T(2,128)(2,1)S(1)}, u32[]{:S(2)}, u32[]{:S(2)}) %collective-permute-start.4) | collective-permute-done | bytes 122912 | tf_op jit(solution)/shard_map/ppermute | solution.py:406
  17.1 0.2 broadcast_select_fusion
  17.6 0.1 collective-permute-start.5
  17.7 3.1 %collective-permute-start.6 = (bf16[20,2,768]{2,1,0:T(2,128)(2,1)S(1)}, bf16[20,2,768]{2,1,0:T(2,128)(2,1)S(1)}, u32[]{:S(2)}, u32[]{:S(2)}) collective-permute-start(bf16[20,2,768]{2,1,0:T(2,128)(2,1)S(1)} %bitcast.26), channel_id=1, source_target_pairs={{0,1},{1,0},{2,3},{3,2},{4,5},{5,4},{6,7},{7,6},{8,9},{9,8},{10,11... | collective-permute-start | bytes 184328 | tf_op jit(solution)/shard_map/ppermute | solution.py:406
  20.8 1.3 %shard_map.152 = (bf16[20,16,512]{2,1,0:T(8,128)(2,1)S(1)}, bf16[20,16,512]{2,1,0:T(8,128)(2,1)S(1)}, bf16[20,16,512]{2,1,0:T(8,128)(2,1)S(1)}, bf16[18,48,256]{...) custom-call(bf16[20,2,1536]{2,1,0:T(2,128)(2,1)S(1)} %get-tuple-element.79.xl_ref, ...), custom_call_target="tpu_custom_call" | custom-call | flops 3000000000 | tf_op jit(solution)/shard_map/pallas_call | solution.py:500
  22.2 0.0 copy-start.5
  22.2 2.2 %shard_map.153 = (bf16[18,32,256]{2,1,0:T(8,128)(2,1)S(1)}, bf16[18,32,128]{2,1,0:T(8,128)(2,1)S(1)}) custom-call(bf16[20,32,512]{2,1,0:T(8,128)(2,1)S(1)} %pad_maximum_fusion.win_ref, bf16[20,32,512]{2,1,0:T(8,128)(2,1)S(1)} %get-tuple-element.45.left_ref, bf16[20,32,512]{2,1,0:T(8,128)(2,1)S(1)} %get-tuple-element.46.right_ref, ...), custom_call_target="tpu_custom_call" | custom-call | flops 4000000000 | tf_op jit(solution)/shard_map/pallas_call | solution.py:491
  24.4 0.1 broadcast_select_fusion.10
  24.6 5.6 %shard_map.154 = (bf16[512,512]{1,0:T(8,128)(2,1)S(1)}, bf16[8,20,512]{2,1,0:T(8,128)(2,1)S(1)}) custom-call(bf16[20,32,128]{2,1,0:T(8,128)(2,1)S(1)} %get-tuple-element.73.zl_ref, bf16[20,32,128]{2,1,0:T(8,128)(2,1)S(1)} %get-tuple-element.72.zr_ref, bf16[20,2,768]{2,1,0:T(2,128)(2,1)S(1)} %get-tuple-element.83.cl_ref, ...), custom_call_target="tpu_custom_call" | custom-call | flops 6000000000 | tf_op jit(solution)/shard_map/pallas_call | solution.py:506
  30.2 0.1 collective-permute-start.7
  30.3 0.3 shard_map.156.t_ref.ta_ref
  30.6 0.9 %collective-permute-done.7 = bf16[2,20,512]{2,1,0:T(8,128)(2,1)S(1)} collective-permute-done((bf16[2,20,512]{2,1,0:T(8,128)(2,1)S(1)}, bf16[2,20,512]{2,1,0:T(8,128)(2,1)S(1)}, u32[]{:S(2)}, u32[]{:S(2)}) %collective-permute-start.7) | collective-permute-done | bytes 40992 | tf_op jit(solution)/shard_map/ppermute | solution.py:406
  31.6 0.2 collective-permute-start.8
  31.8 1.5 %collective-permute-start.9 = (bf16[12,20,256]{2,1,0:T(8,128)(2,1)S(1)}, bf16[12,20,256]{2,1,0:T(8,128)(2,1)S(1)}, u32[]{:S(2)}, u32[]{:S(2)}) collective-permute-start(bf16[12,20,256]{2,1,0:T(8,128)(2,1)S(1)} %get-tuple-element.76), channel_id=1, source_target_pairs={{0,1},{1,0},{2,3},{3,2},{4,5},{5,4},{6,7},{7,6},{8,9},{9,8},{10,11... | collective-permute-start | bytes 368648 | tf_op jit(solution)/shard_map/ppermute | solution.py:406
  33.3 1.0 %shard_map.157 = (bf16[12,32,512]{2,1,0:T(8,128)(2,1)S(1)}, bf16[12,32,512]{2,1,0:T(8,128)(2,1)S(1)}, bf16[12,32,512]{2,1,0:T(8,128)(2,1)S(1)}, bf16[10,16,256]{...) custom-call(bf16[12,20,512]{2,1,0:T(8,128)(2,1)S(1)} %pad_maximum_fusion.1.wide_ref, ...), custom_call_target="tpu_custom_call" | custom-call | flops 3000000000 | tf_op jit(solution)/shard_map/pallas_call | solution.py:532
  34.4 1.3 %shard_map.155 = bf16[512,512]{1,0:T(8,128)(2,1)} custom-call(bf16[512,512]{1,0:T(8,128)(2,1)S(1)} %get-tuple-element.54.feat_ref), custom_call_target="tpu_custom_call" | custom-call | flops 2000000000 | tf_op jit(solution)/shard_map/pallas_call | solution.py:526
  35.6 0.3 shard_map.158.tb_ref
  36.0 1.9 %collective-permute-done.9 = bf16[12,20,256]{2,1,0:T(8,128)(2,1)S(1)} collective-permute-done((bf16[12,20,256]{2,1,0:T(8,128)(2,1)S(1)}, bf16[12,20,256]{2,1,0:T(8,128)(2,1)S(1)}, u32[]{:S(2)}, u32[]{:S(2)}) %collective-permute-start.9) | collective-permute-done | bytes 122912 | tf_op jit(solution)/shard_map/ppermute | solution.py:406
  37.9 4.7 %shard_map.159 = bf16[384,128]{1,0:T(8,128)(2,1)} custom-call(bf16[12,32,512]{2,1,0:T(8,128)(2,1)S(1)} %get-tuple-element.57.a0, bf16[12,32,512]{2,1,0:T(8,128)(2,1)S(1)} %get-tuple-element.58.a1, bf16[12,32,512]{2,1,0:T(8,128)(2,1)S(1)} %get-tuple-element.59.a2, bf16[10,16,256]{2,1,0:T(8,128)(2,1)S(1)} %get-tuple-element.60.m0, ...), custom_call_target="tpu_custom_call" | custom-call | flops 5000000000 | tf_op jit(solution)/shard_map/pallas_call | solution.py:538
  (44 shorter events, 0.5 us)
Async XLA Ops:
  0.6 4.6 %copy-start.7 = (f32[96]{0:T(128)S(1)}, f32[96]{0:T(128)}, u32[]{:S(2)}) copy-start(f32[96]{0:T(128)} %param.23) | copy-start | bytes 1156
  0.7 4.6 %copy-start.8 = (f32[96]{0:T(128)S(1)}, f32[96]{0:T(128)}, u32[]{:S(2)}) copy-start(f32[96]{0:T(128)} %param.25) | copy-start | bytes 1156
  0.7 4.6 %copy-start.9 = (f32[96]{0:T(128)S(1)}, f32[96]{0:T(128)}, u32[]{:S(2)}) copy-start(f32[96]{0:T(128)} %param.27) | copy-start | bytes 1156
  0.7 4.6 %copy-start.6 = (bf16[8,96,64]{1,2,0:T(8,128)(2,1)S(1)}, bf16[8,96,64]{1,2,0:T(8,128)(2,1)}, u32[]{:S(2)}) copy-start(bf16[8,96,64]{1,2,0:T(8,128)(2,1)} %param.22) | copy-start | bytes 294916
  0.7 4.7 %copy-start.4 = (bf16[27,64,64]{2,1,0:T(8,128)(2,1)S(1)}, bf16[27,64,64]{2,1,0:T(8,128)(2,1)}, u32[]{:S(2)}) copy-start(bf16[27,64,64]{2,1,0:T(8,128)(2,1)} %w_ref.2) | copy-start | bytes 663556
  4.7 1.4 %collective-permute-start = (bf16[2,32,512]{2,1,0:T(8,128)(2,1)S(1)}, bf16[2,32,512]{2,1,0:T(8,128)(2,1)S(1)}, u32[]{:S(2)}, u32[]{:S(2)}) collective-permute-start(bf16[2,32,512]{2,1,0:T(8,128)(2,1)S(1)} %slice_select_fusion), channel_id=1, source_target_pairs={{0,4},{1,5},{2,6},{3,7},{4,0},{5,1},{6,2},{7,3},{8,12},{9,13},{10,... | collective-permute-start | bytes 196616 | tf_op jit(solution)/shard_map/ppermute | solution.py:406
  6.0 8.4 %copy-start = (bf16[27,64,64]{2,1,0:T(8,128)(2,1)S(1)}, bf16[27,64,64]{2,1,0:T(8,128)(2,1)}, u32[]{:S(2)}) copy-start(bf16[27,64,64]{2,1,0:T(8,128)(2,1)} %w_ref.3) | copy-start | bytes 663556
  6.0 8.4 %copy-start.1 = (f32[64]{0:T(128)S(1)}, f32[64]{0:T(128)}, u32[]{:S(2)}) copy-start(f32[64]{0:T(128)} %param.19) | copy-start | bytes 772
  6.7 9.3 %collective-permute-start.3 = (bf16[20,2,1536]{2,1,0:T(2,128)(2,1)S(1)}, bf16[20,2,1536]{2,1,0:T(2,128)(2,1)S(1)}, u32[]{:S(2)}, u32[]{:S(2)}) collective-permute-start(bf16[20,2,1536]{2,1,0:T(2,128)(2,1)S(1)} %get-tuple-element.81), channel_id=1, source_target_pairs={{0,4},{1,5},{2,6},{3,7},{4,0},{5,1},{6,2},{7,3},{8,16},{9,17},{10,... | collective-permute-start | bytes 368648 | tf_op jit(solution)/shard_map/ppermute | solution.py:406
  7.2 10.0 %collective-permute-start.4 = (bf16[20,2,1536]{2,1,0:T(2,128)(2,1)S(1)}, bf16[20,2,1536]{2,1,0:T(2,128)(2,1)S(1)}, u32[]{:S(2)}, u32[]{:S(2)}) collective-permute-start(bf16[20,2,1536]{2,1,0:T(2,128)(2,1)S(1)} %get-tuple-element.80), channel_id=1, source_target_pairs={{0,8},{1,9},{2,10},{3,11},{4,12},{5,13},{6,14},{7,15},{8,0},{9,1},... | collective-permute-start | bytes 368648 | tf_op jit(solution)/shard_map/ppermute | solution.py:406
  11.2 11.0 %collective-permute-start.1 = (bf16[20,32,128]{2,1,0:T(8,128)(2,1)S(1)}, bf16[20,32,128]{2,1,0:T(8,128)(2,1)S(1)}, u32[]{:S(2)}, u32[]{:S(2)}) collective-permute-start(bf16[20,32,128]{2,1,0:T(8,128)(2,1)S(1)} %get-tuple-element.71), channel_id=1, source_target_pairs={{0,4},{1,2},{2,1},{3,7},{4,0},{5,6},{6,5},{7,3},{8,12},{9,10},{10,... | collective-permute-start | bytes 491528 | tf_op jit(solution)/shard_map/ppermute | solution.py:406
  11.2 10.9 %collective-permute-start.2 = (bf16[20,32,128]{2,1,0:T(8,128)(2,1)S(1)}, bf16[20,32,128]{2,1,0:T(8,128)(2,1)S(1)}, u32[]{:S(2)}, u32[]{:S(2)}) collective-permute-start(bf16[20,32,128]{2,1,0:T(8,128)(2,1)S(1)} %get-tuple-element.70), channel_id=1, source_target_pairs={{0,1},{1,0},{2,3},{3,2},{4,5},{5,4},{6,7},{7,6},{8,9},{9,8},{10,11... | collective-permute-start | bytes 491528 | tf_op jit(solution)/shard_map/ppermute | solution.py:406
  17.6 6.8 %collective-permute-start.5 = (bf16[20,2,768]{2,1,0:T(2,128)(2,1)S(1)}, bf16[20,2,768]{2,1,0:T(2,128)(2,1)S(1)}, u32[]{:S(2)}, u32[]{:S(2)}) collective-permute-start(bf16[20,2,768]{2,1,0:T(2,128)(2,1)S(1)} %bitcast.27), channel_id=1, source_target_pairs={{0,4},{1,2},{2,1},{3,7},{4,0},{5,6},{6,5},{7,3},{8,12},{9,10},{10,... | collective-permute-start | bytes 184328 | tf_op jit(solution)/shard_map/ppermute | solution.py:406
  17.7 6.7 %collective-permute-start.6 = (bf16[20,2,768]{2,1,0:T(2,128)(2,1)S(1)}, bf16[20,2,768]{2,1,0:T(2,128)(2,1)S(1)}, u32[]{:S(2)}, u32[]{:S(2)}) collective-permute-start(bf16[20,2,768]{2,1,0:T(2,128)(2,1)S(1)} %bitcast.26), channel_id=1, source_target_pairs={{0,1},{1,0},{2,3},{3,2},{4,5},{5,4},{6,7},{7,6},{8,9},{9,8},{10,11... | collective-permute-start | bytes 184328 | tf_op jit(solution)/shard_map/ppermute | solution.py:406
  22.2 2.3 %copy-start.5 = (f32[64]{0:T(128)S(1)}, f32[64]{0:T(128)}, u32[]{:S(2)}) copy-start(f32[64]{0:T(128)} %param.21) | copy-start | bytes 772
  24.5 5.7 %copy-start.2 = (bf16[27,96,96]{2,1,0:T(8,128)(2,1)S(1)}, bf16[27,96,96]{2,1,0:T(8,128)(2,1)}, u32[]{:S(2)}) copy-start(bf16[27,96,96]{2,1,0:T(8,128)(2,1)} %w_ref.4) | copy-start | bytes 1492996
  30.2 1.3 %collective-permute-start.7 = (bf16[2,20,512]{2,1,0:T(8,128)(2,1)S(1)}, bf16[2,20,512]{2,1,0:T(8,128)(2,1)S(1)}, u32[]{:S(2)}, u32[]{:S(2)}) collective-permute-start(bf16[2,20,512]{2,1,0:T(8,128)(2,1)S(1)} %slice_select_fusion.1), channel_id=1, source_target_pairs={{0,4},{1,5},{2,6},{3,7},{4,0},{5,1},{6,2},{7,3},{8,12},{9,13},{10,... | collective-permute-start | bytes 122888 | tf_op jit(solution)/shard_map/ppermute | solution.py:406
  31.6 4.4 %collective-permute-start.8 = (bf16[12,20,256]{2,1,0:T(8,128)(2,1)S(1)}, bf16[12,20,256]{2,1,0:T(8,128)(2,1)S(1)}, u32[]{:S(2)}, u32[]{:S(2)}) collective-permute-start(bf16[12,20,256]{2,1,0:T(8,128)(2,1)S(1)} %get-tuple-element.77), channel_id=1, source_target_pairs={{0,4},{1,2},{2,1},{3,7},{4,0},{5,6},{6,5},{7,3},{8,12},{9,10},{10,... | collective-permute-start | bytes 368648 | tf_op jit(solution)/shard_map/ppermute | solution.py:406
  31.8 6.1 %collective-permute-start.9 = (bf16[12,20,256]{2,1,0:T(8,128)(2,1)S(1)}, bf16[12,20,256]{2,1,0:T(8,128)(2,1)S(1)}, u32[]{:S(2)}, u32[]{:S(2)}) collective-permute-start(bf16[12,20,256]{2,1,0:T(8,128)(2,1)S(1)} %get-tuple-element.76), channel_id=1, source_target_pairs={{0,1},{1,0},{2,3},{3,2},{4,5},{5,4},{6,7},{7,6},{8,9},{9,8},{10,11... | collective-permute-start | bytes 368648 | tf_op jit(solution)/shard_map/ppermute | solution.py:406
  34.3 1.3 %copy-start.3 = (bf16[27,96,96]{2,1,0:T(8,128)(2,1)S(1)}, bf16[27,96,96]{2,1,0:T(8,128)(2,1)}, u32[]{:S(2)}) copy-start(bf16[27,96,96]{2,1,0:T(8,128)(2,1)} %w_ref.5) | copy-start | bytes 1492996

commit v14 on v13

--- a/solution.py
+++ b/solution.py
@@ -155,12 +155,12 @@
         for i in range(3):
             for zo in range(group):
                 for k in range(3):
-                    lane = i * (group + 2) * pad + (zo + k) * pad
-                    t_ref[j, zo * pad : zo * pad + chan, lane : lane + chan] = w_ref[9 * i + 3 * j + k]
+                    lane = (3 * j + i) * (group + 2) * pad + (zo + k) * pad
+                    t_ref[zo * pad : zo * pad + chan, lane : lane + chan] = w_ref[9 * i + 3 * j + k]
 
 
 def banded_shape(group, pad):
-    return shaped(3, group * pad, 3 * (group + 2) * pad)
+    return shaped(group * pad, 9 * (group + 2) * pad)
 
 
 def banded(weights, group, pad):
@@ -172,27 +172,16 @@
     )(weights)
 
 
-def conv_groups(groups, t_ref, rows, group_out, group_full):
-    pitch = groups[0][0][0][0].shape[1]
-    width = sum(piece[2] for piece in groups[0][0])
-    total = None
-    for j in range(3):
-        left = []
-        for taps in groups:
-            parts = [ref[j : j + rows, :, lane : lane + n] for tap in taps for ref, lane, n in tap]
-            left.append(jnp.concatenate([p.reshape(rows * pitch, p.shape[2]) for p in parts], axis=1))
-        if width == group_full:
-            right = t_ref[j, 0:group_out, :]
-        else:
-            right = jnp.concatenate([t_ref[j, 0:group_out, i * group_full : i * group_full + width] for i in range(3)], axis=1)
-        term = mm(jnp.concatenate(left, axis=0), right, NT)
-        total = term if total is None else total + term
-    size = rows * pitch
-    return [total[g * size : g * size + size] for g in range(len(groups))]
-
-
 def conv_group(taps, t_ref, rows, group_out, group_full):
-    return conv_groups([taps], t_ref, rows, group_out, group_full)[0]
+    pitch = taps[0][0][0].shape[1]
+    width = sum(piece[2] for piece in taps[0])
+    parts = [ref[j : j + rows, :, lane : lane + n] for j in range(3) for tap in taps for ref, lane, n in tap]
+    left = jnp.concatenate([p.reshape(rows * pitch, p.shape[2]) for p in parts], axis=1)
+    if width == group_full:
+        right = t_ref[0:group_out, :]
+    else:
+        right = jnp.concatenate([t_ref[0:group_out, n * group_full : n * group_full + width] for n in range(9)], axis=1)
+    return mm(left, right, NT)
 
 
 def finish(acc, bias, mask, rows):
@@ -345,14 +334,14 @@
             copy[:, :, lane : lane + 128] = jnp.concatenate([line[:, i:], spare], axis=1)
 
 
-def level_two_groups(groups, t_ref, b_ref, masks, moved):
+def level_two_group(taps, t_ref, b_ref, masks, moved):
     rows = Y2 + 2
-    for g, acc in enumerate(conv_groups(groups, t_ref, rows, 256, 512)):
-        for q in range(2):
-            cut = slice(q * 128, q * 128 + 128)
-            value = finish(acc[:, cut], b_ref[...], masks[g][q], rows)
-            for i, ref in enumerate(moved[g]):
-                ref[:, :, cut] = value[:, i : i + X2]
+    acc = conv_group(taps, t_ref, rows, 256, 512)
+    for q in range(2):
+        cut = slice(q * 128, q * 128 + 128)
+        value = finish(acc[:, cut], b_ref[...], masks[q], rows)
+        for i, ref in enumerate(moved):
+            ref[:, :, cut] = value[:, i : i + X2]
 
 
 def level_two_masks(tab_ref):
@@ -363,7 +352,7 @@
 def level_two_middle_kernel(wide_ref, t_ref, b_ref, tab_ref, a0, a1, a2, m0, m1, m2):
     fill_pitch((a0, a1, a2), wide_ref[...])
     here = level_two_masks(tab_ref)[1]
-    level_two_groups([[[(a, 0, 512)] for a in (a0, a1, a2)]], t_ref, b_ref, [(here, here)], [(m0, m1, m2)])
+    level_two_group([[(a, 0, 512)] for a in (a0, a1, a2)], t_ref, b_ref, (here, here), (m0, m1, m2))
 
 
 def level_two_kernel(
@@ -374,13 +363,14 @@
     fill_pitch((h0, h1, h2), zr_ref[...])
     below, here, above = level_two_masks(tab_ref)
     own, mid, low, high = (a0, a1, a2), (m0, m1, m2), (i0, i1, i2), (j0, j1, j2)
-    first = [[(z, 0, 256), (a, 0, 256)] for z, a in zip((l0, l1, l2), own)]
-    second = [[(a, 256, 256), (z, 0, 256)] for z, a in zip((h0, h1, h2), own)]
-    level_two_groups([first, second], ta_ref, ba_ref, [(below, here), (here, above)], [low, high])
+    taps = [[(z, 0, 256), (a, 0, 256)] for z, a in zip((l0, l1, l2), own)]
+    level_two_group(taps, ta_ref, ba_ref, (below, here), low)
+    taps = [[(a, 256, 256), (z, 0, 256)] for z, a in zip((h0, h1, h2), own)]
+    level_two_group(taps, ta_ref, ba_ref, (here, above), high)
     mask = mask_rows(tab_ref[:, 128:256], 0, Y2, X2, lambda x: x, 2)
-    groups = [[[(a, 0, 256), (b, 0, 256)] for a, b in zip(*pair)] for pair in ((low, mid), (mid, high))]
     feat = []
-    for acc in conv_groups(groups, tb_ref, Y2, 256, 512):
+    for pair in ((low, mid), (mid, high)):
+        acc = conv_group([[(a, 0, 256), (b, 0, 256)] for a, b in zip(*pair)], tb_ref, Y2, 256, 512)
         for q in range(2):
             feat.append((jnp.maximum(acc[:, q * 128 : q * 128 + 128] + bb_ref[...], 0.0) * mask).astype(BF))
     r = iota((C2 * Z2, 128), 0)
@@ -418,11 +408,15 @@
     return below, above
 
 
-def shift_along(low_edge, high_edge, axis):
+def swaps(low_edge, high_edge, axis):
     even = parity(axis)
     first = swap(jnp.where(even, high_edge, low_edge), {axis: 0})
     second = swap(jnp.where(even, low_edge, high_edge), {axis: 1}) if lax.axis_size(axis) > 2 else first
-    return sides(first, second, axis)
+    return first, second
+
+
+def shift_along(low_edge, high_edge, axis):
+    return sides(*swaps(low_edge, high_edge, axis), axis)
 
 
 def column_pairs(field):
@@ -475,7 +469,7 @@
     win = jnp.concatenate([y_below, own, y_above], axis=0)
     z_below, z_above = shift_along(win[:, :, :128], win[:, :, lanes1 - 128 :], "gz")
     low, high = win[:, :HALO_X], win[:, X1 - HALO_X :]
-    x_below, x_above = shift_along(column_pairs(low), column_pairs(high), "gx")
+    x_got = lax.optimization_barrier(swaps(column_pairs(low), column_pairs(high), "gx"))
     rows = Y1 + 2
     left, right, g2, t1b = pl.pallas_call(
         middle_kernel,
@@ -484,9 +478,13 @@
         cost_estimate=cost(1e-7),
     )(win, t1a, bias1a, tab1, w_conv1b)
 
-    corner = [jnp.concatenate(column_lanes(x, at), axis=2) for at in (0, lanes1 - 128) for x in (x_below, x_above)]
-    low, high = jnp.concatenate(corner[:2], axis=2), jnp.concatenate(corner[2:], axis=2)
-    low, high, g2 = lax.optimization_barrier((low, high, g2))
+    corner = []
+    for lane in (0, lanes1 - 128):
+        cut = [jnp.concatenate(column_lanes(got, lane), axis=2) for got in x_got]
+        corner.append(jnp.concatenate(sides(*cut, "gx"), axis=2))
+    low, high = corner
+    low, high, g2, *x_got = lax.optimization_barrier((low, high, g2, *x_got))
+    x_below, x_above = sides(*x_got, "gx")
     corner_below, corner_above = shift_along(low, high, "gz")
     g1, g3 = pl.pallas_call(
         outer_kernel,

time: 42.8 us -> 40.7 us (0.951)
  the two profiles are of different devices: /device:TPU:0 before, /device:TPU:2 now
where the time goes in v14:
time: 40.7 us; the launch traced here: 40.5 us
  Pallas kernels  22.1 us (54%)
  starting transfers between devices  11.3 us (28%)
  waiting for transfers between devices  4.37 us (11%)
  other arithmetic  1.22 us (3%)
  between operations  1.14 us (3%)
    ppermute x10, starting transfers between devices, swap(): return lax.ppermute(value, axes, pairs)  11.3 us
    pallas_call x1, Pallas kernels, local(): pl.pallas_call(level_one_kernel, out_shape=[shaped(Y1 * X1, lanes1), shap...  5.31 us
    ppermute x10, waiting for transfers between devices, swap(): return lax.ppermute(value, axes, pairs)  4.37 us
    pallas_call x1, Pallas kernels, local(): pl.pallas_call(level_two_kernel, out_shape=shaped(C2 * Z2, Y2 * X2), scra...  4.28 us
    pallas_call x1, Pallas kernels, local(): pl.pallas_call(down1_kernel, in_specs=[pl.BlockSpec(memory_space=pltpu.HB...  4.02 us
    pallas_call x1, Pallas kernels, local(): pl.pallas_call(outer_kernel, out_shape=[shaped(rows, X1, 256), shaped(row...  2.04 us
    pallas_call x1, Pallas kernels, local(): pl.pallas_call(middle_kernel, out_shape=[shaped(ROWS1, X1, lanes1), shape...  1.58 us
    pallas_call x1, Pallas kernels, local(): pl.pallas_call(one_kernel, out_shape=shaped(lanes1, Y1 * X1), compiler_pa...  1.27 us
  transfers between devices with their start and end apart: 10, of which 4 were waited for; matrix products, arithmetic and copies ran while one was open for 2% of the time, Pallas kernels for 21%

profile of v14, /device:TPU:2, one launch (start us, length us, event | category | flops | bytes accessed | tf_op | source)
XLA Modules:
  0.0 40.5 jit_solution(1660752292865100376)
XLA Ops:
  0.7 4.0 %shard_map.149 = (bf16[16,32,512]{2,1,0:T(8,128)(2,1)S(1)}, bf16[128,384]{1,0:T(8,128)(2,1)S(1)}, bf16[128,384]{1,0:T(8,128)(2,1)S(1)}) custom-call(bf16[48,2,8,2048]{3,2,1,0:T(8,128)(2,1)} %bitcast.28, bf16[8,48,64]{2,1,0:T(8,128)(2,1)} %bitcast.29, f32[1,64]{1,0:T(1,128)} %bitcast.31, s32[8,4,32]{2,1,0:T(4,128)} %bitcast.30), custom_call_target="tpu_custom_call" | custom-call | flops 4000000000 | tf_op jit(solution)/shard_map/pallas_call | solution.py:451
  4.7 0.1 collective-permute-start
  5.0 0.6 %shard_map.150.t_ref.ta_ref = bf16[256,3456]{1,0:T(8,128)(2,1)S(1)} custom-call(bf16[27,64,64]{2,1,0:T(8,128)(2,1)S(1)} %copy-done.4), custom_call_target="tpu_custom_call" | custom-call | flops 1000000000 | tf_op jit(solution)/shard_map/pallas_call | solution.py:170
  5.6 0.4 %collective-permute-done = bf16[2,32,512]{2,1,0:T(8,128)(2,1)S(1)} collective-permute-done((bf16[2,32,512]{2,1,0:T(8,128)(2,1)S(1)}, bf16[2,32,512]{2,1,0:T(8,128)(2,1)S(1)}, u32[]{:S(2)}, u32[]{:S(2)}) %collective-permute-start) | collective-permute-done | bytes 65568 | tf_op jit(solution)/shard_map/ppermute | solution.py:396
  6.1 0.1 pad_maximum_fusion.win_ref
  6.2 0.2 fusion
  6.4 0.3 broadcast_select_fusion.4
  6.6 0.1 collective-permute-start.3
  6.7 3.0 %collective-permute-start.4 = (bf16[20,2,1536]{2,1,0:T(2,128)(2,1)S(1)}, bf16[20,2,1536]{2,1,0:T(2,128)(2,1)S(1)}, u32[]{:S(2)}, u32[]{:S(2)}) collective-permute-start(bf16[20,2,1536]{2,1,0:T(2,128)(2,1)S(1)} %get-tuple-element.88), channel_id=1, source_target_pairs={{0,4},{1,5},{2,6},{3,7},{4,0},{5,1},{6,2},{7,3},{8,16},{9,17},{10,... | collective-permute-start | bytes 368648 | tf_op jit(solution)/shard_map/ppermute | solution.py:396
  9.7 0.1 collective-permute-start.1
  9.8 3.1 %collective-permute-start.2 = (bf16[20,32,128]{2,1,0:T(8,128)(2,1)S(1)}, bf16[20,32,128]{2,1,0:T(8,128)(2,1)S(1)}, u32[]{:S(2)}, u32[]{:S(2)}) collective-permute-start(bf16[20,32,128]{2,1,0:T(8,128)(2,1)S(1)} %get-tuple-element.78), channel_id=1, source_target_pairs={{0,1},{1,0},{2,3},{3,2},{4,5},{5,4},{6,7},{7,6},{8,9},{9,8},{10,11... | collective-permute-start | bytes 491528 | tf_op jit(solution)/shard_map/ppermute | solution.py:396
  12.9 1.6 %shard_map.151 = (bf16[20,32,512]{2,1,0:T(8,128)(2,1)S(1)}, bf16[20,32,512]{2,1,0:T(8,128)(2,1)S(1)}, bf16[18,32,256]{2,1,0:T(8,128)(2,1)S(1)}, bf16[256,3456]{1,0:T(8,128)(2,1)S(1)}) custom-call(bf16[20,32,512]{2,1,0:T(8,128)(2,1)S(1)} %pad_maximum_fusion.win_ref, bf16[256,3456]{1,0:T(8,128)(2,1)S(1)} %shard_map.150.t_ref.ta_ref, f32[1,64]{1,0:T(1,128)S(1)} %bitcast.18, ...), custom_call_target="tpu_custom_call" | custom-call | flops 100000000 | tf_op jit(solution)/shard_map/pallas_call | solution.py:474
  14.5 1.1 %collective-permute-done.4 = bf16[20,2,1536]{2,1,0:T(2,128)(2,1)S(1)} collective-permute-done((bf16[20,2,1536]{2,1,0:T(2,128)(2,1)S(1)}, bf16[20,2,1536]{2,1,0:T(2,128)(2,1)S(1)}, u32[]{:S(2)}, u32[]{:S(2)}) %collective-permute-start.4) | collective-permute-done | bytes 122912 | tf_op jit(solution)/shard_map/ppermute | solution.py:396
  15.7 0.1 fusion.1
  15.8 0.1 broadcast_select_fusion.24
  15.9 0.1 broadcast_select_fusion.25
  16.1 0.1 collective-permute-start.5
  16.2 3.1 %collective-permute-start.6 = (bf16[20,2,768]{2,1,0:T(2,128)(2,1)S(1)}, bf16[20,2,768]{2,1,0:T(2,128)(2,1)S(1)}, u32[]{:S(2)}, u32[]{:S(2)}) collective-permute-start(bf16[20,2,768]{2,1,0:T(2,128)(2,1)S(1)} %bitcast.26), channel_id=1, source_target_pairs={{0,1},{1,0},{2,3},{3,2},{4,5},{5,4},{6,7},{7,6},{8,9},{9,8},{10,11... | collective-permute-start | bytes 184328 | tf_op jit(solution)/shard_map/ppermute | solution.py:396
  19.3 0.2 broadcast_select_fusion
  19.6 1.2 %shard_map.152 = (bf16[20,16,512]{2,1,0:T(8,128)(2,1)S(1)}, bf16[20,16,512]{2,1,0:T(8,128)(2,1)S(1)}, bf16[20,16,512]{2,1,0:T(8,128)(2,1)S(1)}, bf16[18,48,256]{...) custom-call(bf16[20,2,1536]{2,1,0:T(2,128)(2,1)S(1)} %get-tuple-element.87.xl_ref, ...), custom_call_target="tpu_custom_call" | custom-call | flops 3000000000 | tf_op jit(solution)/shard_map/pallas_call | solution.py:498
  20.9 2.0 %shard_map.153 = (bf16[18,32,256]{2,1,0:T(8,128)(2,1)S(1)}, bf16[18,32,128]{2,1,0:T(8,128)(2,1)S(1)}) custom-call(bf16[20,32,512]{2,1,0:T(8,128)(2,1)S(1)} %pad_maximum_fusion.win_ref, bf16[20,32,512]{2,1,0:T(8,128)(2,1)S(1)} %get-tuple-element.53.left_ref, bf16[20,32,512]{2,1,0:T(8,128)(2,1)S(1)} %get-tuple-element.54.right_ref, ...), custom_call_target="tpu_custom_call" | custom-call | flops 4000000000 | tf_op jit(solution)/shard_map/pallas_call | solution.py:489
  23.0 0.1 broadcast_select_fusion.10
  23.1 5.3 %shard_map.154 = (bf16[512,512]{1,0:T(8,128)(2,1)S(1)}, bf16[8,20,512]{2,1,0:T(8,128)(2,1)S(1)}) custom-call(bf16[20,32,128]{2,1,0:T(8,128)(2,1)S(1)} %get-tuple-element.81.zl_ref, bf16[20,32,128]{2,1,0:T(8,128)(2,1)S(1)} %get-tuple-element.80.zr_ref, bf16[20,2,768]{2,1,0:T(2,128)(2,1)S(1)} %get-tuple-element.91.cl_ref, ...), custom_call_target="tpu_custom_call" | custom-call | flops 6000000000 | tf_op jit(solution)/shard_map/pallas_call | solution.py:504
  28.6 0.3 shard_map.156.t_ref.ta_ref
  28.9 0.9 %collective-permute-done.7 = bf16[2,20,512]{2,1,0:T(8,128)(2,1)S(1)} collective-permute-done((bf16[2,20,512]{2,1,0:T(8,128)(2,1)S(1)}, bf16[2,20,512]{2,1,0:T(8,128)(2,1)S(1)}, u32[]{:S(2)}, u32[]{:S(2)}) %collective-permute-start.7) | collective-permute-done | bytes 40992 | tf_op jit(solution)/shard_map/ppermute | solution.py:396
  29.9 0.2 collective-permute-start.8
  30.1 1.5 %collective-permute-start.9 = (bf16[12,20,256]{2,1,0:T(8,128)(2,1)S(1)}, bf16[12,20,256]{2,1,0:T(8,128)(2,1)S(1)}, u32[]{:S(2)}, u32[]{:S(2)}) collective-permute-start(bf16[12,20,256]{2,1,0:T(8,128)(2,1)S(1)} %get-tuple-element.84), channel_id=1, source_target_pairs={{0,1},{1,0},{2,3},{3,2},{4,5},{5,4},{6,7},{7,6},{8,9},{9,8},{10,11... | collective-permute-start | bytes 368648 | tf_op jit(solution)/shard_map/ppermute | solution.py:396
  31.6 1.1 %shard_map.157 = (bf16[12,32,512]{2,1,0:T(8,128)(2,1)S(1)}, bf16[12,32,512]{2,1,0:T(8,128)(2,1)S(1)}, bf16[12,32,512]{2,1,0:T(8,128)(2,1)S(1)}, bf16[10,16,256]{...) custom-call(bf16[12,20,512]{2,1,0:T(8,128)(2,1)S(1)} %pad_maximum_fusion.1.wide_ref, ...), custom_call_target="tpu_custom_call" | custom-call | flops 3000000000 | tf_op jit(solution)/shard_map/pallas_call | solution.py:530
  32.7 1.3 %shard_map.155 = bf16[512,512]{1,0:T(8,128)(2,1)} custom-call(bf16[512,512]{1,0:T(8,128)(2,1)S(1)} %get-tuple-element.62.feat_ref), custom_call_target="tpu_custom_call" | custom-call | flops 2000000000 | tf_op jit(solution)/shard_map/pallas_call | solution.py:524
  34.0 0.3 shard_map.158.tb_ref
  34.3 1.9 %collective-permute-done.9 = bf16[12,20,256]{2,1,0:T(8,128)(2,1)S(1)} collective-permute-done((bf16[12,20,256]{2,1,0:T(8,128)(2,1)S(1)}, bf16[12,20,256]{2,1,0:T(8,128)(2,1)S(1)}, u32[]{:S(2)}, u32[]{:S(2)}) %collective-permute-start.9) | collective-permute-done | bytes 122912 | tf_op jit(solution)/shard_map/ppermute | solution.py:396
  36.2 4.3 %shard_map.159 = bf16[384,128]{1,0:T(8,128)(2,1)} custom-call(bf16[12,32,512]{2,1,0:T(8,128)(2,1)S(1)} %get-tuple-element.65.a0, bf16[12,32,512]{2,1,0:T(8,128)(2,1)S(1)} %get-tuple-element.66.a1, bf16[12,32,512]{2,1,0:T(8,128)(2,1)S(1)} %get-tuple-element.67.a2, bf16[10,16,256]{2,1,0:T(8,128)(2,1)S(1)} %get-tuple-element.68.m0, ...), custom_call_target="tpu_custom_call" | custom-call | flops 5000000000 | tf_op jit(solution)/shard_map/pallas_call | solution.py:536
  (43 shorter events, 0.5 us)
Async XLA Ops:
  0.6 4.2 %copy-start.7 = (f32[96]{0:T(128)S(1)}, f32[96]{0:T(128)}, u32[]{:S(2)}) copy-start(f32[96]{0:T(128)} %param.23) | copy-start | bytes 1156
  0.7 4.2 %copy-start.8 = (f32[96]{0:T(128)S(1)}, f32[96]{0:T(128)}, u32[]{:S(2)}) copy-start(f32[96]{0:T(128)} %param.25) | copy-start | bytes 1156
  0.7 4.2 %copy-start.9 = (f32[96]{0:T(128)S(1)}, f32[96]{0:T(128)}, u32[]{:S(2)}) copy-start(f32[96]{0:T(128)} %param.27) | copy-start | bytes 1156
  0.7 4.3 %copy-start.6 = (bf16[8,96,64]{1,2,0:T(8,128)(2,1)S(1)}, bf16[8,96,64]{1,2,0:T(8,128)(2,1)}, u32[]{:S(2)}) copy-start(bf16[8,96,64]{1,2,0:T(8,128)(2,1)} %param.22) | copy-start | bytes 294916
  0.7 4.3 %copy-start.4 = (bf16[27,64,64]{2,1,0:T(8,128)(2,1)S(1)}, bf16[27,64,64]{2,1,0:T(8,128)(2,1)}, u32[]{:S(2)}) copy-start(bf16[27,64,64]{2,1,0:T(8,128)(2,1)} %w_ref.2) | copy-start | bytes 663556
  4.7 1.3 %collective-permute-start = (bf16[2,32,512]{2,1,0:T(8,128)(2,1)S(1)}, bf16[2,32,512]{2,1,0:T(8,128)(2,1)S(1)}, u32[]{:S(2)}, u32[]{:S(2)}) collective-permute-start(bf16[2,32,512]{2,1,0:T(8,128)(2,1)S(1)} %slice_select_fusion), channel_id=1, source_target_pairs={{0,4},{1,5},{2,6},{3,7},{4,0},{5,1},{6,2},{7,3},{8,12},{9,13},{10,... | collective-permute-start | bytes 196616 | tf_op jit(solution)/shard_map/ppermute | solution.py:396
  5.6 7.3 %copy-start = (bf16[27,64,64]{2,1,0:T(8,128)(2,1)S(1)}, bf16[27,64,64]{2,1,0:T(8,128)(2,1)}, u32[]{:S(2)}) copy-start(bf16[27,64,64]{2,1,0:T(8,128)(2,1)} %w_ref.3) | copy-start | bytes 663556
  5.6 7.3 %copy-start.1 = (f32[64]{0:T(128)S(1)}, f32[64]{0:T(128)}, u32[]{:S(2)}) copy-start(f32[64]{0:T(128)} %param.19) | copy-start | bytes 772
  6.6 7.9 %collective-permute-start.3 = (bf16[20,2,1536]{2,1,0:T(2,128)(2,1)S(1)}, bf16[20,2,1536]{2,1,0:T(2,128)(2,1)S(1)}, u32[]{:S(2)}, u32[]{:S(2)}) collective-permute-start(bf16[20,2,1536]{2,1,0:T(2,128)(2,1)S(1)} %get-tuple-element.89), channel_id=1, source_target_pairs={{0,8},{1,9},{2,10},{3,11},{4,12},{5,13},{6,14},{7,15},{8,0},{9,1},... | collective-permute-start | bytes 368648 | tf_op jit(solution)/shard_map/ppermute | solution.py:396
  6.7 9.0 %collective-permute-start.4 = (bf16[20,2,1536]{2,1,0:T(2,128)(2,1)S(1)}, bf16[20,2,1536]{2,1,0:T(2,128)(2,1)S(1)}, u32[]{:S(2)}, u32[]{:S(2)}) collective-permute-start(bf16[20,2,1536]{2,1,0:T(2,128)(2,1)S(1)} %get-tuple-element.88), channel_id=1, source_target_pairs={{0,4},{1,5},{2,6},{3,7},{4,0},{5,1},{6,2},{7,3},{8,16},{9,17},{10,... | collective-permute-start | bytes 368648 | tf_op jit(solution)/shard_map/ppermute | solution.py:396
  9.7 11.1 %collective-permute-start.1 = (bf16[20,32,128]{2,1,0:T(8,128)(2,1)S(1)}, bf16[20,32,128]{2,1,0:T(8,128)(2,1)S(1)}, u32[]{:S(2)}, u32[]{:S(2)}) collective-permute-start(bf16[20,32,128]{2,1,0:T(8,128)(2,1)S(1)} %get-tuple-element.79), channel_id=1, source_target_pairs={{0,4},{1,2},{2,1},{3,7},{4,0},{5,6},{6,5},{7,3},{8,12},{9,10},{10,... | collective-permute-start | bytes 491528 | tf_op jit(solution)/shard_map/ppermute | solution.py:396
  9.8 11.0 %collective-permute-start.2 = (bf16[20,32,128]{2,1,0:T(8,128)(2,1)S(1)}, bf16[20,32,128]{2,1,0:T(8,128)(2,1)S(1)}, u32[]{:S(2)}, u32[]{:S(2)}) collective-permute-start(bf16[20,32,128]{2,1,0:T(8,128)(2,1)S(1)} %get-tuple-element.78), channel_id=1, source_target_pairs={{0,1},{1,0},{2,3},{3,2},{4,5},{5,4},{6,7},{7,6},{8,9},{9,8},{10,11... | collective-permute-start | bytes 491528 | tf_op jit(solution)/shard_map/ppermute | solution.py:396
  16.1 6.8 %collective-permute-start.5 = (bf16[20,2,768]{2,1,0:T(2,128)(2,1)S(1)}, bf16[20,2,768]{2,1,0:T(2,128)(2,1)S(1)}, u32[]{:S(2)}, u32[]{:S(2)}) collective-permute-start(bf16[20,2,768]{2,1,0:T(2,128)(2,1)S(1)} %bitcast.27), channel_id=1, source_target_pairs={{0,4},{1,2},{2,1},{3,7},{4,0},{5,6},{6,5},{7,3},{8,12},{9,10},{10,... | collective-permute-start | bytes 184328 | tf_op jit(solution)/shard_map/ppermute | solution.py:396
  16.2 6.8 %collective-permute-start.6 = (bf16[20,2,768]{2,1,0:T(2,128)(2,1)S(1)}, bf16[20,2,768]{2,1,0:T(2,128)(2,1)S(1)}, u32[]{:S(2)}, u32[]{:S(2)}) collective-permute-start(bf16[20,2,768]{2,1,0:T(2,128)(2,1)S(1)} %bitcast.26), channel_id=1, source_target_pairs={{0,1},{1,0},{2,3},{3,2},{4,5},{5,4},{6,7},{7,6},{8,9},{9,8},{10,11... | collective-permute-start | bytes 184328 | tf_op jit(solution)/shard_map/ppermute | solution.py:396
  20.9 2.2 %copy-start.5 = (f32[64]{0:T(128)S(1)}, f32[64]{0:T(128)}, u32[]{:S(2)}) copy-start(f32[64]{0:T(128)} %param.21) | copy-start | bytes 772
  23.1 5.4 %copy-start.2 = (bf16[27,96,96]{2,1,0:T(8,128)(2,1)S(1)}, bf16[27,96,96]{2,1,0:T(8,128)(2,1)}, u32[]{:S(2)}) copy-start(bf16[27,96,96]{2,1,0:T(8,128)(2,1)} %w_ref.4) | copy-start | bytes 1492996
  28.5 1.3 %collective-permute-start.7 = (bf16[2,20,512]{2,1,0:T(8,128)(2,1)S(1)}, bf16[2,20,512]{2,1,0:T(8,128)(2,1)S(1)}, u32[]{:S(2)}, u32[]{:S(2)}) collective-permute-start(bf16[2,20,512]{2,1,0:T(8,128)(2,1)S(1)} %slice_select_fusion.1), channel_id=1, source_target_pairs={{0,4},{1,5},{2,6},{3,7},{4,0},{5,1},{6,2},{7,3},{8,12},{9,13},{10,... | collective-permute-start | bytes 122888 | tf_op jit(solution)/shard_map/ppermute | solution.py:396
  29.9 4.4 %collective-permute-start.8 = (bf16[12,20,256]{2,1,0:T(8,128)(2,1)S(1)}, bf16[12,20,256]{2,1,0:T(8,128)(2,1)S(1)}, u32[]{:S(2)}, u32[]{:S(2)}) collective-permute-start(bf16[12,20,256]{2,1,0:T(8,128)(2,1)S(1)} %get-tuple-element.85), channel_id=1, source_target_pairs={{0,4},{1,2},{2,1},{3,7},{4,0},{5,6},{6,5},{7,3},{8,12},{9,10},{10,... | collective-permute-start | bytes 368648 | tf_op jit(solution)/shard_map/ppermute | solution.py:396
  30.1 6.1 %collective-permute-start.9 = (bf16[12,20,256]{2,1,0:T(8,128)(2,1)S(1)}, bf16[12,20,256]{2,1,0:T(8,128)(2,1)S(1)}, u32[]{:S(2)}, u32[]{:S(2)}) collective-permute-start(bf16[12,20,256]{2,1,0:T(8,128)(2,1)S(1)} %get-tuple-element.84), channel_id=1, source_target_pairs={{0,1},{1,0},{2,3},{3,2},{4,5},{5,4},{6,7},{7,6},{8,9},{9,8},{10,11... | collective-permute-start | bytes 368648 | tf_op jit(solution)/shard_map/ppermute | solution.py:396
  32.7 1.3 %copy-start.3 = (bf16[27,96,96]{2,1,0:T(8,128)(2,1)S(1)}, bf16[27,96,96]{2,1,0:T(8,128)(2,1)}, u32[]{:S(2)}) copy-start(bf16[27,96,96]{2,1,0:T(8,128)(2,1)} %w_ref.5) | copy-start | bytes 1492996

commit v15 on v14

--- a/solution.py
+++ b/solution.py
@@ -30,6 +30,7 @@
 ROWS2 = Y2 + 2 * HALO
 EDGE = 16
 PITCH2 = 32
+FACE = HALO_X // 2 * Z1 * C1
 BF = jnp.bfloat16
 F32 = jnp.float32
 NN = (((1,), (0,)), ((), ()))
@@ -60,7 +61,7 @@
     y_block = (iota(shape, 0) + (y_start + cell)) >> bits
     x_block = jnp.minimum((x_of(iota(shape, 1)) + XB_BELOW * cell) >> bits, XB - 1)
     hit = one_hot(y_block * XB_PITCH + x_block == iota(shape, 2)).reshape(rows * pitch, 128)
-    return mm(hit, tab)
+    return mm(hit, tab).astype(BF)
 
 
 def tissue_tables(t_ref):
@@ -89,8 +90,13 @@
     return spread(64, 320), spread(128, 256)
 
 
+def second_cell(r):
+    return jnp.where(r < X1, r, jnp.where(r < X1 + 8, r - X1 - 4, r - 8))
+
+
 def down1_kernel(
-    v_hbm, wd_hbm, b_hbm, t_hbm, out_ref, tab_ref, tab2_ref, v_ref, w_ref, b_ref, t_ref, wd_ref, cells_ref, sems
+    v_hbm, wd_hbm, b_hbm, t_hbm, out_ref, face_ref, inner_ref, edge_ref, second_ref, down_ref, two_ref, last_ref,
+    v_ref, w_ref, b_ref, t_ref, wd_ref, cells_ref, sems,
 ):
     half = v_ref.shape[2]
     kz = C0 * half
@@ -106,8 +112,14 @@
 
     copies[0].wait()
     tab, tab2 = tissue_tables(t_ref)
-    tab_ref[...] = tab
-    tab2_ref[...] = tab2
+    here, here2 = tab[:, 128:256], tab2[:, 128:256]
+    inner_ref[...] = mask_rows(tab, -1, Y1 + 2, X1, lambda x: x, 4)
+    edge_ref[...] = mask_rows(tab, -1, Y1 + 2, EDGE, lambda r: jnp.where(r < 8, r - 5, r + X1 - 9), 4)
+    second_ref[...] = mask_rows(here, 0, Y1, X1 + EDGE, second_cell, 4)
+    down_ref[: Y2 * X2] = mask_rows(here2, 0, Y2, X2, lambda x: x, 2)
+    down_ref[Y2 * X2 :] = mask_rows(here2, 0, Y2, EDGE // 2, lambda r: jnp.where(r < 4, r - 2, r + X2 - 4), 2)
+    two_ref[...] = mask_rows(tab2, -1, Y2 + 2, PITCH2, lambda x: x - 1, 2)
+    last_ref[...] = mask_rows(here2, 0, Y2, X2, lambda x: x, 2)
     copies[1].wait()
     copies[2].wait()
     r = iota((kz, 2 * C0), 0)
@@ -136,12 +148,17 @@
                     piece = cells[64 * ab : 64 * ab + 64, h * part : h * part + part]
                     cells_ref[n, h, m * 64 : m * 64 + 64, ab * part : ab * part + part] = piece
         acc = [acc[h] + mm(cells_ref[n, h], wd_ref[n]) for h in range(2)]
-    mask = mask_rows(tab[:, 128:256], 0, Y1, X1, lambda x: x, 4)
+    mask = inner_ref[X1 : X1 + Y1 * X1, 128:256]
     bias = twice(b_ref)
     for h in range(2):
         for q in range(2):
             value = finish(acc[h][:, q * 128 : q * 128 + 128], bias, mask, Y1)
-            out_ref[:, :, (2 * h + q) * 128 : (2 * h + q + 1) * 128] = value
+            chunk = 2 * h + q
+            out_ref[:, :, chunk * 128 : chunk * 128 + 128] = value
+            for side, start in enumerate((0, X1 - HALO_X)):
+                for pair in range(HALO_X // 2):
+                    lane = side * FACE + (chunk * (HALO_X // 2) + pair) * 128
+                    face_ref[:, :, lane : lane + 128] = value[:, start + 2 * pair : start + 2 * pair + 2]
 
 
 def twice(b_ref):
@@ -172,16 +189,20 @@
     )(weights)
 
 
-def conv_group(taps, t_ref, rows, group_out, group_full):
+def conv_group(taps, t_ref, rows, group_out, group_full, split=False):
     pitch = taps[0][0][0].shape[1]
     width = sum(piece[2] for piece in taps[0])
-    parts = [ref[j : j + rows, :, lane : lane + n] for j in range(3) for tap in taps for ref, lane, n in tap]
-    left = jnp.concatenate([p.reshape(rows * pitch, p.shape[2]) for p in parts], axis=1)
-    if width == group_full:
-        right = t_ref[0:group_out, :]
-    else:
-        right = jnp.concatenate([t_ref[0:group_out, n * group_full : n * group_full + width] for n in range(9)], axis=1)
-    return mm(left, right, NT)
+    total = 0.0
+    for js in ((0,), (1,), (2,)) if split else ((0, 1, 2),):
+        parts = [ref[j : j + rows, :, lane : lane + n] for j in js for tap in taps for ref, lane, n in tap]
+        left = jnp.concatenate([p.reshape(rows * pitch, p.shape[2]) for p in parts], axis=1)
+        first, last = 3 * js[0], 3 * js[-1] + 3
+        if width == group_full:
+            right = t_ref[0:group_out, first * group_full : last * group_full]
+        else:
+            right = jnp.concatenate([t_ref[0:group_out, n * group_full : n * group_full + width] for n in range(first, last)], axis=1)
+        total = total + mm(left, right, NT)
+    return total
 
 
 def finish(acc, bias, mask, rows):
@@ -196,24 +217,23 @@
     right[:, :, cut] = jnp.concatenate([inner[:, 1:], none], axis=1)
 
 
-def middle_kernel(win_ref, t_ref, b_ref, tab_ref, w_ref, left_ref, right_ref, out_ref, next_ref):
+def middle_kernel(win_ref, t_ref, b_ref, mask_ref, w_ref, left_ref, right_ref, out_ref, next_ref):
     fill_banded(w_ref, next_ref, 4, C1)
     for q in range(4):
         fill_sides(left_ref, right_ref, q * 128, win_ref[:, :, q * 128 : q * 128 + 128])
     rows = Y1 + 2
-    mask = mask_rows(tab_ref[:, 128:256], -1, rows, X1, lambda x: x, 4)
+    mask = mask_ref[:, 128:256]
     acc = conv_group([[(ref, 128, 384)] for ref in (left_ref, win_ref, right_ref)], t_ref, rows, 256, 384)
     for q in range(2):
         cut = slice(q * 128, q * 128 + 128)
         out_ref[:, :, cut] = finish(acc[:, cut], twice(b_ref), mask, rows)
 
 
-def outer_kernel(win_ref, left_ref, right_ref, zl_ref, zr_ref, t_ref, b_ref, tab_ref, low_ref, high_ref, ll, lr, hl, hr):
+def outer_kernel(win_ref, left_ref, right_ref, zl_ref, zr_ref, t_ref, b_ref, mask, low_ref, high_ref, ll, lr, hl, hr):
     fill_sides(ll, lr, 0, zl_ref[...])
     fill_sides(hl, hr, 0, zr_ref[...])
     own = (left_ref, win_ref, right_ref)
     rows = Y1 + 2
-    mask = mask_rows(tab_ref[...], -1, rows, X1, lambda x: x, 4)
     taps = [[(z, 0, 128), (ref, 0, 256)] for z, ref in zip((ll, zl_ref, lr), own)]
     acc = conv_group(taps, t_ref, rows, 256, 384)
     for q in range(2):
@@ -231,9 +251,8 @@
         copies[i][...] = jnp.concatenate([line[:, i:], jnp.zeros_like(line[:, :i])], axis=1)
 
 
-def edge_masks(tab_ref):
-    mask = mask_rows(tab_ref[...], -1, Y1 + 2, EDGE, lambda r: jnp.where(r < 8, r - 5, r + X1 - 9), 4)
-    return [mask[:, q * 128 : q * 128 + 128] for q in range(3)]
+def lane_chunks(ref):
+    return [ref[:, lane : lane + 128] for lane in range(0, ref.shape[1], 128)]
 
 
 def edge_group(taps, t_ref, b_ref, masks, inner_ref, moved):
@@ -252,46 +271,42 @@
             copy[:, X1:, cut] = jnp.concatenate([edge[:, i:], jnp.zeros((rows, i, 128), BF)], axis=1)
 
 
-def column_lanes(field, lane, stride=Z1 * C1):
-    return [field[:, :, first : first + 128] for first in range(lane, field.shape[2], stride)]
-
-
-def edge_middle_kernel(xl_ref, win_ref, xr_ref, g_ref, t_ref, b_ref, tab_ref, e0, e1, e2, m0, m1, m2):
+def column_pieces(ref, chunk, side=0):
+    first = (side + chunk) * (HALO_X // 2) * 128
+    return [ref[:, :, lane : lane + 128] for lane in range(first, first + HALO_X // 2 * 128, 128)]
+
+
+def edge_middle_kernel(xl_ref, win_ref, xr_ref, g_ref, t_ref, b_ref, mask_ref, e0, e1, e2, m0, m1, m2):
     for lane in range(0, Z1 * C1, 128):
         cut = slice(lane, lane + 128)
         inner = win_ref[:, :, cut]
-        left, right = (column_lanes(ref, lane) for ref in (xl_ref, xr_ref))
+        left, right = (column_pieces(ref, lane // 128) for ref in (xl_ref, xr_ref))
         pieces = left + [inner[:, :2], inner[:, X1 - 2 :]] + right
         fill_edges([e.at[:, :, cut] for e in (e0, e1, e2)], pieces)
-    here = edge_masks(tab_ref)[1]
+    here = mask_ref[:, 128:256]
     edge_group([[(e, 128, 384)] for e in (e0, e1, e2)], t_ref, b_ref, (here, here), g_ref, (m0, m1, m2))
 
 
 def level_one_kernel(
-    zl_ref, zr_ref, cl_ref, cr_ref, e0, e1, e2, m0, m1, m2, g1_ref, g3_ref, ta_ref, tb_ref, ba_ref, bb_ref, wd_ref, bd_ref, tab_ref,
-    tab2_ref, feat_ref, down_ref, l0, l1, l2, h0, h1, h2, i0, i1, i2, j0, j1, j2, side_ref, d_ref,
+    zl_ref, zr_ref, cl_ref, cr_ref, e0, e1, e2, m0, m1, m2, g1_ref, g3_ref, ta_ref, tb_ref, ba_ref, bb_ref, wd_ref, bd_ref, edge_ref,
+    second_ref, last_ref, feat_ref, down_ref, l0, l1, l2, h0, h1, h2, i0, i1, i2, j0, j1, j2, side_ref, d_ref,
 ):
     own, mid, low, high = (e0, e1, e2), (m0, m1, m2), (i0, i1, i2), (j0, j1, j2)
     for z_ref, c_ref, copies in ((zl_ref, cl_ref, (l0, l1, l2)), (zr_ref, cr_ref, (h0, h1, h2))):
         inner = z_ref[...]
-        corner = column_lanes(c_ref, 0, 128)
-        fill_edges(copies, corner[:3] + [inner[:, :2], inner[:, X1 - 2 :]] + corner[3:])
-    below, here, above = edge_masks(tab_ref)
+        fill_edges(copies, column_pieces(c_ref, 0) + [inner[:, :2], inner[:, X1 - 2 :]] + column_pieces(c_ref, 1))
+    below, here, above = lane_chunks(edge_ref)
     taps = [[(z, 0, 128), (e, 0, 256)] for z, e in zip((l0, l1, l2), own)]
     edge_group(taps, ta_ref, ba_ref, (below, here), g1_ref, low)
     taps = [[(e, 384, 128), (z, 0, 128)] for z, e in zip((h0, h1, h2), own)]
     edge_group(taps, ta_ref, ba_ref, (above,), g3_ref, high)
 
-    def cell_of(r):
-        return jnp.where(r < X1, r, jnp.where(r < X1 + 8, r - X1 - 4, r - 8))
-
-    mask = mask_rows(tab_ref[:, 128:256], 0, Y1, X1 + EDGE, cell_of, 4)
     first = [[(a, 0, 256), (b, 0, 128)] for a, b in zip(low, mid)]
     second = [[(a, 0, 256), (b, 0, 128)] for a, b in zip(mid, high)]
     for g, taps in enumerate((first, second)):
         acc = conv_group(taps, tb_ref, Y1, 256, 384)
         for q in range(2):
-            value = finish(acc[:, q * 128 : q * 128 + 128], twice(bb_ref), mask, Y1)
+            value = finish(acc[:, q * 128 : q * 128 + 128], twice(bb_ref), second_ref[...], Y1)
             cut = slice((2 * g + q) * 128, (2 * g + q + 1) * 128)
             feat_ref[:, cut] = value[:, :X1].reshape(Y1 * X1, 128)
             side_ref[:, cut] = value[:, X1:].reshape(Y1 * EDGE, 128)
@@ -308,13 +323,11 @@
     cells = mm(select, side_ref[...]).astype(BF)
     for q in range(4):
         d_ref[q, Y2 * X2 :, :] = cells[q * quarter : (q + 1) * quarter]
-    inner_mask = mask_rows(tab2_ref[:, 128:256], 0, Y2, X2, lambda x: x, 2)
-    side_mask = mask_rows(tab2_ref[:, 128:256], 0, Y2, EDGE // 2, lambda r: jnp.where(r < 4, r - 2, r + X2 - 4), 2)
     for z in range(Z2):
         left = jnp.concatenate([d_ref[q, :, z * 128 : z * 128 + 128] for q in range(4)], axis=1)
         acc = mm(left, wd_ref[...])
-        inner = finish(acc[: Y2 * X2], bd_ref[...], inner_mask, Y2)
-        side = finish(acc[Y2 * X2 :], bd_ref[...], side_mask, Y2)
+        inner = finish(acc[: Y2 * X2], bd_ref[...], last_ref[: Y2 * X2], Y2)
+        side = finish(acc[Y2 * X2 :], bd_ref[...], last_ref[Y2 * X2 :], Y2)
         down_ref[:, :, z * CP : z * CP + CP] = jnp.concatenate([side[:, 0:2], inner, side[:, 4:6]], axis=1)
 
 
@@ -336,7 +349,7 @@
 
 def level_two_group(taps, t_ref, b_ref, masks, moved):
     rows = Y2 + 2
-    acc = conv_group(taps, t_ref, rows, 256, 512)
+    acc = conv_group(taps, t_ref, rows, 256, 512, split=True)
     for q in range(2):
         cut = slice(q * 128, q * 128 + 128)
         value = finish(acc[:, cut], b_ref[...], masks[q], rows)
@@ -344,35 +357,29 @@
             ref[:, :, cut] = value[:, i : i + X2]
 
 
-def level_two_masks(tab_ref):
-    mask = mask_rows(tab_ref[...], -1, Y2 + 2, PITCH2, lambda x: x - 1, 2)
-    return [mask[:, q * 128 : q * 128 + 128] for q in range(3)]
-
-
-def level_two_middle_kernel(wide_ref, t_ref, b_ref, tab_ref, a0, a1, a2, m0, m1, m2):
+def level_two_middle_kernel(wide_ref, t_ref, b_ref, mask_ref, a0, a1, a2, m0, m1, m2):
     fill_pitch((a0, a1, a2), wide_ref[...])
-    here = level_two_masks(tab_ref)[1]
+    here = mask_ref[:, 128:256]
     level_two_group([[(a, 0, 512)] for a in (a0, a1, a2)], t_ref, b_ref, (here, here), (m0, m1, m2))
 
 
 def level_two_kernel(
-    a0, a1, a2, m0, m1, m2, zl_ref, zr_ref, ta_ref, tb_ref, ba_ref, bb_ref, tab_ref, out_ref,
+    a0, a1, a2, m0, m1, m2, zl_ref, zr_ref, ta_ref, tb_ref, ba_ref, bb_ref, mask_ref, last_ref, out_ref,
     l0, l1, l2, h0, h1, h2, i0, i1, i2, j0, j1, j2,
 ):
     fill_pitch((l0, l1, l2), zl_ref[...])
     fill_pitch((h0, h1, h2), zr_ref[...])
-    below, here, above = level_two_masks(tab_ref)
+    below, here, above = lane_chunks(mask_ref)
     own, mid, low, high = (a0, a1, a2), (m0, m1, m2), (i0, i1, i2), (j0, j1, j2)
     taps = [[(z, 0, 256), (a, 0, 256)] for z, a in zip((l0, l1, l2), own)]
     level_two_group(taps, ta_ref, ba_ref, (below, here), low)
     taps = [[(a, 256, 256), (z, 0, 256)] for z, a in zip((h0, h1, h2), own)]
     level_two_group(taps, ta_ref, ba_ref, (here, above), high)
-    mask = mask_rows(tab_ref[:, 128:256], 0, Y2, X2, lambda x: x, 2)
     feat = []
     for pair in ((low, mid), (mid, high)):
-        acc = conv_group([[(a, 0, 256), (b, 0, 256)] for a, b in zip(*pair)], tb_ref, Y2, 256, 512)
+        acc = conv_group([[(a, 0, 256), (b, 0, 256)] for a, b in zip(*pair)], tb_ref, Y2, 256, 512, split=True)
         for q in range(2):
-            feat.append((jnp.maximum(acc[:, q * 128 : q * 128 + 128] + bb_ref[...], 0.0) * mask).astype(BF))
+            feat.append(finish(acc[:, q * 128 : q * 128 + 128], bb_ref[...], last_ref[...], 1)[0])
     r = iota((C2 * Z2, 128), 0)
     order = one_hot_rows(((r & 3) << 7) | (r >> 2), Z2 * CP)
     out_ref[...] = mm(order, jnp.concatenate(feat, axis=1), NT).astype(BF)
@@ -419,10 +426,6 @@
     return sides(*swaps(low_edge, high_edge, axis), axis)
 
 
-def column_pairs(field):
-    return jnp.concatenate([field[:, i : i + 2] for i in range(0, field.shape[1], 2)], axis=2)
-
-
 def params():
     return pltpu.CompilerParams(vmem_limit_bytes=VMEM_BYTES)
 
@@ -448,10 +451,19 @@
     half = depth // 2
     operands = [volume.reshape(C0, 2, half, -1), jnp.swapaxes(w_down1, 1, 2), b_down1[None], tissue.transpose(1, 2, 0)]
     operands = [pltpu.with_memory_space_constraint(x, pltpu.HBM) for x in operands]
-    own, tab1, tab2 = pl.pallas_call(
+    own, faces, inner_mask, edge_mask, second_mask, down_mask, two_mask, last_mask = pl.pallas_call(
         down1_kernel,
         in_specs=[pl.BlockSpec(memory_space=pltpu.HBM)] * 4,
-        out_shape=[shaped(Y1, X1, lanes1), shaped(128, 384), shaped(128, 384)],
+        out_shape=[
+            shaped(Y1, X1, lanes1),
+            shaped(Y1, 2, 2 * FACE),
+            shaped((Y1 + 2) * X1, 384),
+            shaped((Y1 + 2) * EDGE, 384),
+            shaped(Y1 * (X1 + EDGE), 128),
+            shaped(Y2 * (X2 + EDGE // 2), 128),
+            shaped((Y2 + 2) * PITCH2, 384),
+            shaped(Y2 * X2, 128),
+        ],
         scratch_shapes=[pltpu.VMEM(x.shape, x.dtype) for x in operands]
         + [
             pltpu.VMEM((C0 // 16, 64 * half, lanes1 // 2), BF),
@@ -465,42 +477,46 @@
     t1a = banded(w_conv1a, 4, C1)
     bias1a = b_conv1a[None]
 
-    y_below, y_above = shift_along(own[:HALO], own[Y1 - HALO :], "gy")
-    win = jnp.concatenate([y_below, own, y_above], axis=0)
+    def with_halo(field):
+        below, above = shift_along(field[:HALO], field[field.shape[0] - HALO :], "gy")
+        return jnp.concatenate([below, field, above], axis=0)
+
+    faces = with_halo(faces)
+    win = with_halo(own)
     z_below, z_above = shift_along(win[:, :, :128], win[:, :, lanes1 - 128 :], "gz")
-    low, high = win[:, :HALO_X], win[:, X1 - HALO_X :]
-    x_got = lax.optimization_barrier(swaps(column_pairs(low), column_pairs(high), "gx"))
+    x_got = lax.optimization_barrier(swaps(faces[:, :, :FACE], faces[:, :, FACE:], "gx"))
     rows = Y1 + 2
     left, right, g2, t1b = pl.pallas_call(
         middle_kernel,
         out_shape=[shaped(ROWS1, X1, lanes1), shaped(ROWS1, X1, lanes1), shaped(rows, X1, 256), banded_shape(4, C1)],
         compiler_params=params(),
         cost_estimate=cost(1e-7),
-    )(win, t1a, bias1a, tab1, w_conv1b)
-
-    corner = []
-    for lane in (0, lanes1 - 128):
-        cut = [jnp.concatenate(column_lanes(got, lane), axis=2) for got in x_got]
-        corner.append(jnp.concatenate(sides(*cut, "gx"), axis=2))
-    low, high = corner
+    )(win, t1a, bias1a, inner_mask, w_conv1b)
+
+    corner = HALO_X // 2 * 2 * C1
+    low, high = (jnp.concatenate([got[:, :, cut] for got in x_got], axis=2) for cut in (slice(corner), slice(FACE - corner, FACE)))
     low, high, g2, *x_got = lax.optimization_barrier((low, high, g2, *x_got))
     x_below, x_above = sides(*x_got, "gx")
-    corner_below, corner_above = shift_along(low, high, "gz")
+    corner_got = swaps(low, high, "gz")
     g1, g3 = pl.pallas_call(
         outer_kernel,
         out_shape=[shaped(rows, X1, 256), shaped(rows, X1, 128)],
         scratch_shapes=[pltpu.VMEM((ROWS1, X1, 128), BF)] * 4,
         compiler_params=params(),
         cost_estimate=cost(4e-6),
-    )(win, left, right, z_below, z_above, t1a, bias1a, tab1)
-
+    )(win, left, right, z_below, z_above, t1a, bias1a, inner_mask)
+
+    *corner_got, g1, g3 = lax.optimization_barrier((*corner_got, g1, g3))
+    corner_below, corner_above = (
+        jnp.concatenate(sides(got[:, :, :corner], got[:, :, corner:], "gx"), axis=2) for got in sides(*corner_got, "gz")
+    )
     wide_x = X1 + EDGE
     edges = pl.pallas_call(
         edge_middle_kernel,
         out_shape=[shaped(ROWS1, EDGE, lanes1)] * 3 + [shaped(rows, wide_x, 256)] * 3,
         compiler_params=params(),
         cost_estimate=cost(3e-6),
-    )(x_below, win, x_above, g2, t1a, bias1a, tab1)
+    )(x_below, win, x_above, g2, t1a, bias1a, edge_mask)
     feat, down = pl.pallas_call(
         level_one_kernel,
         out_shape=[shaped(Y1 * X1, lanes1), shaped(Y2, X2 + 2 * HALO_X2, Z2 * CP)],
@@ -512,13 +528,12 @@
         cost_estimate=cost(6e-6),
     )(
         z_below, z_above, corner_below, corner_above, *edges, g1, g3, t1a, t1b, bias1a, b_conv1b[None],
-        pad_lanes(jnp.swapaxes(w_down2, 1, 2).reshape(8 * C1, C2)), pad_lanes(b_down2[None]), tab1, tab2,
+        pad_lanes(jnp.swapaxes(w_down2, 1, 2).reshape(8 * C1, C2)), pad_lanes(b_down2[None]), edge_mask, second_mask, down_mask,
     )
 
     down, w_conv2a = lax.optimization_barrier((down, w_conv2a))
     t2a = banded(w_conv2a, 2, CP)
-    y_below, y_above = shift_along(down[:HALO], down[Y2 - HALO :], "gy")
-    wide = jnp.concatenate([y_below, down, y_above], axis=0)
+    wide = with_halo(down)
     feat, wide, w_conv2b = lax.optimization_barrier((feat, wide, w_conv2b))
     t2b = banded(w_conv2b, 2, CP)
     one = pl.pallas_call(
@@ -532,14 +547,14 @@
         out_shape=[shaped(ROWS2, PITCH2, Z2 * CP)] * 3 + moved,
         compiler_params=params(),
         cost_estimate=cost(3e-6),
-    )(wide, t2a, bias2a, tab2)
+    )(wide, t2a, bias2a, two_mask)
     two = pl.pallas_call(
         level_two_kernel,
         out_shape=shaped(C2 * Z2, Y2 * X2),
         scratch_shapes=[pltpu.VMEM((ROWS2, PITCH2, 2 * CP), BF)] * 6 + [pltpu.VMEM((Y2 + 2, X2, 2 * CP), BF)] * 6,
         compiler_params=params(),
         cost_estimate=cost(5e-6),
-    )(*middle, z_below, z_above, t2a, t2b, bias2a, pad_lanes(b_conv2b[None]), tab2)
+    )(*middle, z_below, z_above, t2a, t2b, bias2a, pad_lanes(b_conv2b[None]), two_mask, last_mask)
     return one.reshape(C1, Z1, Y1 * X1), two.reshape(C2, Z2, Y2 * X2)
 
 

time: 40.7 us -> 45 us (1.11)
  the two profiles are of different devices: /device:TPU:2 before, /device:TPU:10 now
where the time goes in v15:
time: 45 us; the launch traced here: 44.8 us
  Pallas kernels  22.4 us (50%)
  starting transfers between devices  10.8 us (24%)
  waiting for transfers between devices  4.38 us (10%)
  other arithmetic  3.6 us (8%)
  local copies, waits for them, and re-layouts  2.48 us (6%)
  between operations  1.13 us (3%)
    ppermute x11, starting transfers between devices, swap(): return lax.ppermute(value, axes, pairs)  10.8 us
    pallas_call x1, Pallas kernels, local(): pl.pallas_call(level_one_kernel, out_shape=[shaped(Y1 * X1, lanes1), shap...  5.32 us
    pallas_call x1, Pallas kernels, local(): pl.pallas_call(down1_kernel, in_specs=[pl.BlockSpec(memory_space=pltpu.HB...  4.41 us
    ppermute x11, waiting for transfers between devices, swap(): return lax.ppermute(value, axes, pairs)  4.38 us
    pallas_call x1, Pallas kernels, local(): pl.pallas_call(level_two_kernel, out_shape=shaped(C2 * Z2, Y2 * X2), scra...  4.27 us
    pallas_call x1, Pallas kernels, local(): pl.pallas_call(outer_kernel, out_shape=[shaped(rows, X1, 256), shaped(row...  1.98 us
    pallas_call x1, Pallas kernels, local(): pl.pallas_call(middle_kernel, out_shape=[shaped(ROWS1, X1, lanes1), shape...  1.54 us
    unnamed x30, local copies, waits for them, and re-layouts  1.41 us
  transfers between devices with their start and end apart: 11, of which 4 were waited for; matrix products, arithmetic and copies ran while one was open for 8% of the time, Pallas kernels for 19%

profile of v15, /device:TPU:10, one launch (start us, length us, event | category | flops | bytes accessed | tf_op | source)
XLA Modules:
  0.0 44.8 jit_solution(12728857376483430756)
XLA Ops:
  0.7 4.4 %shard_map.149 = (bf16[16,32,512]{2,1,0:T(8,128)(2,1)S(1)}, bf16[16,2,3072]{2,1,0:T(2,128)(2,1)S(1)}, bf16[576,384]{1,0:T(8,128)(2,1)S(1)}, bf16[288,384]{1,0:T(...) custom-call(bf16[48,2,8,2048]{3,2,1,0:T(8,128)(2,1)} %bitcast.28, ...), custom_call_target="tpu_custom_call" | custom-call | flops 4000000000 | tf_op jit(solution)/shard_map/pallas_call | solution.py:454
  5.1 0.7 %copy-done.8 = bf16[288,384]{1,0:T(8,128)(2,1)} copy-done((bf16[288,384]{1,0:T(8,128)(2,1)}, bf16[288,384]{1,0:T(8,128)(2,1)S(1)}, u32[]{:S(2)}) %copy-start.8) | copy-done | bytes 221208
  5.8 0.7 %copy-done.10 = bf16[768,128]{1,0:T(8,128)(2,1)} copy-done((bf16[768,128]{1,0:T(8,128)(2,1)}, bf16[768,128]{1,0:T(8,128)(2,1)S(1)}, u32[]{:S(2)}) %copy-start.10) | copy-done | bytes 196632
  6.4 0.6 %slice_select_fusion = bf16[2,32,512]{2,1,0:T(8,128)(2,1)} fusion(bf16[16,32,512]{2,1,0:T(8,128)(2,1)S(1)} %get-tuple-element.46, pred[]{:T(512)S(6)} %eq.40), kind=kLoop, calls=%fused_computation.23 | loop fusion | flops 32768 | bytes 196609 | tf_op jit(solution)/shard_map/jit(_where)/select_n | solution.py:420
  7.1 0.6 %broadcast_select_fusion.29 = bf16[2,2,3072]{2,1,0:T(2,128)(2,1)} fusion(pred[]{:T(512)S(6)} %eq.40, bf16[16,2,3072]{2,1,0:T(2,128)(2,1)S(1)} %get-tuple-element.47), kind=kLoop, calls=%fused_computation.42 | loop fusion | flops 12288 | bytes 73729 | tf_op jit(solution)/shard_map/jit(_where)/select_n | solution.py:420
  7.7 0.5 %collective-permute-start.3 = (bf16[2,2,3072]{2,1,0:T(2,128)(2,1)}, bf16[2,2,3072]{2,1,0:T(2,128)(2,1)}, u32[]{:S(2)}, u32[]{:S(2)}) collective-permute-start(bf16[2,2,3072]{2,1,0:T(2,128)(2,1)} %broadcast_select_fusion.29), channel_id=1, source_target_pairs={{0,4},{1,5},{2,6},{3,7},{4,0},{5,1},{6,2},{7,3},{8,12},{9,13},{10,... | collective-permute-start | bytes 73736 | tf_op jit(solution)/shard_map/ppermute | solution.py:403
  8.2 0.6 %shard_map.150.t_ref.ta_ref = bf16[256,3456]{1,0:T(8,128)(2,1)S(1)} custom-call(bf16[27,64,64]{2,1,0:T(8,128)(2,1)S(1)} %copy-done.4), custom_call_target="tpu_custom_call" | custom-call | flops 1000000000 | tf_op jit(solution)/shard_map/pallas_call | solution.py:187
  9.0 1.0 %pad.14.wd_ref = bf16[512,128]{1,0:T(8,128)(2,1)S(1)} pad(bf16[512,96]{1,0:T(8,128)(2,1)} %bitcast.25, bf16[]{:T(256)} %constant.72.clone.1), padding=0_0x0_32 | pad | bytes 229378 | tf_op jit(solution)/shard_map/jit(_pad)/pad | solution.py:442
  10.0 0.8 %broadcast_select_fusion.30 = (bf16[2,2,3072]{2,1,0:T(2,128)(2,1)S(1)}, bf16[2,2,3072]{2,1,0:T(2,128)(2,1)S(1)}) fusion(bf16[2,2,3072]{2,1,0:T(2,128)(2,1)} %collective-permute-done.3, pred[]{:T(512)S(6)} %gt.7, pred[]{:T(512)S(6)} %lt.57), kind=kLoop, calls=%fused_computation.43 | loop fusion | flops 24576 | bytes 73730 | tf_op jit(solution)/shard_map/jit(_where)/select_n | solution.py:413
  10.7 0.4 pad_maximum_fusion.2
  11.1 0.2 broadcast_select_fusion.4
  11.3 0.6 %collective-permute-start.4 = (bf16[20,2,1536]{2,1,0:T(2,128)(2,1)S(1)}, bf16[20,2,1536]{2,1,0:T(2,128)(2,1)S(1)}, u32[]{:S(2)}, u32[]{:S(2)}) collective-permute-start(bf16[20,2,1536]{2,1,0:T(2,128)(2,1)S(1)} %get-tuple-element.101), channel_id=1, source_target_pairs={{0,8},{1,9},{2,10},{3,11},{4,12},{5,13},{6,14},{7,15},{8,0},{9,1},... | collective-permute-start | bytes 368648 | tf_op jit(solution)/shard_map/ppermute | solution.py:403
  11.9 2.4 %collective-permute-start.5 = (bf16[20,2,1536]{2,1,0:T(2,128)(2,1)S(1)}, bf16[20,2,1536]{2,1,0:T(2,128)(2,1)S(1)}, u32[]{:S(2)}, u32[]{:S(2)}) collective-permute-start(bf16[20,2,1536]{2,1,0:T(2,128)(2,1)S(1)} %get-tuple-element.100), channel_id=1, source_target_pairs={{0,4},{1,5},{2,6},{3,7},{4,0},{5,1},{6,2},{7,3},{8,16},{9,17},{10,... | collective-permute-start | bytes 368648 | tf_op jit(solution)/shard_map/ppermute | solution.py:403
  14.5 0.5 %collective-permute-start.2 = (bf16[20,32,128]{2,1,0:T(8,128)(2,1)S(1)}, bf16[20,32,128]{2,1,0:T(8,128)(2,1)S(1)}, u32[]{:S(2)}, u32[]{:S(2)}) collective-permute-start(bf16[20,32,128]{2,1,0:T(8,128)(2,1)S(1)} %get-tuple-element.90), channel_id=1, source_target_pairs={{0,1},{1,0},{2,3},{3,2},{4,5},{5,4},{6,7},{7,6},{8,9},{9,8},{10,11... | collective-permute-start | bytes 491528 | tf_op jit(solution)/shard_map/ppermute | solution.py:403
  15.0 2.7 %collective-permute-start.1 = (bf16[20,32,128]{2,1,0:T(8,128)(2,1)S(1)}, bf16[20,32,128]{2,1,0:T(8,128)(2,1)S(1)}, u32[]{:S(2)}, u32[]{:S(2)}) collective-permute-start(bf16[20,32,128]{2,1,0:T(8,128)(2,1)S(1)} %get-tuple-element.91), channel_id=1, source_target_pairs={{0,4},{1,2},{2,1},{3,7},{4,0},{5,6},{6,5},{7,3},{8,12},{9,10},{10,... | collective-permute-start | bytes 491528 | tf_op jit(solution)/shard_map/ppermute | solution.py:403
  17.7 1.5 %shard_map.151 = (bf16[20,32,512]{2,1,0:T(8,128)(2,1)S(1)}, bf16[20,32,512]{2,1,0:T(8,128)(2,1)S(1)}, bf16[18,32,256]{2,1,0:T(8,128)(2,1)S(1)}, bf16[256,3456]{1,0:T(8,128)(2,1)S(1)}) custom-call(bf16[20,32,512]{2,1,0:T(8,128)(2,1)S(1)} %pad_maximum_fusion.win_ref, bf16[256,3456]{1,0:T(8,128)(2,1)S(1)} %shard_map.150.t_ref.ta_ref, f32[1,64]{1,0:T(1,128)S(1)} %bitcast.18, ...), custom_call_target="tpu_custom_call" | custom-call | flops 100000000 | tf_op jit(solution)/shard_map/pallas_call | solution.py:489
  19.3 0.9 %collective-permute-done.5 = bf16[20,2,1536]{2,1,0:T(2,128)(2,1)S(1)} collective-permute-done((bf16[20,2,1536]{2,1,0:T(2,128)(2,1)S(1)}, bf16[20,2,1536]{2,1,0:T(2,128)(2,1)S(1)}, u32[]{:S(2)}, u32[]{:S(2)}) %collective-permute-start.5) | collective-permute-done | bytes 122912 | tf_op jit(solution)/shard_map/ppermute | solution.py:403
  20.4 0.5 %collective-permute-start.6 = (bf16[20,2,768]{2,1,0:T(2,128)(2,1)S(1)}, bf16[20,2,768]{2,1,0:T(2,128)(2,1)S(1)}, u32[]{:S(2)}, u32[]{:S(2)}) collective-permute-start(bf16[20,2,768]{2,1,0:T(2,128)(2,1)S(1)} %bitcast.27), channel_id=1, source_target_pairs={{0,1},{1,0},{2,3},{3,2},{4,5},{5,4},{6,7},{7,6},{8,9},{9,8},{10,11... | collective-permute-start | bytes 184328 | tf_op jit(solution)/shard_map/ppermute | solution.py:403
  21.0 2.7 %collective-permute-start.7 = (bf16[20,2,768]{2,1,0:T(2,128)(2,1)S(1)}, bf16[20,2,768]{2,1,0:T(2,128)(2,1)S(1)}, u32[]{:S(2)}, u32[]{:S(2)}) collective-permute-start(bf16[20,2,768]{2,1,0:T(2,128)(2,1)S(1)} %bitcast.26), channel_id=1, source_target_pairs={{0,4},{1,2},{2,1},{3,7},{4,0},{5,6},{6,5},{7,3},{8,12},{9,10},{10,... | collective-permute-start | bytes 184328 | tf_op jit(solution)/shard_map/ppermute | solution.py:403
  23.7 0.2 broadcast_select_fusion
  23.9 1.2 %shard_map.153 = (bf16[20,16,512]{2,1,0:T(8,128)(2,1)S(1)}, bf16[20,16,512]{2,1,0:T(8,128)(2,1)S(1)}, bf16[20,16,512]{2,1,0:T(8,128)(2,1)S(1)}, bf16[18,48,256]{...) custom-call(bf16[20,2,1536]{2,1,0:T(2,128)(2,1)S(1)} %get-tuple-element.99.xl_ref, ...), custom_call_target="tpu_custom_call" | custom-call | flops 3000000000 | tf_op jit(solution)/shard_map/pallas_call | solution.py:514
  25.2 2.0 %shard_map.152 = (bf16[18,32,256]{2,1,0:T(8,128)(2,1)S(1)}, bf16[18,32,128]{2,1,0:T(8,128)(2,1)S(1)}) custom-call(bf16[20,32,512]{2,1,0:T(8,128)(2,1)S(1)} %pad_maximum_fusion.win_ref, bf16[20,32,512]{2,1,0:T(8,128)(2,1)S(1)} %get-tuple-element.54.left_ref, bf16[20,32,512]{2,1,0:T(8,128)(2,1)S(1)} %get-tuple-element.55.right_ref, ...), custom_call_target="tpu_custom_call" | custom-call | flops 4000000000 | tf_op jit(solution)/shard_map/pallas_call | solution.py:501
  27.2 0.1 broadcast_select_fusion.10
  27.7 5.3 %shard_map.154 = (bf16[512,512]{1,0:T(8,128)(2,1)S(1)}, bf16[8,20,512]{2,1,0:T(8,128)(2,1)S(1)}) custom-call(bf16[20,32,128]{2,1,0:T(8,128)(2,1)S(1)} %get-tuple-element.93.zl_ref, bf16[20,32,128]{2,1,0:T(8,128)(2,1)S(1)} %get-tuple-element.92.zr_ref, bf16[20,2,768]{2,1,0:T(2,128)(2,1)S(1)} %pad_maximum_fusion.5.cl_ref, ...), custom_call_target="tpu_custom_call" | custom-call | flops 6000000000 | tf_op jit(solution)/shard_map/pallas_call | solution.py:520
  33.1 0.3 shard_map.156.t_ref.ta_ref
  33.4 0.9 %collective-permute-done.8 = bf16[2,20,512]{2,1,0:T(8,128)(2,1)S(1)} collective-permute-done((bf16[2,20,512]{2,1,0:T(8,128)(2,1)S(1)}, bf16[2,20,512]{2,1,0:T(8,128)(2,1)S(1)}, u32[]{:S(2)}, u32[]{:S(2)}) %collective-permute-start.8) | collective-permute-done | bytes 40992 | tf_op jit(solution)/shard_map/ppermute | solution.py:403
  34.5 0.7 %collective-permute-start.9 = (bf16[12,20,256]{2,1,0:T(8,128)(2,1)S(1)}, bf16[12,20,256]{2,1,0:T(8,128)(2,1)S(1)}, u32[]{:S(2)}, u32[]{:S(2)}) collective-permute-start(bf16[12,20,256]{2,1,0:T(8,128)(2,1)S(1)} %get-tuple-element.97), channel_id=1, source_target_pairs={{0,4},{1,2},{2,1},{3,7},{4,0},{5,6},{6,5},{7,3},{8,12},{9,10},{10,... | collective-permute-start | bytes 368648 | tf_op jit(solution)/shard_map/ppermute | solution.py:403
  35.2 1.1 %shard_map.157 = (bf16[12,32,512]{2,1,0:T(8,128)(2,1)S(1)}, bf16[12,32,512]{2,1,0:T(8,128)(2,1)S(1)}, bf16[12,32,512]{2,1,0:T(8,128)(2,1)S(1)}, bf16[10,16,256]{...) custom-call(bf16[12,20,512]{2,1,0:T(8,128)(2,1)S(1)} %pad_maximum_fusion.1.wide_ref, ...), custom_call_target="tpu_custom_call" | custom-call | flops 3000000000 | tf_op jit(solution)/shard_map/pallas_call | solution.py:545
  36.3 1.3 %shard_map.155 = bf16[512,512]{1,0:T(8,128)(2,1)} custom-call(bf16[512,512]{1,0:T(8,128)(2,1)S(1)} %get-tuple-element.78.feat_ref), custom_call_target="tpu_custom_call" | custom-call | flops 2000000000 | tf_op jit(solution)/shard_map/pallas_call | solution.py:539
  37.6 0.3 shard_map.158.tb_ref
  37.9 2.5 %collective-permute-done.10 = bf16[12,20,256]{2,1,0:T(8,128)(2,1)S(1)} collective-permute-done((bf16[12,20,256]{2,1,0:T(8,128)(2,1)S(1)}, bf16[12,20,256]{2,1,0:T(8,128)(2,1)S(1)}, u32[]{:S(2)}, u32[]{:S(2)}) %collective-permute-start.10) | collective-permute-done | bytes 122912 | tf_op jit(solution)/shard_map/ppermute | solution.py:403
  40.5 4.3 %shard_map.159 = bf16[384,128]{1,0:T(8,128)(2,1)} custom-call(bf16[12,32,512]{2,1,0:T(8,128)(2,1)S(1)} %get-tuple-element.82.a0, bf16[12,32,512]{2,1,0:T(8,128)(2,1)S(1)} %get-tuple-element.83.a1, bf16[12,32,512]{2,1,0:T(8,128)(2,1)S(1)} %get-tuple-element.84.a2, bf16[10,16,256]{2,1,0:T(8,128)(2,1)S(1)} %get-tuple-element.85.m0, ...), custom_call_target="tpu_custom_call" | custom-call | flops 5000000000 | tf_op jit(solution)/shard_map/pallas_call | solution.py:551
  (59 shorter events, 1.1 us)
Async XLA Ops:
  0.6 7.6 %copy-start.4 = (bf16[27,64,64]{2,1,0:T(8,128)(2,1)S(1)}, bf16[27,64,64]{2,1,0:T(8,128)(2,1)}, u32[]{:S(2)}) copy-start(bf16[27,64,64]{2,1,0:T(8,128)(2,1)} %w_ref.2) | copy-start | bytes 663556
  5.1 0.7 %copy-start.8 = (bf16[288,384]{1,0:T(8,128)(2,1)}, bf16[288,384]{1,0:T(8,128)(2,1)S(1)}, u32[]{:S(2)}) copy-start(bf16[288,384]{1,0:T(8,128)(2,1)S(1)} %get-tuple-element.63.mask_ref.edge_ref) | copy-start | bytes 663556
  5.8 0.7 %copy-start.10 = (bf16[768,128]{1,0:T(8,128)(2,1)}, bf16[768,128]{1,0:T(8,128)(2,1)S(1)}, u32[]{:S(2)}) copy-start(bf16[768,128]{1,0:T(8,128)(2,1)S(1)} %get-tuple-element.73.second_ref) | copy-start | bytes 589828
  6.4 1.8 %copy-start.6 = (bf16[320,384]{1,0:T(8,128)(2,1)}, bf16[320,384]{1,0:T(8,128)(2,1)S(1)}, u32[]{:S(2)}) copy-start(bf16[320,384]{1,0:T(8,128)(2,1)S(1)} %get-tuple-element.81.mask_ref) | copy-start | bytes 737284
  6.4 2.5 %copy-start.12 = (f32[96]{0:T(128)S(1)}, f32[96]{0:T(128)}, u32[]{:S(2)}) copy-start(f32[96]{0:T(128)} %param.23) | copy-start | bytes 1156
  6.4 2.5 %copy-start.13 = (f32[96]{0:T(128)S(1)}, f32[96]{0:T(128)}, u32[]{:S(2)}) copy-start(f32[96]{0:T(128)} %param.25) | copy-start | bytes 1156
  6.4 2.5 %copy-start.14 = (f32[96]{0:T(128)S(1)}, f32[96]{0:T(128)}, u32[]{:S(2)}) copy-start(f32[96]{0:T(128)} %param.27) | copy-start | bytes 1156
  7.1 7.3 %collective-permute-start = (bf16[2,32,512]{2,1,0:T(8,128)(2,1)}, bf16[2,32,512]{2,1,0:T(8,128)(2,1)S(1)}, u32[]{:S(2)}, u32[]{:S(2)}) collective-permute-start(bf16[2,32,512]{2,1,0:T(8,128)(2,1)} %slice_select_fusion), channel_id=1, source_target_pairs={{0,4},{1,5},{2,6},{3,7},{4,0},{5,1},{6,2},{7,3},{8,12},{9,13},{10,... | collective-permute-start | bytes 196616 | tf_op jit(solution)/shard_map/ppermute | solution.py:403
  7.7 2.2 %collective-permute-start.3 = (bf16[2,2,3072]{2,1,0:T(2,128)(2,1)}, bf16[2,2,3072]{2,1,0:T(2,128)(2,1)}, u32[]{:S(2)}, u32[]{:S(2)}) collective-permute-start(bf16[2,2,3072]{2,1,0:T(2,128)(2,1)} %broadcast_select_fusion.29), channel_id=1, source_target_pairs={{0,4},{1,5},{2,6},{3,7},{4,0},{5,1},{6,2},{7,3},{8,12},{9,13},{10,... | collective-permute-start | bytes 73736 | tf_op jit(solution)/shard_map/ppermute | solution.py:403
  8.8 8.9 %copy-start = (bf16[27,64,64]{2,1,0:T(8,128)(2,1)S(1)}, bf16[27,64,64]{2,1,0:T(8,128)(2,1)}, u32[]{:S(2)}) copy-start(bf16[27,64,64]{2,1,0:T(8,128)(2,1)} %w_ref.3) | copy-start | bytes 663556
  8.9 8.9 %copy-start.1 = (f32[64]{0:T(128)S(1)}, f32[64]{0:T(128)}, u32[]{:S(2)}) copy-start(f32[64]{0:T(128)} %param.19) | copy-start | bytes 772
  11.3 8.0 %collective-permute-start.4 = (bf16[20,2,1536]{2,1,0:T(2,128)(2,1)S(1)}, bf16[20,2,1536]{2,1,0:T(2,128)(2,1)S(1)}, u32[]{:S(2)}, u32[]{:S(2)}) collective-permute-start(bf16[20,2,1536]{2,1,0:T(2,128)(2,1)S(1)} %get-tuple-element.101), channel_id=1, source_target_pairs={{0,8},{1,9},{2,10},{3,11},{4,12},{5,13},{6,14},{7,15},{8,0},{9,1},... | collective-permute-start | bytes 368648 | tf_op jit(solution)/shard_map/ppermute | solution.py:403
  11.9 8.3 %collective-permute-start.5 = (bf16[20,2,1536]{2,1,0:T(2,128)(2,1)S(1)}, bf16[20,2,1536]{2,1,0:T(2,128)(2,1)S(1)}, u32[]{:S(2)}, u32[]{:S(2)}) collective-permute-start(bf16[20,2,1536]{2,1,0:T(2,128)(2,1)S(1)} %get-tuple-element.100), channel_id=1, source_target_pairs={{0,4},{1,5},{2,6},{3,7},{4,0},{5,1},{6,2},{7,3},{8,16},{9,17},{10,... | collective-permute-start | bytes 368648 | tf_op jit(solution)/shard_map/ppermute | solution.py:403
  14.5 9.4 %copy-start.9 = (bf16[288,384]{1,0:T(8,128)(2,1)S(1)}, bf16[288,384]{1,0:T(8,128)(2,1)}, u32[]{:S(2)}) copy-start(bf16[288,384]{1,0:T(8,128)(2,1)} %copy-done.8) | copy-start | bytes 663556
  14.5 10.6 %collective-permute-start.2 = (bf16[20,32,128]{2,1,0:T(8,128)(2,1)S(1)}, bf16[20,32,128]{2,1,0:T(8,128)(2,1)S(1)}, u32[]{:S(2)}, u32[]{:S(2)}) collective-permute-start(bf16[20,32,128]{2,1,0:T(8,128)(2,1)S(1)} %get-tuple-element.90), channel_id=1, source_target_pairs={{0,1},{1,0},{2,3},{3,2},{4,5},{5,4},{6,7},{7,6},{8,9},{9,8},{10,11... | collective-permute-start | bytes 491528 | tf_op jit(solution)/shard_map/ppermute | solution.py:403
  15.0 10.1 %collective-permute-start.1 = (bf16[20,32,128]{2,1,0:T(8,128)(2,1)S(1)}, bf16[20,32,128]{2,1,0:T(8,128)(2,1)S(1)}, u32[]{:S(2)}, u32[]{:S(2)}) collective-permute-start(bf16[20,32,128]{2,1,0:T(8,128)(2,1)S(1)} %get-tuple-element.91), channel_id=1, source_target_pairs={{0,4},{1,2},{2,1},{3,7},{4,0},{5,6},{6,5},{7,3},{8,12},{9,10},{10,... | collective-permute-start | bytes 491528 | tf_op jit(solution)/shard_map/ppermute | solution.py:403
  20.4 6.8 %collective-permute-start.6 = (bf16[20,2,768]{2,1,0:T(2,128)(2,1)S(1)}, bf16[20,2,768]{2,1,0:T(2,128)(2,1)S(1)}, u32[]{:S(2)}, u32[]{:S(2)}) collective-permute-start(bf16[20,2,768]{2,1,0:T(2,128)(2,1)S(1)} %bitcast.27), channel_id=1, source_target_pairs={{0,1},{1,0},{2,3},{3,2},{4,5},{5,4},{6,7},{7,6},{8,9},{9,8},{10,11... | collective-permute-start | bytes 184328 | tf_op jit(solution)/shard_map/ppermute | solution.py:403
  21.0 6.3 %collective-permute-start.7 = (bf16[20,2,768]{2,1,0:T(2,128)(2,1)S(1)}, bf16[20,2,768]{2,1,0:T(2,128)(2,1)S(1)}, u32[]{:S(2)}, u32[]{:S(2)}) collective-permute-start(bf16[20,2,768]{2,1,0:T(2,128)(2,1)S(1)} %bitcast.26), channel_id=1, source_target_pairs={{0,4},{1,2},{2,1},{3,7},{4,0},{5,6},{6,5},{7,3},{8,12},{9,10},{10,... | collective-permute-start | bytes 184328 | tf_op jit(solution)/shard_map/ppermute | solution.py:403
  25.2 2.4 %copy-start.5 = (f32[64]{0:T(128)S(1)}, f32[64]{0:T(128)}, u32[]{:S(2)}) copy-start(f32[64]{0:T(128)} %param.21) | copy-start | bytes 772
  25.2 2.4 %copy-start.11 = (bf16[768,128]{1,0:T(8,128)(2,1)S(1)}, bf16[768,128]{1,0:T(8,128)(2,1)}, u32[]{:S(2)}) copy-start(bf16[768,128]{1,0:T(8,128)(2,1)} %copy-done.10) | copy-start | bytes 589828
  27.7 5.4 %copy-start.2 = (bf16[27,96,96]{2,1,0:T(8,128)(2,1)S(1)}, bf16[27,96,96]{2,1,0:T(8,128)(2,1)}, u32[]{:S(2)}) copy-start(bf16[27,96,96]{2,1,0:T(8,128)(2,1)} %w_ref.4) | copy-start | bytes 1492996
  33.0 2.2 %copy-start.7 = (bf16[320,384]{1,0:T(8,128)(2,1)S(1)}, bf16[320,384]{1,0:T(8,128)(2,1)}, u32[]{:S(2)}) copy-start(bf16[320,384]{1,0:T(8,128)(2,1)} %copy-done.6) | copy-start | bytes 737284
  33.0 1.3 %collective-permute-start.8 = (bf16[2,20,512]{2,1,0:T(8,128)(2,1)S(1)}, bf16[2,20,512]{2,1,0:T(8,128)(2,1)S(1)}, u32[]{:S(2)}, u32[]{:S(2)}) collective-permute-start(bf16[2,20,512]{2,1,0:T(8,128)(2,1)S(1)} %slice_select_fusion.1), channel_id=1, source_target_pairs={{0,4},{1,5},{2,6},{3,7},{4,0},{5,1},{6,2},{7,3},{8,12},{9,13},{10,... | collective-permute-start | bytes 122888 | tf_op jit(solution)/shard_map/ppermute | solution.py:403
  34.4 6.0 %collective-permute-start.10 = (bf16[12,20,256]{2,1,0:T(8,128)(2,1)S(1)}, bf16[12,20,256]{2,1,0:T(8,128)(2,1)S(1)}, u32[]{:S(2)}, u32[]{:S(2)}) collective-permute-start(bf16[12,20,256]{2,1,0:T(8,128)(2,1)S(1)} %get-tuple-element.96), channel_id=1, source_target_pairs={{0,1},{1,0},{2,3},{3,2},{4,5},{5,4},{6,7},{7,6},{8,9},{9,8},{10,11... | collective-permute-start | bytes 368648 | tf_op jit(solution)/shard_map/ppermute | solution.py:403
  34.5 6.0 %collective-permute-start.9 = (bf16[12,20,256]{2,1,0:T(8,128)(2,1)S(1)}, bf16[12,20,256]{2,1,0:T(8,128)(2,1)S(1)}, u32[]{:S(2)}, u32[]{:S(2)}) collective-permute-start(bf16[12,20,256]{2,1,0:T(8,128)(2,1)S(1)} %get-tuple-element.97), channel_id=1, source_target_pairs={{0,4},{1,2},{2,1},{3,7},{4,0},{5,6},{6,5},{7,3},{8,12},{9,10},{10,... | collective-permute-start | bytes 368648 | tf_op jit(solution)/shard_map/ppermute | solution.py:403
  36.3 1.3 %copy-start.3 = (bf16[27,96,96]{2,1,0:T(8,128)(2,1)S(1)}, bf16[27,96,96]{2,1,0:T(8,128)(2,1)}, u32[]{:S(2)}) copy-start(bf16[27,96,96]{2,1,0:T(8,128)(2,1)} %w_ref.5) | copy-start | bytes 1492996

commit v16 on v14

--- a/solution.py
+++ b/solution.py
@@ -30,6 +30,7 @@
 ROWS2 = Y2 + 2 * HALO
 EDGE = 16
 PITCH2 = 32
+FACE = HALO_X // 2 * Z1 * C1
 BF = jnp.bfloat16
 F32 = jnp.float32
 NN = (((1,), (0,)), ((), ()))
@@ -90,7 +91,7 @@
 
 
 def down1_kernel(
-    v_hbm, wd_hbm, b_hbm, t_hbm, out_ref, tab_ref, tab2_ref, v_ref, w_ref, b_ref, t_ref, wd_ref, cells_ref, sems
+    v_hbm, wd_hbm, b_hbm, t_hbm, out_ref, face_ref, tab_ref, tab2_ref, v_ref, w_ref, b_ref, t_ref, wd_ref, cells_ref, sems
 ):
     half = v_ref.shape[2]
     kz = C0 * half
@@ -141,7 +142,12 @@
     for h in range(2):
         for q in range(2):
             value = finish(acc[h][:, q * 128 : q * 128 + 128], bias, mask, Y1)
-            out_ref[:, :, (2 * h + q) * 128 : (2 * h + q + 1) * 128] = value
+            chunk = 2 * h + q
+            out_ref[:, :, chunk * 128 : chunk * 128 + 128] = value
+            for side, start in enumerate((0, X1 - HALO_X)):
+                for pair in range(HALO_X // 2):
+                    lane = side * FACE + (chunk * (HALO_X // 2) + pair) * 128
+                    face_ref[:, :, lane : lane + 128] = value[:, start + 2 * pair : start + 2 * pair + 2]
 
 
 def twice(b_ref):
@@ -252,15 +258,16 @@
             copy[:, X1:, cut] = jnp.concatenate([edge[:, i:], jnp.zeros((rows, i, 128), BF)], axis=1)
 
 
-def column_lanes(field, lane, stride=Z1 * C1):
-    return [field[:, :, first : first + 128] for first in range(lane, field.shape[2], stride)]
+def column_pieces(ref, chunk):
+    first = chunk * (HALO_X // 2) * 128
+    return [ref[:, :, lane : lane + 128] for lane in range(first, first + HALO_X // 2 * 128, 128)]
 
 
 def edge_middle_kernel(xl_ref, win_ref, xr_ref, g_ref, t_ref, b_ref, tab_ref, e0, e1, e2, m0, m1, m2):
     for lane in range(0, Z1 * C1, 128):
         cut = slice(lane, lane + 128)
         inner = win_ref[:, :, cut]
-        left, right = (column_lanes(ref, lane) for ref in (xl_ref, xr_ref))
+        left, right = (column_pieces(ref, lane // 128) for ref in (xl_ref, xr_ref))
         pieces = left + [inner[:, :2], inner[:, X1 - 2 :]] + right
         fill_edges([e.at[:, :, cut] for e in (e0, e1, e2)], pieces)
     here = edge_masks(tab_ref)[1]
@@ -274,8 +281,7 @@
     own, mid, low, high = (e0, e1, e2), (m0, m1, m2), (i0, i1, i2), (j0, j1, j2)
     for z_ref, c_ref, copies in ((zl_ref, cl_ref, (l0, l1, l2)), (zr_ref, cr_ref, (h0, h1, h2))):
         inner = z_ref[...]
-        corner = column_lanes(c_ref, 0, 128)
-        fill_edges(copies, corner[:3] + [inner[:, :2], inner[:, X1 - 2 :]] + corner[3:])
+        fill_edges(copies, column_pieces(c_ref, 0) + [inner[:, :2], inner[:, X1 - 2 :]] + column_pieces(c_ref, 1))
     below, here, above = edge_masks(tab_ref)
     taps = [[(z, 0, 128), (e, 0, 256)] for z, e in zip((l0, l1, l2), own)]
     edge_group(taps, ta_ref, ba_ref, (below, here), g1_ref, low)
@@ -396,31 +402,30 @@
     return lax.ppermute(value, axes, pairs)
 
 
-def parity(axis):
-    return lax.axis_index(axis) % 2 == 0
-
-
-def sides(first, second, axis):
-    index = lax.axis_index(axis)
-    even = parity(axis)
-    below = jnp.where(index > 0, jnp.where(even, second, first), jnp.zeros_like(first))
-    above = jnp.where(index < lax.axis_size(axis) - 1, jnp.where(even, first, second), jnp.zeros_like(first))
+def positions():
+    found = {}
+    for axis in ("gx", "gy", "gz"):
+        index = lax.axis_index(axis)
+        found[axis] = ((index & 1) == 0, index > 0, index < lax.axis_size(axis) - 1)
+    return found
+
+
+def sides(first, second, position):
+    even, has_below, has_above = position
+    below = jnp.where(has_below, jnp.where(even, second, first), jnp.zeros_like(first))
+    above = jnp.where(has_above, jnp.where(even, first, second), jnp.zeros_like(first))
     return below, above
 
 
-def swaps(low_edge, high_edge, axis):
-    even = parity(axis)
+def swaps(low_edge, high_edge, axis, position):
+    even = position[0]
     first = swap(jnp.where(even, high_edge, low_edge), {axis: 0})
     second = swap(jnp.where(even, low_edge, high_edge), {axis: 1}) if lax.axis_size(axis) > 2 else first
     return first, second
 
 
-def shift_along(low_edge, high_edge, axis):
-    return sides(*swaps(low_edge, high_edge, axis), axis)
-
-
-def column_pairs(field):
-    return jnp.concatenate([field[:, i : i + 2] for i in range(0, field.shape[1], 2)], axis=2)
+def shift_along(low_edge, high_edge, axis, position):
+    return sides(*swaps(low_edge, high_edge, axis, position), position)
 
 
 def params():
@@ -447,11 +452,12 @@
     lanes1 = Z1 * C1
     half = depth // 2
     operands = [volume.reshape(C0, 2, half, -1), jnp.swapaxes(w_down1, 1, 2), b_down1[None], tissue.transpose(1, 2, 0)]
+    at, operands = lax.optimization_barrier((positions(), operands))
     operands = [pltpu.with_memory_space_constraint(x, pltpu.HBM) for x in operands]
-    own, tab1, tab2 = pl.pallas_call(
+    own, faces, tab1, tab2 = pl.pallas_call(
         down1_kernel,
         in_specs=[pl.BlockSpec(memory_space=pltpu.HBM)] * 4,
-        out_shape=[shaped(Y1, X1, lanes1), shaped(128, 384), shaped(128, 384)],
+        out_shape=[shaped(Y1, X1, lanes1), shaped(Y1, 2, 2 * FACE), shaped(128, 384), shaped(128, 384)],
         scratch_shapes=[pltpu.VMEM(x.shape, x.dtype) for x in operands]
         + [
             pltpu.VMEM((C0 // 16, 64 * half, lanes1 // 2), BF),
@@ -465,11 +471,14 @@
     t1a = banded(w_conv1a, 4, C1)
     bias1a = b_conv1a[None]
 
-    y_below, y_above = shift_along(own[:HALO], own[Y1 - HALO :], "gy")
-    win = jnp.concatenate([y_below, own, y_above], axis=0)
-    z_below, z_above = shift_along(win[:, :, :128], win[:, :, lanes1 - 128 :], "gz")
-    low, high = win[:, :HALO_X], win[:, X1 - HALO_X :]
-    x_got = lax.optimization_barrier(swaps(column_pairs(low), column_pairs(high), "gx"))
+    def with_halo(field):
+        below, above = shift_along(field[:HALO], field[field.shape[0] - HALO :], "gy", at["gy"])
+        return jnp.concatenate([below, field, above], axis=0)
+
+    faces = with_halo(faces)
+    win = with_halo(own)
+    z_below, z_above = shift_along(win[:, :, :128], win[:, :, lanes1 - 128 :], "gz", at["gz"])
+    x_got = lax.optimization_barrier(swaps(faces[:, :, :FACE], faces[:, :, FACE:], "gx", at["gx"]))
     rows = Y1 + 2
     left, right, g2, t1b = pl.pallas_call(
         middle_kernel,
@@ -478,14 +487,13 @@
         cost_estimate=cost(1e-7),
     )(win, t1a, bias1a, tab1, w_conv1b)
 
-    corner = []
-    for lane in (0, lanes1 - 128):
-        cut = [jnp.concatenate(column_lanes(got, lane), axis=2) for got in x_got]
-        corner.append(jnp.concatenate(sides(*cut, "gx"), axis=2))
-    low, high = corner
+    corner = HALO_X // 2 * 2 * C1
+    low, high = (
+        jnp.concatenate(sides(*(got[:, :, cut] for got in x_got), at["gx"]), axis=2) for cut in (slice(corner), slice(FACE - corner, FACE))
+    )
     low, high, g2, *x_got = lax.optimization_barrier((low, high, g2, *x_got))
-    x_below, x_above = sides(*x_got, "gx")
-    corner_below, corner_above = shift_along(low, high, "gz")
+    x_below, x_above = sides(*x_got, at["gx"])
+    corner_got = swaps(low, high, "gz", at["gz"])
     g1, g3 = pl.pallas_call(
         outer_kernel,
         out_shape=[shaped(rows, X1, 256), shaped(rows, X1, 128)],
@@ -494,6 +502,8 @@
         cost_estimate=cost(4e-6),
     )(win, left, right, z_below, z_above, t1a, bias1a, tab1)
 
+    *corner_got, g1, g3 = lax.optimization_barrier((*corner_got, g1, g3))
+    corner_below, corner_above = sides(*corner_got, at["gz"])
     wide_x = X1 + EDGE
     edges = pl.pallas_call(
         edge_middle_kernel,
@@ -517,14 +527,13 @@
 
     down, w_conv2a = lax.optimization_barrier((down, w_conv2a))
     t2a = banded(w_conv2a, 2, CP)
-    y_below, y_above = shift_along(down[:HALO], down[Y2 - HALO :], "gy")
-    wide = jnp.concatenate([y_below, down, y_above], axis=0)
+    wide = with_halo(down)
     feat, wide, w_conv2b = lax.optimization_barrier((feat, wide, w_conv2b))
     t2b = banded(w_conv2b, 2, CP)
     one = pl.pallas_call(
         one_kernel, out_shape=shaped(lanes1, Y1 * X1), compiler_params=params(), cost_estimate=cost(2e-6)
     )(feat)
-    z_below, z_above = shift_along(wide[:, :, : 2 * CP], wide[:, :, 2 * CP :], "gz")
+    z_below, z_above = shift_along(wide[:, :, : 2 * CP], wide[:, :, 2 * CP :], "gz", at["gz"])
     bias2a = pad_lanes(b_conv2a[None])
     moved = [shaped(Y2 + 2, X2, 2 * CP)] * 3
     middle = pl.pallas_call(

time: 40.7 us -> 40.8 us (level)
  the two profiles are of different devices: /device:TPU:2 before, /device:TPU:10 now
where the time goes in v16:
time: 40.8 us; the launch traced here: 40.6 us
  Pallas kernels  22.1 us (54%)
  starting transfers between devices  10.9 us (27%)
  waiting for transfers between devices  4.92 us (12%)
  other arithmetic  1.52 us (4%)
  between operations  1.07 us (3%)
    ppermute x11, starting transfers between devices, swap(): return lax.ppermute(value, axes, pairs)  10.9 us
    pallas_call x1, Pallas kernels, local(): pl.pallas_call(level_one_kernel, out_shape=[shaped(Y1 * X1, lanes1), shap...  5.3 us
    ppermute x11, waiting for transfers between devices, swap(): return lax.ppermute(value, axes, pairs)  4.92 us
    pallas_call x1, Pallas kernels, local(): pl.pallas_call(level_two_kernel, out_shape=shaped(C2 * Z2, Y2 * X2), scra...  4.28 us
    pallas_call x1, Pallas kernels, local(): pl.pallas_call(down1_kernel, in_specs=[pl.BlockSpec(memory_space=pltpu.HB...  4.13 us
    pallas_call x1, Pallas kernels, local(): pl.pallas_call(outer_kernel, out_shape=[shaped(rows, X1, 256), shaped(row...  2.04 us
    pallas_call x1, Pallas kernels, local(): pl.pallas_call(middle_kernel, out_shape=[shaped(ROWS1, X1, lanes1), shape...  1.53 us
    pallas_call x1, Pallas kernels, local(): pl.pallas_call(one_kernel, out_shape=shaped(lanes1, Y1 * X1), compiler_pa...  1.27 us
  transfers between devices with their start and end apart: 11, of which 5 were waited for; matrix products, arithmetic and copies ran while one was open for 3% of the time, Pallas kernels for 21%

profile of v16, /device:TPU:10, one launch (start us, length us, event | category | flops | bytes accessed | tf_op | source)
XLA Modules:
  0.0 40.6 jit_solution(9700142124788603971)
XLA Ops:
  0.7 4.1 %shard_map.149 = (bf16[16,32,512]{2,1,0:T(8,128)(2,1)S(1)}, bf16[16,2,3072]{2,1,0:T(2,128)(2,1)S(1)}, bf16[128,384]{1,0:T(8,128)(2,1)S(1)}, bf16[128,384]{1,0:T(8,128)(2,1)S(1)}) custom-call(bf16[48,2,8,2048]{3,2,1,0:T(8,128)(2,1)} %bitcast.28, bf16[8,48,64]{2,1,0:T(8,128)(2,1)} %bitcast.29, f32[1,64]{1,0:T(1,128)} %bitcast.31, s32[8,4,32]{2,1,0:T(4,128)} %bitcast.30), custom_call_target="tpu_custom_call" | custom-call | flops 4000000000 | tf_op jit(solution)/shard_map/pallas_call | solution.py:457
  5.0 0.6 %collective-permute-start.3 = (bf16[2,2,3072]{2,1,0:T(2,128)(2,1)S(1)}, bf16[2,2,3072]{2,1,0:T(2,128)(2,1)S(1)}, u32[]{:S(2)}, u32[]{:S(2)}) collective-permute-start(bf16[2,2,3072]{2,1,0:T(2,128)(2,1)S(1)} %broadcast_select_fusion.29), channel_id=1, source_target_pairs={{0,4},{1,5},{2,6},{3,7},{4,0},{5,1},{6,2},{7,3},{8,12},{9,13},{10,... | collective-permute-start | bytes 73736 | tf_op jit(solution)/shard_map/ppermute | solution.py:402
  5.5 0.6 %shard_map.150.t_ref.ta_ref = bf16[256,3456]{1,0:T(8,128)(2,1)S(1)} custom-call(bf16[27,64,64]{2,1,0:T(8,128)(2,1)S(1)} %copy-done.4), custom_call_target="tpu_custom_call" | custom-call | flops 1000000000 | tf_op jit(solution)/shard_map/pallas_call | solution.py:176
  6.3 0.1 collective-permute-done.3
  6.4 0.4 pad_maximum_fusion.2
  6.8 0.2 broadcast_select_fusion.4
  7.0 0.6 %collective-permute-start.4 = (bf16[20,2,1536]{2,1,0:T(2,128)(2,1)S(1)}, bf16[20,2,1536]{2,1,0:T(2,128)(2,1)S(1)}, u32[]{:S(2)}, u32[]{:S(2)}) collective-permute-start(bf16[20,2,1536]{2,1,0:T(2,128)(2,1)S(1)} %get-tuple-element.123), channel_id=1, source_target_pairs={{0,8},{1,9},{2,10},{3,11},{4,12},{5,13},{6,14},{7,15},{8,0},{9,1},... | collective-permute-start | bytes 368648 | tf_op jit(solution)/shard_map/ppermute | solution.py:402
  7.6 2.4 %collective-permute-start.5 = (bf16[20,2,1536]{2,1,0:T(2,128)(2,1)S(1)}, bf16[20,2,1536]{2,1,0:T(2,128)(2,1)S(1)}, u32[]{:S(2)}, u32[]{:S(2)}) collective-permute-start(bf16[20,2,1536]{2,1,0:T(2,128)(2,1)S(1)} %get-tuple-element.122), channel_id=1, source_target_pairs={{0,4},{1,5},{2,6},{3,7},{4,0},{5,1},{6,2},{7,3},{8,16},{9,17},{10,... | collective-permute-start | bytes 368648 | tf_op jit(solution)/shard_map/ppermute | solution.py:402
  10.1 0.1 pad_maximum_fusion.win_ref
  10.2 0.5 %collective-permute-start.2 = (bf16[20,32,128]{2,1,0:T(8,128)(2,1)S(1)}, bf16[20,32,128]{2,1,0:T(8,128)(2,1)S(1)}, u32[]{:S(2)}, u32[]{:S(2)}) collective-permute-start(bf16[20,32,128]{2,1,0:T(8,128)(2,1)S(1)} %get-tuple-element.108), channel_id=1, source_target_pairs={{0,1},{1,0},{2,3},{3,2},{4,5},{5,4},{6,7},{7,6},{8,9},{9,8},{10,11... | collective-permute-start | bytes 491528 | tf_op jit(solution)/shard_map/ppermute | solution.py:402
  10.7 2.7 %collective-permute-start.1 = (bf16[20,32,128]{2,1,0:T(8,128)(2,1)S(1)}, bf16[20,32,128]{2,1,0:T(8,128)(2,1)S(1)}, u32[]{:S(2)}, u32[]{:S(2)}) collective-permute-start(bf16[20,32,128]{2,1,0:T(8,128)(2,1)S(1)} %get-tuple-element.109), channel_id=1, source_target_pairs={{0,4},{1,2},{2,1},{3,7},{4,0},{5,6},{6,5},{7,3},{8,12},{9,10},{10,... | collective-permute-start | bytes 491528 | tf_op jit(solution)/shard_map/ppermute | solution.py:402
  13.4 1.5 %shard_map.151 = (bf16[20,32,512]{2,1,0:T(8,128)(2,1)S(1)}, bf16[20,32,512]{2,1,0:T(8,128)(2,1)S(1)}, bf16[18,32,256]{2,1,0:T(8,128)(2,1)S(1)}, bf16[256,3456]{1,0:T(8,128)(2,1)S(1)}) custom-call(bf16[20,32,512]{2,1,0:T(8,128)(2,1)S(1)} %pad_maximum_fusion.win_ref, bf16[256,3456]{1,0:T(8,128)(2,1)S(1)} %shard_map.150.t_ref.ta_ref, f32[1,64]{1,0:T(1,128)S(1)} %bitcast.18, ...), custom_call_target="tpu_custom_call" | custom-call | flops 100000000 | tf_op jit(solution)/shard_map/pallas_call | solution.py:483
  15.0 1.3 %collective-permute-done.5 = bf16[20,2,1536]{2,1,0:T(2,128)(2,1)S(1)} collective-permute-done((bf16[20,2,1536]{2,1,0:T(2,128)(2,1)S(1)}, bf16[20,2,1536]{2,1,0:T(2,128)(2,1)S(1)}, u32[]{:S(2)}, u32[]{:S(2)}) %collective-permute-start.5) | collective-permute-done | bytes 122912 | tf_op jit(solution)/shard_map/ppermute | solution.py:402
  16.2 0.1 broadcast_select_fusion.24
  16.4 0.1 pad_maximum_fusion.3
  16.5 0.5 %collective-permute-start.6 = (bf16[20,2,768]{2,1,0:T(2,128)(2,1)S(1)}, bf16[20,2,768]{2,1,0:T(2,128)(2,1)S(1)}, u32[]{:S(2)}, u32[]{:S(2)}) collective-permute-start(bf16[20,2,768]{2,1,0:T(2,128)(2,1)S(1)} %bitcast.27), channel_id=1, source_target_pairs={{0,1},{1,0},{2,3},{3,2},{4,5},{5,4},{6,7},{7,6},{8,9},{9,8},{10,11... | collective-permute-start | bytes 184328 | tf_op jit(solution)/shard_map/ppermute | solution.py:402
  17.0 2.7 %collective-permute-start.7 = (bf16[20,2,768]{2,1,0:T(2,128)(2,1)S(1)}, bf16[20,2,768]{2,1,0:T(2,128)(2,1)S(1)}, u32[]{:S(2)}, u32[]{:S(2)}) collective-permute-start(bf16[20,2,768]{2,1,0:T(2,128)(2,1)S(1)} %bitcast.26), channel_id=1, source_target_pairs={{0,4},{1,2},{2,1},{3,7},{4,0},{5,6},{6,5},{7,3},{8,12},{9,10},{10,... | collective-permute-start | bytes 184328 | tf_op jit(solution)/shard_map/ppermute | solution.py:402
  19.7 0.2 broadcast_select_fusion
  20.0 1.3 %shard_map.153 = (bf16[20,16,512]{2,1,0:T(8,128)(2,1)S(1)}, bf16[20,16,512]{2,1,0:T(8,128)(2,1)S(1)}, bf16[20,16,512]{2,1,0:T(8,128)(2,1)S(1)}, bf16[18,48,256]{...) custom-call(bf16[20,2,1536]{2,1,0:T(2,128)(2,1)S(1)} %get-tuple-element.117.xl_ref, ...), custom_call_target="tpu_custom_call" | custom-call | flops 3000000000 | tf_op jit(solution)/shard_map/pallas_call | solution.py:508
  21.3 2.0 %shard_map.152 = (bf16[18,32,256]{2,1,0:T(8,128)(2,1)S(1)}, bf16[18,32,128]{2,1,0:T(8,128)(2,1)S(1)}) custom-call(bf16[20,32,512]{2,1,0:T(8,128)(2,1)S(1)} %pad_maximum_fusion.win_ref, bf16[20,32,512]{2,1,0:T(8,128)(2,1)S(1)} %get-tuple-element.76.left_ref, bf16[20,32,512]{2,1,0:T(8,128)(2,1)S(1)} %get-tuple-element.77.right_ref, ...), custom_call_target="tpu_custom_call" | custom-call | flops 4000000000 | tf_op jit(solution)/shard_map/pallas_call | solution.py:497
  23.4 0.1 broadcast_select_fusion.10
  23.5 5.3 %shard_map.154 = (bf16[512,512]{1,0:T(8,128)(2,1)S(1)}, bf16[8,20,512]{2,1,0:T(8,128)(2,1)S(1)}) custom-call(bf16[20,32,128]{2,1,0:T(8,128)(2,1)S(1)} %get-tuple-element.111.zl_ref, bf16[20,32,128]{2,1,0:T(8,128)(2,1)S(1)} %get-tuple-element.110.zr_ref, bf16[20,2,768]{2,1,0:T(2,128)(2,1)S(1)} %get-tuple-element.125.cl_ref, ...), custom_call_target="tpu_custom_call" | custom-call | flops 6000000000 | tf_op jit(solution)/shard_map/pallas_call | solution.py:514
  28.8 0.1 collective-permute-start.8
  28.9 0.3 shard_map.156.t_ref.ta_ref
  29.3 0.9 %collective-permute-done.8 = bf16[2,20,512]{2,1,0:T(8,128)(2,1)S(1)} collective-permute-done((bf16[2,20,512]{2,1,0:T(8,128)(2,1)S(1)}, bf16[2,20,512]{2,1,0:T(8,128)(2,1)S(1)}, u32[]{:S(2)}, u32[]{:S(2)}) %collective-permute-start.8) | collective-permute-done | bytes 40992 | tf_op jit(solution)/shard_map/ppermute | solution.py:402
  30.3 0.6 %collective-permute-start.9 = (bf16[12,20,256]{2,1,0:T(8,128)(2,1)S(1)}, bf16[12,20,256]{2,1,0:T(8,128)(2,1)S(1)}, u32[]{:S(2)}, u32[]{:S(2)}) collective-permute-start(bf16[12,20,256]{2,1,0:T(8,128)(2,1)S(1)} %get-tuple-element.115), channel_id=1, source_target_pairs={{0,4},{1,2},{2,1},{3,7},{4,0},{5,6},{6,5},{7,3},{8,12},{9,10},{10,... | collective-permute-start | bytes 368648 | tf_op jit(solution)/shard_map/ppermute | solution.py:402
  31.0 1.0 %shard_map.157 = (bf16[12,32,512]{2,1,0:T(8,128)(2,1)S(1)}, bf16[12,32,512]{2,1,0:T(8,128)(2,1)S(1)}, bf16[12,32,512]{2,1,0:T(8,128)(2,1)S(1)}, bf16[10,16,256]{...) custom-call(bf16[12,20,512]{2,1,0:T(8,128)(2,1)S(1)} %pad_maximum_fusion.1.wide_ref, ...), custom_call_target="tpu_custom_call" | custom-call | flops 3000000000 | tf_op jit(solution)/shard_map/pallas_call | solution.py:539
  32.0 1.3 %shard_map.155 = bf16[512,512]{1,0:T(8,128)(2,1)} custom-call(bf16[512,512]{1,0:T(8,128)(2,1)S(1)} %get-tuple-element.98.feat_ref), custom_call_target="tpu_custom_call" | custom-call | flops 2000000000 | tf_op jit(solution)/shard_map/pallas_call | solution.py:533
  33.3 0.3 shard_map.158.tb_ref
  33.6 2.6 %collective-permute-done.10 = bf16[12,20,256]{2,1,0:T(8,128)(2,1)S(1)} collective-permute-done((bf16[12,20,256]{2,1,0:T(8,128)(2,1)S(1)}, bf16[12,20,256]{2,1,0:T(8,128)(2,1)S(1)}, u32[]{:S(2)}, u32[]{:S(2)}) %collective-permute-start.10) | collective-permute-done | bytes 122912 | tf_op jit(solution)/shard_map/ppermute | solution.py:402
  36.2 0.1 collective-permute-done.9
  36.3 4.3 %shard_map.159 = bf16[384,128]{1,0:T(8,128)(2,1)} custom-call(bf16[12,32,512]{2,1,0:T(8,128)(2,1)S(1)} %get-tuple-element.101.a0, bf16[12,32,512]{2,1,0:T(8,128)(2,1)S(1)} %get-tuple-element.102.a1, bf16[12,32,512]{2,1,0:T(8,128)(2,1)S(1)} %get-tuple-element.103.a2, bf16[10,16,256]{2,1,0:T(8,128)(2,1)S(1)} %get-tuple-element.104.m0, ...), custom_call_target="tpu_custom_call" | custom-call | flops 5000000000 | tf_op jit(solution)/shard_map/pallas_call | solution.py:545
  (44 shorter events, 0.6 us)
Async XLA Ops:
  0.7 4.9 %copy-start.4 = (bf16[27,64,64]{2,1,0:T(8,128)(2,1)S(1)}, bf16[27,64,64]{2,1,0:T(8,128)(2,1)}, u32[]{:S(2)}) copy-start(bf16[27,64,64]{2,1,0:T(8,128)(2,1)} %w_ref.2) | copy-start | bytes 663556
  4.8 1.4 %copy-start.7 = (f32[96]{0:T(128)S(1)}, f32[96]{0:T(128)}, u32[]{:S(2)}) copy-start(f32[96]{0:T(128)} %param.23) | copy-start | bytes 1156
  4.8 1.4 %copy-start.8 = (f32[96]{0:T(128)S(1)}, f32[96]{0:T(128)}, u32[]{:S(2)}) copy-start(f32[96]{0:T(128)} %param.25) | copy-start | bytes 1156
  4.8 1.4 %copy-start.9 = (f32[96]{0:T(128)S(1)}, f32[96]{0:T(128)}, u32[]{:S(2)}) copy-start(f32[96]{0:T(128)} %param.27) | copy-start | bytes 1156
  4.8 1.4 %copy-start.6 = (bf16[8,96,64]{1,2,0:T(8,128)(2,1)S(1)}, bf16[8,96,64]{1,2,0:T(8,128)(2,1)}, u32[]{:S(2)}) copy-start(bf16[8,96,64]{1,2,0:T(8,128)(2,1)} %param.22) | copy-start | bytes 294916
  4.9 5.2 %collective-permute-start = (bf16[2,32,512]{2,1,0:T(8,128)(2,1)S(1)}, bf16[2,32,512]{2,1,0:T(8,128)(2,1)S(1)}, u32[]{:S(2)}, u32[]{:S(2)}) collective-permute-start(bf16[2,32,512]{2,1,0:T(8,128)(2,1)S(1)} %slice_select_fusion), channel_id=1, source_target_pairs={{0,4},{1,5},{2,6},{3,7},{4,0},{5,1},{6,2},{7,3},{8,12},{9,13},{10,... | collective-permute-start | bytes 196616 | tf_op jit(solution)/shard_map/ppermute | solution.py:402
  5.0 1.4 %collective-permute-start.3 = (bf16[2,2,3072]{2,1,0:T(2,128)(2,1)S(1)}, bf16[2,2,3072]{2,1,0:T(2,128)(2,1)S(1)}, u32[]{:S(2)}, u32[]{:S(2)}) collective-permute-start(bf16[2,2,3072]{2,1,0:T(2,128)(2,1)S(1)} %broadcast_select_fusion.29), channel_id=1, source_target_pairs={{0,4},{1,5},{2,6},{3,7},{4,0},{5,1},{6,2},{7,3},{8,12},{9,13},{10,... | collective-permute-start | bytes 73736 | tf_op jit(solution)/shard_map/ppermute | solution.py:402
  6.2 7.3 %copy-start = (bf16[27,64,64]{2,1,0:T(8,128)(2,1)S(1)}, bf16[27,64,64]{2,1,0:T(8,128)(2,1)}, u32[]{:S(2)}) copy-start(bf16[27,64,64]{2,1,0:T(8,128)(2,1)} %w_ref.3) | copy-start | bytes 663556
  6.2 7.2 %copy-start.1 = (f32[64]{0:T(128)S(1)}, f32[64]{0:T(128)}, u32[]{:S(2)}) copy-start(f32[64]{0:T(128)} %param.19) | copy-start | bytes 772
  7.0 8.0 %collective-permute-start.4 = (bf16[20,2,1536]{2,1,0:T(2,128)(2,1)S(1)}, bf16[20,2,1536]{2,1,0:T(2,128)(2,1)S(1)}, u32[]{:S(2)}, u32[]{:S(2)}) collective-permute-start(bf16[20,2,1536]{2,1,0:T(2,128)(2,1)S(1)} %get-tuple-element.123), channel_id=1, source_target_pairs={{0,8},{1,9},{2,10},{3,11},{4,12},{5,13},{6,14},{7,15},{8,0},{9,1},... | collective-permute-start | bytes 368648 | tf_op jit(solution)/shard_map/ppermute | solution.py:402
  7.6 8.6 %collective-permute-start.5 = (bf16[20,2,1536]{2,1,0:T(2,128)(2,1)S(1)}, bf16[20,2,1536]{2,1,0:T(2,128)(2,1)S(1)}, u32[]{:S(2)}, u32[]{:S(2)}) collective-permute-start(bf16[20,2,1536]{2,1,0:T(2,128)(2,1)S(1)} %get-tuple-element.122), channel_id=1, source_target_pairs={{0,4},{1,5},{2,6},{3,7},{4,0},{5,1},{6,2},{7,3},{8,16},{9,17},{10,... | collective-permute-start | bytes 368648 | tf_op jit(solution)/shard_map/ppermute | solution.py:402
  10.2 11.0 %collective-permute-start.2 = (bf16[20,32,128]{2,1,0:T(8,128)(2,1)S(1)}, bf16[20,32,128]{2,1,0:T(8,128)(2,1)S(1)}, u32[]{:S(2)}, u32[]{:S(2)}) collective-permute-start(bf16[20,32,128]{2,1,0:T(8,128)(2,1)S(1)} %get-tuple-element.108), channel_id=1, source_target_pairs={{0,1},{1,0},{2,3},{3,2},{4,5},{5,4},{6,7},{7,6},{8,9},{9,8},{10,11... | collective-permute-start | bytes 491528 | tf_op jit(solution)/shard_map/ppermute | solution.py:402
  10.7 10.5 %collective-permute-start.1 = (bf16[20,32,128]{2,1,0:T(8,128)(2,1)S(1)}, bf16[20,32,128]{2,1,0:T(8,128)(2,1)S(1)}, u32[]{:S(2)}, u32[]{:S(2)}) collective-permute-start(bf16[20,32,128]{2,1,0:T(8,128)(2,1)S(1)} %get-tuple-element.109), channel_id=1, source_target_pairs={{0,4},{1,2},{2,1},{3,7},{4,0},{5,6},{6,5},{7,3},{8,12},{9,10},{10,... | collective-permute-start | bytes 491528 | tf_op jit(solution)/shard_map/ppermute | solution.py:402
  16.5 6.8 %collective-permute-start.6 = (bf16[20,2,768]{2,1,0:T(2,128)(2,1)S(1)}, bf16[20,2,768]{2,1,0:T(2,128)(2,1)S(1)}, u32[]{:S(2)}, u32[]{:S(2)}) collective-permute-start(bf16[20,2,768]{2,1,0:T(2,128)(2,1)S(1)} %bitcast.27), channel_id=1, source_target_pairs={{0,1},{1,0},{2,3},{3,2},{4,5},{5,4},{6,7},{7,6},{8,9},{9,8},{10,11... | collective-permute-start | bytes 184328 | tf_op jit(solution)/shard_map/ppermute | solution.py:402
  17.0 6.3 %collective-permute-start.7 = (bf16[20,2,768]{2,1,0:T(2,128)(2,1)S(1)}, bf16[20,2,768]{2,1,0:T(2,128)(2,1)S(1)}, u32[]{:S(2)}, u32[]{:S(2)}) collective-permute-start(bf16[20,2,768]{2,1,0:T(2,128)(2,1)S(1)} %bitcast.26), channel_id=1, source_target_pairs={{0,4},{1,2},{2,1},{3,7},{4,0},{5,6},{6,5},{7,3},{8,12},{9,10},{10,... | collective-permute-start | bytes 184328 | tf_op jit(solution)/shard_map/ppermute | solution.py:402
  21.3 2.2 %copy-start.5 = (f32[64]{0:T(128)S(1)}, f32[64]{0:T(128)}, u32[]{:S(2)}) copy-start(f32[64]{0:T(128)} %param.21) | copy-start | bytes 772
  23.5 5.4 %copy-start.2 = (bf16[27,96,96]{2,1,0:T(8,128)(2,1)S(1)}, bf16[27,96,96]{2,1,0:T(8,128)(2,1)}, u32[]{:S(2)}) copy-start(bf16[27,96,96]{2,1,0:T(8,128)(2,1)} %w_ref.4) | copy-start | bytes 1492996
  28.8 1.3 %collective-permute-start.8 = (bf16[2,20,512]{2,1,0:T(8,128)(2,1)S(1)}, bf16[2,20,512]{2,1,0:T(8,128)(2,1)S(1)}, u32[]{:S(2)}, u32[]{:S(2)}) collective-permute-start(bf16[2,20,512]{2,1,0:T(8,128)(2,1)S(1)} %slice_select_fusion.1), channel_id=1, source_target_pairs={{0,4},{1,5},{2,6},{3,7},{4,0},{5,1},{6,2},{7,3},{8,12},{9,13},{10,... | collective-permute-start | bytes 122888 | tf_op jit(solution)/shard_map/ppermute | solution.py:402
  30.2 6.0 %collective-permute-start.10 = (bf16[12,20,256]{2,1,0:T(8,128)(2,1)S(1)}, bf16[12,20,256]{2,1,0:T(8,128)(2,1)S(1)}, u32[]{:S(2)}, u32[]{:S(2)}) collective-permute-start(bf16[12,20,256]{2,1,0:T(8,128)(2,1)S(1)} %get-tuple-element.114), channel_id=1, source_target_pairs={{0,1},{1,0},{2,3},{3,2},{4,5},{5,4},{6,7},{7,6},{8,9},{9,8},{10,11... | collective-permute-start | bytes 368648 | tf_op jit(solution)/shard_map/ppermute | solution.py:402
  30.3 6.0 %collective-permute-start.9 = (bf16[12,20,256]{2,1,0:T(8,128)(2,1)S(1)}, bf16[12,20,256]{2,1,0:T(8,128)(2,1)S(1)}, u32[]{:S(2)}, u32[]{:S(2)}) collective-permute-start(bf16[12,20,256]{2,1,0:T(8,128)(2,1)S(1)} %get-tuple-element.115), channel_id=1, source_target_pairs={{0,4},{1,2},{2,1},{3,7},{4,0},{5,6},{6,5},{7,3},{8,12},{9,10},{10,... | collective-permute-start | bytes 368648 | tf_op jit(solution)/shard_map/ppermute | solution.py:402
  32.0 1.3 %copy-start.3 = (bf16[27,96,96]{2,1,0:T(8,128)(2,1)S(1)}, bf16[27,96,96]{2,1,0:T(8,128)(2,1)}, u32[]{:S(2)}) copy-start(bf16[27,96,96]{2,1,0:T(8,128)(2,1)} %w_ref.5) | copy-start | bytes 1492996

commit v17 on v14

--- a/solution.py
+++ b/solution.py
@@ -156,32 +156,40 @@
             for zo in range(group):
                 for k in range(3):
                     lane = (3 * j + i) * (group + 2) * pad + (zo + k) * pad
-                    t_ref[zo * pad : zo * pad + chan, lane : lane + chan] = w_ref[9 * i + 3 * j + k]
-
-
-def banded_shape(group, pad):
-    return shaped(group * pad, 9 * (group + 2) * pad)
-
-
-def banded(weights, group, pad):
+                    cut, lane = divmod(lane, t_ref.shape[2])
+                    t_ref[cut, zo * pad : zo * pad + chan, lane : lane + chan] = w_ref[9 * i + 3 * j + k]
+
+
+def banded_shape(group, pad, cuts):
+    return shaped(cuts, group * pad, 9 * (group + 2) * pad // cuts)
+
+
+def banded(weights, group, pad, cuts):
     def kernel(w_ref, t_ref):
         fill_banded(w_ref, t_ref, group, pad)
 
     return pl.pallas_call(
-        kernel, out_shape=banded_shape(group, pad), compiler_params=params(), cost_estimate=cost(1e-6)
+        kernel, out_shape=banded_shape(group, pad, cuts), compiler_params=params(), cost_estimate=cost(1e-6)
     )(weights)
 
 
 def conv_group(taps, t_ref, rows, group_out, group_full):
     pitch = taps[0][0][0].shape[1]
     width = sum(piece[2] for piece in taps[0])
-    parts = [ref[j : j + rows, :, lane : lane + n] for j in range(3) for tap in taps for ref, lane, n in tap]
-    left = jnp.concatenate([p.reshape(rows * pitch, p.shape[2]) for p in parts], axis=1)
-    if width == group_full:
-        right = t_ref[0:group_out, :]
-    else:
-        right = jnp.concatenate([t_ref[0:group_out, n * group_full : n * group_full + width] for n in range(9)], axis=1)
-    return mm(left, right, NT)
+    cuts = t_ref.shape[0]
+    total = None
+    for cut in range(cuts):
+        js = range(3 * cut // cuts, 3 * (cut + 1) // cuts)
+        parts = [ref[j : j + rows, :, lane : lane + n] for j in js for tap in taps for ref, lane, n in tap]
+        left = jnp.concatenate([p.reshape(rows * pitch, p.shape[2]) for p in parts], axis=1)
+        if width == group_full:
+            right = t_ref[cut, 0:group_out, :]
+        else:
+            starts = range(0, t_ref.shape[2], group_full)
+            right = jnp.concatenate([t_ref[cut, 0:group_out, lane : lane + width] for lane in starts], axis=1)
+        term = mm(left, right, NT)
+        total = term if total is None else total + term
+    return total
 
 
 def finish(acc, bias, mask, rows):
@@ -462,7 +470,7 @@
         cost_estimate=cost(4e-6),
     )(*operands)
 
-    t1a = banded(w_conv1a, 4, C1)
+    t1a = banded(w_conv1a, 4, C1, 1)
     bias1a = b_conv1a[None]
 
     y_below, y_above = shift_along(own[:HALO], own[Y1 - HALO :], "gy")
@@ -473,7 +481,7 @@
     rows = Y1 + 2
     left, right, g2, t1b = pl.pallas_call(
         middle_kernel,
-        out_shape=[shaped(ROWS1, X1, lanes1), shaped(ROWS1, X1, lanes1), shaped(rows, X1, 256), banded_shape(4, C1)],
+        out_shape=[shaped(ROWS1, X1, lanes1), shaped(ROWS1, X1, lanes1), shaped(rows, X1, 256), banded_shape(4, C1, 1)],
         compiler_params=params(),
         cost_estimate=cost(1e-7),
     )(win, t1a, bias1a, tab1, w_conv1b)
@@ -516,11 +524,11 @@
     )
 
     down, w_conv2a = lax.optimization_barrier((down, w_conv2a))
-    t2a = banded(w_conv2a, 2, CP)
+    t2a = banded(w_conv2a, 2, CP, 3)
     y_below, y_above = shift_along(down[:HALO], down[Y2 - HALO :], "gy")
     wide = jnp.concatenate([y_below, down, y_above], axis=0)
     feat, wide, w_conv2b = lax.optimization_barrier((feat, wide, w_conv2b))
-    t2b = banded(w_conv2b, 2, CP)
+    t2b = banded(w_conv2b, 2, CP, 3)
     one = pl.pallas_call(
         one_kernel, out_shape=shaped(lanes1, Y1 * X1), compiler_params=params(), cost_estimate=cost(2e-6)
     )(feat)

time: 40.7 us -> 40.4 us (level)
  no operation moved by 1% of the time
where the time goes in v17:
time: 40.4 us; the launch traced here: 40.3 us
  Pallas kernels  21.8 us (54%)
  starting transfers between devices  11.3 us (28%)
  waiting for transfers between devices  4.37 us (11%)
  other arithmetic  1.22 us (3%)
  between operations  1.14 us (3%)
    ppermute x10, starting transfers between devices, swap(): return lax.ppermute(value, axes, pairs)  11.3 us
    pallas_call x1, Pallas kernels, local(): pl.pallas_call(level_one_kernel, out_shape=[shaped(Y1 * X1, lanes1), shap...  5.31 us
    ppermute x10, waiting for transfers between devices, swap(): return lax.ppermute(value, axes, pairs)  4.37 us
    pallas_call x1, Pallas kernels, local(): pl.pallas_call(level_two_kernel, out_shape=shaped(C2 * Z2, Y2 * X2), scra...  4.03 us
    pallas_call x1, Pallas kernels, local(): pl.pallas_call(down1_kernel, in_specs=[pl.BlockSpec(memory_space=pltpu.HB...  4.02 us
    pallas_call x1, Pallas kernels, local(): pl.pallas_call(outer_kernel, out_shape=[shaped(rows, X1, 256), shaped(row...  2.04 us
    pallas_call x1, Pallas kernels, local(): pl.pallas_call(middle_kernel, out_shape=[shaped(ROWS1, X1, lanes1), shape...  1.58 us
    pallas_call x1, Pallas kernels, local(): pl.pallas_call(one_kernel, out_shape=shaped(lanes1, Y1 * X1), compiler_pa...  1.27 us
  transfers between devices with their start and end apart: 10, of which 4 were waited for; matrix products, arithmetic and copies ran while one was open for 2% of the time, Pallas kernels for 21%

profile of v17, /device:TPU:2, one launch (start us, length us, event | category | flops | bytes accessed | tf_op | source)
XLA Modules:
  0.0 40.3 jit_solution(12802385145233915039)
XLA Ops:
  0.7 4.0 %shard_map.149 = (bf16[16,32,512]{2,1,0:T(8,128)(2,1)S(1)}, bf16[128,384]{1,0:T(8,128)(2,1)S(1)}, bf16[128,384]{1,0:T(8,128)(2,1)S(1)}) custom-call(bf16[48,2,8,2048]{3,2,1,0:T(8,128)(2,1)} %bitcast.28, bf16[8,48,64]{2,1,0:T(8,128)(2,1)} %bitcast.29, f32[1,64]{1,0:T(1,128)} %bitcast.31, s32[8,4,32]{2,1,0:T(4,128)} %bitcast.30), custom_call_target="tpu_custom_call" | custom-call | flops 4000000000 | tf_op jit(solution)/shard_map/pallas_call | solution.py:459
  4.7 0.1 collective-permute-start
  5.0 0.6 %shard_map.150.t_ref.ta_ref = bf16[1,256,3456]{2,1,0:T(8,128)(2,1)S(1)} custom-call(bf16[27,64,64]{2,1,0:T(8,128)(2,1)S(1)} %copy-done.4), custom_call_target="tpu_custom_call" | custom-call | flops 1000000000 | tf_op jit(solution)/shard_map/pallas_call | solution.py:171
  5.6 0.4 %collective-permute-done = bf16[2,32,512]{2,1,0:T(8,128)(2,1)S(1)} collective-permute-done((bf16[2,32,512]{2,1,0:T(8,128)(2,1)S(1)}, bf16[2,32,512]{2,1,0:T(8,128)(2,1)S(1)}, u32[]{:S(2)}, u32[]{:S(2)}) %collective-permute-start) | collective-permute-done | bytes 65568 | tf_op jit(solution)/shard_map/ppermute | solution.py:404
  6.1 0.1 pad_maximum_fusion.win_ref
  6.2 0.2 fusion
  6.4 0.3 broadcast_select_fusion.4
  6.6 0.1 collective-permute-start.3
  6.7 3.0 %collective-permute-start.4 = (bf16[20,2,1536]{2,1,0:T(2,128)(2,1)S(1)}, bf16[20,2,1536]{2,1,0:T(2,128)(2,1)S(1)}, u32[]{:S(2)}, u32[]{:S(2)}) collective-permute-start(bf16[20,2,1536]{2,1,0:T(2,128)(2,1)S(1)} %get-tuple-element.88), channel_id=1, source_target_pairs={{0,4},{1,5},{2,6},{3,7},{4,0},{5,1},{6,2},{7,3},{8,16},{9,17},{10,... | collective-permute-start | bytes 368648 | tf_op jit(solution)/shard_map/ppermute | solution.py:404
  9.8 3.1 %collective-permute-start.2 = (bf16[20,32,128]{2,1,0:T(8,128)(2,1)S(1)}, bf16[20,32,128]{2,1,0:T(8,128)(2,1)S(1)}, u32[]{:S(2)}, u32[]{:S(2)}) collective-permute-start(bf16[20,32,128]{2,1,0:T(8,128)(2,1)S(1)} %get-tuple-element.78), channel_id=1, source_target_pairs={{0,1},{1,0},{2,3},{3,2},{4,5},{5,4},{6,7},{7,6},{8,9},{9,8},{10,11... | collective-permute-start | bytes 491528 | tf_op jit(solution)/shard_map/ppermute | solution.py:404
  12.9 1.6 %shard_map.151 = (bf16[20,32,512]{2,1,0:T(8,128)(2,1)S(1)}, bf16[20,32,512]{2,1,0:T(8,128)(2,1)S(1)}, bf16[18,32,256]{2,1,0:T(8,128)(2,1)S(1)}, bf16[1,256,3456]{2,1,0:T(8,128)(2,1)S(1)}) custom-call(bf16[20,32,512]{2,1,0:T(8,128)(2,1)S(1)} %pad_maximum_fusion.win_ref, bf16[1,256,3456]{2,1,0:T(8,128)(2,1)S(1)} %shard_map.150.t_ref.ta_ref, ...), custom_call_target="tpu_custom_call" | custom-call | flops 100000000 | tf_op jit(solution)/shard_map/pallas_call | solution.py:482
  14.5 1.1 %collective-permute-done.4 = bf16[20,2,1536]{2,1,0:T(2,128)(2,1)S(1)} collective-permute-done((bf16[20,2,1536]{2,1,0:T(2,128)(2,1)S(1)}, bf16[20,2,1536]{2,1,0:T(2,128)(2,1)S(1)}, u32[]{:S(2)}, u32[]{:S(2)}) %collective-permute-start.4) | collective-permute-done | bytes 122912 | tf_op jit(solution)/shard_map/ppermute | solution.py:404
  15.7 0.1 fusion.1
  15.8 0.1 broadcast_select_fusion.24
  15.9 0.1 broadcast_select_fusion.25
  16.1 0.1 collective-permute-start.5
  16.2 3.1 %collective-permute-start.6 = (bf16[20,2,768]{2,1,0:T(2,128)(2,1)S(1)}, bf16[20,2,768]{2,1,0:T(2,128)(2,1)S(1)}, u32[]{:S(2)}, u32[]{:S(2)}) collective-permute-start(bf16[20,2,768]{2,1,0:T(2,128)(2,1)S(1)} %bitcast.26), channel_id=1, source_target_pairs={{0,1},{1,0},{2,3},{3,2},{4,5},{5,4},{6,7},{7,6},{8,9},{9,8},{10,11... | collective-permute-start | bytes 184328 | tf_op jit(solution)/shard_map/ppermute | solution.py:404
  19.3 0.2 broadcast_select_fusion
  19.6 1.2 %shard_map.152 = (bf16[20,16,512]{2,1,0:T(8,128)(2,1)S(1)}, bf16[20,16,512]{2,1,0:T(8,128)(2,1)S(1)}, bf16[20,16,512]{2,1,0:T(8,128)(2,1)S(1)}, bf16[18,48,256]{...) custom-call(bf16[20,2,1536]{2,1,0:T(2,128)(2,1)S(1)} %get-tuple-element.87.xl_ref, ...), custom_call_target="tpu_custom_call" | custom-call | flops 3000000000 | tf_op jit(solution)/shard_map/pallas_call | solution.py:506
  20.9 2.0 %shard_map.153 = (bf16[18,32,256]{2,1,0:T(8,128)(2,1)S(1)}, bf16[18,32,128]{2,1,0:T(8,128)(2,1)S(1)}) custom-call(bf16[20,32,512]{2,1,0:T(8,128)(2,1)S(1)} %pad_maximum_fusion.win_ref, bf16[20,32,512]{2,1,0:T(8,128)(2,1)S(1)} %get-tuple-element.53.left_ref, bf16[20,32,512]{2,1,0:T(8,128)(2,1)S(1)} %get-tuple-element.54.right_ref, ...), custom_call_target="tpu_custom_call" | custom-call | flops 4000000000 | tf_op jit(solution)/shard_map/pallas_call | solution.py:497
  23.0 0.1 broadcast_select_fusion.10
  23.1 5.3 %shard_map.154 = (bf16[512,512]{1,0:T(8,128)(2,1)S(1)}, bf16[8,20,512]{2,1,0:T(8,128)(2,1)S(1)}) custom-call(bf16[20,32,128]{2,1,0:T(8,128)(2,1)S(1)} %get-tuple-element.81.zl_ref, bf16[20,32,128]{2,1,0:T(8,128)(2,1)S(1)} %get-tuple-element.80.zr_ref, bf16[20,2,768]{2,1,0:T(2,128)(2,1)S(1)} %get-tuple-element.91.cl_ref, ...), custom_call_target="tpu_custom_call" | custom-call | flops 6000000000 | tf_op jit(solution)/shard_map/pallas_call | solution.py:512
  28.5 0.1 collective-permute-start.7
  28.6 0.3 shard_map.156.t_ref.ta_ref
  28.9 0.9 %collective-permute-done.7 = bf16[2,20,512]{2,1,0:T(8,128)(2,1)S(1)} collective-permute-done((bf16[2,20,512]{2,1,0:T(8,128)(2,1)S(1)}, bf16[2,20,512]{2,1,0:T(8,128)(2,1)S(1)}, u32[]{:S(2)}, u32[]{:S(2)}) %collective-permute-start.7) | collective-permute-done | bytes 40992 | tf_op jit(solution)/shard_map/ppermute | solution.py:404
  29.9 0.2 collective-permute-start.8
  30.1 1.5 %collective-permute-start.9 = (bf16[12,20,256]{2,1,0:T(8,128)(2,1)S(1)}, bf16[12,20,256]{2,1,0:T(8,128)(2,1)S(1)}, u32[]{:S(2)}, u32[]{:S(2)}) collective-permute-start(bf16[12,20,256]{2,1,0:T(8,128)(2,1)S(1)} %get-tuple-element.84), channel_id=1, source_target_pairs={{0,1},{1,0},{2,3},{3,2},{4,5},{5,4},{6,7},{7,6},{8,9},{9,8},{10,11... | collective-permute-start | bytes 368648 | tf_op jit(solution)/shard_map/ppermute | solution.py:404
  31.6 1.1 %shard_map.157 = (bf16[12,32,512]{2,1,0:T(8,128)(2,1)S(1)}, bf16[12,32,512]{2,1,0:T(8,128)(2,1)S(1)}, bf16[12,32,512]{2,1,0:T(8,128)(2,1)S(1)}, bf16[10,16,256]{...) custom-call(bf16[12,20,512]{2,1,0:T(8,128)(2,1)S(1)} %pad_maximum_fusion.1.wide_ref, ...), custom_call_target="tpu_custom_call" | custom-call | flops 3000000000 | tf_op jit(solution)/shard_map/pallas_call | solution.py:538
  32.7 1.3 %shard_map.155 = bf16[512,512]{1,0:T(8,128)(2,1)} custom-call(bf16[512,512]{1,0:T(8,128)(2,1)S(1)} %get-tuple-element.62.feat_ref), custom_call_target="tpu_custom_call" | custom-call | flops 2000000000 | tf_op jit(solution)/shard_map/pallas_call | solution.py:532
  34.0 0.3 shard_map.158.tb_ref
  34.3 1.9 %collective-permute-done.9 = bf16[12,20,256]{2,1,0:T(8,128)(2,1)S(1)} collective-permute-done((bf16[12,20,256]{2,1,0:T(8,128)(2,1)S(1)}, bf16[12,20,256]{2,1,0:T(8,128)(2,1)S(1)}, u32[]{:S(2)}, u32[]{:S(2)}) %collective-permute-start.9) | collective-permute-done | bytes 122912 | tf_op jit(solution)/shard_map/ppermute | solution.py:404
  36.2 4.0 %shard_map.159 = bf16[384,128]{1,0:T(8,128)(2,1)} custom-call(bf16[12,32,512]{2,1,0:T(8,128)(2,1)S(1)} %get-tuple-element.65.a0, bf16[12,32,512]{2,1,0:T(8,128)(2,1)S(1)} %get-tuple-element.66.a1, bf16[12,32,512]{2,1,0:T(8,128)(2,1)S(1)} %get-tuple-element.67.a2, bf16[10,16,256]{2,1,0:T(8,128)(2,1)S(1)} %get-tuple-element.68.m0, ...), custom_call_target="tpu_custom_call" | custom-call | flops 5000000000 | tf_op jit(solution)/shard_map/pallas_call | solution.py:544
  (43 shorter events, 0.5 us)
Async XLA Ops:
  0.6 4.2 %copy-start.7 = (f32[96]{0:T(128)S(1)}, f32[96]{0:T(128)}, u32[]{:S(2)}) copy-start(f32[96]{0:T(128)} %param.23) | copy-start | bytes 1156
  0.7 4.2 %copy-start.8 = (f32[96]{0:T(128)S(1)}, f32[96]{0:T(128)}, u32[]{:S(2)}) copy-start(f32[96]{0:T(128)} %param.25) | copy-start | bytes 1156
  0.7 4.2 %copy-start.9 = (f32[96]{0:T(128)S(1)}, f32[96]{0:T(128)}, u32[]{:S(2)}) copy-start(f32[96]{0:T(128)} %param.27) | copy-start | bytes 1156
  0.7 4.3 %copy-start.6 = (bf16[8,96,64]{1,2,0:T(8,128)(2,1)S(1)}, bf16[8,96,64]{1,2,0:T(8,128)(2,1)}, u32[]{:S(2)}) copy-start(bf16[8,96,64]{1,2,0:T(8,128)(2,1)} %param.22) | copy-start | bytes 294916
  0.7 4.3 %copy-start.4 = (bf16[27,64,64]{2,1,0:T(8,128)(2,1)S(1)}, bf16[27,64,64]{2,1,0:T(8,128)(2,1)}, u32[]{:S(2)}) copy-start(bf16[27,64,64]{2,1,0:T(8,128)(2,1)} %w_ref.2) | copy-start | bytes 663556
  4.7 1.3 %collective-permute-start = (bf16[2,32,512]{2,1,0:T(8,128)(2,1)S(1)}, bf16[2,32,512]{2,1,0:T(8,128)(2,1)S(1)}, u32[]{:S(2)}, u32[]{:S(2)}) collective-permute-start(bf16[2,32,512]{2,1,0:T(8,128)(2,1)S(1)} %slice_select_fusion), channel_id=1, source_target_pairs={{0,4},{1,5},{2,6},{3,7},{4,0},{5,1},{6,2},{7,3},{8,12},{9,13},{10,... | collective-permute-start | bytes 196616 | tf_op jit(solution)/shard_map/ppermute | solution.py:404
  5.6 7.3 %copy-start = (bf16[27,64,64]{2,1,0:T(8,128)(2,1)S(1)}, bf16[27,64,64]{2,1,0:T(8,128)(2,1)}, u32[]{:S(2)}) copy-start(bf16[27,64,64]{2,1,0:T(8,128)(2,1)} %w_ref.3) | copy-start | bytes 663556
  5.6 7.3 %copy-start.1 = (f32[64]{0:T(128)S(1)}, f32[64]{0:T(128)}, u32[]{:S(2)}) copy-start(f32[64]{0:T(128)} %param.19) | copy-start | bytes 772
  6.6 7.9 %collective-permute-start.3 = (bf16[20,2,1536]{2,1,0:T(2,128)(2,1)S(1)}, bf16[20,2,1536]{2,1,0:T(2,128)(2,1)S(1)}, u32[]{:S(2)}, u32[]{:S(2)}) collective-permute-start(bf16[20,2,1536]{2,1,0:T(2,128)(2,1)S(1)} %get-tuple-element.89), channel_id=1, source_target_pairs={{0,8},{1,9},{2,10},{3,11},{4,12},{5,13},{6,14},{7,15},{8,0},{9,1},... | collective-permute-start | bytes 368648 | tf_op jit(solution)/shard_map/ppermute | solution.py:404
  6.7 9.0 %collective-permute-start.4 = (bf16[20,2,1536]{2,1,0:T(2,128)(2,1)S(1)}, bf16[20,2,1536]{2,1,0:T(2,128)(2,1)S(1)}, u32[]{:S(2)}, u32[]{:S(2)}) collective-permute-start(bf16[20,2,1536]{2,1,0:T(2,128)(2,1)S(1)} %get-tuple-element.88), channel_id=1, source_target_pairs={{0,4},{1,5},{2,6},{3,7},{4,0},{5,1},{6,2},{7,3},{8,16},{9,17},{10,... | collective-permute-start | bytes 368648 | tf_op jit(solution)/shard_map/ppermute | solution.py:404
  9.7 11.1 %collective-permute-start.1 = (bf16[20,32,128]{2,1,0:T(8,128)(2,1)S(1)}, bf16[20,32,128]{2,1,0:T(8,128)(2,1)S(1)}, u32[]{:S(2)}, u32[]{:S(2)}) collective-permute-start(bf16[20,32,128]{2,1,0:T(8,128)(2,1)S(1)} %get-tuple-element.79), channel_id=1, source_target_pairs={{0,4},{1,2},{2,1},{3,7},{4,0},{5,6},{6,5},{7,3},{8,12},{9,10},{10,... | collective-permute-start | bytes 491528 | tf_op jit(solution)/shard_map/ppermute | solution.py:404
  9.8 11.0 %collective-permute-start.2 = (bf16[20,32,128]{2,1,0:T(8,128)(2,1)S(1)}, bf16[20,32,128]{2,1,0:T(8,128)(2,1)S(1)}, u32[]{:S(2)}, u32[]{:S(2)}) collective-permute-start(bf16[20,32,128]{2,1,0:T(8,128)(2,1)S(1)} %get-tuple-element.78), channel_id=1, source_target_pairs={{0,1},{1,0},{2,3},{3,2},{4,5},{5,4},{6,7},{7,6},{8,9},{9,8},{10,11... | collective-permute-start | bytes 491528 | tf_op jit(solution)/shard_map/ppermute | solution.py:404
  16.1 6.8 %collective-permute-start.5 = (bf16[20,2,768]{2,1,0:T(2,128)(2,1)S(1)}, bf16[20,2,768]{2,1,0:T(2,128)(2,1)S(1)}, u32[]{:S(2)}, u32[]{:S(2)}) collective-permute-start(bf16[20,2,768]{2,1,0:T(2,128)(2,1)S(1)} %bitcast.27), channel_id=1, source_target_pairs={{0,4},{1,2},{2,1},{3,7},{4,0},{5,6},{6,5},{7,3},{8,12},{9,10},{10,... | collective-permute-start | bytes 184328 | tf_op jit(solution)/shard_map/ppermute | solution.py:404
  16.2 6.8 %collective-permute-start.6 = (bf16[20,2,768]{2,1,0:T(2,128)(2,1)S(1)}, bf16[20,2,768]{2,1,0:T(2,128)(2,1)S(1)}, u32[]{:S(2)}, u32[]{:S(2)}) collective-permute-start(bf16[20,2,768]{2,1,0:T(2,128)(2,1)S(1)} %bitcast.26), channel_id=1, source_target_pairs={{0,1},{1,0},{2,3},{3,2},{4,5},{5,4},{6,7},{7,6},{8,9},{9,8},{10,11... | collective-permute-start | bytes 184328 | tf_op jit(solution)/shard_map/ppermute | solution.py:404
  20.9 2.2 %copy-start.5 = (f32[64]{0:T(128)S(1)}, f32[64]{0:T(128)}, u32[]{:S(2)}) copy-start(f32[64]{0:T(128)} %param.21) | copy-start | bytes 772
  23.1 5.4 %copy-start.2 = (bf16[27,96,96]{2,1,0:T(8,128)(2,1)S(1)}, bf16[27,96,96]{2,1,0:T(8,128)(2,1)}, u32[]{:S(2)}) copy-start(bf16[27,96,96]{2,1,0:T(8,128)(2,1)} %w_ref.4) | copy-start | bytes 1492996
  28.5 1.3 %collective-permute-start.7 = (bf16[2,20,512]{2,1,0:T(8,128)(2,1)S(1)}, bf16[2,20,512]{2,1,0:T(8,128)(2,1)S(1)}, u32[]{:S(2)}, u32[]{:S(2)}) collective-permute-start(bf16[2,20,512]{2,1,0:T(8,128)(2,1)S(1)} %slice_select_fusion.1), channel_id=1, source_target_pairs={{0,4},{1,5},{2,6},{3,7},{4,0},{5,1},{6,2},{7,3},{8,12},{9,13},{10,... | collective-permute-start | bytes 122888 | tf_op jit(solution)/shard_map/ppermute | solution.py:404
  29.9 4.4 %collective-permute-start.8 = (bf16[12,20,256]{2,1,0:T(8,128)(2,1)S(1)}, bf16[12,20,256]{2,1,0:T(8,128)(2,1)S(1)}, u32[]{:S(2)}, u32[]{:S(2)}) collective-permute-start(bf16[12,20,256]{2,1,0:T(8,128)(2,1)S(1)} %get-tuple-element.85), channel_id=1, source_target_pairs={{0,4},{1,2},{2,1},{3,7},{4,0},{5,6},{6,5},{7,3},{8,12},{9,10},{10,... | collective-permute-start | bytes 368648 | tf_op jit(solution)/shard_map/ppermute | solution.py:404
  30.1 6.1 %collective-permute-start.9 = (bf16[12,20,256]{2,1,0:T(8,128)(2,1)S(1)}, bf16[12,20,256]{2,1,0:T(8,128)(2,1)S(1)}, u32[]{:S(2)}, u32[]{:S(2)}) collective-permute-start(bf16[12,20,256]{2,1,0:T(8,128)(2,1)S(1)} %get-tuple-element.84), channel_id=1, source_target_pairs={{0,1},{1,0},{2,3},{3,2},{4,5},{5,4},{6,7},{7,6},{8,9},{9,8},{10,11... | collective-permute-start | bytes 368648 | tf_op jit(solution)/shard_map/ppermute | solution.py:404
  32.7 1.3 %copy-start.3 = (bf16[27,96,96]{2,1,0:T(8,128)(2,1)S(1)}, bf16[27,96,96]{2,1,0:T(8,128)(2,1)}, u32[]{:S(2)}) copy-start(bf16[27,96,96]{2,1,0:T(8,128)(2,1)} %w_ref.5) | copy-start | bytes 1492996

commit v18 on v17

--- a/solution.py
+++ b/solution.py
@@ -98,8 +98,8 @@
     lanes = Z1 // 2 * C1
     small = ((t_hbm, t_ref), (wd_hbm, w_ref), (b_hbm, b_ref))
     copies = [pltpu.make_async_copy(src, dst, sems.at[n]) for n, (src, dst) in enumerate(small)]
-    for n in range(C0 // 16):
-        cut = slice(n * 16, n * 16 + 16)
+    for n in range(C0 // 4):
+        cut = slice(n * 4, n * 4 + 4)
         copies.append(pltpu.make_async_copy(v_hbm.at[cut], v_ref.at[cut], sems.at[len(small) + n]))
     for copy in copies:
         copy.start()
@@ -126,8 +126,9 @@
     select = one_hot_rows(((r & 32) << 2) | (r & 64) | ((r & 31) << 1) | (r >> 7), 4 * CX)
     part = 16 * half
     acc = [0.0, 0.0]
-    for n, copy in enumerate(copies[3:]):
-        copy.wait()
+    for n in range(C0 // 16):
+        for copy in copies[3 + 4 * n : 7 + 4 * n]:
+            copy.wait()
         for m in range(v_ref.shape[3] // 256):
             v = [v_ref[n * 16 : n * 16 + 16, h, :, m * 256 : m * 256 + 256].reshape(part, 256) for h in range(2)]
             cells = mm(select, jnp.concatenate(v, axis=0), NT).astype(BF)
@@ -464,7 +465,7 @@
         + [
             pltpu.VMEM((C0 // 16, 64 * half, lanes1 // 2), BF),
             pltpu.VMEM((C0 // 16, 2, Y1 * X1, 64 * half), BF),
-            pltpu.SemaphoreType.DMA((3 + C0 // 16,)),
+            pltpu.SemaphoreType.DMA((3 + C0 // 4,)),
         ],
         compiler_params=params(),
         cost_estimate=cost(4e-6),

time: 40.4 us -> 40.5 us (level)
  no operation moved by 1% of the time
where the time goes in v18:
time: 40.5 us; the launch traced here: 40.4 us
  Pallas kernels  21.9 us (54%)
  starting transfers between devices  11.3 us (28%)
  waiting for transfers between devices  4.37 us (11%)
  other arithmetic  1.22 us (3%)
  between operations  1.14 us (3%)
    ppermute x10, starting transfers between devices, swap(): return lax.ppermute(value, axes, pairs)  11.3 us
    pallas_call x1, Pallas kernels, local(): pl.pallas_call(level_one_kernel, out_shape=[shaped(Y1 * X1, lanes1), shap...  5.3 us
    ppermute x10, waiting for transfers between devices, swap(): return lax.ppermute(value, axes, pairs)  4.37 us
    pallas_call x1, Pallas kernels, local(): pl.pallas_call(down1_kernel, in_specs=[pl.BlockSpec(memory_space=pltpu.HB...  4.12 us
    pallas_call x1, Pallas kernels, local(): pl.pallas_call(level_two_kernel, out_shape=shaped(C2 * Z2, Y2 * X2), scra...  4.03 us
    pallas_call x1, Pallas kernels, local(): pl.pallas_call(outer_kernel, out_shape=[shaped(rows, X1, 256), shaped(row...  2.04 us
    pallas_call x1, Pallas kernels, local(): pl.pallas_call(middle_kernel, out_shape=[shaped(ROWS1, X1, lanes1), shape...  1.58 us
    pallas_call x1, Pallas kernels, local(): pl.pallas_call(one_kernel, out_shape=shaped(lanes1, Y1 * X1), compiler_pa...  1.27 us
  transfers between devices with their start and end apart: 10, of which 4 were waited for; matrix products, arithmetic and copies ran while one was open for 2% of the time, Pallas kernels for 21%

profile of v18, /device:TPU:2, one launch (start us, length us, event | category | flops | bytes accessed | tf_op | source)
XLA Modules:
  0.0 40.4 jit_solution(34841012511636189)
XLA Ops:
  0.7 4.1 %shard_map.149 = (bf16[16,32,512]{2,1,0:T(8,128)(2,1)S(1)}, bf16[128,384]{1,0:T(8,128)(2,1)S(1)}, bf16[128,384]{1,0:T(8,128)(2,1)S(1)}) custom-call(bf16[48,2,8,2048]{3,2,1,0:T(8,128)(2,1)} %bitcast.28, bf16[8,48,64]{2,1,0:T(8,128)(2,1)} %bitcast.29, f32[1,64]{1,0:T(1,128)} %bitcast.31, s32[8,4,32]{2,1,0:T(4,128)} %bitcast.30), custom_call_target="tpu_custom_call" | custom-call | flops 4000000000 | tf_op jit(solution)/shard_map/pallas_call | solution.py:460
  4.8 0.1 collective-permute-start
  5.1 0.6 %shard_map.150.t_ref.ta_ref = bf16[1,256,3456]{2,1,0:T(8,128)(2,1)S(1)} custom-call(bf16[27,64,64]{2,1,0:T(8,128)(2,1)S(1)} %copy-done.4), custom_call_target="tpu_custom_call" | custom-call | flops 1000000000 | tf_op jit(solution)/shard_map/pallas_call | solution.py:172
  5.7 0.4 %collective-permute-done = bf16[2,32,512]{2,1,0:T(8,128)(2,1)S(1)} collective-permute-done((bf16[2,32,512]{2,1,0:T(8,128)(2,1)S(1)}, bf16[2,32,512]{2,1,0:T(8,128)(2,1)S(1)}, u32[]{:S(2)}, u32[]{:S(2)}) %collective-permute-start) | collective-permute-done | bytes 65568 | tf_op jit(solution)/shard_map/ppermute | solution.py:405
  6.2 0.1 pad_maximum_fusion.win_ref
  6.3 0.2 fusion
  6.5 0.3 broadcast_select_fusion.4
  6.7 0.1 collective-permute-start.3
  6.8 3.0 %collective-permute-start.4 = (bf16[20,2,1536]{2,1,0:T(2,128)(2,1)S(1)}, bf16[20,2,1536]{2,1,0:T(2,128)(2,1)S(1)}, u32[]{:S(2)}, u32[]{:S(2)}) collective-permute-start(bf16[20,2,1536]{2,1,0:T(2,128)(2,1)S(1)} %get-tuple-element.88), channel_id=1, source_target_pairs={{0,4},{1,5},{2,6},{3,7},{4,0},{5,1},{6,2},{7,3},{8,16},{9,17},{10,... | collective-permute-start | bytes 368648 | tf_op jit(solution)/shard_map/ppermute | solution.py:405
  9.8 0.1 collective-permute-start.1
  9.9 3.1 %collective-permute-start.2 = (bf16[20,32,128]{2,1,0:T(8,128)(2,1)S(1)}, bf16[20,32,128]{2,1,0:T(8,128)(2,1)S(1)}, u32[]{:S(2)}, u32[]{:S(2)}) collective-permute-start(bf16[20,32,128]{2,1,0:T(8,128)(2,1)S(1)} %get-tuple-element.78), channel_id=1, source_target_pairs={{0,1},{1,0},{2,3},{3,2},{4,5},{5,4},{6,7},{7,6},{8,9},{9,8},{10,11... | collective-permute-start | bytes 491528 | tf_op jit(solution)/shard_map/ppermute | solution.py:405
  13.0 1.6 %shard_map.151 = (bf16[20,32,512]{2,1,0:T(8,128)(2,1)S(1)}, bf16[20,32,512]{2,1,0:T(8,128)(2,1)S(1)}, bf16[18,32,256]{2,1,0:T(8,128)(2,1)S(1)}, bf16[1,256,3456]{2,1,0:T(8,128)(2,1)S(1)}) custom-call(bf16[20,32,512]{2,1,0:T(8,128)(2,1)S(1)} %pad_maximum_fusion.win_ref, bf16[1,256,3456]{2,1,0:T(8,128)(2,1)S(1)} %shard_map.150.t_ref.ta_ref, ...), custom_call_target="tpu_custom_call" | custom-call | flops 100000000 | tf_op jit(solution)/shard_map/pallas_call | solution.py:483
  14.6 1.1 %collective-permute-done.4 = bf16[20,2,1536]{2,1,0:T(2,128)(2,1)S(1)} collective-permute-done((bf16[20,2,1536]{2,1,0:T(2,128)(2,1)S(1)}, bf16[20,2,1536]{2,1,0:T(2,128)(2,1)S(1)}, u32[]{:S(2)}, u32[]{:S(2)}) %collective-permute-start.4) | collective-permute-done | bytes 122912 | tf_op jit(solution)/shard_map/ppermute | solution.py:405
  15.8 0.1 fusion.1
  15.9 0.1 broadcast_select_fusion.24
  16.0 0.1 broadcast_select_fusion.25
  16.2 0.1 collective-permute-start.5
  16.3 3.1 %collective-permute-start.6 = (bf16[20,2,768]{2,1,0:T(2,128)(2,1)S(1)}, bf16[20,2,768]{2,1,0:T(2,128)(2,1)S(1)}, u32[]{:S(2)}, u32[]{:S(2)}) collective-permute-start(bf16[20,2,768]{2,1,0:T(2,128)(2,1)S(1)} %bitcast.26), channel_id=1, source_target_pairs={{0,1},{1,0},{2,3},{3,2},{4,5},{5,4},{6,7},{7,6},{8,9},{9,8},{10,11... | collective-permute-start | bytes 184328 | tf_op jit(solution)/shard_map/ppermute | solution.py:405
  19.4 0.2 broadcast_select_fusion
  19.7 1.2 %shard_map.152 = (bf16[20,16,512]{2,1,0:T(8,128)(2,1)S(1)}, bf16[20,16,512]{2,1,0:T(8,128)(2,1)S(1)}, bf16[20,16,512]{2,1,0:T(8,128)(2,1)S(1)}, bf16[18,48,256]{...) custom-call(bf16[20,2,1536]{2,1,0:T(2,128)(2,1)S(1)} %get-tuple-element.87.xl_ref, ...), custom_call_target="tpu_custom_call" | custom-call | flops 3000000000 | tf_op jit(solution)/shard_map/pallas_call | solution.py:507
  21.0 2.0 %shard_map.153 = (bf16[18,32,256]{2,1,0:T(8,128)(2,1)S(1)}, bf16[18,32,128]{2,1,0:T(8,128)(2,1)S(1)}) custom-call(bf16[20,32,512]{2,1,0:T(8,128)(2,1)S(1)} %pad_maximum_fusion.win_ref, bf16[20,32,512]{2,1,0:T(8,128)(2,1)S(1)} %get-tuple-element.53.left_ref, bf16[20,32,512]{2,1,0:T(8,128)(2,1)S(1)} %get-tuple-element.54.right_ref, ...), custom_call_target="tpu_custom_call" | custom-call | flops 4000000000 | tf_op jit(solution)/shard_map/pallas_call | solution.py:498
  23.1 0.1 broadcast_select_fusion.10
  23.2 5.3 %shard_map.154 = (bf16[512,512]{1,0:T(8,128)(2,1)S(1)}, bf16[8,20,512]{2,1,0:T(8,128)(2,1)S(1)}) custom-call(bf16[20,32,128]{2,1,0:T(8,128)(2,1)S(1)} %get-tuple-element.81.zl_ref, bf16[20,32,128]{2,1,0:T(8,128)(2,1)S(1)} %get-tuple-element.80.zr_ref, bf16[20,2,768]{2,1,0:T(2,128)(2,1)S(1)} %get-tuple-element.91.cl_ref, ...), custom_call_target="tpu_custom_call" | custom-call | flops 6000000000 | tf_op jit(solution)/shard_map/pallas_call | solution.py:513
  28.7 0.3 shard_map.156.t_ref.ta_ref
  29.0 0.9 %collective-permute-done.7 = bf16[2,20,512]{2,1,0:T(8,128)(2,1)S(1)} collective-permute-done((bf16[2,20,512]{2,1,0:T(8,128)(2,1)S(1)}, bf16[2,20,512]{2,1,0:T(8,128)(2,1)S(1)}, u32[]{:S(2)}, u32[]{:S(2)}) %collective-permute-start.7) | collective-permute-done | bytes 40992 | tf_op jit(solution)/shard_map/ppermute | solution.py:405
  30.0 0.2 collective-permute-start.8
  30.2 1.5 %collective-permute-start.9 = (bf16[12,20,256]{2,1,0:T(8,128)(2,1)S(1)}, bf16[12,20,256]{2,1,0:T(8,128)(2,1)S(1)}, u32[]{:S(2)}, u32[]{:S(2)}) collective-permute-start(bf16[12,20,256]{2,1,0:T(8,128)(2,1)S(1)} %get-tuple-element.84), channel_id=1, source_target_pairs={{0,1},{1,0},{2,3},{3,2},{4,5},{5,4},{6,7},{7,6},{8,9},{9,8},{10,11... | collective-permute-start | bytes 368648 | tf_op jit(solution)/shard_map/ppermute | solution.py:405
  31.7 1.1 %shard_map.157 = (bf16[12,32,512]{2,1,0:T(8,128)(2,1)S(1)}, bf16[12,32,512]{2,1,0:T(8,128)(2,1)S(1)}, bf16[12,32,512]{2,1,0:T(8,128)(2,1)S(1)}, bf16[10,16,256]{...) custom-call(bf16[12,20,512]{2,1,0:T(8,128)(2,1)S(1)} %pad_maximum_fusion.1.wide_ref, ...), custom_call_target="tpu_custom_call" | custom-call | flops 3000000000 | tf_op jit(solution)/shard_map/pallas_call | solution.py:539
  32.8 1.3 %shard_map.155 = bf16[512,512]{1,0:T(8,128)(2,1)} custom-call(bf16[512,512]{1,0:T(8,128)(2,1)S(1)} %get-tuple-element.62.feat_ref), custom_call_target="tpu_custom_call" | custom-call | flops 2000000000 | tf_op jit(solution)/shard_map/pallas_call | solution.py:533
  34.0 0.3 shard_map.158.tb_ref
  34.4 1.9 %collective-permute-done.9 = bf16[12,20,256]{2,1,0:T(8,128)(2,1)S(1)} collective-permute-done((bf16[12,20,256]{2,1,0:T(8,128)(2,1)S(1)}, bf16[12,20,256]{2,1,0:T(8,128)(2,1)S(1)}, u32[]{:S(2)}, u32[]{:S(2)}) %collective-permute-start.9) | collective-permute-done | bytes 122912 | tf_op jit(solution)/shard_map/ppermute | solution.py:405
  36.3 4.0 %shard_map.159 = bf16[384,128]{1,0:T(8,128)(2,1)} custom-call(bf16[12,32,512]{2,1,0:T(8,128)(2,1)S(1)} %get-tuple-element.65.a0, bf16[12,32,512]{2,1,0:T(8,128)(2,1)S(1)} %get-tuple-element.66.a1, bf16[12,32,512]{2,1,0:T(8,128)(2,1)S(1)} %get-tuple-element.67.a2, bf16[10,16,256]{2,1,0:T(8,128)(2,1)S(1)} %get-tuple-element.68.m0, ...), custom_call_target="tpu_custom_call" | custom-call | flops 5000000000 | tf_op jit(solution)/shard_map/pallas_call | solution.py:545
  (43 shorter events, 0.5 us)
Async XLA Ops:
  0.6 4.3 %copy-start.7 = (f32[96]{0:T(128)S(1)}, f32[96]{0:T(128)}, u32[]{:S(2)}) copy-start(f32[96]{0:T(128)} %param.23) | copy-start | bytes 1156
  0.7 4.3 %copy-start.8 = (f32[96]{0:T(128)S(1)}, f32[96]{0:T(128)}, u32[]{:S(2)}) copy-start(f32[96]{0:T(128)} %param.25) | copy-start | bytes 1156
  0.7 4.3 %copy-start.9 = (f32[96]{0:T(128)S(1)}, f32[96]{0:T(128)}, u32[]{:S(2)}) copy-start(f32[96]{0:T(128)} %param.27) | copy-start | bytes 1156
  0.7 4.4 %copy-start.6 = (bf16[8,96,64]{1,2,0:T(8,128)(2,1)S(1)}, bf16[8,96,64]{1,2,0:T(8,128)(2,1)}, u32[]{:S(2)}) copy-start(bf16[8,96,64]{1,2,0:T(8,128)(2,1)} %param.22) | copy-start | bytes 294916
  0.7 4.4 %copy-start.4 = (bf16[27,64,64]{2,1,0:T(8,128)(2,1)S(1)}, bf16[27,64,64]{2,1,0:T(8,128)(2,1)}, u32[]{:S(2)}) copy-start(bf16[27,64,64]{2,1,0:T(8,128)(2,1)} %w_ref.2) | copy-start | bytes 663556
  4.8 1.3 %collective-permute-start = (bf16[2,32,512]{2,1,0:T(8,128)(2,1)S(1)}, bf16[2,32,512]{2,1,0:T(8,128)(2,1)S(1)}, u32[]{:S(2)}, u32[]{:S(2)}) collective-permute-start(bf16[2,32,512]{2,1,0:T(8,128)(2,1)S(1)} %slice_select_fusion), channel_id=1, source_target_pairs={{0,4},{1,5},{2,6},{3,7},{4,0},{5,1},{6,2},{7,3},{8,12},{9,13},{10,... | collective-permute-start | bytes 196616 | tf_op jit(solution)/shard_map/ppermute | solution.py:405
  5.7 7.3 %copy-start = (bf16[27,64,64]{2,1,0:T(8,128)(2,1)S(1)}, bf16[27,64,64]{2,1,0:T(8,128)(2,1)}, u32[]{:S(2)}) copy-start(bf16[27,64,64]{2,1,0:T(8,128)(2,1)} %w_ref.3) | copy-start | bytes 663556
  5.7 7.3 %copy-start.1 = (f32[64]{0:T(128)S(1)}, f32[64]{0:T(128)}, u32[]{:S(2)}) copy-start(f32[64]{0:T(128)} %param.19) | copy-start | bytes 772
  6.7 7.9 %collective-permute-start.3 = (bf16[20,2,1536]{2,1,0:T(2,128)(2,1)S(1)}, bf16[20,2,1536]{2,1,0:T(2,128)(2,1)S(1)}, u32[]{:S(2)}, u32[]{:S(2)}) collective-permute-start(bf16[20,2,1536]{2,1,0:T(2,128)(2,1)S(1)} %get-tuple-element.89), channel_id=1, source_target_pairs={{0,8},{1,9},{2,10},{3,11},{4,12},{5,13},{6,14},{7,15},{8,0},{9,1},... | collective-permute-start | bytes 368648 | tf_op jit(solution)/shard_map/ppermute | solution.py:405
  6.8 9.0 %collective-permute-start.4 = (bf16[20,2,1536]{2,1,0:T(2,128)(2,1)S(1)}, bf16[20,2,1536]{2,1,0:T(2,128)(2,1)S(1)}, u32[]{:S(2)}, u32[]{:S(2)}) collective-permute-start(bf16[20,2,1536]{2,1,0:T(2,128)(2,1)S(1)} %get-tuple-element.88), channel_id=1, source_target_pairs={{0,4},{1,5},{2,6},{3,7},{4,0},{5,1},{6,2},{7,3},{8,16},{9,17},{10,... | collective-permute-start | bytes 368648 | tf_op jit(solution)/shard_map/ppermute | solution.py:405
  9.8 11.1 %collective-permute-start.1 = (bf16[20,32,128]{2,1,0:T(8,128)(2,1)S(1)}, bf16[20,32,128]{2,1,0:T(8,128)(2,1)S(1)}, u32[]{:S(2)}, u32[]{:S(2)}) collective-permute-start(bf16[20,32,128]{2,1,0:T(8,128)(2,1)S(1)} %get-tuple-element.79), channel_id=1, source_target_pairs={{0,4},{1,2},{2,1},{3,7},{4,0},{5,6},{6,5},{7,3},{8,12},{9,10},{10,... | collective-permute-start | bytes 491528 | tf_op jit(solution)/shard_map/ppermute | solution.py:405
  9.9 11.1 %collective-permute-start.2 = (bf16[20,32,128]{2,1,0:T(8,128)(2,1)S(1)}, bf16[20,32,128]{2,1,0:T(8,128)(2,1)S(1)}, u32[]{:S(2)}, u32[]{:S(2)}) collective-permute-start(bf16[20,32,128]{2,1,0:T(8,128)(2,1)S(1)} %get-tuple-element.78), channel_id=1, source_target_pairs={{0,1},{1,0},{2,3},{3,2},{4,5},{5,4},{6,7},{7,6},{8,9},{9,8},{10,11... | collective-permute-start | bytes 491528 | tf_op jit(solution)/shard_map/ppermute | solution.py:405
  16.2 6.8 %collective-permute-start.5 = (bf16[20,2,768]{2,1,0:T(2,128)(2,1)S(1)}, bf16[20,2,768]{2,1,0:T(2,128)(2,1)S(1)}, u32[]{:S(2)}, u32[]{:S(2)}) collective-permute-start(bf16[20,2,768]{2,1,0:T(2,128)(2,1)S(1)} %bitcast.27), channel_id=1, source_target_pairs={{0,4},{1,2},{2,1},{3,7},{4,0},{5,6},{6,5},{7,3},{8,12},{9,10},{10,... | collective-permute-start | bytes 184328 | tf_op jit(solution)/shard_map/ppermute | solution.py:405
  16.3 6.8 %collective-permute-start.6 = (bf16[20,2,768]{2,1,0:T(2,128)(2,1)S(1)}, bf16[20,2,768]{2,1,0:T(2,128)(2,1)S(1)}, u32[]{:S(2)}, u32[]{:S(2)}) collective-permute-start(bf16[20,2,768]{2,1,0:T(2,128)(2,1)S(1)} %bitcast.26), channel_id=1, source_target_pairs={{0,1},{1,0},{2,3},{3,2},{4,5},{5,4},{6,7},{7,6},{8,9},{9,8},{10,11... | collective-permute-start | bytes 184328 | tf_op jit(solution)/shard_map/ppermute | solution.py:405
  21.0 2.2 %copy-start.5 = (f32[64]{0:T(128)S(1)}, f32[64]{0:T(128)}, u32[]{:S(2)}) copy-start(f32[64]{0:T(128)} %param.21) | copy-start | bytes 772
  23.2 5.4 %copy-start.2 = (bf16[27,96,96]{2,1,0:T(8,128)(2,1)S(1)}, bf16[27,96,96]{2,1,0:T(8,128)(2,1)}, u32[]{:S(2)}) copy-start(bf16[27,96,96]{2,1,0:T(8,128)(2,1)} %w_ref.4) | copy-start | bytes 1492996
  28.6 1.3 %collective-permute-start.7 = (bf16[2,20,512]{2,1,0:T(8,128)(2,1)S(1)}, bf16[2,20,512]{2,1,0:T(8,128)(2,1)S(1)}, u32[]{:S(2)}, u32[]{:S(2)}) collective-permute-start(bf16[2,20,512]{2,1,0:T(8,128)(2,1)S(1)} %slice_select_fusion.1), channel_id=1, source_target_pairs={{0,4},{1,5},{2,6},{3,7},{4,0},{5,1},{6,2},{7,3},{8,12},{9,13},{10,... | collective-permute-start | bytes 122888 | tf_op jit(solution)/shard_map/ppermute | solution.py:405
  30.0 4.4 %collective-permute-start.8 = (bf16[12,20,256]{2,1,0:T(8,128)(2,1)S(1)}, bf16[12,20,256]{2,1,0:T(8,128)(2,1)S(1)}, u32[]{:S(2)}, u32[]{:S(2)}) collective-permute-start(bf16[12,20,256]{2,1,0:T(8,128)(2,1)S(1)} %get-tuple-element.85), channel_id=1, source_target_pairs={{0,4},{1,2},{2,1},{3,7},{4,0},{5,6},{6,5},{7,3},{8,12},{9,10},{10,... | collective-permute-start | bytes 368648 | tf_op jit(solution)/shard_map/ppermute | solution.py:405
  30.2 6.1 %collective-permute-start.9 = (bf16[12,20,256]{2,1,0:T(8,128)(2,1)S(1)}, bf16[12,20,256]{2,1,0:T(8,128)(2,1)S(1)}, u32[]{:S(2)}, u32[]{:S(2)}) collective-permute-start(bf16[12,20,256]{2,1,0:T(8,128)(2,1)S(1)} %get-tuple-element.84), channel_id=1, source_target_pairs={{0,1},{1,0},{2,3},{3,2},{4,5},{5,4},{6,7},{7,6},{8,9},{9,8},{10,11... | collective-permute-start | bytes 368648 | tf_op jit(solution)/shard_map/ppermute | solution.py:405
  32.8 1.3 %copy-start.3 = (bf16[27,96,96]{2,1,0:T(8,128)(2,1)S(1)}, bf16[27,96,96]{2,1,0:T(8,128)(2,1)}, u32[]{:S(2)}) copy-start(bf16[27,96,96]{2,1,0:T(8,128)(2,1)} %w_ref.5) | copy-start | bytes 1492996

commit v19 on v17

--- a/solution.py
+++ b/solution.py
@@ -477,7 +477,10 @@
     win = jnp.concatenate([y_below, own, y_above], axis=0)
     z_below, z_above = shift_along(win[:, :, :128], win[:, :, lanes1 - 128 :], "gz")
     low, high = win[:, :HALO_X], win[:, X1 - HALO_X :]
-    x_got = lax.optimization_barrier(swaps(column_pairs(low), column_pairs(high), "gx"))
+    even = parity("gx")
+    faces = lax.optimization_barrier((jnp.where(even, high, low), jnp.where(even, low, high)))
+    x_got = tuple(swap(column_pairs(face), {"gx": n}) for n, face in enumerate(faces))
+    x_got = lax.optimization_barrier(x_got[::-1])[::-1]
     rows = Y1 + 2
     left, right, g2, t1b = pl.pallas_call(
         middle_kernel,

time: 40.4 us -> 40.3 us (level)
  no operation moved by 1% of the time
where the time goes in v19:
time: 40.3 us; the launch traced here: 40.2 us
  Pallas kernels  21.8 us (54%)
  starting transfers between devices  11.4 us (28%)
  waiting for transfers between devices  4.19 us (10%)
  other arithmetic  1.23 us (3%)
  between operations  1.16 us (3%)
    ppermute x10, starting transfers between devices, swap(): return lax.ppermute(value, axes, pairs)  11.4 us
    pallas_call x1, Pallas kernels, local(): pl.pallas_call(level_one_kernel, out_shape=[shaped(Y1 * X1, lanes1), shap...  5.31 us
    ppermute x10, waiting for transfers between devices, swap(): return lax.ppermute(value, axes, pairs)  4.19 us
    pallas_call x1, Pallas kernels, local(): pl.pallas_call(level_two_kernel, out_shape=shaped(C2 * Z2, Y2 * X2), scra...  4.03 us
    pallas_call x1, Pallas kernels, local(): pl.pallas_call(down1_kernel, in_specs=[pl.BlockSpec(memory_space=pltpu.HB...  4.02 us
    pallas_call x1, Pallas kernels, local(): pl.pallas_call(outer_kernel, out_shape=[shaped(rows, X1, 256), shaped(row...  2.04 us
    pallas_call x1, Pallas kernels, local(): pl.pallas_call(middle_kernel, out_shape=[shaped(ROWS1, X1, lanes1), shape...  1.58 us
    pallas_call x1, Pallas kernels, local(): pl.pallas_call(one_kernel, out_shape=shaped(lanes1, Y1 * X1), compiler_pa...  1.27 us
  transfers between devices with their start and end apart: 10, of which 4 were waited for; matrix products, arithmetic and copies ran while one was open for 2% of the time, Pallas kernels for 21%

profile of v19, /device:TPU:2, one launch (start us, length us, event | category | flops | bytes accessed | tf_op | source)
XLA Modules:
  0.0 40.2 jit_solution(7657705051895335357)
XLA Ops:
  0.7 4.0 %shard_map.149 = (bf16[16,32,512]{2,1,0:T(8,128)(2,1)S(1)}, bf16[128,384]{1,0:T(8,128)(2,1)S(1)}, bf16[128,384]{1,0:T(8,128)(2,1)S(1)}) custom-call(bf16[48,2,8,2048]{3,2,1,0:T(8,128)(2,1)} %bitcast.28, bf16[8,48,64]{2,1,0:T(8,128)(2,1)} %bitcast.29, f32[1,64]{1,0:T(1,128)} %bitcast.31, s32[8,4,32]{2,1,0:T(4,128)} %bitcast.30), custom_call_target="tpu_custom_call" | custom-call | flops 4000000000 | tf_op jit(solution)/shard_map/pallas_call | solution.py:459
  4.7 0.1 collective-permute-start
  5.0 0.6 %shard_map.150.t_ref.ta_ref = bf16[1,256,3456]{2,1,0:T(8,128)(2,1)S(1)} custom-call(bf16[27,64,64]{2,1,0:T(8,128)(2,1)S(1)} %copy-done.4), custom_call_target="tpu_custom_call" | custom-call | flops 1000000000 | tf_op jit(solution)/shard_map/pallas_call | solution.py:171
  5.6 0.4 %collective-permute-done = bf16[2,32,512]{2,1,0:T(8,128)(2,1)S(1)} collective-permute-done((bf16[2,32,512]{2,1,0:T(8,128)(2,1)S(1)}, bf16[2,32,512]{2,1,0:T(8,128)(2,1)S(1)}, u32[]{:S(2)}, u32[]{:S(2)}) %collective-permute-start) | collective-permute-done | bytes 65568 | tf_op jit(solution)/shard_map/ppermute | solution.py:404
  6.1 0.1 pad_maximum_fusion.win_ref
  6.2 0.2 fusion
  6.4 0.1 pad_maximum_fusion.3
  6.6 0.1 pad_maximum_fusion.2
  6.7 3.0 %collective-permute-start.3 = (bf16[20,2,1536]{2,1,0:T(2,128)(2,1)S(1)}, bf16[20,2,1536]{2,1,0:T(2,128)(2,1)S(1)}, u32[]{:S(2)}, u32[]{:S(2)}) collective-permute-start(bf16[20,2,1536]{2,1,0:T(2,128)(2,1)S(1)} %pad_maximum_fusion.2), channel_id=1, source_target_pairs={{0,4},{1,5},{2,6},{3,7},{4,0},{5,1},{6,2},{7,3},{8,16},{9,17},{10,... | collective-permute-start | bytes 368648 | tf_op jit(solution)/shard_map/ppermute | solution.py:404
  9.8 0.1 collective-permute-start.1
  9.9 3.1 %collective-permute-start.2 = (bf16[20,32,128]{2,1,0:T(8,128)(2,1)S(1)}, bf16[20,32,128]{2,1,0:T(8,128)(2,1)S(1)}, u32[]{:S(2)}, u32[]{:S(2)}) collective-permute-start(bf16[20,32,128]{2,1,0:T(8,128)(2,1)S(1)} %get-tuple-element.78), channel_id=1, source_target_pairs={{0,1},{1,0},{2,3},{3,2},{4,5},{5,4},{6,7},{7,6},{8,9},{9,8},{10,11... | collective-permute-start | bytes 491528 | tf_op jit(solution)/shard_map/ppermute | solution.py:404
  13.0 1.6 %shard_map.151 = (bf16[20,32,512]{2,1,0:T(8,128)(2,1)S(1)}, bf16[20,32,512]{2,1,0:T(8,128)(2,1)S(1)}, bf16[18,32,256]{2,1,0:T(8,128)(2,1)S(1)}, bf16[1,256,3456]{2,1,0:T(8,128)(2,1)S(1)}) custom-call(bf16[20,32,512]{2,1,0:T(8,128)(2,1)S(1)} %pad_maximum_fusion.win_ref, bf16[1,256,3456]{2,1,0:T(8,128)(2,1)S(1)} %shard_map.150.t_ref.ta_ref, ...), custom_call_target="tpu_custom_call" | custom-call | flops 100000000 | tf_op jit(solution)/shard_map/pallas_call | solution.py:485
  14.6 1.0 %collective-permute-done.3 = bf16[20,2,1536]{2,1,0:T(2,128)(2,1)S(1)} collective-permute-done((bf16[20,2,1536]{2,1,0:T(2,128)(2,1)S(1)}, bf16[20,2,1536]{2,1,0:T(2,128)(2,1)S(1)}, u32[]{:S(2)}, u32[]{:S(2)}) %collective-permute-start.3) | collective-permute-done | bytes 122912 | tf_op jit(solution)/shard_map/ppermute | solution.py:404
  15.7 0.1 broadcast_select_fusion.24
  15.8 0.1 broadcast_select_fusion.25
  16.0 0.1 collective-permute-start.5
  16.1 3.1 %collective-permute-start.6 = (bf16[20,2,768]{2,1,0:T(2,128)(2,1)S(1)}, bf16[20,2,768]{2,1,0:T(2,128)(2,1)S(1)}, u32[]{:S(2)}, u32[]{:S(2)}) collective-permute-start(bf16[20,2,768]{2,1,0:T(2,128)(2,1)S(1)} %bitcast.26), channel_id=1, source_target_pairs={{0,1},{1,0},{2,3},{3,2},{4,5},{5,4},{6,7},{7,6},{8,9},{9,8},{10,11... | collective-permute-start | bytes 184328 | tf_op jit(solution)/shard_map/ppermute | solution.py:404
  19.2 0.2 broadcast_select_fusion
  19.5 1.2 %shard_map.152 = (bf16[20,16,512]{2,1,0:T(8,128)(2,1)S(1)}, bf16[20,16,512]{2,1,0:T(8,128)(2,1)S(1)}, bf16[20,16,512]{2,1,0:T(8,128)(2,1)S(1)}, bf16[18,48,256]{...) custom-call(bf16[20,2,1536]{2,1,0:T(2,128)(2,1)S(1)} %get-tuple-element.87.xl_ref, ...), custom_call_target="tpu_custom_call" | custom-call | flops 3000000000 | tf_op jit(solution)/shard_map/pallas_call | solution.py:509
  20.8 2.0 %shard_map.153 = (bf16[18,32,256]{2,1,0:T(8,128)(2,1)S(1)}, bf16[18,32,128]{2,1,0:T(8,128)(2,1)S(1)}) custom-call(bf16[20,32,512]{2,1,0:T(8,128)(2,1)S(1)} %pad_maximum_fusion.win_ref, bf16[20,32,512]{2,1,0:T(8,128)(2,1)S(1)} %get-tuple-element.57.left_ref, bf16[20,32,512]{2,1,0:T(8,128)(2,1)S(1)} %get-tuple-element.58.right_ref, ...), custom_call_target="tpu_custom_call" | custom-call | flops 4000000000 | tf_op jit(solution)/shard_map/pallas_call | solution.py:500
  22.9 0.1 broadcast_select_fusion.10
  23.0 5.3 %shard_map.154 = (bf16[512,512]{1,0:T(8,128)(2,1)S(1)}, bf16[8,20,512]{2,1,0:T(8,128)(2,1)S(1)}) custom-call(bf16[20,32,128]{2,1,0:T(8,128)(2,1)S(1)} %get-tuple-element.81.zl_ref, bf16[20,32,128]{2,1,0:T(8,128)(2,1)S(1)} %get-tuple-element.80.zr_ref, bf16[20,2,768]{2,1,0:T(2,128)(2,1)S(1)} %get-tuple-element.95.cl_ref, ...), custom_call_target="tpu_custom_call" | custom-call | flops 6000000000 | tf_op jit(solution)/shard_map/pallas_call | solution.py:515
  28.4 0.1 collective-permute-start.7
  28.5 0.3 shard_map.156.t_ref.ta_ref
  28.8 0.9 %collective-permute-done.7 = bf16[2,20,512]{2,1,0:T(8,128)(2,1)S(1)} collective-permute-done((bf16[2,20,512]{2,1,0:T(8,128)(2,1)S(1)}, bf16[2,20,512]{2,1,0:T(8,128)(2,1)S(1)}, u32[]{:S(2)}, u32[]{:S(2)}) %collective-permute-start.7) | collective-permute-done | bytes 40992 | tf_op jit(solution)/shard_map/ppermute | solution.py:404
  29.8 0.2 collective-permute-start.8
  30.0 1.5 %collective-permute-start.9 = (bf16[12,20,256]{2,1,0:T(8,128)(2,1)S(1)}, bf16[12,20,256]{2,1,0:T(8,128)(2,1)S(1)}, u32[]{:S(2)}, u32[]{:S(2)}) collective-permute-start(bf16[12,20,256]{2,1,0:T(8,128)(2,1)S(1)} %get-tuple-element.84), channel_id=1, source_target_pairs={{0,1},{1,0},{2,3},{3,2},{4,5},{5,4},{6,7},{7,6},{8,9},{9,8},{10,11... | collective-permute-start | bytes 368648 | tf_op jit(solution)/shard_map/ppermute | solution.py:404
  31.5 1.1 %shard_map.157 = (bf16[12,32,512]{2,1,0:T(8,128)(2,1)S(1)}, bf16[12,32,512]{2,1,0:T(8,128)(2,1)S(1)}, bf16[12,32,512]{2,1,0:T(8,128)(2,1)S(1)}, bf16[10,16,256]{...) custom-call(bf16[12,20,512]{2,1,0:T(8,128)(2,1)S(1)} %pad_maximum_fusion.1.wide_ref, ...), custom_call_target="tpu_custom_call" | custom-call | flops 3000000000 | tf_op jit(solution)/shard_map/pallas_call | solution.py:541
  32.6 1.3 %shard_map.155 = bf16[512,512]{1,0:T(8,128)(2,1)} custom-call(bf16[512,512]{1,0:T(8,128)(2,1)S(1)} %get-tuple-element.66.feat_ref), custom_call_target="tpu_custom_call" | custom-call | flops 2000000000 | tf_op jit(solution)/shard_map/pallas_call | solution.py:535
  33.9 0.3 shard_map.158.tb_ref
  34.2 1.9 %collective-permute-done.9 = bf16[12,20,256]{2,1,0:T(8,128)(2,1)S(1)} collective-permute-done((bf16[12,20,256]{2,1,0:T(8,128)(2,1)S(1)}, bf16[12,20,256]{2,1,0:T(8,128)(2,1)S(1)}, u32[]{:S(2)}, u32[]{:S(2)}) %collective-permute-start.9) | collective-permute-done | bytes 122912 | tf_op jit(solution)/shard_map/ppermute | solution.py:404
  36.1 4.0 %shard_map.159 = bf16[384,128]{1,0:T(8,128)(2,1)} custom-call(bf16[12,32,512]{2,1,0:T(8,128)(2,1)S(1)} %get-tuple-element.69.a0, bf16[12,32,512]{2,1,0:T(8,128)(2,1)S(1)} %get-tuple-element.70.a1, bf16[12,32,512]{2,1,0:T(8,128)(2,1)S(1)} %get-tuple-element.71.a2, bf16[10,16,256]{2,1,0:T(8,128)(2,1)S(1)} %get-tuple-element.72.m0, ...), custom_call_target="tpu_custom_call" | custom-call | flops 5000000000 | tf_op jit(solution)/shard_map/pallas_call | solution.py:547
  (46 shorter events, 0.7 us)
Async XLA Ops:
  0.6 4.2 %copy-start.7 = (f32[96]{0:T(128)S(1)}, f32[96]{0:T(128)}, u32[]{:S(2)}) copy-start(f32[96]{0:T(128)} %param.23) | copy-start | bytes 1156
  0.7 4.2 %copy-start.8 = (f32[96]{0:T(128)S(1)}, f32[96]{0:T(128)}, u32[]{:S(2)}) copy-start(f32[96]{0:T(128)} %param.25) | copy-start | bytes 1156
  0.7 4.2 %copy-start.9 = (f32[96]{0:T(128)S(1)}, f32[96]{0:T(128)}, u32[]{:S(2)}) copy-start(f32[96]{0:T(128)} %param.27) | copy-start | bytes 1156
  0.7 4.3 %copy-start.6 = (bf16[8,96,64]{1,2,0:T(8,128)(2,1)S(1)}, bf16[8,96,64]{1,2,0:T(8,128)(2,1)}, u32[]{:S(2)}) copy-start(bf16[8,96,64]{1,2,0:T(8,128)(2,1)} %param.22) | copy-start | bytes 294916
  0.7 4.3 %copy-start.4 = (bf16[27,64,64]{2,1,0:T(8,128)(2,1)S(1)}, bf16[27,64,64]{2,1,0:T(8,128)(2,1)}, u32[]{:S(2)}) copy-start(bf16[27,64,64]{2,1,0:T(8,128)(2,1)} %w_ref.2) | copy-start | bytes 663556
  4.7 1.3 %collective-permute-start = (bf16[2,32,512]{2,1,0:T(8,128)(2,1)S(1)}, bf16[2,32,512]{2,1,0:T(8,128)(2,1)S(1)}, u32[]{:S(2)}, u32[]{:S(2)}) collective-permute-start(bf16[2,32,512]{2,1,0:T(8,128)(2,1)S(1)} %slice_select_fusion), channel_id=1, source_target_pairs={{0,4},{1,5},{2,6},{3,7},{4,0},{5,1},{6,2},{7,3},{8,12},{9,13},{10,... | collective-permute-start | bytes 196616 | tf_op jit(solution)/shard_map/ppermute | solution.py:404
  5.6 7.4 %copy-start = (bf16[27,64,64]{2,1,0:T(8,128)(2,1)S(1)}, bf16[27,64,64]{2,1,0:T(8,128)(2,1)}, u32[]{:S(2)}) copy-start(bf16[27,64,64]{2,1,0:T(8,128)(2,1)} %w_ref.3) | copy-start | bytes 663556
  5.6 7.4 %copy-start.1 = (f32[64]{0:T(128)S(1)}, f32[64]{0:T(128)}, u32[]{:S(2)}) copy-start(f32[64]{0:T(128)} %param.19) | copy-start | bytes 772
  6.5 8.1 %collective-permute-start.4 = (bf16[20,2,1536]{2,1,0:T(2,128)(2,1)S(1)}, bf16[20,2,1536]{2,1,0:T(2,128)(2,1)S(1)}, u32[]{:S(2)}, u32[]{:S(2)}) collective-permute-start(bf16[20,2,1536]{2,1,0:T(2,128)(2,1)S(1)} %pad_maximum_fusion.3), channel_id=1, source_target_pairs={{0,8},{1,9},{2,10},{3,11},{4,12},{5,13},{6,14},{7,15},{8,0},{9,1},... | collective-permute-start | bytes 368648 | tf_op jit(solution)/shard_map/ppermute | solution.py:404
  6.7 8.9 %collective-permute-start.3 = (bf16[20,2,1536]{2,1,0:T(2,128)(2,1)S(1)}, bf16[20,2,1536]{2,1,0:T(2,128)(2,1)S(1)}, u32[]{:S(2)}, u32[]{:S(2)}) collective-permute-start(bf16[20,2,1536]{2,1,0:T(2,128)(2,1)S(1)} %pad_maximum_fusion.2), channel_id=1, source_target_pairs={{0,4},{1,5},{2,6},{3,7},{4,0},{5,1},{6,2},{7,3},{8,16},{9,17},{10,... | collective-permute-start | bytes 368648 | tf_op jit(solution)/shard_map/ppermute | solution.py:404
  9.8 11.0 %collective-permute-start.1 = (bf16[20,32,128]{2,1,0:T(8,128)(2,1)S(1)}, bf16[20,32,128]{2,1,0:T(8,128)(2,1)S(1)}, u32[]{:S(2)}, u32[]{:S(2)}) collective-permute-start(bf16[20,32,128]{2,1,0:T(8,128)(2,1)S(1)} %get-tuple-element.79), channel_id=1, source_target_pairs={{0,4},{1,2},{2,1},{3,7},{4,0},{5,6},{6,5},{7,3},{8,12},{9,10},{10,... | collective-permute-start | bytes 491528 | tf_op jit(solution)/shard_map/ppermute | solution.py:404
  9.9 10.9 %collective-permute-start.2 = (bf16[20,32,128]{2,1,0:T(8,128)(2,1)S(1)}, bf16[20,32,128]{2,1,0:T(8,128)(2,1)S(1)}, u32[]{:S(2)}, u32[]{:S(2)}) collective-permute-start(bf16[20,32,128]{2,1,0:T(8,128)(2,1)S(1)} %get-tuple-element.78), channel_id=1, source_target_pairs={{0,1},{1,0},{2,3},{3,2},{4,5},{5,4},{6,7},{7,6},{8,9},{9,8},{10,11... | collective-permute-start | bytes 491528 | tf_op jit(solution)/shard_map/ppermute | solution.py:404
  16.0 6.8 %collective-permute-start.5 = (bf16[20,2,768]{2,1,0:T(2,128)(2,1)S(1)}, bf16[20,2,768]{2,1,0:T(2,128)(2,1)S(1)}, u32[]{:S(2)}, u32[]{:S(2)}) collective-permute-start(bf16[20,2,768]{2,1,0:T(2,128)(2,1)S(1)} %bitcast.27), channel_id=1, source_target_pairs={{0,4},{1,2},{2,1},{3,7},{4,0},{5,6},{6,5},{7,3},{8,12},{9,10},{10,... | collective-permute-start | bytes 184328 | tf_op jit(solution)/shard_map/ppermute | solution.py:404
  16.1 6.8 %collective-permute-start.6 = (bf16[20,2,768]{2,1,0:T(2,128)(2,1)S(1)}, bf16[20,2,768]{2,1,0:T(2,128)(2,1)S(1)}, u32[]{:S(2)}, u32[]{:S(2)}) collective-permute-start(bf16[20,2,768]{2,1,0:T(2,128)(2,1)S(1)} %bitcast.26), channel_id=1, source_target_pairs={{0,1},{1,0},{2,3},{3,2},{4,5},{5,4},{6,7},{7,6},{8,9},{9,8},{10,11... | collective-permute-start | bytes 184328 | tf_op jit(solution)/shard_map/ppermute | solution.py:404
  20.8 2.2 %copy-start.5 = (f32[64]{0:T(128)S(1)}, f32[64]{0:T(128)}, u32[]{:S(2)}) copy-start(f32[64]{0:T(128)} %param.21) | copy-start | bytes 772
  23.0 5.4 %copy-start.2 = (bf16[27,96,96]{2,1,0:T(8,128)(2,1)S(1)}, bf16[27,96,96]{2,1,0:T(8,128)(2,1)}, u32[]{:S(2)}) copy-start(bf16[27,96,96]{2,1,0:T(8,128)(2,1)} %w_ref.4) | copy-start | bytes 1492996
  28.4 1.3 %collective-permute-start.7 = (bf16[2,20,512]{2,1,0:T(8,128)(2,1)S(1)}, bf16[2,20,512]{2,1,0:T(8,128)(2,1)S(1)}, u32[]{:S(2)}, u32[]{:S(2)}) collective-permute-start(bf16[2,20,512]{2,1,0:T(8,128)(2,1)S(1)} %slice_select_fusion.1), channel_id=1, source_target_pairs={{0,4},{1,5},{2,6},{3,7},{4,0},{5,1},{6,2},{7,3},{8,12},{9,13},{10,... | collective-permute-start | bytes 122888 | tf_op jit(solution)/shard_map/ppermute | solution.py:404
  29.8 4.4 %collective-permute-start.8 = (bf16[12,20,256]{2,1,0:T(8,128)(2,1)S(1)}, bf16[12,20,256]{2,1,0:T(8,128)(2,1)S(1)}, u32[]{:S(2)}, u32[]{:S(2)}) collective-permute-start(bf16[12,20,256]{2,1,0:T(8,128)(2,1)S(1)} %get-tuple-element.85), channel_id=1, source_target_pairs={{0,4},{1,2},{2,1},{3,7},{4,0},{5,6},{6,5},{7,3},{8,12},{9,10},{10,... | collective-permute-start | bytes 368648 | tf_op jit(solution)/shard_map/ppermute | solution.py:404
  30.0 6.1 %collective-permute-start.9 = (bf16[12,20,256]{2,1,0:T(8,128)(2,1)S(1)}, bf16[12,20,256]{2,1,0:T(8,128)(2,1)S(1)}, u32[]{:S(2)}, u32[]{:S(2)}) collective-permute-start(bf16[12,20,256]{2,1,0:T(8,128)(2,1)S(1)} %get-tuple-element.84), channel_id=1, source_target_pairs={{0,1},{1,0},{2,3},{3,2},{4,5},{5,4},{6,7},{7,6},{8,9},{9,8},{10,11... | collective-permute-start | bytes 368648 | tf_op jit(solution)/shard_map/ppermute | solution.py:404
  32.6 1.3 %copy-start.3 = (bf16[27,96,96]{2,1,0:T(8,128)(2,1)S(1)}, bf16[27,96,96]{2,1,0:T(8,128)(2,1)}, u32[]{:S(2)}) copy-start(bf16[27,96,96]{2,1,0:T(8,128)(2,1)} %w_ref.5) | copy-start | bytes 1492996

commit v20 on v19

--- a/solution.py
+++ b/solution.py
@@ -478,9 +478,18 @@
     z_below, z_above = shift_along(win[:, :, :128], win[:, :, lanes1 - 128 :], "gz")
     low, high = win[:, :HALO_X], win[:, X1 - HALO_X :]
     even = parity("gx")
+    trim = lax.axis_size("gy") == 2
+    first_row = lax.axis_index("gy") == 0
+    if trim:
+        low, high = (jnp.where(first_row, e[HALO:], e[:-HALO]) for e in (low, high))
     faces = lax.optimization_barrier((jnp.where(even, high, low), jnp.where(even, low, high)))
     x_got = tuple(swap(column_pairs(face), {"gx": n}) for n, face in enumerate(faces))
     x_got = lax.optimization_barrier(x_got[::-1])[::-1]
+    if trim:
+        rim = jnp.zeros_like(x_got[0][:HALO])
+        x_got = [
+            jnp.where(first_row, jnp.concatenate([rim, got], axis=0), jnp.concatenate([got, rim], axis=0)) for got in x_got
+        ]
     rows = Y1 + 2
     left, right, g2, t1b = pl.pallas_call(
         middle_kernel,

time: 40.3 us -> 40.1 us (level)
  waiting for transfers between devices: 4.19 us -> 3.58 us
    ppermute x10, waiting for transfers between devices: 4.19 us -> 3.58 us  [swap(): return lax.ppermute(value, axes, pairs)]
  transfers between devices with their start and end apart: 10 -> 10, of which waited for: 4 -> 4; matrix products, arithmetic and copies ran while one was open for 2% -> 3% of each run, Pallas kernels for 21% -> 21%
where the time goes in v20:
time: 40.1 us; the launch traced here: 39.9 us
  Pallas kernels  21.8 us (54%)
  starting transfers between devices  11.4 us (28%)
  waiting for transfers between devices  3.58 us (9%)
  other arithmetic  1.58 us (4%)
  between operations  1.18 us (3%)
    ppermute x10, starting transfers between devices, swap(): return lax.ppermute(value, axes, pairs)  11.4 us
    pallas_call x1, Pallas kernels, local(): pl.pallas_call(level_one_kernel, out_shape=[shaped(Y1 * X1, lanes1), shap...  5.3 us
    pallas_call x1, Pallas kernels, local(): pl.pallas_call(level_two_kernel, out_shape=shaped(C2 * Z2, Y2 * X2), scra...  4.03 us
    pallas_call x1, Pallas kernels, local(): pl.pallas_call(down1_kernel, in_specs=[pl.BlockSpec(memory_space=pltpu.HB...  4.02 us
    ppermute x10, waiting for transfers between devices, swap(): return lax.ppermute(value, axes, pairs)  3.58 us
    pallas_call x1, Pallas kernels, local(): pl.pallas_call(outer_kernel, out_shape=[shaped(rows, X1, 256), shaped(row...  2.04 us
    pallas_call x1, Pallas kernels, local(): pl.pallas_call(middle_kernel, out_shape=[shaped(ROWS1, X1, lanes1), shape...  1.58 us
    pallas_call x1, Pallas kernels, local(): pl.pallas_call(one_kernel, out_shape=shaped(lanes1, Y1 * X1), compiler_pa...  1.27 us
  transfers between devices with their start and end apart: 10, of which 4 were waited for; matrix products, arithmetic and copies ran while one was open for 3% of the time, Pallas kernels for 21%

profile of v20, /device:TPU:2, one launch (start us, length us, event | category | flops | bytes accessed | tf_op | source)
XLA Modules:
  0.0 39.9 jit_solution(3646406267604713581)
XLA Ops:
  0.7 4.0 %shard_map.149 = (bf16[16,32,512]{2,1,0:T(8,128)(2,1)S(1)}, bf16[128,384]{1,0:T(8,128)(2,1)S(1)}, bf16[128,384]{1,0:T(8,128)(2,1)S(1)}) custom-call(bf16[48,2,8,2048]{3,2,1,0:T(8,128)(2,1)} %bitcast.28, bf16[8,48,64]{2,1,0:T(8,128)(2,1)} %bitcast.29, f32[1,64]{1,0:T(1,128)} %bitcast.31, s32[8,4,32]{2,1,0:T(4,128)} %bitcast.30), custom_call_target="tpu_custom_call" | custom-call | flops 4000000000 | tf_op jit(solution)/shard_map/pallas_call | solution.py:459
  4.7 0.1 collective-permute-start
  5.0 0.6 %shard_map.150.t_ref.ta_ref = bf16[1,256,3456]{2,1,0:T(8,128)(2,1)S(1)} custom-call(bf16[27,64,64]{2,1,0:T(8,128)(2,1)S(1)} %copy-done.4), custom_call_target="tpu_custom_call" | custom-call | flops 1000000000 | tf_op jit(solution)/shard_map/pallas_call | solution.py:171
  5.6 0.4 %collective-permute-done = bf16[2,32,512]{2,1,0:T(8,128)(2,1)S(1)} collective-permute-done((bf16[2,32,512]{2,1,0:T(8,128)(2,1)S(1)}, bf16[2,32,512]{2,1,0:T(8,128)(2,1)S(1)}, u32[]{:S(2)}, u32[]{:S(2)}) %collective-permute-start) | collective-permute-done | bytes 65568 | tf_op jit(solution)/shard_map/ppermute | solution.py:404
  6.1 0.1 pad_maximum_fusion.win_ref
  6.2 0.1 broadcast_select_fusion.10
  6.3 0.1 fusion.2
  6.4 0.1 pad_maximum_fusion.5
  6.6 0.1 fusion.3
  6.7 0.1 pad_maximum_fusion.4
  6.8 3.0 %collective-permute-start.3 = (bf16[18,2,1536]{2,1,0:T(2,128)(2,1)S(1)}, bf16[18,2,1536]{2,1,0:T(2,128)(2,1)S(1)}, u32[]{:S(2)}, u32[]{:S(2)}) collective-permute-start(bf16[18,2,1536]{2,1,0:T(2,128)(2,1)S(1)} %pad_maximum_fusion.4), channel_id=1, source_target_pairs={{0,4},{1,5},{2,6},{3,7},{4,0},{5,1},{6,2},{7,3},{8,16},{9,17},{10,... | collective-permute-start | bytes 331784 | tf_op jit(solution)/shard_map/ppermute | solution.py:404
  9.9 3.1 %collective-permute-start.2 = (bf16[20,32,128]{2,1,0:T(8,128)(2,1)S(1)}, bf16[20,32,128]{2,1,0:T(8,128)(2,1)S(1)}, u32[]{:S(2)}, u32[]{:S(2)}) collective-permute-start(bf16[20,32,128]{2,1,0:T(8,128)(2,1)S(1)} %get-tuple-element.79), channel_id=1, source_target_pairs={{0,1},{1,0},{2,3},{3,2},{4,5},{5,4},{6,7},{7,6},{8,9},{9,8},{10,11... | collective-permute-start | bytes 491528 | tf_op jit(solution)/shard_map/ppermute | solution.py:404
  13.1 1.6 %shard_map.151 = (bf16[20,32,512]{2,1,0:T(8,128)(2,1)S(1)}, bf16[20,32,512]{2,1,0:T(8,128)(2,1)S(1)}, bf16[18,32,256]{2,1,0:T(8,128)(2,1)S(1)}, bf16[1,256,3456]{2,1,0:T(8,128)(2,1)S(1)}) custom-call(bf16[20,32,512]{2,1,0:T(8,128)(2,1)S(1)} %pad_maximum_fusion.win_ref, bf16[1,256,3456]{2,1,0:T(8,128)(2,1)S(1)} %shard_map.150.t_ref.ta_ref, ...), custom_call_target="tpu_custom_call" | custom-call | flops 100000000 | tf_op jit(solution)/shard_map/pallas_call | solution.py:494
  14.7 0.4 collective-permute-done.3
  15.0 0.3 broadcast_select_fusion.4
  15.4 0.1 broadcast_select_fusion.26
  15.6 0.1 broadcast_select_fusion.27
  15.9 3.1 %collective-permute-start.6 = (bf16[20,2,768]{2,1,0:T(2,128)(2,1)S(1)}, bf16[20,2,768]{2,1,0:T(2,128)(2,1)S(1)}, u32[]{:S(2)}, u32[]{:S(2)}) collective-permute-start(bf16[20,2,768]{2,1,0:T(2,128)(2,1)S(1)} %bitcast.26), channel_id=1, source_target_pairs={{0,1},{1,0},{2,3},{3,2},{4,5},{5,4},{6,7},{7,6},{8,9},{9,8},{10,11... | collective-permute-start | bytes 184328 | tf_op jit(solution)/shard_map/ppermute | solution.py:404
  19.0 0.2 broadcast_select_fusion
  19.2 1.2 %shard_map.152 = (bf16[20,16,512]{2,1,0:T(8,128)(2,1)S(1)}, bf16[20,16,512]{2,1,0:T(8,128)(2,1)S(1)}, bf16[20,16,512]{2,1,0:T(8,128)(2,1)S(1)}, bf16[18,48,256]{...) custom-call(bf16[20,2,1536]{2,1,0:T(2,128)(2,1)S(1)} %get-tuple-element.88.xl_ref, ...), custom_call_target="tpu_custom_call" | custom-call | flops 3000000000 | tf_op jit(solution)/shard_map/pallas_call | solution.py:518
  20.6 2.0 %shard_map.153 = (bf16[18,32,256]{2,1,0:T(8,128)(2,1)S(1)}, bf16[18,32,128]{2,1,0:T(8,128)(2,1)S(1)}) custom-call(bf16[20,32,512]{2,1,0:T(8,128)(2,1)S(1)} %pad_maximum_fusion.win_ref, bf16[20,32,512]{2,1,0:T(8,128)(2,1)S(1)} %get-tuple-element.57.left_ref, bf16[20,32,512]{2,1,0:T(8,128)(2,1)S(1)} %get-tuple-element.58.right_ref, ...), custom_call_target="tpu_custom_call" | custom-call | flops 4000000000 | tf_op jit(solution)/shard_map/pallas_call | solution.py:509
  22.6 0.1 broadcast_select_fusion.12
  22.8 5.3 %shard_map.154 = (bf16[512,512]{1,0:T(8,128)(2,1)S(1)}, bf16[8,20,512]{2,1,0:T(8,128)(2,1)S(1)}) custom-call(bf16[20,32,128]{2,1,0:T(8,128)(2,1)S(1)} %get-tuple-element.82.zl_ref, bf16[20,32,128]{2,1,0:T(8,128)(2,1)S(1)} %get-tuple-element.81.zr_ref, bf16[20,2,768]{2,1,0:T(2,128)(2,1)S(1)} %get-tuple-element.96.cl_ref, ...), custom_call_target="tpu_custom_call" | custom-call | flops 6000000000 | tf_op jit(solution)/shard_map/pallas_call | solution.py:524
  28.2 0.3 shard_map.156.t_ref.ta_ref
  28.5 0.9 %collective-permute-done.7 = bf16[2,20,512]{2,1,0:T(8,128)(2,1)S(1)} collective-permute-done((bf16[2,20,512]{2,1,0:T(8,128)(2,1)S(1)}, bf16[2,20,512]{2,1,0:T(8,128)(2,1)S(1)}, u32[]{:S(2)}, u32[]{:S(2)}) %collective-permute-start.7) | collective-permute-done | bytes 40992 | tf_op jit(solution)/shard_map/ppermute | solution.py:404
  29.5 0.2 collective-permute-start.8
  29.7 1.5 %collective-permute-start.9 = (bf16[12,20,256]{2,1,0:T(8,128)(2,1)S(1)}, bf16[12,20,256]{2,1,0:T(8,128)(2,1)S(1)}, u32[]{:S(2)}, u32[]{:S(2)}) collective-permute-start(bf16[12,20,256]{2,1,0:T(8,128)(2,1)S(1)} %get-tuple-element.85), channel_id=1, source_target_pairs={{0,1},{1,0},{2,3},{3,2},{4,5},{5,4},{6,7},{7,6},{8,9},{9,8},{10,11... | collective-permute-start | bytes 368648 | tf_op jit(solution)/shard_map/ppermute | solution.py:404
  31.2 1.1 %shard_map.157 = (bf16[12,32,512]{2,1,0:T(8,128)(2,1)S(1)}, bf16[12,32,512]{2,1,0:T(8,128)(2,1)S(1)}, bf16[12,32,512]{2,1,0:T(8,128)(2,1)S(1)}, bf16[10,16,256]{...) custom-call(bf16[12,20,512]{2,1,0:T(8,128)(2,1)S(1)} %pad_maximum_fusion.1.wide_ref, ...), custom_call_target="tpu_custom_call" | custom-call | flops 3000000000 | tf_op jit(solution)/shard_map/pallas_call | solution.py:550
  32.3 1.3 %shard_map.155 = bf16[512,512]{1,0:T(8,128)(2,1)} custom-call(bf16[512,512]{1,0:T(8,128)(2,1)S(1)} %get-tuple-element.66.feat_ref), custom_call_target="tpu_custom_call" | custom-call | flops 2000000000 | tf_op jit(solution)/shard_map/pallas_call | solution.py:544
  33.6 0.3 shard_map.158.tb_ref
  33.9 1.9 %collective-permute-done.9 = bf16[12,20,256]{2,1,0:T(8,128)(2,1)S(1)} collective-permute-done((bf16[12,20,256]{2,1,0:T(8,128)(2,1)S(1)}, bf16[12,20,256]{2,1,0:T(8,128)(2,1)S(1)}, u32[]{:S(2)}, u32[]{:S(2)}) %collective-permute-start.9) | collective-permute-done | bytes 122912 | tf_op jit(solution)/shard_map/ppermute | solution.py:404
  35.9 4.0 %shard_map.159 = bf16[384,128]{1,0:T(8,128)(2,1)} custom-call(bf16[12,32,512]{2,1,0:T(8,128)(2,1)S(1)} %get-tuple-element.69.a0, bf16[12,32,512]{2,1,0:T(8,128)(2,1)S(1)} %get-tuple-element.70.a1, bf16[12,32,512]{2,1,0:T(8,128)(2,1)S(1)} %get-tuple-element.71.a2, bf16[10,16,256]{2,1,0:T(8,128)(2,1)S(1)} %get-tuple-element.72.m0, ...), custom_call_target="tpu_custom_call" | custom-call | flops 5000000000 | tf_op jit(solution)/shard_map/pallas_call | solution.py:556
  (49 shorter events, 0.8 us)
Async XLA Ops:
  0.6 4.2 %copy-start.7 = (f32[96]{0:T(128)S(1)}, f32[96]{0:T(128)}, u32[]{:S(2)}) copy-start(f32[96]{0:T(128)} %param.23) | copy-start | bytes 1156
  0.7 4.2 %copy-start.8 = (f32[96]{0:T(128)S(1)}, f32[96]{0:T(128)}, u32[]{:S(2)}) copy-start(f32[96]{0:T(128)} %param.25) | copy-start | bytes 1156
  0.7 4.2 %copy-start.9 = (f32[96]{0:T(128)S(1)}, f32[96]{0:T(128)}, u32[]{:S(2)}) copy-start(f32[96]{0:T(128)} %param.27) | copy-start | bytes 1156
  0.7 4.3 %copy-start.6 = (bf16[8,96,64]{1,2,0:T(8,128)(2,1)S(1)}, bf16[8,96,64]{1,2,0:T(8,128)(2,1)}, u32[]{:S(2)}) copy-start(bf16[8,96,64]{1,2,0:T(8,128)(2,1)} %param.22) | copy-start | bytes 294916
  0.7 4.3 %copy-start.4 = (bf16[27,64,64]{2,1,0:T(8,128)(2,1)S(1)}, bf16[27,64,64]{2,1,0:T(8,128)(2,1)}, u32[]{:S(2)}) copy-start(bf16[27,64,64]{2,1,0:T(8,128)(2,1)} %w_ref.2) | copy-start | bytes 663556
  4.7 1.3 %collective-permute-start = (bf16[2,32,512]{2,1,0:T(8,128)(2,1)S(1)}, bf16[2,32,512]{2,1,0:T(8,128)(2,1)S(1)}, u32[]{:S(2)}, u32[]{:S(2)}) collective-permute-start(bf16[2,32,512]{2,1,0:T(8,128)(2,1)S(1)} %slice_select_fusion), channel_id=1, source_target_pairs={{0,4},{1,5},{2,6},{3,7},{4,0},{5,1},{6,2},{7,3},{8,12},{9,13},{10,... | collective-permute-start | bytes 196616 | tf_op jit(solution)/shard_map/ppermute | solution.py:404
  5.6 7.4 %copy-start = (bf16[27,64,64]{2,1,0:T(8,128)(2,1)S(1)}, bf16[27,64,64]{2,1,0:T(8,128)(2,1)}, u32[]{:S(2)}) copy-start(bf16[27,64,64]{2,1,0:T(8,128)(2,1)} %w_ref.3) | copy-start | bytes 663556
  5.6 7.4 %copy-start.1 = (f32[64]{0:T(128)S(1)}, f32[64]{0:T(128)}, u32[]{:S(2)}) copy-start(f32[64]{0:T(128)} %param.19) | copy-start | bytes 772
  6.5 8.1 %collective-permute-start.4 = (bf16[18,2,1536]{2,1,0:T(2,128)(2,1)S(1)}, bf16[18,2,1536]{2,1,0:T(2,128)(2,1)S(1)}, u32[]{:S(2)}, u32[]{:S(2)}) collective-permute-start(bf16[18,2,1536]{2,1,0:T(2,128)(2,1)S(1)} %pad_maximum_fusion.5), channel_id=1, source_target_pairs={{0,8},{1,9},{2,10},{3,11},{4,12},{5,13},{6,14},{7,15},{8,0},{9,1},... | collective-permute-start | bytes 331784 | tf_op jit(solution)/shard_map/ppermute | solution.py:404
  6.8 8.2 %collective-permute-start.3 = (bf16[18,2,1536]{2,1,0:T(2,128)(2,1)S(1)}, bf16[18,2,1536]{2,1,0:T(2,128)(2,1)S(1)}, u32[]{:S(2)}, u32[]{:S(2)}) collective-permute-start(bf16[18,2,1536]{2,1,0:T(2,128)(2,1)S(1)} %pad_maximum_fusion.4), channel_id=1, source_target_pairs={{0,4},{1,5},{2,6},{3,7},{4,0},{5,1},{6,2},{7,3},{8,16},{9,17},{10,... | collective-permute-start | bytes 331784 | tf_op jit(solution)/shard_map/ppermute | solution.py:404
  9.8 10.7 %collective-permute-start.1 = (bf16[20,32,128]{2,1,0:T(8,128)(2,1)S(1)}, bf16[20,32,128]{2,1,0:T(8,128)(2,1)S(1)}, u32[]{:S(2)}, u32[]{:S(2)}) collective-permute-start(bf16[20,32,128]{2,1,0:T(8,128)(2,1)S(1)} %get-tuple-element.80), channel_id=1, source_target_pairs={{0,4},{1,2},{2,1},{3,7},{4,0},{5,6},{6,5},{7,3},{8,12},{9,10},{10,... | collective-permute-start | bytes 491528 | tf_op jit(solution)/shard_map/ppermute | solution.py:404
  9.9 10.6 %collective-permute-start.2 = (bf16[20,32,128]{2,1,0:T(8,128)(2,1)S(1)}, bf16[20,32,128]{2,1,0:T(8,128)(2,1)S(1)}, u32[]{:S(2)}, u32[]{:S(2)}) collective-permute-start(bf16[20,32,128]{2,1,0:T(8,128)(2,1)S(1)} %get-tuple-element.79), channel_id=1, source_target_pairs={{0,1},{1,0},{2,3},{3,2},{4,5},{5,4},{6,7},{7,6},{8,9},{9,8},{10,11... | collective-permute-start | bytes 491528 | tf_op jit(solution)/shard_map/ppermute | solution.py:404
  15.8 6.8 %collective-permute-start.5 = (bf16[20,2,768]{2,1,0:T(2,128)(2,1)S(1)}, bf16[20,2,768]{2,1,0:T(2,128)(2,1)S(1)}, u32[]{:S(2)}, u32[]{:S(2)}) collective-permute-start(bf16[20,2,768]{2,1,0:T(2,128)(2,1)S(1)} %bitcast.27), channel_id=1, source_target_pairs={{0,4},{1,2},{2,1},{3,7},{4,0},{5,6},{6,5},{7,3},{8,12},{9,10},{10,... | collective-permute-start | bytes 184328 | tf_op jit(solution)/shard_map/ppermute | solution.py:404
  15.9 6.8 %collective-permute-start.6 = (bf16[20,2,768]{2,1,0:T(2,128)(2,1)S(1)}, bf16[20,2,768]{2,1,0:T(2,128)(2,1)S(1)}, u32[]{:S(2)}, u32[]{:S(2)}) collective-permute-start(bf16[20,2,768]{2,1,0:T(2,128)(2,1)S(1)} %bitcast.26), channel_id=1, source_target_pairs={{0,1},{1,0},{2,3},{3,2},{4,5},{5,4},{6,7},{7,6},{8,9},{9,8},{10,11... | collective-permute-start | bytes 184328 | tf_op jit(solution)/shard_map/ppermute | solution.py:404
  20.6 2.2 %copy-start.5 = (f32[64]{0:T(128)S(1)}, f32[64]{0:T(128)}, u32[]{:S(2)}) copy-start(f32[64]{0:T(128)} %param.21) | copy-start | bytes 772
  22.8 5.4 %copy-start.2 = (bf16[27,96,96]{2,1,0:T(8,128)(2,1)S(1)}, bf16[27,96,96]{2,1,0:T(8,128)(2,1)}, u32[]{:S(2)}) copy-start(bf16[27,96,96]{2,1,0:T(8,128)(2,1)} %w_ref.4) | copy-start | bytes 1492996
  28.1 1.3 %collective-permute-start.7 = (bf16[2,20,512]{2,1,0:T(8,128)(2,1)S(1)}, bf16[2,20,512]{2,1,0:T(8,128)(2,1)S(1)}, u32[]{:S(2)}, u32[]{:S(2)}) collective-permute-start(bf16[2,20,512]{2,1,0:T(8,128)(2,1)S(1)} %slice_select_fusion.1), channel_id=1, source_target_pairs={{0,4},{1,5},{2,6},{3,7},{4,0},{5,1},{6,2},{7,3},{8,12},{9,13},{10,... | collective-permute-start | bytes 122888 | tf_op jit(solution)/shard_map/ppermute | solution.py:404
  29.5 4.4 %collective-permute-start.8 = (bf16[12,20,256]{2,1,0:T(8,128)(2,1)S(1)}, bf16[12,20,256]{2,1,0:T(8,128)(2,1)S(1)}, u32[]{:S(2)}, u32[]{:S(2)}) collective-permute-start(bf16[12,20,256]{2,1,0:T(8,128)(2,1)S(1)} %get-tuple-element.86), channel_id=1, source_target_pairs={{0,4},{1,2},{2,1},{3,7},{4,0},{5,6},{6,5},{7,3},{8,12},{9,10},{10,... | collective-permute-start | bytes 368648 | tf_op jit(solution)/shard_map/ppermute | solution.py:404
  29.7 6.1 %collective-permute-start.9 = (bf16[12,20,256]{2,1,0:T(8,128)(2,1)S(1)}, bf16[12,20,256]{2,1,0:T(8,128)(2,1)S(1)}, u32[]{:S(2)}, u32[]{:S(2)}) collective-permute-start(bf16[12,20,256]{2,1,0:T(8,128)(2,1)S(1)} %get-tuple-element.85), channel_id=1, source_target_pairs={{0,1},{1,0},{2,3},{3,2},{4,5},{5,4},{6,7},{7,6},{8,9},{9,8},{10,11... | collective-permute-start | bytes 368648 | tf_op jit(solution)/shard_map/ppermute | solution.py:404
  32.3 1.3 %copy-start.3 = (bf16[27,96,96]{2,1,0:T(8,128)(2,1)S(1)}, bf16[27,96,96]{2,1,0:T(8,128)(2,1)}, u32[]{:S(2)}) copy-start(bf16[27,96,96]{2,1,0:T(8,128)(2,1)} %w_ref.5) | copy-start | bytes 1492996
